TPU v7x, 32 devices: a whole 2x2x4 slice. The times are simulated.
32 devices in a mesh: dp: 4 (over z), seq: 8 (over y, x, core).
Axes of the slice: x: 2, y: 2, z: 4, core: 2. Of those that a mesh axis runs over, the one named last changes fastest.
Arguments:
- block_input: bfloat16 [4, 1024, 2048], P('dp', 'seq'), may hold values from -6 to 6
- cotangent: bfloat16 [4, 1024, 2048], P('dp', 'seq'), may hold values from -6 to 6
- doc_lengths: int32 [4, 4], P('dp'), may hold values from 1 to 1021, as said below
- owners: int32 [16], replicated, may hold values from 0 to 3, as said below
- master: float32 [2048, 32, 2048], P('seq', 'dp'), may hold values from -1.06066017 to 1.06066017
- first_moment: float32 [2048, 32, 2048], P('seq', 'dp'), may hold values from -256 to 256
- second_moment: float32 [2048, 32, 2048], P('seq', 'dp'), may hold values from 0 to 6144
Outputs:
- block_output: bfloat16 [4, 1024, 2048], P('dp', 'seq')
- input_grad: float32 [4, 1024, 2048], P('dp', 'seq')
- owned_grads: float32 [2048, 32, 2048], P('seq', 'dp')
- new_first: float32 [2048, 32, 2048], P('seq', 'dp')
- new_second: float32 [2048, 32, 2048], P('seq', 'dp')
- new_master: float32 [2048, 32, 2048], P('seq', 'dp')
Inputs may be any that keep to these rules, and one draw needn't show every extreme that they name: `owners`: no index of dp holds more than 8 units, and in every draw some index holds exactly 8. `doc_lengths`: each row holds 4 document lengths, each at least 1, that fill the 1024 positions of its sequence in order; in every draw some document has exactly 1021 positions.
All inputs are finite; a program needn't handle non-finite values.
Results may differ from a plain program's by a relative error of at most 0.012.
Values may be sent and summed in bfloat16 or wider, within the bound.
A program may use at most 704 MiB of HBM per device.

v0:
```python
import jax
import jax.numpy as jnp
from jax import lax
from jax.sharding import PartitionSpec as P

D = 2048
H = 16
HD = 128
FF = 8192
STEP = 5


norm_eps = 1e-05
rope_base = 10000.0
beta_one = 0.5
beta_two = 0.5
learn_rate = 0.01
decay_rate = 0.1
adam_eps = 1e-08
masked_score = -1000000000.0


def unit_slots(owners, per_owner):
    unit_count = owners.shape[0]
    unit_order = jnp.arange(unit_count, dtype=jnp.int32)
    matching = owners[:, None] == owners[None, :]
    before = unit_order[None, :] < unit_order[:, None]
    places = jnp.sum(jnp.where(matching & before, 1, 0), axis=1).astype(jnp.int32)
    return owners * per_owner + places


def norm_parts(values):
    center = values - jnp.mean(values, axis=-1, keepdims=True)
    spread = jnp.mean(center * center, axis=-1, keepdims=True)
    scale_inv = lax.rsqrt(spread + norm_eps)
    return (center * scale_inv, scale_inv)


def norm_back(normed, scale_inv, upstream):
    upstream_mean = jnp.mean(upstream, axis=-1, keepdims=True)
    cross_mean = jnp.mean(upstream * normed, axis=-1, keepdims=True)
    return scale_inv * (upstream - upstream_mean - normed * cross_mean)


def rope_tables(positions, head_dim):
    half_dim = head_dim // 2
    frequency = jnp.power(rope_base, -(jnp.arange(half_dim, dtype=jnp.float32) * 2.0) / head_dim)
    angles = positions[:, None] * frequency[None, :]
    cosine_half = jnp.cos(angles)
    sine_half = jnp.sin(angles)
    return (
        jnp.concatenate([cosine_half, cosine_half], axis=-1),
        jnp.concatenate([sine_half, sine_half], axis=-1),
    )


def rotate(values, cosine, sine):
    half_dim = values.shape[-1] // 2
    turned = jnp.concatenate([-values[..., half_dim:], values[..., :half_dim]], axis=-1)
    return values * cosine + turned * sine


def rotate_back(grads, cosine, sine):
    half_dim = grads.shape[-1] // 2
    scaled = grads * sine
    turned = jnp.concatenate([scaled[..., half_dim:], -scaled[..., :half_dim]], axis=-1)
    return grads * cosine + turned


def local(block_input, cotangent, doc_lengths, owners, master, first_moment, second_moment):
    seq_count = lax.axis_size("seq")
    dp_count = lax.axis_size("dp")
    seq_index = lax.axis_index("seq")
    dp_index = lax.axis_index("dp")
    seq_dev, shard_len, model_width = block_input.shape
    head_count = H
    head_dim = HD
    ff_blocks = FF // D
    shard_rows = master.shape[0]
    per_owner = master.shape[1]
    seq_len = shard_len * seq_count
    token_count = seq_dev * shard_len
    head_group = 4
    group_count = head_count // head_group
    score_scale = float(head_dim) ** (-0.5)
    unit_slot = unit_slots(owners, per_owner)
    own_slots = dp_index * per_owner + jnp.arange(per_owner, dtype=jnp.int32)
    occupied = jnp.any(unit_slot[None, :] == own_slots[:, None], axis=1)
    master_low = master.astype(jnp.bfloat16)
    every_slot = lax.all_gather(master_low, "dp", axis=1, tiled=True)
    weight_shard = jnp.take(every_slot, unit_slot, axis=1)
    bounds = [
        (0, 3),
        (3, 4),
        (4, 4 + ff_blocks),
        (4 + ff_blocks, 4 + 2 * ff_blocks),
        (4 + 2 * ff_blocks, 4 + 3 * ff_blocks),
    ]

    def gather_rows(group_id):
        return lax.all_gather(
            weight_shard[:, bounds[group_id][0] : bounds[group_id][1], :], "seq", axis=0, tiled=True
        )

    def gather_again(group_id):
        return lax.all_gather(
            weight_shard[:, bounds[group_id][0] : bounds[group_id][1], :], "seq", axis=0, tiled=True
        )

    tokens = block_input.astype(jnp.float32).reshape(token_count, model_width)
    normed_one, inv_one = norm_parts(tokens)
    normed_one_low = normed_one.astype(jnp.bfloat16)
    qkv_weight = gather_rows(0)
    qkv_proj = jnp.dot(
        normed_one_low,
        qkv_weight.reshape(model_width, 3 * model_width),
        preferred_element_type=jnp.float32,
    )
    qkv_proj = qkv_proj.reshape(seq_dev, shard_len, 3, head_count, head_dim)
    positions = seq_index * shard_len + jnp.arange(shard_len, dtype=jnp.int32)
    cosine_table, sine_table = rope_tables(positions.astype(jnp.float32), head_dim)
    cosine_table = cosine_table[:, None, :]
    sine_table = sine_table[:, None, :]
    queries = rotate(qkv_proj[:, :, 0], cosine_table, sine_table).astype(jnp.bfloat16)
    key_rows = rotate(qkv_proj[:, :, 1], cosine_table, sine_table).astype(jnp.bfloat16)
    value_rows = qkv_proj[:, :, 2].astype(jnp.bfloat16)
    all_keys, all_values = (
        lax.all_gather(key_rows, "seq", axis=1, tiled=True),
        lax.all_gather(value_rows, "seq", axis=1, tiled=True),
    )
    doc_ends = jnp.cumsum(doc_lengths, axis=1)
    key_pos = jnp.arange(seq_len, dtype=jnp.int32)
    key_doc = jnp.sum((key_pos[None, :, None] >= doc_ends[:, None, :]).astype(jnp.int32), axis=2)
    query_doc = jnp.sum(
        (positions[None, :, None] >= doc_ends[:, None, :]).astype(jnp.int32), axis=2
    )
    allowed = (query_doc[:, :, None] == key_doc[:, None, :]) & (
        key_pos[None, None, :] <= positions[None, :, None]
    )

    def head_slice(values, group_id):
        return lax.dynamic_slice_in_dim(values, group_id * head_group, head_group, axis=2)

    def scores_for(group_id):
        raw_scores = (
            jnp.einsum(
                "bqhd,bkhd->bhqk",
                head_slice(queries, group_id),
                head_slice(all_keys, group_id),
                preferred_element_type=jnp.float32,
            )
            * score_scale
        )
        return jnp.where(allowed[:, None], raw_scores, masked_score)

    def attend_group(group_id):
        scores = scores_for(group_id)
        row_peak = jnp.max(scores, axis=-1, keepdims=True)
        raised = jnp.exp(scores - row_peak)
        row_total = jnp.sum(raised, axis=-1, keepdims=True)
        probability = (raised / row_total).astype(jnp.bfloat16)
        mixed = jnp.einsum(
            "bhqk,bkhd->bqhd",
            probability,
            head_slice(all_values, group_id),
            preferred_element_type=jnp.float32,
        )
        return (mixed, (row_peak + jnp.log(row_total))[..., 0])

    mixed_groups, log_totals = lax.map(attend_group, jnp.arange(group_count, dtype=jnp.int32))
    attended = jnp.moveaxis(mixed_groups, 0, 2).reshape(token_count, model_width)
    attended_low = attended.astype(jnp.bfloat16)
    out_weight = gather_rows(1)
    attn_out = jnp.dot(
        attended_low,
        out_weight.reshape(model_width, model_width),
        preferred_element_type=jnp.float32,
    )
    residual = tokens + attn_out
    normed_two, inv_two = norm_parts(residual)
    normed_two_low = normed_two.astype(jnp.bfloat16)
    up_weight = gather_rows(2)
    gate_weight = gather_rows(3)
    up_proj = jnp.dot(
        normed_two_low,
        up_weight.reshape(model_width, ff_blocks * model_width),
        preferred_element_type=jnp.float32,
    )
    gate_proj = jnp.dot(
        normed_two_low,
        gate_weight.reshape(model_width, ff_blocks * model_width),
        preferred_element_type=jnp.float32,
    )
    gate_sig = jax.nn.sigmoid(gate_proj)
    silu_value = gate_proj * gate_sig
    hidden_low = (silu_value * up_proj).astype(jnp.bfloat16)
    hidden_blocks = hidden_low.reshape(token_count, ff_blocks, model_width)
    down_weight = gather_rows(4)
    ff_out = jnp.einsum(
        "tjr,rjc->tc", hidden_blocks, down_weight, preferred_element_type=jnp.float32
    )
    block_output = (residual + ff_out).astype(jnp.bfloat16).reshape(seq_dev, shard_len, model_width)
    back_weights = [gather_again(group_id) for group_id in range(5)]
    upstream = cotangent.reshape(token_count, model_width)
    upstream_full = upstream.astype(jnp.float32)
    hidden_grad = jnp.einsum(
        "tc,rjc->tjr", upstream, back_weights[4], preferred_element_type=jnp.float32
    ).reshape(token_count, ff_blocks * model_width)
    up_grad_low = (hidden_grad * silu_value).astype(jnp.bfloat16)
    gate_grad_low = (
        hidden_grad * up_proj * (gate_sig + gate_proj * gate_sig * (1.0 - gate_sig))
    ).astype(jnp.bfloat16)
    norm_two_grad = jnp.einsum(
        "tf,rf->tr",
        up_grad_low,
        back_weights[2].reshape(model_width, ff_blocks * model_width),
        preferred_element_type=jnp.float32,
    )
    norm_two_grad = norm_two_grad + jnp.einsum(
        "tf,rf->tr",
        gate_grad_low,
        back_weights[3].reshape(model_width, ff_blocks * model_width),
        preferred_element_type=jnp.float32,
    )
    residual_grad = upstream_full + norm_back(normed_two, inv_two, norm_two_grad)
    residual_grad_low = residual_grad.astype(jnp.bfloat16)
    mixed_grad = jnp.einsum(
        "tc,rc->tr",
        residual_grad_low,
        back_weights[1].reshape(model_width, model_width),
        preferred_element_type=jnp.float32,
    )
    mixed_grad = mixed_grad.astype(jnp.bfloat16).reshape(seq_dev, shard_len, head_count, head_dim)

    def attend_back(group_id):
        scores = scores_for(group_id)
        probability = jnp.exp(scores - log_totals[group_id][..., None])
        prob_low = probability.astype(jnp.bfloat16)
        part_grad = head_slice(mixed_grad, group_id)
        value_grad = jnp.einsum(
            "bhqk,bqhd->bkhd", prob_low, part_grad, preferred_element_type=jnp.float32
        )
        prob_grad = jnp.einsum(
            "bqhd,bkhd->bhqk",
            part_grad,
            head_slice(all_values, group_id),
            preferred_element_type=jnp.float32,
        )
        inner_sum = jnp.sum(probability * prob_grad, axis=-1, keepdims=True)
        score_grad = (probability * (prob_grad - inner_sum) * score_scale).astype(jnp.bfloat16)
        query_grad = jnp.einsum(
            "bhqk,bkhd->bqhd",
            score_grad,
            head_slice(all_keys, group_id),
            preferred_element_type=jnp.float32,
        )
        key_grad = jnp.einsum(
            "bhqk,bqhd->bkhd",
            score_grad,
            head_slice(queries, group_id),
            preferred_element_type=jnp.float32,
        )
        return (query_grad, key_grad, value_grad)

    query_parts, key_parts, value_parts = lax.map(
        attend_back, jnp.arange(group_count, dtype=jnp.int32)
    )
    query_grad = jnp.moveaxis(query_parts, 0, 2).reshape(seq_dev, shard_len, head_count, head_dim)
    key_full = jnp.moveaxis(key_parts, 0, 2).reshape(seq_dev, seq_len, head_count, head_dim)
    value_full = jnp.moveaxis(value_parts, 0, 2).reshape(seq_dev, seq_len, head_count, head_dim)
    key_grad, value_grad = (
        lax.psum_scatter(key_full, "seq", scatter_dimension=1, tiled=True),
        lax.psum_scatter(value_full, "seq", scatter_dimension=1, tiled=True),
    )
    qkv_grad = jnp.stack(
        [
            rotate_back(query_grad, cosine_table, sine_table),
            rotate_back(key_grad, cosine_table, sine_table),
            value_grad,
        ],
        axis=2,
    )
    qkv_grad_low = qkv_grad.astype(jnp.bfloat16).reshape(token_count, 3 * model_width)
    norm_one_grad = jnp.einsum(
        "tf,rf->tr",
        qkv_grad_low,
        back_weights[0].reshape(model_width, 3 * model_width),
        preferred_element_type=jnp.float32,
    )
    input_grad = (residual_grad + norm_back(normed_one, inv_one, norm_one_grad)).reshape(
        seq_dev, shard_len, model_width
    )

    def weight_grad(left_rows, right_rows, pattern):
        return lax.psum_scatter(
            jnp.einsum(pattern, left_rows, right_rows, preferred_element_type=jnp.float32),
            "seq",
            scatter_dimension=0,
            tiled=True,
        )

    grad_groups = [
        weight_grad(
            normed_one_low, qkv_grad_low.reshape(token_count, 3, model_width), "tr,tuc->ruc"
        ),
        weight_grad(
            attended_low, residual_grad_low.reshape(token_count, 1, model_width), "tr,tuc->ruc"
        ),
        weight_grad(
            normed_two_low, up_grad_low.reshape(token_count, ff_blocks, model_width), "tr,tuc->ruc"
        ),
        weight_grad(
            normed_two_low,
            gate_grad_low.reshape(token_count, ff_blocks, model_width),
            "tr,tuc->ruc",
        ),
        weight_grad(hidden_blocks, upstream, "tjr,tc->rjc"),
    ]
    grads_shard = jnp.concatenate(grad_groups, axis=1)
    spread_buffer = (
        jnp.zeros((shard_rows, per_owner * dp_count, model_width), jnp.float32)
        .at[:, unit_slot, :]
        .set(grads_shard)
    )
    owned_grads = lax.psum_scatter(spread_buffer, "dp", scatter_dimension=1, tiled=True)
    keep_slot = occupied.astype(jnp.float32)[None, :, None]
    new_first = (beta_one * first_moment + (1.0 - beta_one) * owned_grads) * keep_slot
    new_second = (
        beta_two * second_moment + (1.0 - beta_two) * owned_grads * owned_grads
    ) * keep_slot
    fixed_first = new_first / (1.0 - beta_one**STEP)
    fixed_second = new_second / (1.0 - beta_two**STEP)
    new_master = (
        master
        - learn_rate * (fixed_first / (jnp.sqrt(fixed_second) + adam_eps) + decay_rate * master)
    ) * keep_slot
    return (block_output, input_grad, owned_grads, new_first, new_second, new_master)


def solution(mesh):
    placed = (
        P("dp", "seq", None),
        P("dp", "seq", None),
        P("dp", None),
        P(),
        P("seq", "dp", None),
        P("seq", "dp", None),
        P("seq", "dp", None),
    )
    return jax.shard_map(
        local,
        mesh=mesh,
        in_specs=placed,
        out_specs=(
            P("dp", "seq", None),
            P("dp", "seq", None),
            P("seq", "dp", None),
            P("seq", "dp", None),
            P("seq", "dp", None),
            P("seq", "dp", None),
        ),
        check_vma=False,
    )
```

profile of v0, /device:TPU:0, one launch (start us, length us, event | category | flops | bytes accessed | tf_op | source)
XLA Modules:
  0.0 4661.5 jit_solution(3725648313762716780)
XLA Ops:
  26.4 562.3 %all-gather.10.cloned.1.call-done = bf16[256,32,2048]{2,0,1:T(8,128)(2,1)} async-done(((bf16[256,8,2048]{2,0,1:T(8,128)(2,1)}), bf16[256,32,2048]{2,0,1:T(8,128)(2,1)}) %all-gather.10.cloned.1.call-update) | async-done | bytes 33554448 | tf_op jit(solution)/shard_map/all_gather | solution.py:90
  618.2 122.9 %all-gather.12.cloned.1.call-done = bf16[2048,3,2048]{2,0,1:T(8,128)(2,1)} async-done(((bf16[256,3,2048]{2,0,1:T(8,128)(2,1)}), bf16[2048,3,2048]{2,0,1:T(8,128)(2,1)}) %all-gather.12.cloned.1.call-update) | async-done | bytes 25165840 | tf_op jit(solution)/shard_map/all_gather | solution.py:101
  741.1 33.3 copy.115
  833.2 33.4 all-gather.24.cloned.1.call-done
  890.8 32.5 all-gather.16.cloned.1.call-done
  928.6 157.9 %all-gather.22.cloned.1.call-done = bf16[2048,4,2048]{2,0,1:T(8,128)(2,1)} async-done(((bf16[256,4,2048]{2,0,1:T(8,128)(2,1)}), bf16[2048,4,2048]{2,0,1:T(8,128)(2,1)}) %all-gather.22.cloned.1.call-update) | async-done | bytes 33554448 | tf_op jit(solution)/shard_map/all_gather | solution.py:101
  1111.3 138.0 %all-gather.18.cloned.1.call-done = bf16[2048,4,2048]{2,0,1:T(8,128)(2,1)} async-done(((bf16[256,4,2048]{2,0,1:T(8,128)(2,1)}), bf16[2048,4,2048]{2,0,1:T(8,128)(2,1)}) %all-gather.18.cloned.1.call-update) | async-done | bytes 33554448 | tf_op jit(solution)/shard_map/all_gather | solution.py:101
  1249.2 43.6 copy.118
  1310.2 101.7 %all-gather.20.cloned.1.call-done = bf16[2048,4,2048]{2,0,1:T(8,128)(2,1)} async-done(((bf16[256,4,2048]{2,0,1:T(8,128)(2,1)}), bf16[2048,4,2048]{2,0,1:T(8,128)(2,1)}) %all-gather.20.cloned.1.call-update) | async-done | bytes 33554448 | tf_op jit(solution)/shard_map/all_gather | solution.py:101
  1412.0 42.7 copy.119
  1511.0 77.9 %while.31 = (s32[]{:T(128)}, f32[4,1,128,4,128]{2,4,3,1,0:T(8,128)}, f32[4,1,1024,4,128]{2,4,3,1,0:T(8,128)}, f32[4,1,1024,4,128]{2,4,3,1,0:T(8,128)}, s32[4]{0:...) while((s32[]{:T(128)}, ...), condition=%wide.region_16.17_spmd.clone.clone, body=%wide.region_14.16_spmd.clone.sunk.clone | while | flops 678824960 | bytes 31731968 | solution.py:265
  1593.7 66.7 %reduce-scatter.13.cloned.1.call-done = f32[1,128,16,128]{1,3,2,0:T(8,128)} async-done(((f32[1,1024,16,128]{1,3,2,0:T(8,128)}), f32[1,128,16,128]{1,3,2,0:T(8,128)}) %reduce-scatter.13.cloned.1.call-update) | async-done | bytes 1048592 | tf_op jit(solution)/shard_map/reduce_scatter | solution.py:273
  1664.6 71.4 %reduce-scatter.11.cloned.1.call-done = f32[1,128,16,128]{1,3,2,0:T(8,128)} async-done(((f32[1,1024,16,128]{1,3,2,0:T(8,128)}), f32[1,128,16,128]{1,3,2,0:T(8,128)}) %reduce-scatter.11.cloned.1.call-update) | async-done | bytes 1048592 | tf_op jit(solution)/shard_map/reduce_scatter | solution.py:272
  1783.3 42.4 fusion.83
  1827.8 25.1 fusion.80
  1856.2 26.3 convolution_bitcast_fusion.1
  1882.6 171.9 %reduce-scatter.15.cloned.1.call-done = f32[256,3,2048]{2,0,1:T(8,128)} async-done(((f32[2048,3,2048]{2,0,1:T(8,128)}), f32[256,3,2048]{2,0,1:T(8,128)}) %reduce-scatter.15.cloned.1.call-update) | async-done | bytes 6291472 | tf_op jit(solution)/shard_map/reduce_scatter | solution.py:295
  2060.8 114.1 %reduce-scatter.17.cloned.1.call-done = f32[256,1,2048]{2,0,1:T(8,128)} async-done(((f32[2048,1,2048]{2,0,1:T(8,128)}), f32[256,1,2048]{2,0,1:T(8,128)}) %reduce-scatter.17.cloned.1.call-update) | async-done | bytes 2097168 | tf_op jit(solution)/shard_map/reduce_scatter | solution.py:295
  2178.0 384.6 %reduce-scatter.19.cloned.1.call-done = f32[256,4,2048]{2,0,1:T(8,128)} async-done(((f32[2048,4,2048]{2,0,1:T(8,128)}), f32[256,4,2048]{2,0,1:T(8,128)}) %reduce-scatter.19.cloned.1.call-update) | async-done | bytes 8388624 | tf_op jit(solution)/shard_map/reduce_scatter | solution.py:295
  2570.4 379.4 %reduce-scatter.21.cloned.1.call-done = f32[256,4,2048]{2,0,1:T(8,128)} async-done(((f32[2048,4,2048]{2,0,1:T(8,128)}), f32[256,4,2048]{2,0,1:T(8,128)}) %reduce-scatter.21.cloned.1.call-update) | async-done | bytes 8388624 | tf_op jit(solution)/shard_map/reduce_scatter | solution.py:295
  2957.6 379.8 %reduce-scatter.23.cloned.1.call-done = f32[256,4,2048]{2,0,1:T(8,128)} async-done(((f32[2048,4,2048]{2,0,1:T(8,128)}), f32[256,4,2048]{2,0,1:T(8,128)}) %reduce-scatter.23.cloned.1.call-update) | async-done | bytes 8388624 | tf_op jit(solution)/shard_map/reduce_scatter | solution.py:295
  3366.5 59.8 %scatter_fusion = f32[256,32,2048]{2,0,1:T(8,128)} fusion(f32[256,32,2048]{2,0,1:T(8,128)} %broadcast_in_dim.103, s32[16]{0:T(128)S(1)} %copy-done.33, f32[16,256,2048]{2,1,0:T(8,128)} %bitcast.309), kind=kCustom, calls=%fused_computation.1 | custom fusion | bytes 100663360 | tf_op jit(solution)/shard_map/scatter | solution.py:323
  3455.1 1066.1 %reduce-scatter.25.cloned.1.call-done = f32[256,8,2048]{2,0,1:T(8,128)} async-done(((f32[256,32,2048]{2,0,1:T(8,128)}), f32[256,8,2048]{2,0,1:T(8,128)}) %reduce-scatter.25.cloned.1.call-update) | async-done | bytes 16777232
  4521.1 54.0 %subtract_multiply_fusion = (f32[256,8,2048]{2,0,1:T(8,128)}, f32[256,8,2048]{2,0,1:T(8,128)}, f32[256,8,2048]{2,0,1:T(8,128)}) fusion(f32[256,8,2048]{2,1,0:T(8,128)} %param.15, f32[8]{0:T(128)S(1)} %convert_element_type.170, f32[256,8,2048]{2,0,1:T(8,128)} %reduce-scatter.25.cloned.1.call-done, f32[256,8,2048]{2,1,0:T(8,128)} %param.17, ...), kind=kLoop, calls=%fused_computation.75 | loop fusion | flops 71303168 | bytes 117440544 | tf_op jit(solution)/shard_map/mul | solution.py:333
  (277 shorter events, 547.4 us)
Async XLA Ops:
  7.2 581.5 %all-gather.10.cloned.1.call-start = ((), (), s32[]{:S(2)}) async-start(), calls=%async_computation.8 | async-start | bytes 41943040 | tf_op jit(solution)/shard_map/all_gather | solution.py:90
  24.4 716.7 %all-gather.12.cloned.1.call-start = ((), (), s32[]{:S(2)}) async-start(), calls=%async_computation.9 | async-start | bytes 28311552 | tf_op jit(solution)/shard_map/all_gather | solution.py:101
  617.4 209.4 %all-gather.14.cloned.1.call-start = ((), (), s32[]{:S(2)}) async-start(), calls=%async_computation.10 | async-start | bytes 4718592 | tf_op jit(solution)/shard_map/all_gather | solution.py:128
  617.7 169.0 %copy-start.22 = (f32[128,128]{0,1:T(8,128)}, f32[128,128]{0,1:T(8,128)S(1)}, u32[]{:S(2)}) copy-start(f32[128,128]{0,1:T(8,128)S(1)} %get-tuple-element.372) | copy-start | bytes 196612
  617.7 169.0 %copy-start.24 = (f32[128,128]{0,1:T(8,128)}, f32[128,128]{0,1:T(8,128)S(1)}, u32[]{:S(2)}) copy-start(f32[128,128]{0,1:T(8,128)S(1)} %get-tuple-element.373) | copy-start | bytes 196612
  617.9 156.5 %copy-start.26 = (f32[128]{0:T(128)}, f32[128]{0:T(128)S(1)}, u32[]{:S(2)}) copy-start(f32[128]{0:T(128)S(1)} %broadcast_multiply_fusion.7) | copy-start | bytes 1540
  618.2 156.2 %copy-start.29 = (f32[128]{0:T(128)}, f32[128]{0:T(128)S(1)}, u32[]{:S(2)}) copy-start(f32[128]{0:T(128)S(1)} %add_rsqrt_fusion.1) | copy-start | bytes 1540
  789.2 77.4 %all-gather.24.cloned.1.call-start = ((), (), s32[]{:S(2)}) async-start(), calls=%async_computation.22 | async-start | bytes 4718592 | tf_op jit(solution)/shard_map/all_gather | solution.py:129
  791.4 132.0 %all-gather.16.cloned.1.call-start = ((), (), s32[]{:S(2)}) async-start(), calls=%async_computation.11 | async-start | bytes 9437184 | tf_op jit(solution)/shard_map/all_gather | solution.py:101
  793.7 292.8 %all-gather.22.cloned.1.call-start = ((), (), s32[]{:S(2)}) async-start(), calls=%async_computation.14 | async-start | bytes 37748736 | tf_op jit(solution)/shard_map/all_gather | solution.py:101
  803.7 445.5 %all-gather.18.cloned.1.call-start = ((), (), s32[]{:S(2)}) async-start(), calls=%async_computation.12 | async-start | bytes 37748736 | tf_op jit(solution)/shard_map/all_gather | solution.py:101
  804.5 607.5 %all-gather.20.cloned.1.call-start = ((), (), s32[]{:S(2)}) async-start(), calls=%async_computation.13 | async-start | bytes 37748736 | tf_op jit(solution)/shard_map/all_gather | solution.py:101
  805.2 855.2 %reduce-scatter.13.cloned.1.call-start = ((), (), s32[]{:S(2)}) async-start(), calls=%async_computation.16 | async-start | bytes 9437184 | tf_op jit(solution)/shard_map/reduce_scatter | solution.py:273
  928.1 574.7 %copy-start.1 = (f32[128,2048]{1,0:T(8,128)}, f32[128,2048]{1,0:T(8,128)S(1)}, u32[]{:S(2)}) copy-start(f32[128,2048]{1,0:T(8,128)S(1)} %get-tuple-element.367) | copy-start | bytes 3145732
  1589.0 147.0 %reduce-scatter.11.cloned.1.call-start = ((), (), s32[]{:S(2)}) async-start(), calls=%async_computation.15 | async-start | bytes 9437184 | tf_op jit(solution)/shard_map/reduce_scatter | solution.py:272
  1589.6 146.4 %copy-start.25 = (f32[128,128]{0,1:T(8,128)S(1)}, f32[128,128]{0,1:T(8,128)}, u32[]{:S(2)}) copy-start(f32[128,128]{0,1:T(8,128)} %copy-done.24) | copy-start | bytes 196612
  1589.6 464.9 %reduce-scatter.15.cloned.1.call-start = ((), (), s32[]{:S(2)}) async-start(), calls=%async_computation.17 | async-start | bytes 56623104 | tf_op jit(solution)/shard_map/reduce_scatter | solution.py:295
  1768.5 406.4 %reduce-scatter.17.cloned.1.call-start = ((), (), s32[]{:S(2)}) async-start(), calls=%async_computation.18 | async-start | bytes 18874368 | tf_op jit(solution)/shard_map/reduce_scatter | solution.py:295
  1781.2 781.4 %reduce-scatter.19.cloned.1.call-start = ((), (), s32[]{:S(2)}) async-start(), calls=%async_computation.19 | async-start | bytes 75497472 | tf_op jit(solution)/shard_map/reduce_scatter | solution.py:295
  1825.7 1124.2 %reduce-scatter.21.cloned.1.call-start = ((), (), s32[]{:S(2)}) async-start(), calls=%async_computation.20 | async-start | bytes 75497472 | tf_op jit(solution)/shard_map/reduce_scatter | solution.py:295
  1852.9 1484.5 %reduce-scatter.23.cloned.1.call-start = ((), (), s32[]{:S(2)}) async-start(), calls=%async_computation.21 | async-start | bytes 75497472 | tf_op jit(solution)/shard_map/reduce_scatter | solution.py:295
  1882.5 2638.6 %reduce-scatter.25.cloned.1.call-start = ((), (), s32[]{:S(2)}) async-start(), calls=%async_computation.23 | async-start | bytes 83886080
  4593.3 40.9 slice-start
  4593.3 40.9 slice-start.1
  (38 other events, 409.0 us)
Sparse Core Ops, SparseCore 0:
  24.5 564.0 all-gather.9
  617.5 123.5 all-gather.11
  789.3 37.4 all-gather.13
  829.1 37.4 all-gather.23
  868.9 54.3 all-gather.15
  925.7 160.7 all-gather.21
  1088.4 160.7 all-gather.17
  1251.1 160.7 all-gather.19
  1589.1 71.2 reduce-scatter.12
  1664.7 71.2 reduce-scatter.10
  1768.6 285.8 reduce-scatter.14
  2058.9 115.9 reduce-scatter.16
  2178.9 383.7 reduce-scatter.18
  2566.0 383.7 reduce-scatter.20
  2953.7 383.7 reduce-scatter.22
  3426.5 1094.6 reduce-scatter.24
where the time goes:
time: 4670 us; the launch traced here: 4660 us
  waiting for transfers between devices  3810 us (82%)
  local copies, waits for them, and re-layouts  410 us (9%)
  matrix products  335 us (7%)
  other arithmetic  82.4 us (2%)
    reduce_scatter x5, waiting for transfers between devices, weight_grad(): lax.psum_scatter(jnp.einsum(pattern, left_rows, right_rows, preferred_ele...  1430 us
    unnamed x17, waiting for transfers between devices  1070 us
    all_gather x1, waiting for transfers between devices, local(): every_slot = lax.all_gather(master_low, 'dp', axis=1, tiled=True)  562 us
    all_gather x5, waiting for transfers between devices, gather_rows(): lax.all_gather(weight_shard[:, bounds[group_id][0]:bounds[group_id][1], :...  553 us
    unnamed x104, local copies, waits for them, and re-layouts  146 us
    dot_general x5, matrix products, weight_grad(): jnp.einsum(pattern, left_rows, right_rows, preferred_element_type=jnp.flo...  126 us
    all_gather x3, local copies, waits for them, and re-layouts, gather_rows(): lax.all_gather(weight_shard[:, bounds[group_id][0]:bounds[group_id][1], :...  120 us
  transfers between devices with their start and end apart: 16, of which 16 were waited for; matrix products, arithmetic and copies ran while one was open for 7% of the time, Pallas kernels for 0%

commit v1 on v0

v1 whole, which is shorter than its diff:
```python
import jax
import jax.numpy as jnp
from jax import lax
from jax.sharding import PartitionSpec as P

D = 2048
H = 16
HD = 128
FF = 8192
STEP = 5


norm_eps = 1e-05
rope_base = 10000.0
beta_one = 0.5
beta_two = 0.5
learn_rate = 0.01
decay_rate = 0.1
adam_eps = 1e-08
masked_score = -1000000000.0


def unit_slots(owners, per_owner):
    unit_count = owners.shape[0]
    unit_order = jnp.arange(unit_count, dtype=jnp.int32)
    matching = owners[:, None] == owners[None, :]
    before = unit_order[None, :] < unit_order[:, None]
    places = jnp.sum(jnp.where(matching & before, 1, 0), axis=1).astype(jnp.int32)
    return owners * per_owner + places


def norm_parts(values):
    center = values - jnp.mean(values, axis=-1, keepdims=True)
    spread = jnp.mean(center * center, axis=-1, keepdims=True)
    scale_inv = lax.rsqrt(spread + norm_eps)
    return (center * scale_inv, scale_inv)


def norm_back(normed, scale_inv, upstream):
    upstream_mean = jnp.mean(upstream, axis=-1, keepdims=True)
    cross_mean = jnp.mean(upstream * normed, axis=-1, keepdims=True)
    return scale_inv * (upstream - upstream_mean - normed * cross_mean)


def rope_tables(positions, head_dim):
    half_dim = head_dim // 2
    frequency = jnp.power(rope_base, -(jnp.arange(half_dim, dtype=jnp.float32) * 2.0) / head_dim)
    angles = positions[:, None] * frequency[None, :]
    cosine_half = jnp.cos(angles)
    sine_half = jnp.sin(angles)
    return (
        jnp.concatenate([cosine_half, cosine_half], axis=-1),
        jnp.concatenate([sine_half, sine_half], axis=-1),
    )


def rotate(values, cosine, sine):
    half_dim = values.shape[-1] // 2
    turned = jnp.concatenate([-values[..., half_dim:], values[..., :half_dim]], axis=-1)
    return values * cosine + turned * sine


def rotate_back(grads, cosine, sine):
    half_dim = grads.shape[-1] // 2
    scaled = grads * sine
    turned = jnp.concatenate([scaled[..., half_dim:], -scaled[..., :half_dim]], axis=-1)
    return grads * cosine + turned


def local(block_input, cotangent, doc_lengths, owners, master, first_moment, second_moment):
    n_seq = lax.axis_size("seq")
    n_dp = lax.axis_size("dp")
    seq_index = lax.axis_index("seq")
    dp_index = lax.axis_index("dp")
    core = seq_index % 2
    _, shard_len, width = block_input.shape
    rows = master.shape[0]
    per_owner = master.shape[1]
    chips = n_seq // 2
    sub = rows // n_dp
    wide = width // n_dp
    half = chips * sub
    heads = H // n_seq
    head_cols = heads * HD
    seq_len = shard_len * n_seq
    ff_blocks = FF // D
    first_slots = min(4, per_owner)
    unit_count = owners.shape[0]
    bf = jnp.bfloat16
    f32 = jnp.float32
    score_scale = float(HD) ** (-0.5)

    unit_slot = unit_slots(owners, per_owner)
    place = unit_slot - owners * per_owner
    all_slots = jnp.arange(n_dp * per_owner, dtype=jnp.int32)
    match = unit_slot[None, :] == all_slots[:, None]
    slot_unit = jnp.sum(
        jnp.where(match, jnp.arange(unit_count, dtype=jnp.int32)[None, :] + 1, 0), axis=1
    ) - 1
    slot_unit = slot_unit.reshape(n_dp, per_owner)
    own_units = lax.dynamic_index_in_dim(slot_unit, dp_index, 0, keepdims=False)
    is_col = (own_units >= 4) & (own_units < 4 + 2 * ff_blocks)
    chip_groups = [[2 * k + c for k in range(chips)] for c in range(2)]

    def shift_pairs(k):
        return [(d, (d + k) % n_dp) for d in range(n_dp)]

    sibling = [(i, i ^ 1) for i in range(n_seq)]

    def pack(slots, col_flags):
        count = slots.shape[1]
        low = slots.astype(bf)
        col = low.reshape(rows, count, chips, 2, n_dp, sub).transpose(4, 1, 0, 3, 2, 5)
        col = col.reshape(n_dp, count, rows, wide)
        row = low.reshape(n_dp, sub, count, n_dp, wide).transpose(0, 2, 3, 1, 4)
        row = row.reshape(n_dp, count, rows, wide)
        return jnp.where(col_flags[None, :, None, None], col, row)

    def exchange(packed):
        parts = [lax.dynamic_index_in_dim(packed, dp_index, 0, keepdims=False)]
        for k in range(1, n_dp):
            send = lax.dynamic_index_in_dim(packed, (dp_index + k) % n_dp, 0, keepdims=False)
            parts.append(lax.ppermute(send, "dp", shift_pairs(k)))
        return parts

    first_parts = exchange(pack(master[:, :first_slots], is_col[:first_slots]))
    shift_of = (dp_index - owners) % n_dp
    first_table = jnp.stack(first_parts).reshape(n_dp * first_slots, rows, wide)
    att = jnp.take(first_table, (shift_of * first_slots + place)[:4], axis=0)
    att_rows = att[:3].reshape(3, n_dp, sub, n_seq // n_dp, head_cols)
    att_rows = att_rows.transpose(1, 3, 0, 2, 4).reshape(n_seq, 3, sub, head_cols)
    att_rows = lax.all_to_all(att_rows, "seq", 0, 0)
    att_all = lax.all_gather(
        jnp.concatenate(
            [att_rows.reshape(n_seq * 3 * sub, head_cols), att[3].reshape(-1, head_cols)], axis=0
        ),
        "dp",
        axis=0,
    )
    cut = n_seq * 3 * sub
    qkv_weight = att_all[:, :cut].reshape(n_dp, n_seq, 3, sub, head_cols)
    qkv_weight = qkv_weight.transpose(1, 0, 3, 2, 4).reshape(width, 3 * head_cols)
    out_weight = att_all[:, cut:].reshape(n_dp, n_dp, sub, wide).transpose(0, 2, 1, 3)
    out_weight = out_weight.reshape(rows, width)

    tokens = block_input.astype(f32).reshape(shard_len, width)
    normed_one, inv_one = norm_parts(tokens)
    normed_one_all = lax.all_gather(normed_one.astype(bf), "seq", axis=0, tiled=True)
    qkv_proj = jnp.dot(normed_one_all, qkv_weight, preferred_element_type=f32)
    qkv_proj = qkv_proj.reshape(seq_len, 3, heads, HD)
    positions = jnp.arange(seq_len, dtype=jnp.int32)
    cosine, sine = rope_tables(positions.astype(f32), HD)
    cosine = cosine[:, None, :]
    sine = sine[:, None, :]
    queries = rotate(qkv_proj[:, 0], cosine, sine).astype(bf)
    keys = rotate(qkv_proj[:, 1], cosine, sine).astype(bf)
    values = qkv_proj[:, 2].astype(bf)
    doc_ends = jnp.cumsum(doc_lengths[0])
    doc = jnp.sum((positions[:, None] >= doc_ends[None, :]).astype(jnp.int32), axis=1)
    allowed = (doc[:, None] == doc[None, :]) & (positions[None, :] <= positions[:, None])
    scores = jnp.einsum("qhd,khd->hqk", queries, keys, preferred_element_type=f32) * score_scale
    scores = jnp.where(allowed[None], scores, masked_score)
    peak = jnp.max(scores, axis=-1, keepdims=True)
    raised = jnp.exp(scores - peak)
    prob = raised / jnp.sum(raised, axis=-1, keepdims=True)
    prob_low = prob.astype(bf)
    attended = jnp.einsum("hqk,khd->qhd", prob_low, values, preferred_element_type=f32)
    attended_low = attended.reshape(seq_len, head_cols).astype(bf)
    attn_part = jnp.dot(attended_low, out_weight, preferred_element_type=f32).astype(bf)
    attn_out = lax.psum_scatter(attn_part, "seq", scatter_dimension=0, tiled=True)
    residual = tokens + attn_out.astype(f32)
    normed_two, inv_two = norm_parts(residual)

    if per_owner > first_slots:
        second = exchange(pack(master[:, first_slots:], is_col[first_slots:]))
        second_slots = per_owner - first_slots
        table = jnp.concatenate(
            [first_table, jnp.stack(second).reshape(n_dp * second_slots, rows, wide)], axis=0
        )
        index = jnp.where(
            place < first_slots,
            shift_of * first_slots + place,
            n_dp * first_slots + shift_of * second_slots + place - first_slots,
        )
    else:
        table = first_table
        index = shift_of * first_slots + place
    ff = jnp.take(table, index[4:], axis=0)
    ug = ff[: 2 * ff_blocks]
    mine = lax.dynamic_slice_in_dim(ug, core * half, half, axis=2)
    given = lax.dynamic_slice_in_dim(ug, (1 - core) * half, half, axis=2)
    got = lax.ppermute(given, "seq", sibling)
    ug = jnp.where(
        core == 0, jnp.concatenate([mine, got], axis=1), jnp.concatenate([got, mine], axis=1)
    )
    up_weight = lax.all_gather(
        ug[:ff_blocks], "seq", axis=1, tiled=True, axis_index_groups=chip_groups
    )
    gate_weight = lax.all_gather(
        ug[ff_blocks:], "seq", axis=1, tiled=True, axis_index_groups=chip_groups
    )
    down = ff[2 * ff_blocks :].reshape(ff_blocks, n_dp, sub, wide).transpose(0, 2, 1, 3)
    down_weight = lax.all_gather(
        down.reshape(ff_blocks, sub, width), "seq", axis=1, tiled=True, axis_index_groups=chip_groups
    )

    def gather_tokens(part):
        every = lax.all_gather(part, "dp", axis=0, tiled=True)
        other = lax.ppermute(every, "seq", sibling)
        return jnp.where(
            core == 0,
            jnp.concatenate([every, other], axis=0),
            jnp.concatenate([other, every], axis=0),
        )

    def scatter_tokens(part):
        count = n_dp * shard_len
        kept = lax.dynamic_slice_in_dim(part, core * count, count, axis=0)
        sent = lax.dynamic_slice_in_dim(part, (1 - core) * count, count, axis=0)
        got = lax.ppermute(sent.astype(bf), "seq", sibling)
        total = (kept + got.astype(f32)).astype(bf)
        return lax.psum_scatter(total, "dp", scatter_dimension=0, tiled=True).astype(f32)

    upstream = cotangent.reshape(shard_len, width)
    upstream_all = gather_tokens(upstream)
    normed_two_all = gather_tokens(normed_two.astype(bf))
    up_proj = jnp.einsum("tr,jrc->tjc", normed_two_all, up_weight, preferred_element_type=f32)
    gate_proj = jnp.einsum("tr,jrc->tjc", normed_two_all, gate_weight, preferred_element_type=f32)
    gate_sig = jax.nn.sigmoid(gate_proj)
    silu_value = gate_proj * gate_sig
    hidden_low = (silu_value * up_proj).astype(bf)
    ff_out = scatter_tokens(
        jnp.einsum("tjh,jhc->tc", hidden_low, down_weight, preferred_element_type=f32)
    )
    block_output = (residual + ff_out).astype(bf).reshape(block_input.shape)
    hidden_grad = jnp.einsum("tc,jhc->tjh", upstream_all, down_weight, preferred_element_type=f32)
    up_grad_low = (hidden_grad * silu_value).astype(bf)
    gate_grad_low = (
        hidden_grad * up_proj * (gate_sig + gate_proj * gate_sig * (1.0 - gate_sig))
    ).astype(bf)

    def chip_sum(part):
        return lax.psum_scatter(
            part.astype(bf),
            "seq",
            scatter_dimension=1,
            tiled=True,
            axis_index_groups=chip_groups,
        )

    down_grad = chip_sum(
        jnp.einsum("tjh,tc->jhc", hidden_low, upstream_all, preferred_element_type=f32)
    )
    up_grad = chip_sum(
        jnp.einsum("tr,tjc->jrc", normed_two_all, up_grad_low, preferred_element_type=f32)
    )
    gate_grad = chip_sum(
        jnp.einsum("tr,tjc->jrc", normed_two_all, gate_grad_low, preferred_element_type=f32)
    )
    norm_two_grad = jnp.einsum("tjc,jrc->tr", up_grad_low, up_weight, preferred_element_type=f32)
    norm_two_grad = norm_two_grad + jnp.einsum(
        "tjc,jrc->tr", gate_grad_low, gate_weight, preferred_element_type=f32
    )
    norm_two_grad = scatter_tokens(norm_two_grad)
    residual_grad = upstream.astype(f32) + norm_back(normed_two, inv_two, norm_two_grad)
    residual_grad_all = lax.all_gather(residual_grad.astype(bf), "seq", axis=0, tiled=True)

    attended_grad = jnp.einsum(
        "tc,rc->tr", residual_grad_all, out_weight, preferred_element_type=f32
    )
    attended_grad = attended_grad.astype(bf).reshape(seq_len, heads, HD)
    value_grad = jnp.einsum("hqk,qhd->khd", prob_low, attended_grad, preferred_element_type=f32)
    prob_grad = jnp.einsum("qhd,khd->hqk", attended_grad, values, preferred_element_type=f32)
    inner_sum = jnp.sum(prob * prob_grad, axis=-1, keepdims=True)
    score_grad = (prob * (prob_grad - inner_sum) * score_scale).astype(bf)
    query_grad = jnp.einsum("hqk,khd->qhd", score_grad, keys, preferred_element_type=f32)
    key_grad = jnp.einsum("hqk,qhd->khd", score_grad, queries, preferred_element_type=f32)
    qkv_grad = jnp.stack(
        [
            rotate_back(query_grad, cosine, sine),
            rotate_back(key_grad, cosine, sine),
            value_grad,
        ],
        axis=1,
    )
    qkv_grad_low = qkv_grad.astype(bf).reshape(seq_len, 3 * head_cols)
    norm_one_part = jnp.einsum("tf,rf->tr", qkv_grad_low, qkv_weight, preferred_element_type=f32)
    norm_one_grad = lax.psum_scatter(
        norm_one_part.astype(bf), "seq", scatter_dimension=0, tiled=True
    ).astype(f32)
    input_grad = (residual_grad + norm_back(normed_one, inv_one, norm_one_grad)).reshape(
        block_input.shape
    )

    qkv_wgrad = jnp.einsum(
        "tr,tf->rf", normed_one_all, qkv_grad_low, preferred_element_type=f32
    ).astype(bf)
    qkv_wgrad = qkv_wgrad.reshape(n_seq, n_dp, sub, 3, head_cols).transpose(1, 0, 3, 2, 4)
    out_wgrad = jnp.einsum(
        "tr,tc->rc", attended_low, residual_grad_all, preferred_element_type=f32
    ).astype(bf)
    out_wgrad = out_wgrad.reshape(n_dp, sub, n_dp, wide).transpose(0, 2, 1, 3)
    att_wgrad = lax.psum_scatter(
        jnp.concatenate(
            [
                qkv_wgrad.reshape(n_dp, cut, head_cols),
                out_wgrad.reshape(n_dp, -1, head_cols),
            ],
            axis=1,
        ),
        "dp",
        scatter_dimension=0,
        tiled=True,
    ).reshape(-1, head_cols)
    qkv_piece = att_wgrad[:cut].reshape(n_seq, 3, sub, head_cols)
    qkv_piece = lax.all_to_all(qkv_piece, "seq", 0, 0)
    qkv_piece = qkv_piece.reshape(n_dp, n_seq // n_dp, 3, sub, head_cols).transpose(2, 0, 3, 1, 4)
    qkv_piece = qkv_piece.reshape(3, rows, wide)
    out_piece = att_wgrad[cut:].reshape(1, rows, wide)

    ug_grad = jnp.concatenate([up_grad, gate_grad], axis=0)
    kept = lax.dynamic_slice_in_dim(ug_grad, core * rows, rows, axis=1)
    sent = lax.dynamic_slice_in_dim(ug_grad, (1 - core) * rows, rows, axis=1)
    got = lax.ppermute(sent, "seq", sibling)
    ug_piece = jnp.where(
        core == 0, jnp.concatenate([kept, got], axis=2), jnp.concatenate([got, kept], axis=2)
    )
    down_piece = down_grad.reshape(ff_blocks, sub, n_dp, wide).transpose(0, 2, 1, 3)
    down_piece = down_piece.reshape(ff_blocks, rows, wide)
    ff_pieces = jnp.concatenate([ug_piece, down_piece], axis=0)

    def give_back(pieces, low_slot, high_slot, skipped):
        parts = []
        for k in range(n_dp):
            target = (dp_index + k) % n_dp
            units = lax.dynamic_index_in_dim(slot_unit, target, 0, keepdims=False)
            units = jnp.maximum(units[low_slot:high_slot] - skipped, 0)
            send = jnp.take(pieces, units, axis=0)
            parts.append(send if k == 0 else lax.ppermute(send, "dp", shift_pairs(k)))
        order = (dp_index - jnp.arange(n_dp, dtype=jnp.int32)) % n_dp
        return jnp.take(jnp.stack(parts), order, axis=0)

    def unpack(parts, col_flags):
        count = parts.shape[1]
        col = parts.reshape(n_dp, count, rows, 2, chips, sub).transpose(2, 1, 4, 3, 0, 5)
        col = col.reshape(rows, count, width)
        row = parts.reshape(n_dp, count, n_dp, sub, wide).transpose(0, 3, 1, 2, 4)
        row = row.reshape(rows, count, width)
        return jnp.where(col_flags[None, :, None], col, row)

    grads = []
    if per_owner > first_slots:
        late = give_back(ff_pieces, first_slots, per_owner, 4)
        grads.append(unpack(late, is_col[first_slots:]))
    every_piece = jnp.concatenate([qkv_piece, out_piece, ff_pieces], axis=0)
    early = give_back(every_piece, 0, first_slots, 0)
    grads.insert(0, unpack(early, is_col[:first_slots]))
    keep_slot = (own_units >= 0)[None, :, None]
    owned_grads = jnp.where(keep_slot, jnp.concatenate(grads, axis=1).astype(f32), 0.0)
    keep_slot = keep_slot.astype(f32)
    new_first = (beta_one * first_moment + (1.0 - beta_one) * owned_grads) * keep_slot
    new_second = (
        beta_two * second_moment + (1.0 - beta_two) * owned_grads * owned_grads
    ) * keep_slot
    fixed_first = new_first / (1.0 - beta_one**STEP)
    fixed_second = new_second / (1.0 - beta_two**STEP)
    new_master = (
        master
        - learn_rate * (fixed_first / (jnp.sqrt(fixed_second) + adam_eps) + decay_rate * master)
    ) * keep_slot
    return (block_output, input_grad, owned_grads, new_first, new_second, new_master)


def solution(mesh):
    placed = (
        P("dp", "seq", None),
        P("dp", "seq", None),
        P("dp", None),
        P(),
        P("seq", "dp", None),
        P("seq", "dp", None),
        P("seq", "dp", None),
    )
    return jax.shard_map(
        local,
        mesh=mesh,
        in_specs=placed,
        out_specs=(
            P("dp", "seq", None),
            P("dp", "seq", None),
            P("seq", "dp", None),
            P("seq", "dp", None),
            P("seq", "dp", None),
            P("seq", "dp", None),
        ),
        check_vma=False,
    )
```

time: 4670 us -> 1670 us (0.36)
  waiting for transfers between devices: 3810 us -> 843 us
  matrix products: 335 us -> 177 us
  other arithmetic: 82.4 us -> 165 us
    reduce_scatter x7 -> x8, waiting for transfers between devices: 1570 us -> 315 us  [the longest x1 110 us: local(): lax.psum_scatter(jnp.concatenate([qkv_wgrad.reshape(n_dp, cut, head_cols)...]
    unnamed x17 -> x16, waiting for transfers between devices: 1070 us -> 0.94 us
    all_gather x8, waiting for transfers between devices: 1170 us -> 234 us  [the longest x1 72.8 us: local(): lax.all_gather(jnp.concatenate([att_rows.reshape(n_seq * 3 * sub, head_co...]
    ppermute x0 -> x18, waiting for transfers between devices: none -> 281 us  [the longest x6 243 us: exchange(): parts.append(lax.ppermute(send, 'dp', shift_pairs(k)))]
    dot_general x43 -> x20, matrix products: 335 us -> 169 us  [the longest x1 16.4 us: local(): jnp.einsum('hqk,khd->qhd', score_grad, keys, preferred_element_type=f32)]
    all_gather x3 -> x0, local copies, waits for them, and re-layouts: 120 us -> none  [gather_rows(): lax.all_gather(weight_shard[:, bounds[group_id][0]:bounds[group_id][1], :...]
    reshape x3 -> x24, local copies, waits for them, and re-layouts: 10.2 us -> 117 us  [the longest x4 50.8 us: unpack(): row = row.reshape(rows, count, width)]
    scatter x1 -> x0, local copies, waits for them, and re-layouts: 59.8 us -> none  [local(): spread_buffer = jnp.zeros((shard_rows, per_owner * dp_count, model_width)...]
  transfers between devices with their start and end apart: 16 -> 36, of which waited for: 16 -> 21; matrix products, arithmetic and copies ran while one was open for 7% -> 20% of each run, Pallas kernels for 0% -> 0%
where the time goes in v1:
time: 1670 us; the launch traced here: 1640 us
  waiting for transfers between devices  843 us (50%)
  local copies, waits for them, and re-layouts  409 us (24%)
  matrix products  177 us (11%)
  other arithmetic  165 us (10%)
  starting transfers between devices  32.3 us (2%)
    ppermute x6, waiting for transfers between devices, exchange(): parts.append(lax.ppermute(send, 'dp', shift_pairs(k)))  243 us
    unnamed x106, local copies, waits for them, and re-layouts  148 us
    reduce_scatter x1, waiting for transfers between devices, local(): lax.psum_scatter(jnp.concatenate([qkv_wgrad.reshape(n_dp, cut, head_cols)...  110 us
    reduce_scatter x2, waiting for transfers between devices, scatter_tokens(): lax.psum_scatter(total, 'dp', scatter_dimension=0, tiled=True).astype(f32)  83.9 us
    all_gather x1, waiting for transfers between devices, local(): lax.all_gather(jnp.concatenate([att_rows.reshape(n_seq * 3 * sub, head_co...  72.8 us
    reduce_scatter x1, waiting for transfers between devices, local(): lax.psum_scatter(attn_part, 'seq', scatter_dimension=0, tiled=True)  51.5 us
    all_gather x1, waiting for transfers between devices, local(): lax.all_gather(ug[:ff_blocks], 'seq', axis=1, tiled=True, axis_index_grou...  50.9 us
    reshape x4, local copies, waits for them, and re-layouts, unpack(): row = row.reshape(rows, count, width)  50.8 us
  transfers between devices with their start and end apart: 36, of which 21 were waited for; matrix products, arithmetic and copies ran while one was open for 20% of the time, Pallas kernels for 0%

profile of v1, /device:TPU:0, one launch (start us, length us, event | category | flops | bytes accessed | tf_op | source)
XLA Modules:
  0.0 1641.1 jit_solution(6192071547610746474)
XLA Ops:
  9.7 17.6 %copy.129 = f32[256,8,2048]{0,2,1:T(8,128)} copy(f32[256,8,2048]{2,1,0:T(8,128)} %param.17) | data formatting | bytes 33554432 | tf_op args[4]
  115.6 22.1 %collective-permute-done.2 = bf16[4,256,512]{1,2,0:T(8,128)(2,1)S(1)} collective-permute-done((bf16[4,256,512]{1,2,0:T(8,128)(2,1)S(1)}, bf16[4,256,512]{1,2,0:T(8,128)(2,1)S(1)}, u32[]{:S(2)}, u32[]{:S(2)}) %collective-permute-start.2) | collective-permute-done | bytes 1048608 | tf_op jit(solution)/shard_map/ppermute | solution.py:123
  137.7 66.1 %collective-permute-done.1 = bf16[4,256,512]{1,2,0:T(8,128)(2,1)S(1)} collective-permute-done((bf16[4,256,512]{1,2,0:T(8,128)(2,1)S(1)}, bf16[4,256,512]{1,2,0:T(8,128)(2,1)S(1)}, u32[]{:S(2)}, u32[]{:S(2)}) %collective-permute-start.1) | collective-permute-done | bytes 1048608 | tf_op jit(solution)/shard_map/ppermute | solution.py:123
  241.9 72.8 %all-gather.23.cloned.1.call-done = bf16[8192,256]{1,0:T(8,128)(2,1)} async-done(((bf16[2048,256]{1,0:T(8,128)(2,1)}), bf16[8192,256]{1,0:T(8,128)(2,1)}) %all-gather.23.cloned.1.call-update) | async-done | bytes 4194320 | tf_op jit(solution)/shard_map/all_gather | solution.py:133
  332.1 20.3 %all-gather.11.cloned.1.call-done = bf16[1024,2048]{1,0:T(8,128)(2,1)} async-done(((bf16[128,2048]{1,0:T(8,128)(2,1)}), bf16[1024,2048]{1,0:T(8,128)(2,1)}) %all-gather.11.cloned.1.call-update) | async-done | bytes 4194320 | tf_op jit(solution)/shard_map/all_gather | solution.py:148
  378.2 51.5 %reduce-scatter.9.cloned.1.call-done = bf16[128,2048]{1,0:T(8,128)(2,1)} async-done(((bf16[1024,2048]{1,0:T(8,128)(2,1)}), bf16[128,2048]{1,0:T(8,128)(2,1)}) %reduce-scatter.9.cloned.1.call-update) | async-done | bytes 524304 | tf_op jit(solution)/shard_map/reduce_scatter | solution.py:170
  442.8 49.5 %collective-permute-done.6 = bf16[4,256,512]{1,2,0:T(8,128)(2,1)} collective-permute-done((bf16[4,256,512]{1,2,0:T(8,128)(2,1)}, bf16[4,256,512]{1,2,0:T(8,128)(2,1)}, u32[]{:S(2)}, u32[]{:S(2)}) %collective-permute-start.6) | collective-permute-done | bytes 1048608 | tf_op jit(solution)/shard_map/ppermute | solution.py:123
  492.3 104.9 %collective-permute-done.5 = bf16[4,256,512]{1,2,0:T(8,128)(2,1)} collective-permute-done((bf16[4,256,512]{1,2,0:T(8,128)(2,1)}, bf16[4,256,512]{1,2,0:T(8,128)(2,1)}, u32[]{:S(2)}, u32[]{:S(2)}) %collective-permute-start.5) | collective-permute-done | bytes 1048608 | tf_op jit(solution)/shard_map/ppermute | solution.py:123
  634.7 50.9 %all-gather.17.cloned.1.call-done = bf16[4,2048,256]{2,1,0:T(8,128)(2,1)} async-done(((bf16[4,512,256]{2,1,0:T(8,128)(2,1)}), bf16[4,2048,256]{2,1,0:T(8,128)(2,1)}) %all-gather.17.cloned.1.call-update) | async-done | bytes 4194320 | tf_op jit(solution)/shard_map/all_gather | solution.py:196
  697.0 43.9 %all-gather.15.cloned.1.call-done = bf16[4,2048,256]{2,1,0:T(8,128)(2,1)} async-done(((bf16[4,512,256]{2,1,0:T(8,128)(2,1)}), bf16[4,2048,256]{2,1,0:T(8,128)(2,1)}) %all-gather.15.cloned.1.call-update) | async-done | bytes 4194320 | tf_op jit(solution)/shard_map/all_gather | solution.py:199
  752.2 43.4 %all-gather.19.cloned.1.call-done = bf16[4,256,2048]{2,1,0:T(8,128)(2,1)} async-done(((bf16[4,64,2048]{2,1,0:T(8,128)(2,1)}), bf16[4,256,2048]{2,1,0:T(8,128)(2,1)}) %all-gather.19.cloned.1.call-update) | async-done | bytes 4194320 | tf_op jit(solution)/shard_map/all_gather | solution.py:203
  840.2 44.0 %reduce-scatter.13.cloned.1.call-done = bf16[128,2048]{1,0:T(8,128)(2,1)} async-done(((bf16[512,2048]{1,0:T(8,128)(2,1)}), bf16[128,2048]{1,0:T(8,128)(2,1)}) %reduce-scatter.13.cloned.1.call-update) | async-done | bytes 524304 | tf_op jit(solution)/shard_map/reduce_scatter | solution.py:222
  957.8 16.4 %broadcast_multiply_fusion.1 = (f32[1024,2,128]{0,2,1:T(8,128)}, f32[1024,2,128]{0,2,1:T(8,128)}, f32[1024,2,128]{0,2,1:T(8,128)}) fusion(f32[1024,128]{0,1:T(8,128)S(1)} %copy-done.19, f32[1024,2,128]{0,2,1:T(8,128)S(1)} %fusion.37, bf16[1024,2,128]{0,2,1:T(8,128)(2,1)S(1)} %copy-done.26, f32[2,1024,1024]{1,2,0:T(8,128)} %fusion.71, ...), kind=kOutput, calls=%fused_computation.157 | convolution fusion | flops 552078336 | bytes 22028288 | tf_op jit(solution)/shard_map/hqk,khd->qhd/dot_general | solution.py:276
  1038.6 18.0 %copy.172 = f32[256,8,2048]{0,2,1:T(8,128)} copy(f32[256,8,2048]{2,1,0:T(8,128)} %param.18) | data formatting | bytes 33554432 | tf_op args[5]
  1056.5 17.9 %copy.173 = f32[256,8,2048]{0,2,1:T(8,128)} copy(f32[256,8,2048]{2,1,0:T(8,128)} %param.19) | data formatting | bytes 33554432 | tf_op args[6]
  1128.3 109.7 %reduce-scatter.17.cloned.1.call-done = bf16[1,2048,256]{2,1,0:T(8,128)(2,1)} async-done(((bf16[4,2048,256]{2,1,0:T(8,128)(2,1)}), bf16[1,2048,256]{2,1,0:T(8,128)(2,1)}) %reduce-scatter.17.cloned.1.call-update) | async-done | bytes 1048592 | tf_op jit(solution)/shard_map/reduce_scatter | solution.py:303
  1253.2 49.4 %reduce-scatter.15.cloned.1.call-done = bf16[128,2048]{1,0:T(8,128)(2,1)} async-done(((bf16[1024,2048]{1,0:T(8,128)(2,1)}), bf16[128,2048]{1,0:T(8,128)(2,1)}) %reduce-scatter.15.cloned.1.call-update) | async-done | bytes 524304 | tf_op jit(solution)/shard_map/reduce_scatter | solution.py:288
  1338.1 39.9 %reduce-scatter.11.cloned.1.call-done = bf16[128,2048]{1,0:T(8,128)(2,1)} async-done(((bf16[512,2048]{1,0:T(8,128)(2,1)}), bf16[128,2048]{1,0:T(8,128)(2,1)}) %reduce-scatter.11.cloned.1.call-update) | async-done | bytes 524304 | tf_op jit(solution)/shard_map/reduce_scatter | solution.py:222
  1384.3 30.7 %collective-permute-done.13 = bf16[4,256,512]{1,2,0:T(8,128)(2,1)} collective-permute-done((bf16[4,256,512]{1,2,0:T(8,128)(2,1)}, bf16[4,256,512]{1,2,0:T(8,128)(2,1)}, u32[]{:S(2)}, u32[]{:S(2)}) %collective-permute-start.13) | collective-permute-done | bytes 1048608 | tf_op jit(solution)/shard_map/ppermute | solution.py:339
  1516.3 44.2 %subtract_multiply_fusion = (f32[256,8,2048]{0,2,1:T(8,128)}, f32[256,8,2048]{0,2,1:T(8,128)}, f32[256,8,2048]{0,2,1:T(8,128)}, f32[256,8,2048]{0,2,1:T(8,128)}) fusion(f32[256,8,2048]{0,2,1:T(8,128)} %copy.129, f32[8]{0:T(128)S(1)} %copy-done.40, bf16[256,4,2048]{0,2,1:T(8,128)(2,1)} %bitcast_select_fusion, bf16[256,4,2048]{0,2,1:T(8,128)(2,1)} %bitcast_select_fusion.1, ...), kind=kLoop, calls=%fused_computation.19 | loop fusion | flops 83886080 | bytes 125829160 | tf_op jit(solution)/shard_map/mul | solution.py:367
  1560.5 18.4 %copy.179 = f32[256,8,2048]{2,1,0:T(8,128)} copy(f32[256,8,2048]{0,2,1:T(8,128)} %get-tuple-element.31) | data formatting | bytes 33554432
  1578.9 18.4 %copy.178 = f32[256,8,2048]{2,1,0:T(8,128)} copy(f32[256,8,2048]{0,2,1:T(8,128)} %get-tuple-element.32) | data formatting | bytes 33554432
  1597.3 18.4 %copy.177 = f32[256,8,2048]{2,1,0:T(8,128)} copy(f32[256,8,2048]{0,2,1:T(8,128)} %get-tuple-element.33) | data formatting | bytes 33554432
  1615.7 18.4 %copy.176 = f32[256,8,2048]{2,1,0:T(8,128)} copy(f32[256,8,2048]{0,2,1:T(8,128)} %get-tuple-element.58) | data formatting | bytes 33554432
  (348 shorter events, 639.2 us)
Async XLA Ops:
  114.1 89.7 %collective-permute-start.1 = (bf16[4,256,512]{1,2,0:T(8,128)(2,1)S(1)}, bf16[4,256,512]{1,2,0:T(8,128)(2,1)S(1)}, u32[]{:S(2)}, u32[]{:S(2)}) collective-permute-start(bf16[4,256,512]{1,2,0:T(8,128)(2,1)S(1)} %get-tuple-element.68), channel_id=1, source_target_pairs={{0,16},{8,24},{16,0},{24,8},{1,17},{9,25},{17,1},{25,9},{2,18},{10... | collective-permute-start | bytes 3145736 | tf_op jit(solution)/shard_map/ppermute | solution.py:123
  114.1 89.7 %collective-permute-start = (bf16[4,256,512]{1,2,0:T(8,128)(2,1)S(1)}, bf16[4,256,512]{1,2,0:T(8,128)(2,1)S(1)}, u32[]{:S(2)}, u32[]{:S(2)}) collective-permute-start(bf16[4,256,512]{1,2,0:T(8,128)(2,1)S(1)} %get-tuple-element.69), channel_id=1, source_target_pairs={{0,8},{8,16},{16,24},{24,0},{1,9},{9,17},{17,25},{25,1},{2,10},{10... | collective-permute-start | bytes 3145736 | tf_op jit(solution)/shard_map/ppermute | solution.py:123
  221.5 93.2 %all-gather.23.cloned.1.call-start = ((), (), s32[]{:S(2)}) async-start(), calls=%async_computation.24 | async-start | bytes 5242880 | tf_op jit(solution)/shard_map/all_gather | solution.py:133
  235.1 117.2 %all-gather.11.cloned.1.call-start = ((), (), s32[]{:S(2)}) async-start(), calls=%async_computation.10 | async-start | bytes 4718592 | tf_op jit(solution)/shard_map/all_gather | solution.py:148
  237.6 192.0 %reduce-scatter.9.cloned.1.call-start = ((), (), s32[]{:S(2)}) async-start(), calls=%async_computation.11 | async-start | bytes 4718592 | tf_op jit(solution)/shard_map/reduce_scatter | solution.py:170
  378.1 256.0 %all-gather.13.cloned.1.call-start = ((), (), s32[]{:S(2)}) async-start(), calls=%async_computation.12 | async-start | bytes 2621440 | tf_op jit(solution)/shard_map/all_gather | solution.py:208
  434.3 200.0 %all-gather.25.cloned.1.call-start = ((), (), s32[]{:S(2)}) async-start(), calls=%async_computation.25 | async-start | bytes 2621440 | tf_op jit(solution)/shard_map/all_gather | solution.py:208
  441.5 155.7 %collective-permute-start.5 = (bf16[4,256,512]{1,2,0:T(8,128)(2,1)}, bf16[4,256,512]{1,2,0:T(8,128)(2,1)}, u32[]{:S(2)}, u32[]{:S(2)}) collective-permute-start(bf16[4,256,512]{1,2,0:T(8,128)(2,1)} %get-tuple-element.72), channel_id=1, source_target_pairs={{0,16},{8,24},{16,0},{24,8},{1,17},{9,25},{17,1},{25,9},{2,18},{10... | collective-permute-start | bytes 3145736 | tf_op jit(solution)/shard_map/ppermute | solution.py:123
  441.5 155.7 %collective-permute-start.4 = (bf16[4,256,512]{1,2,0:T(8,128)(2,1)S(1)}, bf16[4,256,512]{1,2,0:T(8,128)(2,1)}, u32[]{:S(2)}, u32[]{:S(2)}) collective-permute-start(bf16[4,256,512]{1,2,0:T(8,128)(2,1)S(1)} %get-tuple-element.73), channel_id=1, source_target_pairs={{0,8},{8,16},{16,24},{24,0},{1,9},{9,17},{17,25},{25,1},{2,10},{10... | collective-permute-start | bytes 3145736 | tf_op jit(solution)/shard_map/ppermute | solution.py:123
  442.6 242.9 %all-gather.17.cloned.1.call-start = ((), (), s32[]{:S(2)}) async-start(), calls=%async_computation.14 | async-start | bytes 5242880 | tf_op jit(solution)/shard_map/all_gather | solution.py:196
  631.9 109.0 %all-gather.15.cloned.1.call-start = ((), (), s32[]{:S(2)}) async-start(), calls=%async_computation.13 | async-start | bytes 5242880 | tf_op jit(solution)/shard_map/all_gather | solution.py:199
  632.6 163.0 %all-gather.19.cloned.1.call-start = ((), (), s32[]{:S(2)}) async-start(), calls=%async_computation.15 | async-start | bytes 5242880 | tf_op jit(solution)/shard_map/all_gather | solution.py:203
  633.9 250.3 %reduce-scatter.13.cloned.1.call-start = ((), (), s32[]{:S(2)}) async-start(), calls=%async_computation.17 | async-start | bytes 2621440 | tf_op jit(solution)/shard_map/reduce_scatter | solution.py:222
  634.3 117.8 %collective-permute-start.9 = (bf16[512,2048]{1,0:T(8,128)(2,1)}, bf16[512,2048]{1,0:T(8,128)(2,1)}, u32[]{:S(2)}, u32[]{:S(2)}) collective-permute-start(bf16[512,2048]{1,0:T(8,128)(2,1)} %bitcast.334), channel_id=1, source_target_pairs={{0,1},{1,0},{2,3},{3,2},{4,5},{5,4},{6,7},{7,6},{8,9},{9,8},{10,11... | collective-permute-start | bytes 6291464 | tf_op jit(solution)/shard_map/ppermute | solution.py:209
  840.1 84.3 %all-gather.21.cloned.1.call-start = ((), (), s32[]{:S(2)}) async-start(), calls=%async_computation.18 | async-start | bytes 4718592 | tf_op jit(solution)/shard_map/all_gather | solution.py:266
  888.2 137.0 %reduce-scatter.19.cloned.1.call-start = ((), (), s32[]{:S(2)}) async-start(), calls=%async_computation.21 | async-start | bytes 5242880 | tf_op jit(solution)/shard_map/reduce_scatter | solution.py:243
  899.2 136.6 %reduce-scatter.21.cloned.1.call-start = ((), (), s32[]{:S(2)}) async-start(), calls=%async_computation.22 | async-start | bytes 5242880 | tf_op jit(solution)/shard_map/reduce_scatter | solution.py:243
  910.2 181.3 %reduce-scatter.23.cloned.1.call-start = ((), (), s32[]{:S(2)}) async-start(), calls=%async_computation.23 | async-start | bytes 5242880 | tf_op jit(solution)/shard_map/reduce_scatter | solution.py:243
  921.0 316.9 %reduce-scatter.17.cloned.1.call-start = ((), (), s32[]{:S(2)}) async-start(), calls=%async_computation.20 | async-start | bytes 5242880 | tf_op jit(solution)/shard_map/reduce_scatter | solution.py:303
  1003.2 299.4 %reduce-scatter.15.cloned.1.call-start = ((), (), s32[]{:S(2)}) async-start(), calls=%async_computation.19 | async-start | bytes 4718592 | tf_op jit(solution)/shard_map/reduce_scatter | solution.py:288
  1011.6 366.4 %reduce-scatter.11.cloned.1.call-start = ((), (), s32[]{:S(2)}) async-start(), calls=%async_computation.16 | async-start | bytes 2621440 | tf_op jit(solution)/shard_map/reduce_scatter | solution.py:222
  1113.3 131.0 %collective-permute-start.15 = (bf16[4,256,512]{1,2,0:T(8,128)(2,1)}, bf16[4,256,512]{1,2,0:T(8,128)(2,1)}, u32[]{:S(2)}, u32[]{:S(2)}) collective-permute-start(bf16[4,256,512]{1,2,0:T(8,128)(2,1)} %broadcast_select_fusion.5), channel_id=1, source_target_pairs={{0,8},{8,16},{16,24},{24,0},{1,9},{9,17},{17,25},{25,1},{2,10},{10... | collective-permute-start | bytes 3145736 | tf_op jit(solution)/shard_map/ppermute | solution.py:339
  1117.2 127.0 %collective-permute-start.16 = (bf16[4,256,512]{1,2,0:T(8,128)(2,1)}, bf16[4,256,512]{1,2,0:T(8,128)(2,1)}, u32[]{:S(2)}, u32[]{:S(2)}) collective-permute-start(bf16[4,256,512]{1,2,0:T(8,128)(2,1)} %broadcast_select_fusion.4), channel_id=1, source_target_pairs={{0,16},{8,24},{16,0},{24,8},{1,17},{9,25},{17,1},{25,9},{2,18},{10... | collective-permute-start | bytes 3145736 | tf_op jit(solution)/shard_map/ppermute | solution.py:339
  1120.9 123.4 %collective-permute-start.17 = (bf16[4,256,512]{1,2,0:T(8,128)(2,1)}, bf16[4,256,512]{1,2,0:T(8,128)(2,1)}, u32[]{:S(2)}, u32[]{:S(2)}) collective-permute-start(bf16[4,256,512]{1,2,0:T(8,128)(2,1)} %broadcast_select_fusion.3), channel_id=1, source_target_pairs={{0,24},{8,0},{16,8},{24,16},{1,25},{9,1},{17,9},{25,17},{2,26},{10... | collective-permute-start | bytes 3145736 | tf_op jit(solution)/shard_map/ppermute | solution.py:339
  (62 other events, 1521.7 us)
Sparse Core Ops, SparseCore 0:
  235.3 79.3 all-gather.22
  317.1 35.2 all-gather.10
  378.2 51.3 reduce-scatter.8
  434.5 104.7 all-gather.12
  540.8 58.9 all-gather.24
  632.0 53.5 all-gather.16
  688.1 52.6 all-gather.14
  742.9 52.6 all-gather.18
  840.2 43.8 reduce-scatter.12
  888.3 36.0 all-gather.20
  927.4 52.6 reduce-scatter.18
  983.1 52.6 reduce-scatter.20
  1038.8 52.6 reduce-scatter.22
  1093.8 144.1 reduce-scatter.16
  1241.1 61.3 reduce-scatter.14
  1304.8 73.1 reduce-scatter.10

commit v2 on v1

--- a/solution.py
+++ b/solution.py
@@ -1,6 +1,10 @@
+import functools
+
 import jax
 import jax.numpy as jnp
 from jax import lax
+from jax.experimental import pallas as pl
+from jax.experimental.pallas import tpu as pltpu
 from jax.sharding import PartitionSpec as P
 
 D = 2048
@@ -8,6 +12,9 @@
 HD = 128
 FF = 8192
 STEP = 5
+bf = jnp.bfloat16
+f32 = jnp.float32
+MESH = pl.DeviceIdType.MESH
 
 
 norm_eps = 1e-05
@@ -65,6 +72,454 @@
     scaled = grads * sine
     turned = jnp.concatenate([scaled[..., half_dim:], -scaled[..., :half_dim]], axis=-1)
     return grads * cosine + turned
+
+
+def pack_kernel(n_dp, chips, first_slots, flags, m_ref, *outs):
+    rb, slots, width = m_ref.shape
+    rows, wide = outs[0].shape[2:]
+    sub = rows // n_dp
+    start = pl.program_id(0) * rb
+    target = start // sub
+    inner = start % sub
+    for s in range(slots):
+        out = outs[0] if s < first_slots else outs[1]
+        t = s if s < first_slots else s - first_slots
+
+        @pl.when(flags[s] == 1)
+        def _():
+            x = m_ref[:, s, :].astype(bf)
+            for d in range(n_dp):
+                pieces = [
+                    x[:, (2 * k + c) * rows + d * sub : (2 * k + c) * rows + (d + 1) * sub]
+                    for c in range(2)
+                    for k in range(chips)
+                ]
+                out[d, t, pl.ds(pl.multiple_of(start, rb), rb), :] = jnp.concatenate(pieces, axis=1)
+
+        @pl.when(flags[s] == 0)
+        def _():
+            x = m_ref[:, s, :].astype(bf)
+            for g in range(n_dp):
+                out[target, t, pl.ds(pl.multiple_of(g * sub + inner, rb), rb), :] = x[
+                    :, g * wide : (g + 1) * wide
+                ]
+
+def pack(master, flags, n_dp, n_seq, first_slots):
+    rows, slots, width = master.shape
+    wide = width // n_dp
+    rb = min(32, rows // n_dp)
+    counts = [first_slots] + ([slots - first_slots] if slots > first_slots else [])
+    return pl.pallas_call(
+        functools.partial(pack_kernel, n_dp, n_seq // 2, first_slots),
+        out_shape=[jax.ShapeDtypeStruct((n_dp, c, rows, wide), bf) for c in counts],
+        grid_spec=pltpu.PrefetchScalarGridSpec(
+            num_scalar_prefetch=1,
+            grid=(rows // rb,),
+            in_specs=[pl.BlockSpec((rb, slots, width), lambda i, f: (i, 0, 0))],
+            out_specs=[
+                pl.BlockSpec((n_dp, c, rows, wide), lambda i, f: (0, 0, 0, 0)) for c in counts
+            ],
+        ),
+        compiler_params=pltpu.CompilerParams(vmem_limit_bytes=50 << 20),
+        name="pack",
+    )(flags, master)
+
+def adam_kernel(n_dp, chips, first_slots, n_groups, kinds, *refs):
+    cols = refs[:n_groups]
+    rws = refs[n_groups:2*n_groups]
+    m_ref, f_ref, s_ref, g_out, f_out, s_out, m_out = refs[2*n_groups:]
+    rb, slots, width = m_ref.shape
+    wide = width // n_dp
+    rows = wide * n_dp // (2 * chips)
+    sub = rows // n_dp
+    half = chips * sub
+
+    def finish(s, grad):
+        g_out[:, s, :] = grad
+        first = beta_one * f_ref[:, s, :] + (1.0 - beta_one) * grad
+        second = beta_two * s_ref[:, s, :] + (1.0 - beta_two) * grad * grad
+        f_out[:, s, :] = first
+        s_out[:, s, :] = second
+        fixed_first = first * (1.0 / (1.0 - beta_one**STEP))
+        fixed_second = second * (1.0 / (1.0 - beta_two**STEP))
+        old = m_ref[:, s, :]
+        m_out[:, s, :] = old - learn_rate * (
+            fixed_first / (jnp.sqrt(fixed_second) + adam_eps) + decay_rate * old
+        )
+
+    for s in range(slots):
+        grp = 0 if s < first_slots else 1
+        t = s if grp == 0 else s - first_slots
+
+        @pl.when(kinds[s] == 1)
+        def _():
+            pieces = []
+            for i in range(2 * chips):
+                k, c = i // 2, i % 2
+                for d in range(n_dp):
+                    pieces.append(cols[grp][d, t, :, c * half + k * sub : c * half + (k + 1) * sub])
+            finish(s, jnp.concatenate(pieces, axis=1).astype(f32))
+
+        @pl.when(kinds[s] == 0)
+        def _():
+            pieces = [rws[grp][0, t, g, :, :] for g in range(n_dp)]
+            finish(s, jnp.concatenate(pieces, axis=1).astype(f32))
+
+        @pl.when(kinds[s] == 2)
+        def _():
+            zero = jnp.zeros((rb, width), f32)
+            g_out[:, s, :] = zero
+            f_out[:, s, :] = zero
+            s_out[:, s, :] = zero
+            m_out[:, s, :] = zero
+
+def adam(kinds, grads, master, first_moment, second_moment, n_dp, n_seq, first_slots):
+    rows, slots, width = master.shape
+    wide = width // n_dp
+    sub = rows // n_dp
+    rb = min(16, sub)
+    state = pl.BlockSpec((rb, slots, width), lambda i, k: (i, 0, 0))
+    cols = [pl.BlockSpec((n_dp, g.shape[1], rb, wide), lambda i, k: (0, 0, i, 0)) for g in grads]
+    rws = [
+        pl.BlockSpec(
+            (1, g.shape[1], n_dp, rb, wide),
+            lambda i, k: (i * rb // sub, 0, 0, i % (sub // rb), 0),
+        )
+        for g in grads
+    ]
+    return pl.pallas_call(
+        functools.partial(adam_kernel, n_dp, n_seq // 2, first_slots, len(grads)),
+        out_shape=[jax.ShapeDtypeStruct(master.shape, f32)] * 4,
+        grid_spec=pltpu.PrefetchScalarGridSpec(
+            num_scalar_prefetch=1,
+            grid=(rows // rb,),
+            in_specs=cols + rws + [state] * 3,
+            out_specs=[state] * 4,
+        ),
+        compiler_params=pltpu.CompilerParams(vmem_limit_bytes=50 << 20),
+        name="adam",
+    )(
+        kinds,
+        *grads,
+        *[g.reshape(n_dp, g.shape[1], n_dp, sub, wide) for g in grads],
+        master,
+        first_moment,
+        second_moment,
+    )
+
+ANY = pl.BlockSpec(memory_space=pl.ANY)
+VMEM = pl.BlockSpec(memory_space=pltpu.VMEM)
+
+
+def line_place(kind):
+    seq_index = lax.axis_index("seq")
+    core = lax.rem(seq_index, 2)
+    if kind == "seq":
+        return seq_index // 2, lax.axis_size("seq") // 2, core
+    return lax.axis_index("dp"), lax.axis_size("dp"), core
+
+
+def line_device(kind, position, core):
+    if kind == "seq":
+        return (lax.axis_index("dp"), position * 2 + core)
+    return (position, lax.axis_index("seq") - lax.rem(lax.axis_index("seq"), 2) + core)
+
+
+def line_block(kind, position, count, core):
+    return position * 2 + core if kind == "seq" else core * count + position
+
+
+def greet(devices):
+    barrier = pltpu.get_barrier_semaphore()
+    for device in devices:
+        pl.semaphore_signal(barrier, inc=1, device_id=device, device_id_type=MESH)
+    pl.semaphore_wait(barrier, len(devices))
+
+
+def send(src, dst, send_sem, recv_sem, device):
+    return pltpu.make_async_remote_copy(
+        src_ref=src,
+        dst_ref=dst,
+        send_sem=send_sem,
+        recv_sem=recv_sem,
+        device_id=device,
+        device_id_type=MESH,
+    )
+
+
+def gather_kernel(kind, x_ref, out_ref, own_sem, send_sem, recv_sem, pass_sem, take_sem):
+    position, count, core = line_place(kind)
+    peers = [lax.rem(position + k, count) for k in range(count)]
+    sibling = line_device(kind, position, 1 - core)
+    greet([line_device(kind, p, core) for p in peers[1:]] + [sibling])
+    mine = line_block(kind, position, count, core)
+    own = pltpu.make_async_copy(x_ref, out_ref.at[mine], own_sem)
+    own.start()
+    copies = []
+    for k in range(count - 1, 0, -1):
+        copy = send(
+            x_ref, out_ref.at[mine], send_sem.at[k], recv_sem.at[k], line_device(kind, peers[k], core)
+        )
+        copy.start()
+        copies.append((k, copy))
+    first = send(x_ref, out_ref.at[mine], pass_sem.at[0], take_sem.at[0], sibling)
+    first.start()
+    passed = [first]
+    for k, copy in reversed(copies):
+        copy.wait_recv()
+        block = out_ref.at[line_block(kind, lax.rem(position + count - k, count), count, core)]
+        onward = send(block, block, pass_sem.at[k], take_sem.at[k], sibling)
+        onward.start()
+        passed.append(onward)
+    for k, copy in copies:
+        copy.wait_send()
+    for onward in passed:
+        onward.wait()
+    own.wait()
+
+
+def gather_blocks(x, kind, collective_id):
+    count = lax.axis_size("seq") // 2 if kind == "seq" else lax.axis_size("dp")
+    dma = pltpu.SemaphoreType.DMA
+    return pl.pallas_call(
+        functools.partial(gather_kernel, kind),
+        out_shape=jax.ShapeDtypeStruct((2 * count,) + x.shape, x.dtype),
+        in_specs=[ANY],
+        out_specs=ANY,
+        scratch_shapes=[dma, dma((count,)), dma((count,)), dma((count,)), dma((count,))],
+        compiler_params=pltpu.CompilerParams(
+            collective_id=collective_id, has_side_effects=True, vmem_limit_bytes=16 << 20
+        ),
+        name="gather_" + kind,
+    )(x)
+
+
+def sum_kernel(
+    kind, x_ref, out_ref, taken, sent, arrived, pass_sem, take_sem, send_sem, recv_sem
+):
+    position, count, core = line_place(kind)
+    peers = [lax.rem(position + k, count) for k in range(count)]
+    sibling = line_device(kind, position, 1 - core)
+    greet([line_device(kind, p, core) for p in peers[1:]] + [sibling])
+    order = list(range(count - 1, 0, -1)) + [0]
+    passed = {}
+    for k in order:
+        block = x_ref.at[line_block(kind, peers[k], count, 1 - core)]
+        passed[k] = send(block, taken.at[k], pass_sem.at[k], take_sem.at[k], sibling)
+        passed[k].start()
+    copies = {}
+    for k in order[:-1]:
+        passed[k].wait_recv()
+        own = x_ref[line_block(kind, peers[k], count, core)].astype(f32)
+        sent[k] = (own + taken[k].astype(f32)).astype(sent.dtype)
+        copies[k] = send(
+            sent.at[k],
+            arrived.at[k],
+            send_sem.at[k],
+            recv_sem.at[k],
+            line_device(kind, peers[k], core),
+        )
+        copies[k].start()
+    passed[0].wait_recv()
+    total = x_ref[line_block(kind, position, count, core)].astype(f32) + taken[0].astype(f32)
+    for k in range(1, count):
+        copies[k].wait_recv()
+        total = total + arrived[k].astype(f32)
+    out_ref[...] = total
+    for k in order:
+        passed[k].wait_send()
+    for k in order[:-1]:
+        copies[k].wait_send()
+
+
+def sum_blocks(x, kind, collective_id):
+    blocks, rows, columns = x.shape
+    count = blocks // 2
+    dma = pltpu.SemaphoreType.DMA
+    slots = pltpu.VMEM((count, rows, columns), x.dtype)
+    return pl.pallas_call(
+        functools.partial(sum_kernel, kind),
+        out_shape=jax.ShapeDtypeStruct((rows, columns), f32),
+        in_specs=[VMEM],
+        out_specs=VMEM,
+        scratch_shapes=[slots, slots, slots, dma((count,)), dma((count,)), dma((count,)), dma((count,))],
+        compiler_params=pltpu.CompilerParams(
+            collective_id=collective_id, has_side_effects=True, vmem_limit_bytes=40 << 20
+        ),
+        name="sum_" + kind,
+    )(x)
+
+
+def spread_kernel(
+    qkv_ref, out_ref, qkv_all, out_all, own_sem, a_send, a_recv, z_send, z_recv, o_send, o_recv
+):
+    n_seq = lax.axis_size("seq")
+    n_dp = lax.axis_size("dp")
+    seq_index = lax.axis_index("seq")
+    dp_index = lax.axis_index("dp")
+    seq_peers = [lax.rem(seq_index + k, n_seq) for k in range(n_seq)]
+    dp_peers = [lax.rem(dp_index + k, n_dp) for k in range(n_dp)]
+    greet([(dp_index, p) for p in seq_peers[1:]] + [(p, seq_index) for p in dp_peers[1:]])
+    own = [
+        pltpu.make_async_copy(qkv_ref.at[seq_index], qkv_all.at[seq_index, dp_index], own_sem.at[0]),
+        pltpu.make_async_copy(out_ref, out_all.at[dp_index], own_sem.at[1]),
+    ]
+    for copy in own:
+        copy.start()
+    landing = qkv_all.at[seq_index, dp_index]
+    across = {}
+    for k in range(1, n_seq):
+        across[k] = send(
+            qkv_ref.at[seq_peers[k]], landing, a_send.at[k], a_recv.at[k], (dp_index, seq_peers[k])
+        )
+        across[k].start()
+    outs = {}
+    for k in range(1, n_dp):
+        outs[k] = send(
+            out_ref, out_all.at[dp_index], o_send.at[k], o_recv.at[k], (dp_peers[k], seq_index)
+        )
+        outs[k].start()
+    along = []
+    for k in range(n_seq):
+        source = lax.rem(seq_index + n_seq - k, n_seq)
+        block = qkv_all.at[source, dp_index]
+        if k == 0:
+            block_src = qkv_ref.at[seq_index]
+        else:
+            across[k].wait_recv()
+            block_src = block
+        for j in range(n_dp - 1, 0, -1):
+            copy = send(block_src, block, z_send.at[k, j], z_recv.at[k, j], (dp_peers[j], seq_index))
+            copy.start()
+            along.append(copy)
+    for copy in along:
+        copy.wait()
+    for k in range(1, n_dp):
+        outs[k].wait()
+    for k in range(1, n_seq):
+        across[k].wait_send()
+    for copy in own:
+        copy.wait()
+
+
+def spread_attention(qkv, out, collective_id):
+    n_seq = lax.axis_size("seq")
+    n_dp = lax.axis_size("dp")
+    dma = pltpu.SemaphoreType.DMA
+    return pl.pallas_call(
+        spread_kernel,
+        out_shape=[
+            jax.ShapeDtypeStruct((n_seq, n_dp) + qkv.shape[1:], qkv.dtype),
+            jax.ShapeDtypeStruct((n_dp,) + out.shape, out.dtype),
+        ],
+        in_specs=[ANY, ANY],
+        out_specs=[ANY, ANY],
+        scratch_shapes=[
+            dma((2,)),
+            dma((n_seq,)),
+            dma((n_seq,)),
+            dma((n_seq, n_dp)),
+            dma((n_seq, n_dp)),
+            dma((n_dp,)),
+            dma((n_dp,)),
+        ],
+        compiler_params=pltpu.CompilerParams(
+            collective_id=collective_id, has_side_effects=True, vmem_limit_bytes=16 << 20
+        ),
+        name="spread_attention",
+    )(qkv, out)
+
+
+def collect_kernel(
+    qkv_ref, out_ref, qkv_sum, out_sum, qkv_in, out_in, total, own_sem, z_send, z_recv, o_send, o_recv,
+    a_send, a_recv
+):
+    n_seq = lax.axis_size("seq")
+    n_dp = lax.axis_size("dp")
+    seq_index = lax.axis_index("seq")
+    dp_index = lax.axis_index("dp")
+    seq_peers = [lax.rem(seq_index + k, n_seq) for k in range(n_seq)]
+    dp_peers = [lax.rem(dp_index + k, n_dp) for k in range(n_dp)]
+    greet([(dp_index, p) for p in seq_peers[1:]] + [(p, seq_index) for p in dp_peers[1:]])
+    along = {}
+    for k in list(range(1, n_seq)) + [0]:
+        for j in range(n_dp - 1, 0, -1):
+            along[k, j] = send(
+                qkv_ref.at[seq_peers[k], dp_peers[j]],
+                qkv_in.at[k, j],
+                z_send.at[k, j],
+                z_recv.at[k, j],
+                (dp_peers[j], seq_index),
+            )
+            along[k, j].start()
+    outs = {}
+    for j in range(n_dp - 1, 0, -1):
+        outs[j] = send(
+            out_ref.at[dp_peers[j]], out_in.at[j], o_send.at[j], o_recv.at[j], (dp_peers[j], seq_index)
+        )
+        outs[j].start()
+    across = {}
+    for k in list(range(1, n_seq)) + [0]:
+        value = qkv_ref[seq_peers[k], dp_index].astype(f32)
+        for j in range(1, n_dp):
+            along[k, j].wait_recv()
+            value = value + qkv_in[k, j].astype(f32)
+        total[k] = value.astype(total.dtype)
+        if k:
+            across[k] = send(
+                total.at[k],
+                qkv_sum.at[seq_index],
+                a_send.at[k],
+                a_recv.at[k],
+                (dp_index, seq_peers[k]),
+            )
+            across[k].start()
+    own = pltpu.make_async_copy(total.at[0], qkv_sum.at[seq_index], own_sem)
+    own.start()
+    value = out_ref[dp_index].astype(f32)
+    for j in range(1, n_dp):
+        outs[j].wait_recv()
+        value = value + out_in[j].astype(f32)
+    out_sum[...] = value.astype(out_sum.dtype)
+    for copy in along.values():
+        copy.wait_send()
+    for copy in outs.values():
+        copy.wait_send()
+    for copy in across.values():
+        copy.wait()
+    own.wait()
+
+
+def collect_attention(qkv, out, collective_id):
+    n_seq = lax.axis_size("seq")
+    n_dp = lax.axis_size("dp")
+    dma = pltpu.SemaphoreType.DMA
+    tail = qkv.shape[2:]
+    return pl.pallas_call(
+        collect_kernel,
+        out_shape=[
+            jax.ShapeDtypeStruct((n_seq,) + tail, qkv.dtype),
+            jax.ShapeDtypeStruct(out.shape[1:], out.dtype),
+        ],
+        in_specs=[VMEM, VMEM],
+        out_specs=[VMEM, VMEM],
+        scratch_shapes=[
+            pltpu.VMEM((n_seq, n_dp) + tail, qkv.dtype),
+            pltpu.VMEM((n_dp,) + out.shape[1:], out.dtype),
+            pltpu.VMEM((n_seq,) + tail, qkv.dtype),
+            dma,
+            dma((n_seq, n_dp)),
+            dma((n_seq, n_dp)),
+            dma((n_dp,)),
+            dma((n_dp,)),
+            dma((n_seq,)),
+            dma((n_seq,)),
+        ],
+        compiler_params=pltpu.CompilerParams(
+            collective_id=collective_id, has_side_effects=True, vmem_limit_bytes=40 << 20
+        ),
+        name="collect_attention",
+    )(qkv, out)
 
 
 def local(block_input, cotangent, doc_lengths, owners, master, first_moment, second_moment):
@@ -86,8 +541,6 @@
     ff_blocks = FF // D
     first_slots = min(4, per_owner)
     unit_count = owners.shape[0]
-    bf = jnp.bfloat16
-    f32 = jnp.float32
     score_scale = float(HD) ** (-0.5)
 
     unit_slot = unit_slots(owners, per_owner)
@@ -102,50 +555,24 @@
     is_col = (own_units >= 4) & (own_units < 4 + 2 * ff_blocks)
     chip_groups = [[2 * k + c for k in range(chips)] for c in range(2)]
 
-    def shift_pairs(k):
-        return [(d, (d + k) % n_dp) for d in range(n_dp)]
-
     sibling = [(i, i ^ 1) for i in range(n_seq)]
 
-    def pack(slots, col_flags):
-        count = slots.shape[1]
-        low = slots.astype(bf)
-        col = low.reshape(rows, count, chips, 2, n_dp, sub).transpose(4, 1, 0, 3, 2, 5)
-        col = col.reshape(n_dp, count, rows, wide)
-        row = low.reshape(n_dp, sub, count, n_dp, wide).transpose(0, 2, 3, 1, 4)
-        row = row.reshape(n_dp, count, rows, wide)
-        return jnp.where(col_flags[None, :, None, None], col, row)
-
     def exchange(packed):
-        parts = [lax.dynamic_index_in_dim(packed, dp_index, 0, keepdims=False)]
-        for k in range(1, n_dp):
-            send = lax.dynamic_index_in_dim(packed, (dp_index + k) % n_dp, 0, keepdims=False)
-            parts.append(lax.ppermute(send, "dp", shift_pairs(k)))
-        return parts
-
-    first_parts = exchange(pack(master[:, :first_slots], is_col[:first_slots]))
-    shift_of = (dp_index - owners) % n_dp
-    first_table = jnp.stack(first_parts).reshape(n_dp * first_slots, rows, wide)
-    att = jnp.take(first_table, (shift_of * first_slots + place)[:4], axis=0)
+        return lax.all_to_all(packed, "dp", 0, 0)
+
+    packed = pack(master, is_col.astype(jnp.int32), n_dp, n_seq, first_slots)
+    first_table = exchange(packed[0]).reshape(n_dp * first_slots, rows, wide)
+    att = jnp.take(first_table, (owners * first_slots + place)[:4], axis=0)
     att_rows = att[:3].reshape(3, n_dp, sub, n_seq // n_dp, head_cols)
-    att_rows = att_rows.transpose(1, 3, 0, 2, 4).reshape(n_seq, 3, sub, head_cols)
-    att_rows = lax.all_to_all(att_rows, "seq", 0, 0)
-    att_all = lax.all_gather(
-        jnp.concatenate(
-            [att_rows.reshape(n_seq * 3 * sub, head_cols), att[3].reshape(-1, head_cols)], axis=0
-        ),
-        "dp",
-        axis=0,
-    )
-    cut = n_seq * 3 * sub
-    qkv_weight = att_all[:, :cut].reshape(n_dp, n_seq, 3, sub, head_cols)
-    qkv_weight = qkv_weight.transpose(1, 0, 3, 2, 4).reshape(width, 3 * head_cols)
-    out_weight = att_all[:, cut:].reshape(n_dp, n_dp, sub, wide).transpose(0, 2, 1, 3)
+    att_rows = att_rows.transpose(1, 3, 2, 0, 4).reshape(n_seq, sub, 3 * head_cols)
+    att_out = att[3].reshape(n_dp, sub, wide).transpose(1, 0, 2).reshape(sub, width)
+    qkv_weight, out_weight = spread_attention(att_rows, att_out, 1)
+    qkv_weight = qkv_weight.reshape(width, 3 * head_cols)
     out_weight = out_weight.reshape(rows, width)
 
     tokens = block_input.astype(f32).reshape(shard_len, width)
     normed_one, inv_one = norm_parts(tokens)
-    normed_one_all = lax.all_gather(normed_one.astype(bf), "seq", axis=0, tiled=True)
+    normed_one_all = gather_blocks(normed_one.astype(bf), "seq", 2).reshape(seq_len, width)
     qkv_proj = jnp.dot(normed_one_all, qkv_weight, preferred_element_type=f32)
     qkv_proj = qkv_proj.reshape(seq_len, 3, heads, HD)
     positions = jnp.arange(seq_len, dtype=jnp.int32)
@@ -167,24 +594,22 @@
     attended = jnp.einsum("hqk,khd->qhd", prob_low, values, preferred_element_type=f32)
     attended_low = attended.reshape(seq_len, head_cols).astype(bf)
     attn_part = jnp.dot(attended_low, out_weight, preferred_element_type=f32).astype(bf)
-    attn_out = lax.psum_scatter(attn_part, "seq", scatter_dimension=0, tiled=True)
-    residual = tokens + attn_out.astype(f32)
+    attn_out = sum_blocks(attn_part.reshape(n_seq, shard_len, width), "seq", 3)
+    residual = tokens + attn_out
     normed_two, inv_two = norm_parts(residual)
 
     if per_owner > first_slots:
-        second = exchange(pack(master[:, first_slots:], is_col[first_slots:]))
         second_slots = per_owner - first_slots
-        table = jnp.concatenate(
-            [first_table, jnp.stack(second).reshape(n_dp * second_slots, rows, wide)], axis=0
-        )
+        second = exchange(packed[1]).reshape(n_dp * second_slots, rows, wide)
+        table = jnp.concatenate([first_table, second], axis=0)
         index = jnp.where(
             place < first_slots,
-            shift_of * first_slots + place,
-            n_dp * first_slots + shift_of * second_slots + place - first_slots,
+            owners * first_slots + place,
+            n_dp * first_slots + owners * second_slots + place - first_slots,
         )
     else:
         table = first_table
-        index = shift_of * first_slots + place
+        index = owners * first_slots + place
     ff = jnp.take(table, index[4:], axis=0)
     ug = ff[: 2 * ff_blocks]
     mine = lax.dynamic_slice_in_dim(ug, core * half, half, axis=2)
@@ -205,21 +630,10 @@
     )
 
     def gather_tokens(part):
-        every = lax.all_gather(part, "dp", axis=0, tiled=True)
-        other = lax.ppermute(every, "seq", sibling)
-        return jnp.where(
-            core == 0,
-            jnp.concatenate([every, other], axis=0),
-            jnp.concatenate([other, every], axis=0),
-        )
+        return gather_blocks(part, "dp", 4).reshape(-1, width)
 
     def scatter_tokens(part):
-        count = n_dp * shard_len
-        kept = lax.dynamic_slice_in_dim(part, core * count, count, axis=0)
-        sent = lax.dynamic_slice_in_dim(part, (1 - core) * count, count, axis=0)
-        got = lax.ppermute(sent.astype(bf), "seq", sibling)
-        total = (kept + got.astype(f32)).astype(bf)
-        return lax.psum_scatter(total, "dp", scatter_dimension=0, tiled=True).astype(f32)
+        return sum_blocks(part.astype(bf).reshape(2 * n_dp, shard_len, width), "dp", 5)
 
     upstream = cotangent.reshape(shard_len, width)
     upstream_all = gather_tokens(upstream)
@@ -263,7 +677,7 @@
     )
     norm_two_grad = scatter_tokens(norm_two_grad)
     residual_grad = upstream.astype(f32) + norm_back(normed_two, inv_two, norm_two_grad)
-    residual_grad_all = lax.all_gather(residual_grad.astype(bf), "seq", axis=0, tiled=True)
+    residual_grad_all = gather_blocks(residual_grad.astype(bf), "seq", 2).reshape(seq_len, width)
 
     attended_grad = jnp.einsum(
         "tc,rc->tr", residual_grad_all, out_weight, preferred_element_type=f32
@@ -285,9 +699,9 @@
     )
     qkv_grad_low = qkv_grad.astype(bf).reshape(seq_len, 3 * head_cols)
     norm_one_part = jnp.einsum("tf,rf->tr", qkv_grad_low, qkv_weight, preferred_element_type=f32)
-    norm_one_grad = lax.psum_scatter(
-        norm_one_part.astype(bf), "seq", scatter_dimension=0, tiled=True
-    ).astype(f32)
+    norm_one_grad = sum_blocks(
+        norm_one_part.astype(bf).reshape(n_seq, shard_len, width), "seq", 3
+    )
     input_grad = (residual_grad + norm_back(normed_one, inv_one, norm_one_grad)).reshape(
         block_input.shape
     )
@@ -295,28 +709,15 @@
     qkv_wgrad = jnp.einsum(
         "tr,tf->rf", normed_one_all, qkv_grad_low, preferred_element_type=f32
     ).astype(bf)
-    qkv_wgrad = qkv_wgrad.reshape(n_seq, n_dp, sub, 3, head_cols).transpose(1, 0, 3, 2, 4)
     out_wgrad = jnp.einsum(
         "tr,tc->rc", attended_low, residual_grad_all, preferred_element_type=f32
     ).astype(bf)
-    out_wgrad = out_wgrad.reshape(n_dp, sub, n_dp, wide).transpose(0, 2, 1, 3)
-    att_wgrad = lax.psum_scatter(
-        jnp.concatenate(
-            [
-                qkv_wgrad.reshape(n_dp, cut, head_cols),
-                out_wgrad.reshape(n_dp, -1, head_cols),
-            ],
-            axis=1,
-        ),
-        "dp",
-        scatter_dimension=0,
-        tiled=True,
-    ).reshape(-1, head_cols)
-    qkv_piece = att_wgrad[:cut].reshape(n_seq, 3, sub, head_cols)
-    qkv_piece = lax.all_to_all(qkv_piece, "seq", 0, 0)
-    qkv_piece = qkv_piece.reshape(n_dp, n_seq // n_dp, 3, sub, head_cols).transpose(2, 0, 3, 1, 4)
+    qkv_piece, out_piece = collect_attention(
+        qkv_wgrad.reshape(n_seq, n_dp, sub, 3 * head_cols), out_wgrad.reshape(n_dp, sub, width), 6
+    )
+    qkv_piece = qkv_piece.reshape(n_dp, n_seq // n_dp, sub, 3, head_cols).transpose(3, 0, 2, 1, 4)
     qkv_piece = qkv_piece.reshape(3, rows, wide)
-    out_piece = att_wgrad[cut:].reshape(1, rows, wide)
+    out_piece = out_piece.reshape(sub, n_dp, wide).transpose(1, 0, 2).reshape(1, rows, wide)
 
     ug_grad = jnp.concatenate([up_grad, gate_grad], axis=0)
     kept = lax.dynamic_slice_in_dim(ug_grad, core * rows, rows, axis=1)
@@ -330,44 +731,18 @@
     ff_pieces = jnp.concatenate([ug_piece, down_piece], axis=0)
 
     def give_back(pieces, low_slot, high_slot, skipped):
-        parts = []
-        for k in range(n_dp):
-            target = (dp_index + k) % n_dp
-            units = lax.dynamic_index_in_dim(slot_unit, target, 0, keepdims=False)
-            units = jnp.maximum(units[low_slot:high_slot] - skipped, 0)
-            send = jnp.take(pieces, units, axis=0)
-            parts.append(send if k == 0 else lax.ppermute(send, "dp", shift_pairs(k)))
-        order = (dp_index - jnp.arange(n_dp, dtype=jnp.int32)) % n_dp
-        return jnp.take(jnp.stack(parts), order, axis=0)
-
-    def unpack(parts, col_flags):
-        count = parts.shape[1]
-        col = parts.reshape(n_dp, count, rows, 2, chips, sub).transpose(2, 1, 4, 3, 0, 5)
-        col = col.reshape(rows, count, width)
-        row = parts.reshape(n_dp, count, n_dp, sub, wide).transpose(0, 3, 1, 2, 4)
-        row = row.reshape(rows, count, width)
-        return jnp.where(col_flags[None, :, None], col, row)
+        units = jnp.maximum(slot_unit[:, low_slot:high_slot] - skipped, 0)
+        return lax.all_to_all(jnp.take(pieces, units, axis=0), "dp", 0, 0)
 
     grads = []
     if per_owner > first_slots:
-        late = give_back(ff_pieces, first_slots, per_owner, 4)
-        grads.append(unpack(late, is_col[first_slots:]))
+        grads.append(give_back(ff_pieces, first_slots, per_owner, 4))
     every_piece = jnp.concatenate([qkv_piece, out_piece, ff_pieces], axis=0)
-    early = give_back(every_piece, 0, first_slots, 0)
-    grads.insert(0, unpack(early, is_col[:first_slots]))
-    keep_slot = (own_units >= 0)[None, :, None]
-    owned_grads = jnp.where(keep_slot, jnp.concatenate(grads, axis=1).astype(f32), 0.0)
-    keep_slot = keep_slot.astype(f32)
-    new_first = (beta_one * first_moment + (1.0 - beta_one) * owned_grads) * keep_slot
-    new_second = (
-        beta_two * second_moment + (1.0 - beta_two) * owned_grads * owned_grads
-    ) * keep_slot
-    fixed_first = new_first / (1.0 - beta_one**STEP)
-    fixed_second = new_second / (1.0 - beta_two**STEP)
-    new_master = (
-        master
-        - learn_rate * (fixed_first / (jnp.sqrt(fixed_second) + adam_eps) + decay_rate * master)
-    ) * keep_slot
+    grads.insert(0, give_back(every_piece, 0, first_slots, 0))
+    kinds = jnp.where(own_units < 0, 2, is_col.astype(jnp.int32)).astype(jnp.int32)
+    owned_grads, new_first, new_second, new_master = adam(
+        kinds, grads, master, first_moment, second_moment, n_dp, n_seq, first_slots
+    )
     return (block_output, input_grad, owned_grads, new_first, new_second, new_master)
 
 

time: 1670 us -> 1350 us (0.81); the launches traced: 1640 us -> 1340 us
  Pallas kernels: 0 us -> 715 us
  waiting for transfers between devices: 843 us -> 221 us
  local copies, waits for them, and re-layouts: 409 us -> 81.9 us
  other arithmetic: 165 us -> 45.4 us
  blocking collectives: 0 us -> 99.9 us
  matrix products: 177 us -> 147 us
    pallas_call x0 -> x12, Pallas kernels: none -> 715 us  [the longest x4 263 us: sum_blocks(): pl.pallas_call(functools.partial(sum_kernel, kind), out_shape=jax.ShapeDt...]
    reduce_scatter x5 -> x0, waiting for transfers between devices: 294 us -> none  [the longest x1 110 us: local(): lax.psum_scatter(jnp.concatenate([qkv_wgrad.reshape(n_dp, cut, head_cols)...]
    ppermute x16 -> x0, waiting for transfers between devices: 278 us -> none  [the longest x6 243 us: exchange(): parts.append(lax.ppermute(send, 'dp', shift_pairs(k)))]
    all_to_all x2 -> x3, waiting for transfers between devices: 12.4 us -> 150 us  [the longest x1 92.8 us: exchange(): return lax.all_to_all(packed, 'dp', 0, 0)]
    unnamed x106 -> x99, local copies, waits for them, and re-layouts: 148 us -> 22.5 us
    reshape x18 -> x5, local copies, waits for them, and re-layouts: 106 us -> 3 us  [the longest x1 1.68 us: local(): att_rows.transpose(1, 3, 2, 0, 4).reshape(n_seq, sub, 3 * head_cols)]
    all_to_all x0 -> x1, blocking collectives: none -> 99.9 us  [exchange(): return lax.all_to_all(packed, 'dp', 0, 0)]
    all_gather x5 -> x0, waiting for transfers between devices: 96 us -> none  [the longest x1 72.8 us: local(): lax.all_gather(jnp.concatenate([att_rows.reshape(n_seq * 3 * sub, head_co...]
  transfers between devices with their start and end apart: 36 -> 11, of which waited for: 21 -> 5; matrix products, arithmetic and copies ran while one was open for 20% -> 15% of each run, Pallas kernels for 0% -> 47%
where the time goes in v2:
time: 1350 us; the launch traced here: 1340 us
  Pallas kernels  715 us (53%)
  waiting for transfers between devices  221 us (16%)
  matrix products  147 us (11%)
  blocking collectives  99.9 us (7%)
  local copies, waits for them, and re-layouts  81.9 us (6%)
  other arithmetic  45.4 us (3%)
  starting transfers between devices  16.2 us (1%)
  between operations  15.2 us (1%)
    pallas_call x4, Pallas kernels, sum_blocks(): pl.pallas_call(functools.partial(sum_kernel, kind), out_shape=jax.ShapeDt...  263 us
    pallas_call x4, Pallas kernels, gather_blocks(): pl.pallas_call(functools.partial(gather_kernel, kind), out_shape=jax.Shap...  173 us
    all_to_all x1, blocking collectives, exchange(): return lax.all_to_all(packed, 'dp', 0, 0)  99.9 us
    pallas_call x1, Pallas kernels, collect_attention(): pl.pallas_call(collect_kernel, out_shape=[jax.ShapeDtypeStruct((n_seq,) +...  94.9 us
    pallas_call x1, Pallas kernels, spread_attention(): pl.pallas_call(spread_kernel, out_shape=[jax.ShapeDtypeStruct((n_seq, n_d...  94.9 us
    all_to_all x1, waiting for transfers between devices, exchange(): return lax.all_to_all(packed, 'dp', 0, 0)  92.8 us
    reduce_scatter x3, waiting for transfers between devices, chip_sum(): lax.psum_scatter(part.astype(bf), 'seq', scatter_dimension=1, tiled=True,...  68.1 us
    pallas_call x1, Pallas kernels, adam(): pl.pallas_call(functools.partial(adam_kernel, n_dp, n_seq // 2, first_slo...  59.7 us
  transfers between devices with their start and end apart: 11, of which 5 were waited for; matrix products, arithmetic and copies ran while one was open for 15% of the time, Pallas kernels for 47%

profile of v2, /device:TPU:0, one launch (start us, length us, event | category | flops | bytes accessed | tf_op | source)
XLA Modules:
  0.0 1341.8 jit_solution(6565812928843895267)
XLA Ops:
  8.9 29.5 %pack.1 = (bf16[4,4,256,512]{3,2,1,0:T(8,128)(2,1)}, bf16[4,4,256,512]{3,2,1,0:T(8,128)(2,1)}) custom-call(s32[8]{0:T(128)S(1)} %fusion.70.flags, f32[256,8,2048]{2,1,0:T(8,128)} %refs_4_.1), custom_call_target="tpu_custom_call" | custom-call | tf_op jit(solution)/shard_map/pack/pallas_call | solution.py:112
  38.5 99.9 %all_to_all.20 = bf16[4,4,256,512]{3,2,1,0:T(8,128)(2,1)} all-to-all(bf16[4,4,256,512]{3,2,1,0:T(8,128)(2,1)} %get-tuple-element.16), channel_id=1, replica_groups=mesh['dp'=4,'seq'=8] {'dp'}, dimensions={0} | all-to-all | bytes 8388608 | tf_op jit(solution)/shard_map/all_to_all | solution.py:561
  143.4 92.8 %all-to-all-done.1 = bf16[4,4,256,512]{3,2,1,0:T(8,128)(2,1)} async-done(((bf16[4,4,256,512]{3,2,1,0:T(8,128)(2,1)}), bf16[4,4,256,512]{3,2,1,0:T(8,128)(2,1)}, u32[]{:S(2)}, u32[]{:S(2)}) %all-to-all-start.1) | async-done | bytes 4194336 | tf_op jit(solution)/shard_map/all_to_all | solution.py:561
  259.6 41.3 %gather_seq.2 = bf16[8,128,2048]{2,1,0:T(8,128)(2,1)S(1)} custom-call(bf16[128,2048]{1,0:T(8,128)(2,1)S(1)} %fusion.43.x_ref), custom_call_target="tpu_custom_call" | custom-call | tf_op jit(solution)/shard_map/gather_seq/pallas_call | solution.py:284
  302.9 51.3 %gather_dp.3 = bf16[8,128,2048]{2,1,0:T(8,128)(2,1)S(1)} custom-call(bf16[128,2048]{1,0:T(8,128)(2,1)S(1)} %bitcast.206), custom_call_target="tpu_custom_call" | custom-call | tf_op jit(solution)/shard_map/gather_dp/pallas_call | solution.py:284
  366.8 94.9 %spread_attention.1 = (bf16[8,4,64,768]{3,2,1,0:T(8,128)(2,1)S(1)}, bf16[4,64,2048]{2,1,0:T(8,128)(2,1)S(1)}) custom-call(bf16[8,64,768]{2,1,0:T(8,128)(2,1)S(1)} %copy-done.10, bf16[64,2048]{1,0:T(8,128)(2,1)S(1)} %bitcast.207), custom_call_target="tpu_custom_call" | custom-call | tf_op jit(solution)/shard_map/spread_attention/pallas_call | solution.py:409
  479.9 8.5 fusion.85
  494.3 47.3 %sum_seq.2 = f32[128,2048]{1,0:T(8,128)S(1)} custom-call(bf16[8,128,2048]{2,1,0:T(8,128)(2,1)S(1)} %bitcast.189), custom_call_target="tpu_custom_call" | custom-call | tf_op jit(solution)/shard_map/sum_seq/pallas_call | solution.py:340
  542.9 51.8 %gather_dp.2 = bf16[8,128,2048]{2,1,0:T(8,128)(2,1)S(1)} custom-call(bf16[128,2048]{1,0:T(8,128)(2,1)S(1)} %fusion.61.x_ref), custom_call_target="tpu_custom_call" | custom-call | tf_op jit(solution)/shard_map/gather_dp/pallas_call | solution.py:284
  596.6 10.0 fusion.90
  606.6 9.9 fusion.89
  616.5 13.1 fusion.9
  637.4 9.4 convert_bitcast_fusion
  667.6 51.2 %sum_dp.3 = f32[128,2048]{1,0:T(8,128)S(1)} custom-call(bf16[8,128,2048]{2,1,0:T(8,128)(2,1)S(1)} %bitcast.191), custom_call_target="tpu_custom_call" | custom-call | tf_op jit(solution)/shard_map/sum_dp/pallas_call | solution.py:340
  721.4 23.6 %reduce-scatter.6.cloned.1.call-done = bf16[4,512,256]{1,2,0:T(8,128)(2,1)} async-done(((bf16[4,2048,256]{1,2,0:T(8,128)(2,1)}), bf16[4,512,256]{1,2,0:T(8,128)(2,1)}) %reduce-scatter.6.cloned.1.call-update) | async-done | bytes 1048592 | tf_op jit(solution)/shard_map/reduce_scatter | solution.py:657
  756.7 44.4 %reduce-scatter.8.cloned.1.call-done = bf16[4,64,2048]{2,1,0:T(8,128)(2,1)} async-done(((bf16[4,256,2048]{2,1,0:T(8,128)(2,1)}), bf16[4,64,2048]{2,1,0:T(8,128)(2,1)}) %reduce-scatter.8.cloned.1.call-update) | async-done | bytes 1048592 | tf_op jit(solution)/shard_map/reduce_scatter | solution.py:657
  834.7 136.5 %sum_dp.2 = f32[128,2048]{1,0:T(8,128)S(1)} custom-call(bf16[8,128,2048]{2,1,0:T(8,128)(2,1)S(1)} %bitcast.190), custom_call_target="tpu_custom_call" | custom-call | tf_op jit(solution)/shard_map/sum_dp/pallas_call | solution.py:340
  972.8 28.5 %gather_seq.3 = bf16[8,128,2048]{2,1,0:T(8,128)(2,1)S(1)} custom-call(bf16[128,2048]{1,0:T(8,128)(2,1)S(1)} %get-tuple-element.30.x_ref), custom_call_target="tpu_custom_call" | custom-call | tf_op jit(solution)/shard_map/gather_seq/pallas_call | solution.py:284
  1011.6 13.4 %fusion.28 = f32[1024,2,128]{0,2,1:T(8,128)} fusion(bf16[1024,2,128]{0,2,1:T(8,128)(2,1)S(1)} %copy-done.35, f32[2,1024,1024]{1,2,0:T(8,128)} %fusion.66, f32[2,1024,1024]{1,2,0:T(8,128)} %get-tuple-element.74, f32[2,1024]{1,0:T(2,128)S(1)} %get-tuple-element.73), kind=kOutput, calls=%fused_computation.52 | convolution fusion | flops 551554048 | bytes 18358272 | tf_op jit(solution)/shard_map/hqk,qhd->khd/dot_general | solution.py:691
  1025.0 14.8 %broadcast_multiply_fusion.1 = (f32[1024,2,128]{0,2,1:T(8,128)S(1)}, f32[1024,2,128]{0,2,1:T(8,128)S(1)}, f32[1024,2,128]{0,2,1:T(8,128)}) fusion(f32[1024,128]{0,1:T(8,128)S(1)} %copy-done.28, f32[1024,2,128]{0,2,1:T(8,128)} %fusion.28, bf16[1024,2,128]{0,2,1:T(8,128)(2,1)S(1)} %copy-done.34, f32[2,1024,1024]{1,2,0:T(8,128)} %fusion.66, ...), kind=kOutput, calls=%fused_computation.105 | convolution fusion | flops 552078336 | bytes 22028288 | tf_op jit(solution)/shard_map/hqk,khd->qhd/dot_general | solution.py:690
  1054.1 94.9 %collect_attention.1 = (bf16[8,64,768]{2,1,0:T(8,128)(2,1)S(1)}, bf16[64,2048]{1,0:T(8,128)(2,1)S(1)}) custom-call(bf16[8,4,64,768]{3,2,1,0:T(8,128)(2,1)S(1)} %bitcast.205, bf16[4,64,2048]{2,1,0:T(8,128)(2,1)S(1)} %bitcast.208), custom_call_target="tpu_custom_call" | custom-call | tf_op jit(solution)/shard_map/collect_attention/pallas_call | solution.py:498
  1187.1 28.5 %sum_seq.3 = f32[128,2048]{1,0:T(8,128)S(1)} custom-call(bf16[8,128,2048]{2,1,0:T(8,128)(2,1)S(1)} %bitcast.192), custom_call_target="tpu_custom_call" | custom-call | tf_op jit(solution)/shard_map/sum_seq/pallas_call | solution.py:340
  1217.4 57.6 %all-to-all-done.2.refs_0_ = bf16[4,4,256,512]{3,2,1,0:T(8,128)(2,1)} async-done(((bf16[4,4,256,512]{3,2,1,0:T(8,128)(2,1)}), bf16[4,4,256,512]{3,2,1,0:T(8,128)(2,1)}, u32[]{:S(2)}, u32[]{:S(2)}) %all-to-all-start.2) | async-done | bytes 4194336 | tf_op jit(solution)/shard_map/all_to_all | solution.py:735
  1275.0 59.7 %adam.1 = (f32[256,8,2048]{2,1,0:T(8,128)}, f32[256,8,2048]{2,1,0:T(8,128)}, f32[256,8,2048]{2,1,0:T(8,128)}, f32[256,8,2048]{2,1,0:T(8,128)}) custom-call(s32[8]{0:T(128)S(1)} %bitcast_select_fusion.kinds, bf16[4,4,256,512]{3,2,1,0:T(8,128)(2,1)} %all-to-all-done.2.refs_0_, bf16[4,4,256,512]{3,2,1,0:T(8,128)(2,1)} %all-to-all-done.3.refs_1_, ...), custom_call_target="tpu_custom_call" | custom-call | tf_op jit(solution)/shard_map/adam/pallas_call | solution.py:190
  (223 shorter events, 213.8 us)
Async XLA Ops:
  138.3 97.8 %all-to-all-start.1 = ((bf16[4,4,256,512]{3,2,1,0:T(8,128)(2,1)}), bf16[4,4,256,512]{3,2,1,0:T(8,128)(2,1)}, u32[]{:S(2)}, u32[]{:S(2)}) async-start(bf16[4,4,256,512]{3,2,1,0:T(8,128)(2,1)} %get-tuple-element.19), calls=%async_computation.1 | async-start | bytes 8388608 | tf_op jit(solution)/shard_map/all_to_all | solution.py:561
  143.2 453.4 %all-gather.8.cloned.1.call-start = ((), (), s32[]{:S(2)}) async-start(), calls=%async_computation.9 | async-start | bytes 5242880 | tf_op jit(solution)/shard_map/all_gather | solution.py:628
  253.1 353.5 %all-gather.4.cloned.1.call-start = ((), (), s32[]{:S(2)}) async-start(), calls=%async_computation.7 | async-start | bytes 5242880 | tf_op jit(solution)/shard_map/all_gather | solution.py:624
  253.6 2.7 collective-permute-start
  258.3 44.6 %copy-start.11 = (bf16[1,128,2048]{2,1,0:T(8,128)(2,1)S(1)}, bf16[1,128,2048]{2,1,0:T(8,128)(2,1)}, u32[]{:S(2)}) copy-start(bf16[1,128,2048]{2,1,0:T(8,128)(2,1)} %param.8) | copy-start | bytes 1572868
  258.3 358.2 %all-gather.6.cloned.1.call-start = ((), (), s32[]{:S(2)}) async-start(), calls=%async_computation.8 | async-start | bytes 5242880 | tf_op jit(solution)/shard_map/all_gather | solution.py:621
  259.0 95.3 %copy-start.38 = (f32[128]{0:T(128)}, f32[128]{0:T(128)S(1)}, u32[]{:S(2)}) copy-start(f32[128]{0:T(128)S(1)} %broadcast_multiply_fusion.7) | copy-start | bytes 1540
  259.3 95.0 %copy-start.40 = (f32[128]{0:T(128)}, f32[128]{0:T(128)S(1)}, u32[]{:S(2)}) copy-start(f32[128]{0:T(128)S(1)} %add_rsqrt_fusion.1) | copy-start | bytes 1540
  475.2 243.9 %reduce-scatter.4.cloned.1.call-start = ((), (), s32[]{:S(2)}) async-start(), calls=%async_computation.10 | async-start | bytes 5242880 | tf_op jit(solution)/shard_map/reduce_scatter | solution.py:657
  494.3 47.3 %copy-start.19 = (bf16[1,128,2048]{2,1,0:T(8,128)(2,1)S(1)}, bf16[1,128,2048]{2,1,0:T(8,128)(2,1)}, u32[]{:S(2)}) copy-start(bf16[1,128,2048]{2,1,0:T(8,128)(2,1)} %param.7) | copy-start | bytes 1572868
  616.5 14.4 %copy-start.7 = (bf16[8,128,2048]{2,1,0:T(8,128)(2,1)S(1)}, bf16[8,128,2048]{2,1,0:T(8,128)(2,1)}, u32[]{:S(2)}) copy-start(bf16[8,128,2048]{2,1,0:T(8,128)(2,1)} %copy-done.6) | copy-start | bytes 12582916
  629.6 17.2 %copy-start.45 = (bf16[1024,4,256]{2,0,1:T(8,128)(2,1)}, bf16[1024,4,256]{2,0,1:T(8,128)(2,1)S(1)}, u32[]{:S(2)}) copy-start(bf16[1024,4,256]{2,0,1:T(8,128)(2,1)S(1)} %get-tuple-element.40) | copy-start | bytes 6291460
  637.3 107.7 %reduce-scatter.6.cloned.1.call-start = ((), (), s32[]{:S(2)}) async-start(), calls=%async_computation.11 | async-start | bytes 5242880 | tf_op jit(solution)/shard_map/reduce_scatter | solution.py:657
  646.8 154.3 %reduce-scatter.8.cloned.1.call-start = ((), (), s32[]{:S(2)}) async-start(), calls=%async_computation.12 | async-start | bytes 5242880 | tf_op jit(solution)/shard_map/reduce_scatter | solution.py:657
  667.6 51.2 %copy-start.16 = (f32[128,2048]{1,0:T(8,128)S(1)}, f32[128,2048]{1,0:T(8,128)}, u32[]{:S(2)}) copy-start(f32[128,2048]{1,0:T(8,128)} %copy-done.15) | copy-start | bytes 3145732
  750.6 54.3 %collective-permute-start.1 = (bf16[8,256,256]{1,2,0:T(8,128)(2,1)}, bf16[8,256,256]{1,2,0:T(8,128)(2,1)}, u32[]{:S(2)}, u32[]{:S(2)}) collective-permute-start(bf16[8,256,256]{1,2,0:T(8,128)(2,1)} %get-tuple-element.46), channel_id=1, source_target_pairs={{0,1},{1,0},{2,3},{3,2},{4,5},{5,4},{6,7},{7,6},{8,9},{9,8},{10,11... | collective-permute-start | bytes 3145736 | tf_op jit(solution)/shard_map/ppermute | solution.py:725
  827.0 144.1 %copy-start.12 = (bf16[1,128,2048]{2,1,0:T(8,128)(2,1)S(1)}, bf16[1,128,2048]{2,1,0:T(8,128)(2,1)}, u32[]{:S(2)}) copy-start(bf16[1,128,2048]{2,1,0:T(8,128)(2,1)} %param.8) | copy-start | bytes 1572868
  827.0 349.7 %all-to-all-start.3 = ((bf16[4,4,256,512]{3,2,1,0:T(8,128)(2,1)}), bf16[4,4,256,512]{3,2,1,0:T(8,128)(2,1)}, u32[]{:S(2)}, u32[]{:S(2)}) async-start(bf16[4,4,256,512]{3,2,1,0:T(8,128)(2,1)} %broadcast_select_fusion), calls=%async_computation.6 | async-start | bytes 8388608 | tf_op jit(solution)/shard_map/all_to_all | solution.py:735
  834.7 136.5 %copy-start.17 = (f32[128,2048]{1,0:T(8,128)S(1)}, f32[128,2048]{1,0:T(8,128)}, u32[]{:S(2)}) copy-start(f32[128,2048]{1,0:T(8,128)} %copy-done.15) | copy-start | bytes 3145732
  1176.7 98.3 %all-to-all-start.2 = ((bf16[4,4,256,512]{3,2,1,0:T(8,128)(2,1)}), bf16[4,4,256,512]{3,2,1,0:T(8,128)(2,1)}, u32[]{:S(2)}, u32[]{:S(2)}) async-start(bf16[4,4,256,512]{3,2,1,0:T(8,128)(2,1)} %broadcast_select_fusion.1), calls=%async_computation.5 | async-start | bytes 8388608 | tf_op jit(solution)/shard_map/all_to_all | solution.py:735
  1187.0 28.6 %copy-start.20 = (bf16[1,128,2048]{2,1,0:T(8,128)(2,1)S(1)}, bf16[1,128,2048]{2,1,0:T(8,128)(2,1)}, u32[]{:S(2)}) copy-start(bf16[1,128,2048]{2,1,0:T(8,128)(2,1)} %param.7) | copy-start | bytes 1572868
  1187.1 28.6 %copy-start.39 = (f32[128]{0:T(128)S(1)}, f32[128]{0:T(128)}, u32[]{:S(2)}) copy-start(f32[128]{0:T(128)} %copy-done.38) | copy-start | bytes 1540
  1187.1 28.6 %copy-start.41 = (f32[128]{0:T(128)S(1)}, f32[128]{0:T(128)}, u32[]{:S(2)}) copy-start(f32[128]{0:T(128)} %copy-done.40) | copy-start | bytes 1540
  1187.1 28.9 %copy-start.27 = (f32[128,2048]{1,0:T(8,128)S(1)}, f32[128,2048]{1,0:T(8,128)}, u32[]{:S(2)}) copy-start(f32[128,2048]{1,0:T(8,128)} %get-tuple-element.31) | copy-start | bytes 3145732
  (36 other events, 146.1 us)
Sparse Core Ops, SparseCore 0:
  253.2 72.8 all-gather.7
  328.0 61.1 all-gather.3
  475.3 70.6 all-gather.5
  637.4 51.7 reduce-scatter.3
  692.3 52.6 reduce-scatter.5
  748.4 52.6 reduce-scatter.7

commit v3 on v2

--- a/solution.py
+++ b/solution.py
@@ -81,13 +81,14 @@
     start = pl.program_id(0) * rb
     target = start // sub
     inner = start % sub
+    turned = jnp.swapaxes(m_ref[...], 0, 1).astype(bf)
     for s in range(slots):
         out = outs[0] if s < first_slots else outs[1]
         t = s if s < first_slots else s - first_slots
+        x = turned[s]
 
         @pl.when(flags[s] == 1)
         def _():
-            x = m_ref[:, s, :].astype(bf)
             for d in range(n_dp):
                 pieces = [
                     x[:, (2 * k + c) * rows + d * sub : (2 * k + c) * rows + (d + 1) * sub]
@@ -98,11 +99,11 @@
 
         @pl.when(flags[s] == 0)
         def _():
-            x = m_ref[:, s, :].astype(bf)
             for g in range(n_dp):
                 out[target, t, pl.ds(pl.multiple_of(g * sub + inner, rb), rb), :] = x[
                     :, g * wide : (g + 1) * wide
                 ]
+
 
 def pack(master, flags, n_dp, n_seq, first_slots):
     rows, slots, width = master.shape
@@ -124,32 +125,19 @@
         name="pack",
     )(flags, master)
 
+
 def adam_kernel(n_dp, chips, first_slots, n_groups, kinds, *refs):
     cols = refs[:n_groups]
-    rws = refs[n_groups:2*n_groups]
-    m_ref, f_ref, s_ref, g_out, f_out, s_out, m_out = refs[2*n_groups:]
+    rws = refs[n_groups : 2 * n_groups]
+    m_ref, f_ref, s_ref, keep_ref, g_out, f_out, s_out, m_out, held = refs[2 * n_groups :]
     rb, slots, width = m_ref.shape
     wide = width // n_dp
-    rows = wide * n_dp // (2 * chips)
+    rows = width // (2 * chips)
     sub = rows // n_dp
     half = chips * sub
-
-    def finish(s, grad):
-        g_out[:, s, :] = grad
-        first = beta_one * f_ref[:, s, :] + (1.0 - beta_one) * grad
-        second = beta_two * s_ref[:, s, :] + (1.0 - beta_two) * grad * grad
-        f_out[:, s, :] = first
-        s_out[:, s, :] = second
-        fixed_first = first * (1.0 / (1.0 - beta_one**STEP))
-        fixed_second = second * (1.0 / (1.0 - beta_two**STEP))
-        old = m_ref[:, s, :]
-        m_out[:, s, :] = old - learn_rate * (
-            fixed_first / (jnp.sqrt(fixed_second) + adam_eps) + decay_rate * old
-        )
-
     for s in range(slots):
-        grp = 0 if s < first_slots else 1
-        t = s if grp == 0 else s - first_slots
+        group = 0 if s < first_slots else 1
+        t = s if group == 0 else s - first_slots
 
         @pl.when(kinds[s] == 1)
         def _():
@@ -157,21 +145,32 @@
             for i in range(2 * chips):
                 k, c = i // 2, i % 2
                 for d in range(n_dp):
-                    pieces.append(cols[grp][d, t, :, c * half + k * sub : c * half + (k + 1) * sub])
-            finish(s, jnp.concatenate(pieces, axis=1).astype(f32))
+                    begin = c * half + k * sub
+                    pieces.append(cols[group][d, t, :, begin : begin + sub])
+            held[s] = jnp.concatenate(pieces, axis=1).astype(f32)
 
         @pl.when(kinds[s] == 0)
         def _():
-            pieces = [rws[grp][0, t, g, :, :] for g in range(n_dp)]
-            finish(s, jnp.concatenate(pieces, axis=1).astype(f32))
+            for g in range(n_dp):
+                held[s, :, g * wide : (g + 1) * wide] = rws[group][0, t, g, :, :].astype(f32)
 
         @pl.when(kinds[s] == 2)
         def _():
-            zero = jnp.zeros((rb, width), f32)
-            g_out[:, s, :] = zero
-            f_out[:, s, :] = zero
-            s_out[:, s, :] = zero
-            m_out[:, s, :] = zero
+            held[s] = jnp.zeros((rb, width), f32)
+
+    grad = jnp.swapaxes(held[...], 0, 1)
+    keep = keep_ref[...] > 0.0
+    g_out[...] = grad
+    first = jnp.where(keep, beta_one * f_ref[...] + (1.0 - beta_one) * grad, 0.0)
+    f_out[...] = first
+    second = jnp.where(keep, beta_two * s_ref[...] + (1.0 - beta_two) * grad * grad, 0.0)
+    s_out[...] = second
+    fixed_first = first * (1.0 / (1.0 - beta_one**STEP))
+    fixed_second = second * (1.0 / (1.0 - beta_two**STEP))
+    old = m_ref[...]
+    step = fixed_first / (jnp.sqrt(fixed_second) + adam_eps) + decay_rate * old
+    m_out[...] = jnp.where(keep, old - learn_rate * step, 0.0)
+
 
 def adam(kinds, grads, master, first_moment, second_moment, n_dp, n_seq, first_slots):
     rows, slots, width = master.shape
@@ -187,14 +186,19 @@
         )
         for g in grads
     ]
+    keep = jnp.broadcast_to((kinds != 2).astype(f32)[None, :, None], (1, slots, width))
     return pl.pallas_call(
         functools.partial(adam_kernel, n_dp, n_seq // 2, first_slots, len(grads)),
         out_shape=[jax.ShapeDtypeStruct(master.shape, f32)] * 4,
         grid_spec=pltpu.PrefetchScalarGridSpec(
             num_scalar_prefetch=1,
             grid=(rows // rb,),
-            in_specs=cols + rws + [state] * 3,
+            in_specs=cols
+            + rws
+            + [state] * 3
+            + [pl.BlockSpec((1, slots, width), lambda i, k: (0, 0, 0))],
             out_specs=[state] * 4,
+            scratch_shapes=[pltpu.VMEM((slots, rb, width), f32)],
         ),
         compiler_params=pltpu.CompilerParams(vmem_limit_bytes=50 << 20),
         name="adam",
@@ -205,28 +209,29 @@
         master,
         first_moment,
         second_moment,
-    )
+        keep,
+    )
+
 
 ANY = pl.BlockSpec(memory_space=pl.ANY)
 VMEM = pl.BlockSpec(memory_space=pltpu.VMEM)
-
-
-def line_place(kind):
-    seq_index = lax.axis_index("seq")
-    core = lax.rem(seq_index, 2)
-    if kind == "seq":
-        return seq_index // 2, lax.axis_size("seq") // 2, core
-    return lax.axis_index("dp"), lax.axis_size("dp"), core
-
-
-def line_device(kind, position, core):
-    if kind == "seq":
-        return (lax.axis_index("dp"), position * 2 + core)
-    return (position, lax.axis_index("seq") - lax.rem(lax.axis_index("seq"), 2) + core)
-
-
-def line_block(kind, position, count, core):
-    return position * 2 + core if kind == "seq" else core * count + position
+DMA = pltpu.SemaphoreType.DMA
+
+
+def comm_params(collective_id, mib):
+    return pltpu.CompilerParams(
+        collective_id=collective_id, has_side_effects=True, vmem_limit_bytes=mib << 20
+    )
+
+
+def takes(microseconds):
+    return pl.CostEstimate(flops=0, bytes_accessed=int(microseconds * 3e6), transcendentals=0)
+
+
+def places():
+    n_seq = lax.axis_size("seq")
+    n_dp = lax.axis_size("dp")
+    return n_seq, n_dp, lax.axis_index("seq"), lax.axis_index("dp")
 
 
 def greet(devices):
@@ -247,82 +252,287 @@
     )
 
 
-def gather_kernel(kind, x_ref, out_ref, own_sem, send_sem, recv_sem, pass_sem, take_sem):
-    position, count, core = line_place(kind)
-    peers = [lax.rem(position + k, count) for k in range(count)]
-    sibling = line_device(kind, position, 1 - core)
-    greet([line_device(kind, p, core) for p in peers[1:]] + [sibling])
-    mine = line_block(kind, position, count, core)
-    own = pltpu.make_async_copy(x_ref, out_ref.at[mine], own_sem)
-    own.start()
-    copies = []
-    for k in range(count - 1, 0, -1):
+def relay_gather(views, place, count, device_of, send_sem, recv_sem, arrived):
+    def leg(view, way, step, block, target):
+        ref = views[view](block)
+        return send(ref, ref, send_sem.at[view, way, step], recv_sem.at[view, way, step], device_of(target))
+
+    def going(way, step):
+        block = place - (step - 1) if way == 0 else place + (step - 1)
+        target = place + 1 if way == 0 else place - 1
+        inside = (block >= 0) & (block < count) & (target >= 0) & (target < count)
+        return block, target, inside
+
+    for step in range(1, count):
+        for way in range(2):
+            block, target, inside = going(way, step)
+
+            @pl.when(inside)
+            def _():
+                for view in range(len(views)):
+                    leg(view, way, step, block, target).start()
+
+        for way in range(2):
+            block = place - step if way == 0 else place + step
+
+            @pl.when((block >= 0) & (block < count))
+            def _():
+                for view in range(len(views)):
+                    leg(view, way, step, block, lax.rem(place + 1, count)).wait_recv()
+                arrived(block)
+
+    for step in range(1, count):
+        for way in range(2):
+            block, target, inside = going(way, step)
+
+            @pl.when(inside)
+            def _():
+                for view in range(len(views)):
+                    leg(view, way, step, block, target).wait_send()
+
+
+def relay_sum(owns, sent, came, place, count, device_of, send_sem, recv_sem, ready):
+    views = range(len(owns))
+
+    def leg(view, way, block, target):
+        return send(
+            sent[view].at[way, block],
+            came[view].at[way, block],
+            send_sem.at[view, way, block],
+            recv_sem.at[view, way, block],
+            device_of(target),
+        )
+
+    def going(way, step):
+        block = count - 1 - step + place if way == 0 else step - (count - 1 - place)
+        target = place + 1 if way == 0 else place - 1
+        return block, target, (block < count if way == 0 else block >= 0)
+
+    def behind(way):
+        return place > 0 if way == 0 else place < count - 1
+
+    for step in range(count - 1):
+        for way in range(2):
+            block, target, inside = going(way, step)
+
+            @pl.when(inside)
+            def _():
+                ready(block)
+                for view in views:
+
+                    @pl.when(behind(way))
+                    def _():
+                        leg(view, way, block, target).wait_recv()
+                        value = owns[view](block) + came[view][way, block].astype(f32)
+                        sent[view][way, block] = value.astype(sent[view].dtype)
+
+                    @pl.when(jnp.logical_not(behind(way)))
+                    def _():
+                        sent[view][way, block] = owns[view](block).astype(sent[view].dtype)
+
+                    leg(view, way, block, target).start()
+
+    ready(place)
+    for way in range(2):
+
+        @pl.when(behind(way))
+        def _():
+            for view in views:
+                leg(view, way, place, lax.rem(place + 1, count)).wait_recv()
+
+    totals = []
+    for view in views:
+        total = owns[view](place)
+        for way in range(2):
+            value = came[view][way, place].astype(f32)
+            total = total + jnp.where(behind(way), value, 0.0)
+        totals.append(total)
+    for step in range(count - 1):
+        for way in range(2):
+            block, target, inside = going(way, step)
+
+            @pl.when(inside)
+            def _():
+                for view in views:
+                    leg(view, way, block, target).wait_send()
+
+    return totals
+
+
+def front_kernel(
+    packed_ref, x_ref, table_ref, out_ref, own_sem, a_send, a_recv, send_sem, recv_sem, pass_sem, take_sem
+):
+    n_seq, n_dp, seq_index, dp_index = places()
+    chips, chip, core = n_seq // 2, seq_index // 2, lax.rem(seq_index, 2)
+    dp_peers = [lax.rem(dp_index + k, n_dp) for k in range(n_dp)]
+    chip_peers = [lax.rem(chip + k, chips) for k in range(chips)]
+    sibling = (dp_index, chip * 2 + 1 - core)
+    greet(
+        [(p, seq_index) for p in dp_peers[1:]]
+        + [(dp_index, p * 2 + core) for p in chip_peers[1:]]
+        + [sibling]
+    )
+    along = []
+    for k in range(1, n_dp):
         copy = send(
-            x_ref, out_ref.at[mine], send_sem.at[k], recv_sem.at[k], line_device(kind, peers[k], core)
+            packed_ref.at[dp_peers[k]],
+            table_ref.at[dp_index],
+            a_send.at[k],
+            a_recv.at[k],
+            (dp_peers[k], seq_index),
         )
         copy.start()
-        copies.append((k, copy))
-    first = send(x_ref, out_ref.at[mine], pass_sem.at[0], take_sem.at[0], sibling)
-    first.start()
-    passed = [first]
-    for k, copy in reversed(copies):
-        copy.wait_recv()
-        block = out_ref.at[line_block(kind, lax.rem(position + count - k, count), count, core)]
+        along.append(copy)
+    own = [
+        pltpu.make_async_copy(packed_ref.at[dp_index], table_ref.at[dp_index], own_sem.at[0]),
+        pltpu.make_async_copy(x_ref, out_ref.at[seq_index], own_sem.at[1]),
+    ]
+    for copy in own:
+        copy.start()
+    spread_blocks(
+        x_ref, out_ref, chips, chip, core, dp_index, sibling, send_sem, recv_sem, pass_sem, take_sem
+    )
+    for copy in along:
+        copy.wait()
+    for copy in own:
+        copy.wait()
+
+
+def spread_blocks(
+    x_ref, out_ref, chips, chip, core, dp_index, sibling, send_sem, recv_sem, pass_sem, take_sem
+):
+    mine = out_ref.at[chip * 2 + core]
+    copies = {}
+    for k in range(chips - 1, 0, -1):
+        device = (dp_index, lax.rem(chip + k, chips) * 2 + core)
+        copies[k] = send(x_ref, mine, send_sem.at[k], recv_sem.at[k], device)
+        copies[k].start()
+    passed = [send(x_ref, mine, pass_sem.at[0], take_sem.at[0], sibling)]
+    passed[0].start()
+    for k in range(1, chips):
+        copies[k].wait_recv()
+        block = out_ref.at[lax.rem(chip + chips - k, chips) * 2 + core]
         onward = send(block, block, pass_sem.at[k], take_sem.at[k], sibling)
         onward.start()
         passed.append(onward)
-    for k, copy in copies:
+    for copy in copies.values():
         copy.wait_send()
     for onward in passed:
         onward.wait()
+
+
+def front(packed, x, collective_id):
+    chips = lax.axis_size("seq") // 2
+    n_dp = lax.axis_size("dp")
+    return pl.pallas_call(
+        front_kernel,
+        out_shape=[
+            jax.ShapeDtypeStruct(packed.shape, packed.dtype),
+            jax.ShapeDtypeStruct((2 * chips,) + x.shape, x.dtype),
+        ],
+        in_specs=[ANY, ANY],
+        out_specs=[ANY, ANY],
+        scratch_shapes=[DMA((2,)), DMA((n_dp,)), DMA((n_dp,))] + [DMA((chips,))] * 4,
+        compiler_params=comm_params(collective_id, 16),
+        cost_estimate=takes(90),
+        name="front",
+    )(packed, x)
+
+
+def gather_seq_kernel(x_ref, out_ref, own_sem, send_sem, recv_sem, pass_sem, take_sem):
+    n_seq, n_dp, seq_index, dp_index = places()
+    chips, chip, core = n_seq // 2, seq_index // 2, lax.rem(seq_index, 2)
+    chip_peers = [lax.rem(chip + k, chips) for k in range(chips)]
+    sibling = (dp_index, chip * 2 + 1 - core)
+    greet([(dp_index, p * 2 + core) for p in chip_peers[1:]] + [sibling])
+    own = pltpu.make_async_copy(x_ref, out_ref.at[seq_index], own_sem)
+    own.start()
+    spread_blocks(
+        x_ref, out_ref, chips, chip, core, dp_index, sibling, send_sem, recv_sem, pass_sem, take_sem
+    )
     own.wait()
 
 
-def gather_blocks(x, kind, collective_id):
-    count = lax.axis_size("seq") // 2 if kind == "seq" else lax.axis_size("dp")
-    dma = pltpu.SemaphoreType.DMA
+def gather_seq(x, collective_id):
+    chips = lax.axis_size("seq") // 2
     return pl.pallas_call(
-        functools.partial(gather_kernel, kind),
-        out_shape=jax.ShapeDtypeStruct((2 * count,) + x.shape, x.dtype),
+        gather_seq_kernel,
+        out_shape=jax.ShapeDtypeStruct((2 * chips,) + x.shape, x.dtype),
         in_specs=[ANY],
         out_specs=ANY,
-        scratch_shapes=[dma, dma((count,)), dma((count,)), dma((count,)), dma((count,))],
-        compiler_params=pltpu.CompilerParams(
-            collective_id=collective_id, has_side_effects=True, vmem_limit_bytes=16 << 20
-        ),
-        name="gather_" + kind,
+        scratch_shapes=[DMA] + [DMA((chips,))] * 4,
+        compiler_params=comm_params(collective_id, 16),
+        cost_estimate=takes(28),
+        name="gather_seq",
     )(x)
 
 
-def sum_kernel(
-    kind, x_ref, out_ref, taken, sent, arrived, pass_sem, take_sem, send_sem, recv_sem
-):
-    position, count, core = line_place(kind)
-    peers = [lax.rem(position + k, count) for k in range(count)]
-    sibling = line_device(kind, position, 1 - core)
-    greet([line_device(kind, p, core) for p in peers[1:]] + [sibling])
-    order = list(range(count - 1, 0, -1)) + [0]
+def gather_dp_kernel(x_ref, out_ref, own_sem, send_sem, recv_sem, pass_sem, take_sem):
+    n_seq, n_dp, seq_index, dp_index = places()
+    core = lax.rem(seq_index, 2)
+    sibling = (dp_index, seq_index + 1 - 2 * core)
+    greet([(lax.rem(dp_index + k, n_dp), seq_index) for k in range(1, n_dp)] + [sibling])
+    own = pltpu.make_async_copy(x_ref, out_ref.at[core, dp_index], own_sem)
+    own.start()
+    own.wait()
+
+    def onward(block):
+        ref = out_ref.at[core, block]
+        return send(ref, ref, pass_sem.at[block], take_sem.at[block], sibling)
+
+    onward(dp_index).start()
+    relay_gather(
+        [lambda block: out_ref.at[core, block]],
+        dp_index,
+        n_dp,
+        lambda place: (place, seq_index),
+        send_sem,
+        recv_sem,
+        lambda block: onward(block).start(),
+    )
+    for block in range(n_dp):
+        onward(block).wait_send()
+        ref = out_ref.at[1 - core, block]
+        send(ref, ref, pass_sem.at[block], take_sem.at[block], sibling).wait_recv()
+
+
+def gather_dp(x, collective_id):
+    n_dp = lax.axis_size("dp")
+    return pl.pallas_call(
+        gather_dp_kernel,
+        out_shape=jax.ShapeDtypeStruct((2, n_dp) + x.shape, x.dtype),
+        in_specs=[ANY],
+        out_specs=ANY,
+        scratch_shapes=[DMA, DMA((1, 2, n_dp)), DMA((1, 2, n_dp)), DMA((n_dp,)), DMA((n_dp,))],
+        compiler_params=comm_params(collective_id, 16),
+        cost_estimate=takes(40),
+        name="gather_dp",
+    )(x)
+
+
+def sum_seq_kernel(x_ref, out_ref, taken, sent, arrived, pass_sem, take_sem, send_sem, recv_sem):
+    n_seq, n_dp, seq_index, dp_index = places()
+    chips, chip, core = n_seq // 2, seq_index // 2, lax.rem(seq_index, 2)
+    peers = [lax.rem(chip + k, chips) for k in range(chips)]
+    sibling = (dp_index, chip * 2 + 1 - core)
+    greet([(dp_index, p * 2 + core) for p in peers[1:]] + [sibling])
+    order = list(range(chips - 1, 0, -1)) + [0]
     passed = {}
     for k in order:
-        block = x_ref.at[line_block(kind, peers[k], count, 1 - core)]
+        block = x_ref.at[peers[k] * 2 + 1 - core]
         passed[k] = send(block, taken.at[k], pass_sem.at[k], take_sem.at[k], sibling)
         passed[k].start()
     copies = {}
     for k in order[:-1]:
         passed[k].wait_recv()
-        own = x_ref[line_block(kind, peers[k], count, core)].astype(f32)
+        own = x_ref[peers[k] * 2 + core].astype(f32)
         sent[k] = (own + taken[k].astype(f32)).astype(sent.dtype)
-        copies[k] = send(
-            sent.at[k],
-            arrived.at[k],
-            send_sem.at[k],
-            recv_sem.at[k],
-            line_device(kind, peers[k], core),
-        )
+        device = (dp_index, peers[k] * 2 + core)
+        copies[k] = send(sent.at[k], arrived.at[k], send_sem.at[k], recv_sem.at[k], device)
         copies[k].start()
     passed[0].wait_recv()
-    total = x_ref[line_block(kind, position, count, core)].astype(f32) + taken[0].astype(f32)
-    for k in range(1, count):
+    total = x_ref[seq_index].astype(f32) + taken[0].astype(f32)
+    for k in range(1, chips):
         copies[k].wait_recv()
         total = total + arrived[k].astype(f32)
     out_ref[...] = total
@@ -332,34 +542,89 @@
         copies[k].wait_send()
 
 
-def sum_blocks(x, kind, collective_id):
+def sum_seq(x, collective_id):
     blocks, rows, columns = x.shape
-    count = blocks // 2
-    dma = pltpu.SemaphoreType.DMA
-    slots = pltpu.VMEM((count, rows, columns), x.dtype)
+    chips = blocks // 2
+    slots = pltpu.VMEM((chips, rows, columns), x.dtype)
     return pl.pallas_call(
-        functools.partial(sum_kernel, kind),
+        sum_seq_kernel,
         out_shape=jax.ShapeDtypeStruct((rows, columns), f32),
         in_specs=[VMEM],
         out_specs=VMEM,
-        scratch_shapes=[slots, slots, slots, dma((count,)), dma((count,)), dma((count,)), dma((count,))],
-        compiler_params=pltpu.CompilerParams(
-            collective_id=collective_id, has_side_effects=True, vmem_limit_bytes=40 << 20
-        ),
-        name="sum_" + kind,
+        scratch_shapes=[slots, slots, slots] + [DMA((chips,))] * 4,
+        compiler_params=comm_params(collective_id, 40),
+        cost_estimate=takes(28),
+        name="sum_seq",
     )(x)
 
 
+def sum_dp_kernel(x_ref, out_ref, taken, sent, came, pass_sem, take_sem, send_sem, recv_sem):
+    n_seq, n_dp, seq_index, dp_index = places()
+    core = lax.rem(seq_index, 2)
+    sibling = (dp_index, seq_index + 1 - 2 * core)
+    greet([(lax.rem(dp_index + k, n_dp), seq_index) for k in range(1, n_dp)] + [sibling])
+
+    def onward(block):
+        return send(
+            x_ref.at[1 - core, block], taken.at[block], pass_sem.at[block], take_sem.at[block], sibling
+        )
+
+    half = n_dp // 2
+    for block in [b for k in range(half) for b in (n_dp - 1 - k, k)]:
+        onward(block).start()
+    waited = []
+
+    def ready(block):
+        onward(block).wait_recv()
+
+    total = relay_sum(
+        [lambda block: x_ref[core, block].astype(f32) + taken[block].astype(f32)],
+        [sent],
+        [came],
+        dp_index,
+        n_dp,
+        lambda place: (place, seq_index),
+        send_sem,
+        recv_sem,
+        ready,
+    )[0]
+    out_ref[...] = total
+    for block in range(n_dp):
+        onward(block).wait_send()
+
+
+def sum_dp(x, collective_id):
+    _, n_dp, rows, columns = x.shape
+    slots = pltpu.VMEM((2, n_dp, rows, columns), x.dtype)
+    return pl.pallas_call(
+        sum_dp_kernel,
+        out_shape=jax.ShapeDtypeStruct((rows, columns), f32),
+        in_specs=[VMEM],
+        out_specs=VMEM,
+        scratch_shapes=[
+            pltpu.VMEM((n_dp, rows, columns), x.dtype),
+            slots,
+            slots,
+            DMA((n_dp,)),
+            DMA((n_dp,)),
+            DMA((1, 2, n_dp)),
+            DMA((1, 2, n_dp)),
+        ],
+        compiler_params=comm_params(collective_id, 40),
+        cost_estimate=takes(40),
+        name="sum_dp",
+    )(x)
+
+
 def spread_kernel(
-    qkv_ref, out_ref, qkv_all, out_all, own_sem, a_send, a_recv, z_send, z_recv, o_send, o_recv
+    qkv_ref, out_ref, qkv_all, out_all, own_sem, a_send, a_recv, send_sem, recv_sem
 ):
-    n_seq = lax.axis_size("seq")
-    n_dp = lax.axis_size("dp")
-    seq_index = lax.axis_index("seq")
-    dp_index = lax.axis_index("dp")
+    n_seq, n_dp, seq_index, dp_index = places()
     seq_peers = [lax.rem(seq_index + k, n_seq) for k in range(n_seq)]
-    dp_peers = [lax.rem(dp_index + k, n_dp) for k in range(n_dp)]
-    greet([(dp_index, p) for p in seq_peers[1:]] + [(p, seq_index) for p in dp_peers[1:]])
+    greet(
+        [(dp_index, p) for p in seq_peers[1:]]
+        + [(lax.rem(dp_index + k, n_dp), seq_index) for k in range(1, n_dp)]
+    )
     own = [
         pltpu.make_async_copy(qkv_ref.at[seq_index], qkv_all.at[seq_index, dp_index], own_sem.at[0]),
         pltpu.make_async_copy(out_ref, out_all.at[dp_index], own_sem.at[1]),
@@ -367,45 +632,32 @@
     for copy in own:
         copy.start()
     landing = qkv_all.at[seq_index, dp_index]
-    across = {}
+    across = []
     for k in range(1, n_seq):
-        across[k] = send(
-            qkv_ref.at[seq_peers[k]], landing, a_send.at[k], a_recv.at[k], (dp_index, seq_peers[k])
-        )
-        across[k].start()
-    outs = {}
-    for k in range(1, n_dp):
-        outs[k] = send(
-            out_ref, out_all.at[dp_index], o_send.at[k], o_recv.at[k], (dp_peers[k], seq_index)
-        )
-        outs[k].start()
-    along = []
-    for k in range(n_seq):
-        source = lax.rem(seq_index + n_seq - k, n_seq)
-        block = qkv_all.at[source, dp_index]
-        if k == 0:
-            block_src = qkv_ref.at[seq_index]
-        else:
-            across[k].wait_recv()
-            block_src = block
-        for j in range(n_dp - 1, 0, -1):
-            copy = send(block_src, block, z_send.at[k, j], z_recv.at[k, j], (dp_peers[j], seq_index))
-            copy.start()
-            along.append(copy)
-    for copy in along:
-        copy.wait()
-    for k in range(1, n_dp):
-        outs[k].wait()
-    for k in range(1, n_seq):
-        across[k].wait_send()
+        device = (dp_index, seq_peers[k])
+        copy = send(qkv_ref.at[seq_peers[k]], landing, a_send.at[k], a_recv.at[k], device)
+        copy.start()
+        across.append(copy)
     for copy in own:
         copy.wait()
+    for copy in across:
+        copy.wait_recv()
+    relay_gather(
+        [lambda block: qkv_all.at[:, block], lambda block: out_all.at[block]],
+        dp_index,
+        n_dp,
+        lambda place: (place, seq_index),
+        send_sem,
+        recv_sem,
+        lambda block: None,
+    )
+    for copy in across:
+        copy.wait_send()
 
 
 def spread_attention(qkv, out, collective_id):
     n_seq = lax.axis_size("seq")
     n_dp = lax.axis_size("dp")
-    dma = pltpu.SemaphoreType.DMA
     return pl.pallas_call(
         spread_kernel,
         out_shape=[
@@ -414,78 +666,50 @@
         ],
         in_specs=[ANY, ANY],
         out_specs=[ANY, ANY],
-        scratch_shapes=[
-            dma((2,)),
-            dma((n_seq,)),
-            dma((n_seq,)),
-            dma((n_seq, n_dp)),
-            dma((n_seq, n_dp)),
-            dma((n_dp,)),
-            dma((n_dp,)),
-        ],
-        compiler_params=pltpu.CompilerParams(
-            collective_id=collective_id, has_side_effects=True, vmem_limit_bytes=16 << 20
-        ),
+        scratch_shapes=[DMA((2,)), DMA((n_seq,)), DMA((n_seq,)), DMA((2, 2, n_dp)), DMA((2, 2, n_dp))],
+        compiler_params=comm_params(collective_id, 16),
+        cost_estimate=takes(75),
         name="spread_attention",
     )(qkv, out)
 
 
 def collect_kernel(
-    qkv_ref, out_ref, qkv_sum, out_sum, qkv_in, out_in, total, own_sem, z_send, z_recv, o_send, o_recv,
-    a_send, a_recv
+    qkv_ref, out_ref, qkv_sum, out_sum, qkv_sent, qkv_came, out_sent, out_came, total, own_sem,
+    send_sem, recv_sem, a_send, a_recv
 ):
-    n_seq = lax.axis_size("seq")
-    n_dp = lax.axis_size("dp")
-    seq_index = lax.axis_index("seq")
-    dp_index = lax.axis_index("dp")
+    n_seq, n_dp, seq_index, dp_index = places()
     seq_peers = [lax.rem(seq_index + k, n_seq) for k in range(n_seq)]
-    dp_peers = [lax.rem(dp_index + k, n_dp) for k in range(n_dp)]
-    greet([(dp_index, p) for p in seq_peers[1:]] + [(p, seq_index) for p in dp_peers[1:]])
-    along = {}
-    for k in list(range(1, n_seq)) + [0]:
-        for j in range(n_dp - 1, 0, -1):
-            along[k, j] = send(
-                qkv_ref.at[seq_peers[k], dp_peers[j]],
-                qkv_in.at[k, j],
-                z_send.at[k, j],
-                z_recv.at[k, j],
-                (dp_peers[j], seq_index),
-            )
-            along[k, j].start()
-    outs = {}
-    for j in range(n_dp - 1, 0, -1):
-        outs[j] = send(
-            out_ref.at[dp_peers[j]], out_in.at[j], o_send.at[j], o_recv.at[j], (dp_peers[j], seq_index)
+    greet(
+        [(dp_index, p) for p in seq_peers[1:]]
+        + [(lax.rem(dp_index + k, n_dp), seq_index) for k in range(1, n_dp)]
+    )
+    sums = relay_sum(
+        [lambda block: qkv_ref[:, block].astype(f32), lambda block: out_ref[block].astype(f32)],
+        [qkv_sent, out_sent],
+        [qkv_came, out_came],
+        dp_index,
+        n_dp,
+        lambda place: (place, seq_index),
+        send_sem,
+        recv_sem,
+        lambda block: None,
+    )
+    total[...] = sums[0].astype(total.dtype)
+    across = []
+    for k in range(1, n_seq):
+        copy = send(
+            total.at[seq_peers[k]],
+            qkv_sum.at[seq_index],
+            a_send.at[k],
+            a_recv.at[k],
+            (dp_index, seq_peers[k]),
         )
-        outs[j].start()
-    across = {}
-    for k in list(range(1, n_seq)) + [0]:
-        value = qkv_ref[seq_peers[k], dp_index].astype(f32)
-        for j in range(1, n_dp):
-            along[k, j].wait_recv()
-            value = value + qkv_in[k, j].astype(f32)
-        total[k] = value.astype(total.dtype)
-        if k:
-            across[k] = send(
-                total.at[k],
-                qkv_sum.at[seq_index],
-                a_send.at[k],
-                a_recv.at[k],
-                (dp_index, seq_peers[k]),
-            )
-            across[k].start()
-    own = pltpu.make_async_copy(total.at[0], qkv_sum.at[seq_index], own_sem)
+        copy.start()
+        across.append(copy)
+    own = pltpu.make_async_copy(total.at[seq_index], qkv_sum.at[seq_index], own_sem)
     own.start()
-    value = out_ref[dp_index].astype(f32)
-    for j in range(1, n_dp):
-        outs[j].wait_recv()
-        value = value + out_in[j].astype(f32)
-    out_sum[...] = value.astype(out_sum.dtype)
-    for copy in along.values():
-        copy.wait_send()
-    for copy in outs.values():
-        copy.wait_send()
-    for copy in across.values():
+    out_sum[...] = sums[1].astype(out_sum.dtype)
+    for copy in across:
         copy.wait()
     own.wait()
 
@@ -493,8 +717,9 @@
 def collect_attention(qkv, out, collective_id):
     n_seq = lax.axis_size("seq")
     n_dp = lax.axis_size("dp")
-    dma = pltpu.SemaphoreType.DMA
     tail = qkv.shape[2:]
+    q_slots = pltpu.VMEM((2, n_dp, n_seq) + tail, qkv.dtype)
+    o_slots = pltpu.VMEM((2, n_dp) + out.shape[1:], out.dtype)
     return pl.pallas_call(
         collect_kernel,
         out_shape=[
@@ -504,20 +729,19 @@
         in_specs=[VMEM, VMEM],
         out_specs=[VMEM, VMEM],
         scratch_shapes=[
-            pltpu.VMEM((n_seq, n_dp) + tail, qkv.dtype),
-            pltpu.VMEM((n_dp,) + out.shape[1:], out.dtype),
+            q_slots,
+            q_slots,
+            o_slots,
+            o_slots,
             pltpu.VMEM((n_seq,) + tail, qkv.dtype),
-            dma,
-            dma((n_seq, n_dp)),
-            dma((n_seq, n_dp)),
-            dma((n_dp,)),
-            dma((n_dp,)),
-            dma((n_seq,)),
-            dma((n_seq,)),
+            DMA,
+            DMA((2, 2, n_dp)),
+            DMA((2, 2, n_dp)),
+            DMA((n_seq,)),
+            DMA((n_seq,)),
         ],
-        compiler_params=pltpu.CompilerParams(
-            collective_id=collective_id, has_side_effects=True, vmem_limit_bytes=40 << 20
-        ),
+        compiler_params=comm_params(collective_id, 48),
+        cost_estimate=takes(75),
         name="collect_attention",
     )(qkv, out)
 
@@ -560,19 +784,23 @@
     def exchange(packed):
         return lax.all_to_all(packed, "dp", 0, 0)
 
+    tokens = block_input.astype(f32).reshape(shard_len, width)
+    normed_one, inv_one = norm_parts(tokens)
     packed = pack(master, is_col.astype(jnp.int32), n_dp, n_seq, first_slots)
-    first_table = exchange(packed[0]).reshape(n_dp * first_slots, rows, wide)
+    first_table, normed_one_all = front(packed[0], normed_one.astype(bf), 2)
+    first_table = first_table.reshape(n_dp * first_slots, rows, wide)
+    normed_one_all = normed_one_all.reshape(seq_len, width)
     att = jnp.take(first_table, (owners * first_slots + place)[:4], axis=0)
     att_rows = att[:3].reshape(3, n_dp, sub, n_seq // n_dp, head_cols)
     att_rows = att_rows.transpose(1, 3, 2, 0, 4).reshape(n_seq, sub, 3 * head_cols)
     att_out = att[3].reshape(n_dp, sub, wide).transpose(1, 0, 2).reshape(sub, width)
     qkv_weight, out_weight = spread_attention(att_rows, att_out, 1)
+    if per_owner > first_slots:
+        late, qkv_weight = lax.optimization_barrier((packed[1], qkv_weight))
+        late = exchange(late)
     qkv_weight = qkv_weight.reshape(width, 3 * head_cols)
     out_weight = out_weight.reshape(rows, width)
 
-    tokens = block_input.astype(f32).reshape(shard_len, width)
-    normed_one, inv_one = norm_parts(tokens)
-    normed_one_all = gather_blocks(normed_one.astype(bf), "seq", 2).reshape(seq_len, width)
     qkv_proj = jnp.dot(normed_one_all, qkv_weight, preferred_element_type=f32)
     qkv_proj = qkv_proj.reshape(seq_len, 3, heads, HD)
     positions = jnp.arange(seq_len, dtype=jnp.int32)
@@ -594,13 +822,14 @@
     attended = jnp.einsum("hqk,khd->qhd", prob_low, values, preferred_element_type=f32)
     attended_low = attended.reshape(seq_len, head_cols).astype(bf)
     attn_part = jnp.dot(attended_low, out_weight, preferred_element_type=f32).astype(bf)
-    attn_out = sum_blocks(attn_part.reshape(n_seq, shard_len, width), "seq", 3)
+    attn_out = sum_seq(attn_part.reshape(n_seq, shard_len, width), 3)
     residual = tokens + attn_out
     normed_two, inv_two = norm_parts(residual)
 
     if per_owner > first_slots:
         second_slots = per_owner - first_slots
-        second = exchange(packed[1]).reshape(n_dp * second_slots, rows, wide)
+        late, normed_two = lax.optimization_barrier((late, normed_two))
+        second = late.reshape(n_dp * second_slots, rows, wide)
         table = jnp.concatenate([first_table, second], axis=0)
         index = jnp.where(
             place < first_slots,
@@ -630,13 +859,19 @@
     )
 
     def gather_tokens(part):
-        return gather_blocks(part, "dp", 4).reshape(-1, width)
+        return gather_dp(part, 4).reshape(-1, width)
 
     def scatter_tokens(part):
-        return sum_blocks(part.astype(bf).reshape(2 * n_dp, shard_len, width), "dp", 5)
+        return sum_dp(part.astype(bf).reshape(2, n_dp, shard_len, width), 5)
 
     upstream = cotangent.reshape(shard_len, width)
-    upstream_all = gather_tokens(upstream)
+    every = lax.all_gather(upstream, "dp", axis=0, tiled=True)
+    other = lax.ppermute(every, "seq", sibling)
+    upstream_all = jnp.where(
+        core == 0,
+        jnp.concatenate([every, other], axis=0),
+        jnp.concatenate([other, every], axis=0),
+    )
     normed_two_all = gather_tokens(normed_two.astype(bf))
     up_proj = jnp.einsum("tr,jrc->tjc", normed_two_all, up_weight, preferred_element_type=f32)
     gate_proj = jnp.einsum("tr,jrc->tjc", normed_two_all, gate_weight, preferred_element_type=f32)
@@ -677,7 +912,7 @@
     )
     norm_two_grad = scatter_tokens(norm_two_grad)
     residual_grad = upstream.astype(f32) + norm_back(normed_two, inv_two, norm_two_grad)
-    residual_grad_all = gather_blocks(residual_grad.astype(bf), "seq", 2).reshape(seq_len, width)
+    residual_grad_all = gather_seq(residual_grad.astype(bf), 7).reshape(seq_len, width)
 
     attended_grad = jnp.einsum(
         "tc,rc->tr", residual_grad_all, out_weight, preferred_element_type=f32
@@ -699,9 +934,7 @@
     )
     qkv_grad_low = qkv_grad.astype(bf).reshape(seq_len, 3 * head_cols)
     norm_one_part = jnp.einsum("tf,rf->tr", qkv_grad_low, qkv_weight, preferred_element_type=f32)
-    norm_one_grad = sum_blocks(
-        norm_one_part.astype(bf).reshape(n_seq, shard_len, width), "seq", 3
-    )
+    norm_one_grad = sum_seq(norm_one_part.astype(bf).reshape(n_seq, shard_len, width), 3)
     input_grad = (residual_grad + norm_back(normed_one, inv_one, norm_one_grad)).reshape(
         block_input.shape
     )
@@ -719,6 +952,9 @@
     qkv_piece = qkv_piece.reshape(3, rows, wide)
     out_piece = out_piece.reshape(sub, n_dp, wide).transpose(1, 0, 2).reshape(1, rows, wide)
 
+    up_grad, gate_grad, down_grad, _ = lax.optimization_barrier(
+        (up_grad, gate_grad, down_grad, residual_grad_all)
+    )
     ug_grad = jnp.concatenate([up_grad, gate_grad], axis=0)
     kept = lax.dynamic_slice_in_dim(ug_grad, core * rows, rows, axis=1)
     sent = lax.dynamic_slice_in_dim(ug_grad, (1 - core) * rows, rows, axis=1)

time: 1350 us -> 1160 us (0.86)
  blocking collectives: 99.9 us -> 0 us
  Pallas kernels: 715 us -> 648 us
  waiting for transfers between devices: 221 us -> 195 us
    all_to_all x1 -> x0, blocking collectives: 99.9 us -> none  [exchange(): return lax.all_to_all(packed, 'dp', 0, 0)]
    all_to_all x1, waiting for transfers between devices: 92.8 us -> 34.9 us  [exchange(): return lax.all_to_all(packed, 'dp', 0, 0)]
    all_to_all x2, waiting for transfers between devices: 57.7 us -> 0.01 us  [give_back(): return lax.all_to_all(jnp.take(pieces, units, axis=0), 'dp', 0, 0)]
    pallas_call x8 -> x7, Pallas kernels: 436 us -> 382 us  [the longest x2 157 us: sum_dp(): pl.pallas_call(sum_dp_kernel, out_shape=jax.ShapeDtypeStruct((rows, colum...]
    all_gather x1, waiting for transfers between devices: 0.01 us -> 44.6 us  [local(): lax.all_gather(ug[ff_blocks:], 'seq', axis=1, tiled=True, axis_index_grou...]
    all_gather x1, waiting for transfers between devices: 0.01 us -> 44.6 us  [local(): lax.all_gather(down.reshape(ff_blocks, sub, width), 'seq', axis=1, tiled=...]
    pallas_call x1, Pallas kernels: 29.5 us -> 15.6 us  [pack(): pl.pallas_call(functools.partial(pack_kernel, n_dp, n_seq // 2, first_slo...]
  transfers between devices with their start and end apart: 11 -> 13, of which waited for: 5 -> 7; matrix products, arithmetic and copies ran while one was open for 15% -> 19% of each run, Pallas kernels for 47% -> 52%
where the time goes in v3:
time: 1160 us
  Pallas kernels  648 us (56%)
  waiting for transfers between devices  195 us (17%)
  matrix products  158 us (14%)
  local copies, waits for them, and re-layouts  74.2 us (6%)
  other arithmetic  48.7 us (4%)
  starting transfers between devices  16.1 us (1%)
  between operations  15.4 us (1%)
    pallas_call x2, Pallas kernels, sum_dp(): pl.pallas_call(sum_dp_kernel, out_shape=jax.ShapeDtypeStruct((rows, colum...  157 us
    pallas_call x1, Pallas kernels, spread_attention(): pl.pallas_call(spread_kernel, out_shape=[jax.ShapeDtypeStruct((n_seq, n_d...  107 us
    pallas_call x1, Pallas kernels, front(): pl.pallas_call(front_kernel, out_shape=[jax.ShapeDtypeStruct(packed.shape...  94 us
    pallas_call x1, Pallas kernels, collect_attention(): pl.pallas_call(collect_kernel, out_shape=[jax.ShapeDtypeStruct((n_seq,) +...  93.5 us
    reduce_scatter x3, waiting for transfers between devices, chip_sum(): lax.psum_scatter(part.astype(bf), 'seq', scatter_dimension=1, tiled=True,...  60.9 us
    pallas_call x2, Pallas kernels, sum_seq(): pl.pallas_call(sum_seq_kernel, out_shape=jax.ShapeDtypeStruct((rows, colu...  57.2 us
    pallas_call x1, Pallas kernels, adam(): pl.pallas_call(functools.partial(adam_kernel, n_dp, n_seq // 2, first_slo...  50.9 us
    all_gather x1, waiting for transfers between devices, local(): lax.all_gather(ug[ff_blocks:], 'seq', axis=1, tiled=True, axis_index_grou...  44.6 us
  transfers between devices with their start and end apart: 13, of which 7 were waited for; matrix products, arithmetic and copies ran while one was open for 19% of the time, Pallas kernels for 52%

profile of v3, /device:TPU:0, one launch (start us, length us, event | category | flops | bytes accessed | tf_op | source)
XLA Modules:
  0.0 1155.9 jit_solution(14966758051774222044)
XLA Ops:
  13.6 15.6 %pack.1 = (bf16[4,4,256,512]{3,2,1,0:T(8,128)(2,1)}, bf16[4,4,256,512]{3,2,1,0:T(8,128)(2,1)}) custom-call(s32[8]{0:T(128)S(1)} %fusion.71.flags, f32[256,8,2048]{2,1,0:T(8,128)} %refs_4_.1), custom_call_target="tpu_custom_call" | custom-call | tf_op jit(solution)/shard_map/pack/pallas_call | solution.py:113
  31.5 94.0 %front.1 = (bf16[4,4,256,512]{3,2,1,0:T(8,128)(2,1)S(1)}, bf16[8,128,2048]{2,1,0:T(8,128)(2,1)S(1)}) custom-call(bf16[4,4,256,512]{3,2,1,0:T(8,128)(2,1)S(1)} %copy-done.6, bf16[128,2048]{1,0:T(8,128)(2,1)S(1)} %fusion.44.x_ref), custom_call_target="tpu_custom_call" | custom-call | bytes 270000000 | tf_op jit(solution)/shard_map/front/pallas_call | solution.py:427
  136.2 106.6 %spread_attention.1 = (bf16[8,4,64,768]{3,2,1,0:T(8,128)(2,1)S(1)}, bf16[4,64,2048]{2,1,0:T(8,128)(2,1)S(1)}) custom-call(bf16[8,64,768]{2,1,0:T(8,128)(2,1)S(1)} %copy-done.9, bf16[64,2048]{1,0:T(8,128)(2,1)S(1)} %bitcast.207), custom_call_target="tpu_custom_call" | custom-call | bytes 225000000 | tf_op jit(solution)/shard_map/spread_attention/pallas_call | solution.py:661
  275.9 29.0 %sum_seq.2 = f32[128,2048]{1,0:T(8,128)S(1)} custom-call(bf16[8,128,2048]{2,1,0:T(8,128)(2,1)S(1)} %bitcast.192), custom_call_target="tpu_custom_call" | custom-call | bytes 84000000 | tf_op jit(solution)/shard_map/sum_seq/pallas_call | solution.py:549
  306.6 34.9 %all-to-all-done = bf16[4,4,256,512]{3,2,1,0:T(8,128)(2,1)} async-done(((bf16[4,4,256,512]{3,2,1,0:T(8,128)(2,1)}), bf16[4,4,256,512]{3,2,1,0:T(8,128)(2,1)}, u32[]{:S(2)}, u32[]{:S(2)}) %all-to-all-start) | async-done | bytes 4194336 | tf_op jit(solution)/shard_map/all_to_all | solution.py:785
  367.6 41.9 %gather_dp.1 = bf16[2,4,128,2048]{3,2,1,0:T(8,128)(2,1)S(1)} custom-call(bf16[128,2048]{1,0:T(8,128)(2,1)S(1)} %convert_element_type.147.x_ref), custom_call_target="tpu_custom_call" | custom-call | bytes 120000000 | tf_op jit(solution)/shard_map/gather_dp/pallas_call | solution.py:501
  417.7 10.0 fusion.91
  427.7 44.6 %all-gather.6.cloned.1.call-done = bf16[4,2048,256]{2,1,0:T(8,128)(2,1)} async-done(((bf16[4,512,256]{2,1,0:T(8,128)(2,1)}), bf16[4,2048,256]{2,1,0:T(8,128)(2,1)}) %all-gather.6.cloned.1.call-update) | async-done | bytes 4194320 | tf_op jit(solution)/shard_map/all_gather | solution.py:853
  472.3 9.9 fusion.90
  482.2 44.6 %all-gather.10.cloned.1.call-done = bf16[4,256,2048]{2,1,0:T(8,128)(2,1)} async-done(((bf16[4,64,2048]{2,1,0:T(8,128)(2,1)}), bf16[4,256,2048]{2,1,0:T(8,128)(2,1)}) %all-gather.10.cloned.1.call-update) | async-done | bytes 4194320 | tf_op jit(solution)/shard_map/all_gather | solution.py:857
  526.7 14.1 %multiply_convert_fusion.1 = (bf16[1024,4,256]{2,0,1:T(8,128)(2,1)}, bf16[1024,4,256]{2,0,1:T(8,128)(2,1)S(1)}, bf16[1024,4,256]{2,0,1:T(8,128)(2,1)}) fusion(f32[1024,4,256]{2,0,1:T(8,128)} %fusion.91, f32[1024,4,256]{2,0,1:T(8,128)} %fusion.90, bf16[4,256,2048]{2,1,0:T(8,128)(2,1)} %all-gather.10.cloned.1.call-done, ...), kind=kOutput, calls=%fused_computation.21 | convolution fusion | flops 4328521728 | bytes 23068672 | tf_op jit(solution)/shard_map/tc,jhc->tjh/dot_general | solution.py:885
  542.2 8.8 convolution_convert_fusion.2
  551.1 9.4 convert_bitcast_fusion.1
  560.7 9.4 convert_bitcast_fusion
  570.2 11.0 fusion.92
  588.2 44.5 %sum_dp.3 = f32[128,2048]{1,0:T(8,128)S(1)} custom-call(bf16[2,4,128,2048]{3,2,1,0:T(8,128)(2,1)S(1)} %bitcast.195), custom_call_target="tpu_custom_call" | custom-call | bytes 120000000 | tf_op jit(solution)/shard_map/sum_dp/pallas_call | solution.py:599
  634.2 31.9 %gather_seq.1 = bf16[8,128,2048]{2,1,0:T(8,128)(2,1)S(1)} custom-call(bf16[128,2048]{1,0:T(8,128)(2,1)S(1)} %get-tuple-element.50.x_ref), custom_call_target="tpu_custom_call" | custom-call | bytes 84000000 | tf_op jit(solution)/shard_map/gather_seq/pallas_call | solution.py:458
  674.1 54.9 %reduce-scatter.6.cloned.1.call-done = bf16[4,512,256]{1,2,0:T(8,128)(2,1)} async-done(((bf16[4,2048,256]{1,2,0:T(8,128)(2,1)}), bf16[4,512,256]{1,2,0:T(8,128)(2,1)}) %reduce-scatter.6.cloned.1.call-update) | async-done | bytes 1048592 | tf_op jit(solution)/shard_map/reduce_scatter | solution.py:892
  771.8 14.9 %fusion.29 = f32[1024,2,128]{0,2,1:T(8,128)} fusion(bf16[1024,2,128]{0,2,1:T(8,128)(2,1)} %copy-done.35, f32[2,1024,1024]{1,2,0:T(8,128)} %fusion.66, f32[2,1024,1024]{1,2,0:T(8,128)} %get-tuple-element.93, f32[2,1024]{1,0:T(2,128)S(1)} %get-tuple-element.92), kind=kOutput, calls=%fused_computation.52 | convolution fusion | flops 551554048 | bytes 18358272 | tf_op jit(solution)/shard_map/hqk,qhd->khd/dot_general | solution.py:926
  786.7 15.4 %broadcast_multiply_fusion.1 = (f32[1024,2,128]{0,2,1:T(8,128)}, f32[1024,2,128]{0,2,1:T(8,128)}, f32[1024,2,128]{0,2,1:T(8,128)}) fusion(f32[1024,128]{0,1:T(8,128)S(1)} %copy-done.25, f32[1024,2,128]{0,2,1:T(8,128)} %fusion.29, bf16[1024,2,128]{0,2,1:T(8,128)(2,1)S(1)} %copy-done.34, f32[2,1024,1024]{1,2,0:T(8,128)} %fusion.66, ...), kind=kOutput, calls=%fused_computation.104 | convolution fusion | flops 552078336 | bytes 22028288 | tf_op jit(solution)/shard_map/hqk,khd->qhd/dot_general | solution.py:925
  817.6 93.5 %collect_attention.1 = (bf16[8,64,768]{2,1,0:T(8,128)(2,1)S(1)}, bf16[64,2048]{1,0:T(8,128)(2,1)S(1)}) custom-call(bf16[8,4,64,768]{3,2,1,0:T(8,128)(2,1)S(1)} %bitcast.206, bf16[4,64,2048]{2,1,0:T(8,128)(2,1)S(1)} %bitcast.208), custom_call_target="tpu_custom_call" | custom-call | bytes 225000000 | tf_op jit(solution)/shard_map/collect_attention/pallas_call | solution.py:723
  951.5 112.2 %sum_dp.2 = f32[128,2048]{1,0:T(8,128)S(1)} custom-call(bf16[2,4,128,2048]{3,2,1,0:T(8,128)(2,1)S(1)} %bitcast.196), custom_call_target="tpu_custom_call" | custom-call | bytes 120000000 | tf_op jit(solution)/shard_map/sum_dp/pallas_call | solution.py:599
  1067.6 28.2 %sum_seq.3 = f32[128,2048]{1,0:T(8,128)S(1)} custom-call(bf16[8,128,2048]{2,1,0:T(8,128)(2,1)S(1)} %bitcast.197), custom_call_target="tpu_custom_call" | custom-call | bytes 84000000 | tf_op jit(solution)/shard_map/sum_seq/pallas_call | solution.py:549
  1097.9 50.9 %adam.1 = (f32[256,8,2048]{2,1,0:T(8,128)}, f32[256,8,2048]{2,1,0:T(8,128)}, f32[256,8,2048]{2,1,0:T(8,128)}, f32[256,8,2048]{2,1,0:T(8,128)}) custom-call(s32[8]{0:T(128)S(1)} %get-tuple-element.49.kinds, bf16[4,4,256,512]{3,2,1,0:T(8,128)(2,1)} %all-to-all-done.1.refs_0_, bf16[4,4,256,512]{3,2,1,0:T(8,128)(2,1)} %all-to-all-done.2.refs_1_, ...), custom_call_target="tpu_custom_call" | custom-call | tf_op jit(solution)/shard_map/adam/pallas_call | solution.py:190
  (231 shorter events, 210.4 us)
Async XLA Ops:
  7.2 360.2 %all-gather.12.cloned.1.call-start = ((), (), s32[]{:S(2)}) async-start(), calls=%async_computation.12 | async-start | bytes 2621440 | tf_op jit(solution)/shard_map/all_gather | solution.py:868
  10.0 19.2 %copy-start.40 = (f32[128]{0:T(128)}, f32[128]{0:T(128)S(1)}, u32[]{:S(2)}) copy-start(f32[128]{0:T(128)S(1)} %broadcast_multiply_fusion.7) | copy-start | bytes 1540
  243.8 97.7 %all-to-all-start = ((bf16[4,4,256,512]{3,2,1,0:T(8,128)(2,1)}), bf16[4,4,256,512]{3,2,1,0:T(8,128)(2,1)}, u32[]{:S(2)}, u32[]{:S(2)}) async-start(bf16[4,4,256,512]{3,2,1,0:T(8,128)(2,1)} %get-tuple-element.32), calls=%async_computation | async-start | bytes 8388608 | tf_op jit(solution)/shard_map/all_to_all | solution.py:785
  248.8 168.8 %all-gather.8.cloned.1.call-start = ((), (), s32[]{:S(2)}) async-start(), calls=%async_computation.7 | async-start | bytes 5242880 | tf_op jit(solution)/shard_map/all_gather | solution.py:850
  275.9 29.1 %copy-start.14 = (bf16[1,128,2048]{2,1,0:T(8,128)(2,1)S(1)}, bf16[1,128,2048]{2,1,0:T(8,128)(2,1)}, u32[]{:S(2)}) copy-start(bf16[1,128,2048]{2,1,0:T(8,128)(2,1)} %param.7) | copy-start | bytes 1572868
  304.9 44.3 %copy-start = (f32[128,2048]{1,0:T(8,128)}, f32[128,2048]{1,0:T(8,128)S(1)}, u32[]{:S(2)}) copy-start(f32[128,2048]{1,0:T(8,128)S(1)} %sum_seq.2) | copy-start | bytes 3145732
  359.0 2.8 collective-permute-start
  365.3 107.0 %all-gather.6.cloned.1.call-start = ((), (), s32[]{:S(2)}) async-start(), calls=%async_computation.6 | async-start | bytes 5242880 | tf_op jit(solution)/shard_map/all_gather | solution.py:853
  366.0 160.7 %all-gather.10.cloned.1.call-start = ((), (), s32[]{:S(2)}) async-start(), calls=%async_computation.8 | async-start | bytes 5242880 | tf_op jit(solution)/shard_map/all_gather | solution.py:857
  367.3 300.9 %reduce-scatter.8.cloned.1.call-start = ((), (), s32[]{:S(2)}) async-start(), calls=%async_computation.11 | async-start | bytes 5242880 | tf_op jit(solution)/shard_map/reduce_scatter | solution.py:892
  367.3 114.8 %collective-permute-start.1 = (bf16[512,2048]{1,0:T(8,128)(2,1)}, bf16[512,2048]{1,0:T(8,128)(2,1)}, u32[]{:S(2)}, u32[]{:S(2)}) collective-permute-start(bf16[512,2048]{1,0:T(8,128)(2,1)} %bitcast.232), channel_id=1, source_target_pairs={{0,1},{1,0},{2,3},{3,2},{4,5},{5,4},{6,7},{7,6},{8,9},{9,8},{10,11... | collective-permute-start | bytes 6291464 | tf_op jit(solution)/shard_map/ppermute | solution.py:869
  551.1 123.1 %reduce-scatter.4.cloned.1.call-start = ((), (), s32[]{:S(2)}) async-start(), calls=%async_computation.9 | async-start | bytes 5242880 | tf_op jit(solution)/shard_map/reduce_scatter | solution.py:892
  560.5 168.5 %reduce-scatter.6.cloned.1.call-start = ((), (), s32[]{:S(2)}) async-start(), calls=%async_computation.10 | async-start | bytes 5242880 | tf_op jit(solution)/shard_map/reduce_scatter | solution.py:892
  588.2 44.7 %copy-start.26 = (bf16[1,128,2048]{2,1,0:T(8,128)(2,1)S(1)}, bf16[1,128,2048]{2,1,0:T(8,128)(2,1)}, u32[]{:S(2)}) copy-start(bf16[1,128,2048]{2,1,0:T(8,128)(2,1)} %param.8) | copy-start | bytes 1572868
  732.7 2.9 collective-permute-start.2
  756.2 183.3 %all-to-all-start.2 = ((bf16[4,4,256,512]{3,2,1,0:T(8,128)(2,1)}), bf16[4,4,256,512]{3,2,1,0:T(8,128)(2,1)}, u32[]{:S(2)}, u32[]{:S(2)}) async-start(bf16[4,4,256,512]{3,2,1,0:T(8,128)(2,1)} %broadcast_select_fusion), calls=%async_computation.5 | async-start | bytes 8388608 | tf_op jit(solution)/shard_map/all_to_all | solution.py:971
  939.5 158.3 %all-to-all-start.1 = ((bf16[4,4,256,512]{3,2,1,0:T(8,128)(2,1)}), bf16[4,4,256,512]{3,2,1,0:T(8,128)(2,1)}, u32[]{:S(2)}, u32[]{:S(2)}) async-start(bf16[4,4,256,512]{3,2,1,0:T(8,128)(2,1)} %broadcast_select_fusion.1), calls=%async_computation.4 | async-start | bytes 8388608 | tf_op jit(solution)/shard_map/all_to_all | solution.py:971
  951.5 112.3 %copy-start.8 = (bf16[8,4,64,768]{3,2,1,0:T(8,128)(2,1)S(1)}, bf16[8,4,64,768]{3,2,1,0:T(8,128)(2,1)}, u32[]{:S(2)}) copy-start(bf16[8,4,64,768]{3,2,1,0:T(8,128)(2,1)} %copy-done.7) | copy-start | bytes 9437188
  951.5 112.3 %copy-start.28 = (bf16[1024,3,2,128]{0,3,2,1:T(8,128)(2,1)S(1)}, bf16[1024,3,2,128]{0,3,2,1:T(8,128)(2,1)}, u32[]{:S(2)}) copy-start(bf16[1024,3,2,128]{0,3,2,1:T(8,128)(2,1)} %copy-done.27) | copy-start | bytes 4718596
  1067.5 28.3 %copy-start.15 = (bf16[1,128,2048]{2,1,0:T(8,128)(2,1)S(1)}, bf16[1,128,2048]{2,1,0:T(8,128)(2,1)}, u32[]{:S(2)}) copy-start(bf16[1,128,2048]{2,1,0:T(8,128)(2,1)} %param.7) | copy-start | bytes 1572868
  1067.6 28.3 %copy-start.41 = (f32[128]{0:T(128)S(1)}, f32[128]{0:T(128)}, u32[]{:S(2)}) copy-start(f32[128]{0:T(128)} %copy-done.40) | copy-start | bytes 1540
  1067.6 28.3 %copy-start.43 = (f32[128]{0:T(128)S(1)}, f32[128]{0:T(128)}, u32[]{:S(2)}) copy-start(f32[128]{0:T(128)} %copy-done.42) | copy-start | bytes 1540
  1067.6 28.6 %copy-start.1 = (f32[128,2048]{1,0:T(8,128)S(1)}, f32[128,2048]{1,0:T(8,128)}, u32[]{:S(2)}) copy-start(f32[128,2048]{1,0:T(8,128)} %copy-done) | copy-start | bytes 3145732
  1067.6 28.6 %copy-start.23 = (f32[128,2048]{1,0:T(8,128)S(1)}, f32[128,2048]{1,0:T(8,128)}, u32[]{:S(2)}) copy-start(f32[128,2048]{1,0:T(8,128)} %get-tuple-element.51) | copy-start | bytes 3145732
  (40 other events, 218.9 us)
Sparse Core Ops, SparseCore 0:
  9.6 103.0 all-gather.11
  365.4 52.2 all-gather.7
  419.5 52.6 all-gather.5
  474.0 52.6 all-gather.9
  551.2 52.7 reduce-scatter.7
  607.0 67.0 reduce-scatter.3
  677.1 51.8 reduce-scatter.5

commit v4 on v3

--- a/solution.py
+++ b/solution.py
@@ -294,10 +294,13 @@
 def relay_sum(owns, sent, came, place, count, device_of, send_sem, recv_sem, ready):
     views = range(len(owns))
 
-    def leg(view, way, block, target):
+    def spot(way, block, receiver):
+        return jnp.where(block == receiver, count, block) if way else block
+
+    def leg(view, way, block, target, receiver):
         return send(
-            sent[view].at[way, block],
-            came[view].at[way, block],
+            sent[view].at[block],
+            came[view].at[spot(way, block, receiver)],
             send_sem.at[view, way, block],
             recv_sem.at[view, way, block],
             device_of(target),
@@ -322,15 +325,15 @@
 
                     @pl.when(behind(way))
                     def _():
-                        leg(view, way, block, target).wait_recv()
-                        value = owns[view](block) + came[view][way, block].astype(f32)
-                        sent[view][way, block] = value.astype(sent[view].dtype)
+                        leg(view, way, block, target, place).wait_recv()
+                        value = owns[view](block) + came[view][block].astype(f32)
+                        sent[view][block] = value.astype(sent[view].dtype)
 
                     @pl.when(jnp.logical_not(behind(way)))
                     def _():
-                        sent[view][way, block] = owns[view](block).astype(sent[view].dtype)
-
-                    leg(view, way, block, target).start()
+                        sent[view][block] = owns[view](block).astype(sent[view].dtype)
+
+                    leg(view, way, block, target, target).start()
 
     ready(place)
     for way in range(2):
@@ -338,13 +341,13 @@
         @pl.when(behind(way))
         def _():
             for view in views:
-                leg(view, way, place, lax.rem(place + 1, count)).wait_recv()
+                leg(view, way, place, lax.rem(place + 1, count), place).wait_recv()
 
     totals = []
     for view in views:
         total = owns[view](place)
         for way in range(2):
-            value = came[view][way, place].astype(f32)
+            value = came[view][place if way == 0 else count].astype(f32)
             total = total + jnp.where(behind(way), value, 0.0)
         totals.append(total)
     for step in range(count - 1):
@@ -354,7 +357,7 @@
             @pl.when(inside)
             def _():
                 for view in views:
-                    leg(view, way, block, target).wait_send()
+                    leg(view, way, block, target, target).wait_send()
 
     return totals
 
@@ -595,7 +598,6 @@
 
 def sum_dp(x, collective_id):
     _, n_dp, rows, columns = x.shape
-    slots = pltpu.VMEM((2, n_dp, rows, columns), x.dtype)
     return pl.pallas_call(
         sum_dp_kernel,
         out_shape=jax.ShapeDtypeStruct((rows, columns), f32),
@@ -603,8 +605,8 @@
         out_specs=VMEM,
         scratch_shapes=[
             pltpu.VMEM((n_dp, rows, columns), x.dtype),
-            slots,
-            slots,
+            pltpu.VMEM((n_dp, rows, columns), x.dtype),
+            pltpu.VMEM((n_dp + 1, rows, columns), x.dtype),
             DMA((n_dp,)),
             DMA((n_dp,)),
             DMA((1, 2, n_dp)),
@@ -718,8 +720,6 @@
     n_seq = lax.axis_size("seq")
     n_dp = lax.axis_size("dp")
     tail = qkv.shape[2:]
-    q_slots = pltpu.VMEM((2, n_dp, n_seq) + tail, qkv.dtype)
-    o_slots = pltpu.VMEM((2, n_dp) + out.shape[1:], out.dtype)
     return pl.pallas_call(
         collect_kernel,
         out_shape=[
@@ -729,10 +729,10 @@
         in_specs=[VMEM, VMEM],
         out_specs=[VMEM, VMEM],
         scratch_shapes=[
-            q_slots,
-            q_slots,
-            o_slots,
-            o_slots,
+            pltpu.VMEM((n_dp, n_seq) + tail, qkv.dtype),
+            pltpu.VMEM((n_dp + 1, n_seq) + tail, qkv.dtype),
+            pltpu.VMEM((n_dp,) + out.shape[1:], out.dtype),
+            pltpu.VMEM((n_dp + 1,) + out.shape[1:], out.dtype),
             pltpu.VMEM((n_seq,) + tail, qkv.dtype),
             DMA,
             DMA((2, 2, n_dp)),
@@ -744,6 +744,535 @@
         cost_estimate=takes(75),
         name="collect_attention",
     )(qkv, out)
+
+
+def ring_chip(place, chips):
+    return jnp.where(place < chips // 2, 2 * place, 2 * (chips - 1 - place) + 1)
+
+
+def ring_place(chip, chips):
+    line = chip // 2
+    return jnp.where(lax.rem(chip, 2) == 0, line, chips - 1 - line)
+
+
+class Ring:
+    def __init__(self, chips, chip, core, dp_index, send_sem, recv_sem):
+        self.chips = chips
+        self.place = ring_place(chip, chips)
+        self.core = core
+        self.dp_index = dp_index
+        self.send_sem = send_sem
+        self.recv_sem = recv_sem
+        self.last = chips // 2
+
+    def at(self, offset):
+        return ring_chip(lax.rem(self.place + offset + self.chips, self.chips), self.chips)
+
+    def device(self, way):
+        return (self.dp_index, self.at(1 if way == 0 else -1) * 2 + self.core)
+
+    def leg(self, view, way, step, src, dst):
+        return send(
+            src, dst, self.send_sem.at[view, way, step], self.recv_sem.at[view, way, step], self.device(way)
+        )
+
+
+def ring_gather_leg(ring, views, view, way, step, arriving):
+    distance = step if arriving else step - 1
+    block = ring.at(-distance if way == 0 else distance)
+    ref = views[view](block, way if step == ring.last else None)
+    return ring.leg(view, way, step - 1, ref, ref)
+
+
+def pick_kernel(first_slots, ff_blocks, info, first_ref, *refs):
+    late_ref = refs[0] if len(refs) == 5 else None
+    mine_ref, given_ref, down_ref, piece_ref = refs[-4:]
+    unit = pl.program_id(0)
+    rows, wide = piece_ref.shape
+    half = wide // 2
+    sub, width = down_ref.shape[1:]
+    groups = width // wide
+
+    @pl.when(info[2, unit] == 0)
+    def _():
+        piece_ref[...] = first_ref[0]
+
+    if late_ref is not None:
+
+        @pl.when(info[2, unit] != 0)
+        def _():
+            piece_ref[...] = late_ref[0]
+
+    @pl.when(unit < 2 * ff_blocks)
+    def _():
+        @pl.when(info[3, 0] == 0)
+        def _():
+            mine_ref[0] = piece_ref[:, :half]
+            given_ref[0] = piece_ref[:, half:]
+
+        @pl.when(info[3, 0] != 0)
+        def _():
+            mine_ref[0] = piece_ref[:, half:]
+            given_ref[0] = piece_ref[:, :half]
+
+    @pl.when(unit >= 2 * ff_blocks)
+    def _():
+        for g in range(groups):
+            down_ref[0, :, g * wide : (g + 1) * wide] = piece_ref[g * sub : (g + 1) * sub, :]
+
+
+def pick_ff(first_table, late_table, owners, place, core, ff_blocks, sub, first_slots):
+    rows, wide = first_table.shape[1:]
+    width = rows // sub * wide
+    units = 3 * ff_blocks
+    owners, place = owners[4:], place[4:]
+    in_late = place >= first_slots
+    late_slots = 1 if late_table is None else late_table.shape[0] // lax.axis_size("dp")
+    info = jnp.stack(
+        [
+            owners * first_slots + jnp.minimum(place, first_slots - 1),
+            owners * late_slots + jnp.maximum(place - first_slots, 0),
+            in_late.astype(jnp.int32),
+            jnp.full((units,), core, jnp.int32),
+        ]
+    ).astype(jnp.int32)
+    tables = [first_table] if late_table is None else [first_table, late_table]
+    specs = [
+        pl.BlockSpec((1, rows, wide), lambda u, info: (info[0, u], 0, 0)),
+        pl.BlockSpec((1, rows, wide), lambda u, info: (info[1, u], 0, 0)),
+    ]
+    side = pl.BlockSpec(
+        (1, rows, wide // 2), lambda u, info: (jnp.minimum(u, 2 * ff_blocks - 1), 0, 0)
+    )
+    return pl.pallas_call(
+        functools.partial(pick_kernel, first_slots, ff_blocks),
+        out_shape=[
+            jax.ShapeDtypeStruct((2 * ff_blocks, rows, wide // 2), bf),
+            jax.ShapeDtypeStruct((2 * ff_blocks, rows, wide // 2), bf),
+            jax.ShapeDtypeStruct((ff_blocks, sub, width), bf),
+        ],
+        grid_spec=pltpu.PrefetchScalarGridSpec(
+            num_scalar_prefetch=1,
+            grid=(units,),
+            in_specs=specs[: len(tables)],
+            out_specs=[
+                side,
+                side,
+                pl.BlockSpec(
+                    (1, sub, width), lambda u, info: (jnp.maximum(u - 2 * ff_blocks, 0), 0, 0)
+                ),
+            ],
+            scratch_shapes=[pltpu.VMEM((rows, wide), bf)],
+        ),
+        compiler_params=pltpu.CompilerParams(vmem_limit_bytes=16 << 20),
+        cost_estimate=takes(6),
+        name="pick_ff",
+    )(info, *tables)
+
+
+def pick_attention_kernel(info, piece_ref, rows_ref, out_ref):
+    unit = pl.program_id(0)
+    blocks, sub, columns = rows_ref.shape
+    step = columns // 3
+    groups = out_ref.shape[1] // piece_ref.shape[2]
+    wide = piece_ref.shape[2]
+    share = wide // step
+    for u in range(3):
+
+        @pl.when(unit == u)
+        def _():
+            for block in range(blocks):
+                g, h = block // share, block % share
+                rows_ref[block, :, u * step : (u + 1) * step] = piece_ref[
+                    0, g * sub : (g + 1) * sub, h * step : (h + 1) * step
+                ]
+
+    @pl.when(unit == 3)
+    def _():
+        for g in range(groups):
+            out_ref[:, g * wide : (g + 1) * wide] = piece_ref[0, g * sub : (g + 1) * sub, :]
+
+
+def pick_attention(first_table, index, n_seq, sub, width):
+    rows, wide = first_table.shape[1:]
+    columns = 3 * (width // n_seq)
+    return pl.pallas_call(
+        pick_attention_kernel,
+        out_shape=[
+            jax.ShapeDtypeStruct((n_seq, sub, columns), bf),
+            jax.ShapeDtypeStruct((sub, width), bf),
+        ],
+        grid_spec=pltpu.PrefetchScalarGridSpec(
+            num_scalar_prefetch=1,
+            grid=(4,),
+            in_specs=[pl.BlockSpec((1, rows, wide), lambda u, info: (info[u], 0, 0))],
+            out_specs=[
+                pl.BlockSpec((n_seq, sub, columns), lambda u, info: (0, 0, 0)),
+                pl.BlockSpec((sub, width), lambda u, info: (0, 0)),
+            ],
+        ),
+        compiler_params=pltpu.CompilerParams(vmem_limit_bytes=16 << 20),
+        cost_estimate=takes(3),
+        name="pick_attention",
+    )(index.astype(jnp.int32), first_table)
+
+
+def arrange_kernel(ff_blocks, units, ug_ref, down_ref, *refs):
+    piece_ref = refs[-1]
+    unit = units[pl.program_id(0)]
+    rows, wide = piece_ref.shape[1:]
+    sub, width = down_ref.shape[1:]
+    groups = width // wide
+
+    @pl.when((unit >= 4) & (unit < 4 + 2 * ff_blocks))
+    def _():
+        piece_ref[0] = ug_ref[0]
+
+    @pl.when(unit >= 4 + 2 * ff_blocks)
+    def _():
+        for g in range(groups):
+            piece_ref[0, g * sub : (g + 1) * sub, :] = down_ref[0, :, g * wide : (g + 1) * wide]
+
+    if len(refs) == 3:
+        qkv_ref, out_ref = refs[:2]
+        blocks, _, columns = qkv_ref.shape
+        step = columns // 3
+        share = wide // step
+        for u in range(3):
+
+            @pl.when(unit == u)
+            def _():
+                for block in range(blocks):
+                    g, h = block // share, block % share
+                    piece_ref[0, g * sub : (g + 1) * sub, h * step : (h + 1) * step] = qkv_ref[
+                        block, :, u * step : (u + 1) * step
+                    ]
+
+        @pl.when(unit == 3)
+        def _():
+            for g in range(groups):
+                piece_ref[0, g * sub : (g + 1) * sub, :] = out_ref[:, g * wide : (g + 1) * wide]
+
+
+def arrange(units, ug, down, attention):
+    n_dp, slots = units.shape
+    rows, wide = ug.shape[1:]
+    sub, width = down.shape[1:]
+    ff_blocks = down.shape[0]
+    specs = [
+        pl.BlockSpec(
+            (1, rows, wide), lambda k, u: (jnp.clip(u[k] - 4, 0, 2 * ff_blocks - 1), 0, 0)
+        ),
+        pl.BlockSpec(
+            (1, sub, width),
+            lambda k, u: (jnp.clip(u[k] - 4 - 2 * ff_blocks, 0, ff_blocks - 1), 0, 0),
+        ),
+    ]
+    if attention:
+        specs.append(pl.BlockSpec(attention[0].shape, lambda k, u: (0, 0, 0)))
+        specs.append(pl.BlockSpec(attention[1].shape, lambda k, u: (0, 0)))
+    return pl.pallas_call(
+        functools.partial(arrange_kernel, ff_blocks),
+        out_shape=jax.ShapeDtypeStruct((n_dp * slots, rows, wide), bf),
+        grid_spec=pltpu.PrefetchScalarGridSpec(
+            num_scalar_prefetch=1,
+            grid=(n_dp * slots,),
+            in_specs=specs,
+            out_specs=pl.BlockSpec((1, rows, wide), lambda k, u: (k, 0, 0)),
+        ),
+        compiler_params=pltpu.CompilerParams(vmem_limit_bytes=16 << 20),
+        cost_estimate=takes(7),
+        name="arrange",
+    )(units.reshape(-1), ug, down, *attention).reshape(n_dp, slots, rows, wide)
+
+
+def weights_kernel(
+    mine_ref, given_ref, down_ref, x_ref, cot_ref, ug_all, down_all, x_all, cot_all,
+    own_sem, side_send, side_recv, ring_send, ring_recv, send_sem, recv_sem, pass_sem, take_sem
+):
+    n_seq, n_dp, seq_index, dp_index = places()
+    chips, chip, core = n_seq // 2, seq_index // 2, lax.rem(seq_index, 2)
+    sibling = (dp_index, chip * 2 + 1 - core)
+    ring = Ring(chips, chip, core, dp_index, ring_send, ring_recv)
+    blocks = down_ref.shape[0]
+    greet(
+        [(lax.rem(dp_index + k, n_dp), seq_index) for k in range(1, n_dp)]
+        + [sibling, ring.device(0), ring.device(1)]
+    )
+    sides = [
+        send(
+            given_ref.at[pl.ds(k * blocks, blocks)],
+            ug_all.at[pl.ds(k * blocks, blocks), chip, core],
+            side_send.at[k],
+            side_recv.at[k],
+            sibling,
+        )
+        for k in range(2)
+    ]
+    sides.append(send(cot_ref, cot_all.at[core], side_send.at[2], side_recv.at[2], sibling))
+    own = [
+        pltpu.make_async_copy(x_ref, x_all.at[core, dp_index], own_sem.at[0]),
+        pltpu.make_async_copy(down_ref, down_all.at[:, chip], own_sem.at[1]),
+        pltpu.make_async_copy(mine_ref, ug_all.at[:, chip, core], own_sem.at[2]),
+        pltpu.make_async_copy(cot_ref, cot_all.at[core], own_sem.at[3]),
+    ]
+    for copy in sides + own:
+        copy.start()
+
+    def part_of(base, part):
+        if part is None:
+            return pl.ds(base, blocks)
+        return pl.ds(base + part * (blocks // 2), blocks // 2)
+
+    views = [
+        lambda block, part: down_all.at[part_of(0, part), block],
+        lambda block, part: ug_all.at[part_of(0, part), block],
+        lambda block, part: ug_all.at[part_of(blocks, part), block],
+    ]
+    for copy in own:
+        copy.wait()
+    for view in range(3):
+        if view:
+            sides[view - 1].wait_recv()
+        for way in range(2):
+            ring_gather_leg(ring, views, view, way, 1, False).start()
+
+    def onward(block):
+        ref = x_all.at[core, block]
+        return send(ref, ref, pass_sem.at[block], take_sem.at[block], sibling)
+
+    onward(dp_index).start()
+    relay_gather(
+        [lambda block: x_all.at[core, block]],
+        dp_index,
+        n_dp,
+        lambda place: (place, seq_index),
+        send_sem,
+        recv_sem,
+        lambda block: onward(block).start(),
+    )
+    for step in range(2, ring.last + 1):
+        for view in range(3):
+            for way in range(2):
+                ring_gather_leg(ring, views, view, way, step - 1, True).wait_recv()
+                ring_gather_leg(ring, views, view, way, step, False).start()
+    for view in range(3):
+        for way in range(2):
+            ring_gather_leg(ring, views, view, way, ring.last, True).wait_recv()
+    for step in range(1, ring.last + 1):
+        for view in range(3):
+            for way in range(2):
+                ring_gather_leg(ring, views, view, way, step, False).wait_send()
+    for block in range(n_dp):
+        onward(block).wait_send()
+        ref = x_all.at[1 - core, block]
+        send(ref, ref, pass_sem.at[block], take_sem.at[block], sibling).wait_recv()
+    for copy in sides:
+        copy.wait_send()
+    ref = cot_all.at[1 - core]
+    send(ref, ref, side_send.at[2], side_recv.at[2], sibling).wait_recv()
+
+
+def gather_weights(mine, given, down, x, cot, collective_id):
+    n_dp = lax.axis_size("dp")
+    chips = lax.axis_size("seq") // 2
+    units, rows, half = mine.shape
+    blocks, sub, width = down.shape
+    steps = chips // 2
+    return pl.pallas_call(
+        weights_kernel,
+        out_shape=[
+            jax.ShapeDtypeStruct((units, chips, 2, rows, half), bf),
+            jax.ShapeDtypeStruct((blocks, chips, sub, width), bf),
+            jax.ShapeDtypeStruct((2, n_dp) + x.shape, bf),
+            jax.ShapeDtypeStruct((2,) + cot.shape, bf),
+        ],
+        in_specs=[ANY] * 5,
+        out_specs=[ANY] * 4,
+        scratch_shapes=[
+            DMA((4,)),
+            DMA((3,)),
+            DMA((3,)),
+            DMA((3, 2, steps)),
+            DMA((3, 2, steps)),
+            DMA((1, 2, n_dp)),
+            DMA((1, 2, n_dp)),
+            DMA((n_dp,)),
+            DMA((n_dp,)),
+        ],
+        compiler_params=comm_params(collective_id, 16),
+        cost_estimate=takes(100),
+        name="gather_weights",
+    )(mine, given, down, x, cot)
+
+
+def grads_kernel(
+    up_ref, gate_ref, down_ref, x_ref, y_ref, ug_out, down_out, x_out, y_out, *refs
+):
+    half_came, full_sent, full_came, mine = refs[0:3], refs[3:6], refs[6:9], refs[9:12]
+    side_out, x_taken, y_taken, z_sent, z_came = refs[12:17]
+    ring_send, ring_recv, z_send, z_recv, x_pass, x_take, y_pass, y_take = refs[17:25]
+    side_send, side_recv, own_sem = refs[25:]
+    n_seq, n_dp, seq_index, dp_index = places()
+    chips, chip, core = n_seq // 2, seq_index // 2, lax.rem(seq_index, 2)
+    sibling = (dp_index, chip * 2 + 1 - core)
+    ring = Ring(chips, chip, core, dp_index, ring_send, ring_recv)
+    owns = [down_ref, up_ref, gate_ref]
+    blocks = down_ref.shape[0]
+    pair = blocks // 2
+    half = up_ref.shape[-1]
+    greet(
+        [(lax.rem(dp_index + k, n_dp), seq_index) for k in range(1, n_dp)]
+        + [sibling, ring.device(0), ring.device(1)]
+    )
+
+    def leg(view, way, step):
+        if step == 0:
+            src = owns[view].at[pl.ds(way * pair, pair), ring.at(ring.last)]
+            return ring.leg(view, way, step, src, half_came[view].at[way])
+        src, dst = full_sent[view].at[step - 1, way], full_came[view].at[step - 1, way]
+        return ring.leg(view, way, step, src, dst)
+
+    def own_copy(view, way, step):
+        distance = ring.last - step
+        if step == ring.last:
+            return pltpu.make_async_copy(
+                owns[view].at[:, chip], mine[view], own_sem.at[view, 0, step - 1]
+            )
+        src = owns[view].at[:, ring.at(distance if way == 0 else -distance)]
+        return pltpu.make_async_copy(
+            src, full_sent[view].at[step - 1, way], own_sem.at[view, way, step - 1]
+        )
+
+    for view in range(3):
+        for way in range(2):
+            leg(view, way, 0).start()
+    for step in range(1, ring.last + 1):
+        for view in range(3):
+            for way in range(2 if step < ring.last else 1):
+                own_copy(view, way, step).start()
+
+    def column_sum(ref, taken, out, pass_sem, take_sem, z):
+        def onward(block):
+            return send(
+                ref.at[1 - core, block], taken.at[block], pass_sem.at[block], take_sem.at[block], sibling
+            )
+
+        for block in [b for k in range(n_dp // 2) for b in (n_dp - 1 - k, k)]:
+            onward(block).start()
+        total = relay_sum(
+            [lambda block: ref[core, block].astype(f32) + taken[block].astype(f32)],
+            [z_sent.at[z]],
+            [z_came.at[z]],
+            dp_index,
+            n_dp,
+            lambda place: (place, seq_index),
+            z_send.at[z],
+            z_recv.at[z],
+            lambda block: onward(block).wait_recv(),
+        )[0]
+        out[...] = total
+        for block in range(n_dp):
+            onward(block).wait_send()
+
+    def ring_step(step):
+        for view in range(3):
+            for way in range(2):
+                own_copy(view, way, step).wait()
+                leg(view, way, step - 1).wait_recv()
+                for k in range(blocks) if step > 1 else range(way * pair, (way + 1) * pair):
+                    value = full_sent[view][step - 1, way, k].astype(f32)
+                    if step > 1:
+                        value = value + full_came[view][step - 2, way, k].astype(f32)
+                    else:
+                        value = value + half_came[view][way, k - way * pair].astype(f32)
+                    full_sent[view][step - 1, way, k] = value.astype(bf)
+                leg(view, way, step).start()
+
+    column_sum(x_ref, x_taken, x_out, x_pass, x_take, 0)
+    for step in range(1, ring.last):
+        ring_step(step)
+    column_sum(y_ref, y_taken, y_out, y_pass, y_take, 1)
+    for view in range(3):
+        own_copy(view, 0, ring.last).wait()
+        for way in range(2):
+            leg(view, way, ring.last - 1).wait_recv()
+        for k in range(blocks):
+            if ring.last > 1:
+                came = full_came[view]
+                sums = [came[ring.last - 2, way, k].astype(f32) for way in range(2)]
+                value = mine[view][k].astype(f32) + sums[0] + sums[1]
+            else:
+                came = half_came[view][k // pair, k % pair].astype(f32)
+                value = mine[view][k].astype(f32) + came
+            value = value.astype(bf)
+            if view == 0:
+                down_out[k] = value
+            else:
+                unit = (view - 1) * blocks + k
+
+                @pl.when(core == 0)
+                def _():
+                    ug_out[unit, :, :half] = value[0]
+                    side_out[unit] = value[1]
+
+                @pl.when(core != 0)
+                def _():
+                    ug_out[unit, :, half:] = value[1]
+                    side_out[unit] = value[0]
+
+    place = pl.ds(pl.multiple_of(core * half, half), half)
+    side = send(side_out, ug_out.at[:, :, place], side_send, side_recv, sibling)
+    side.start()
+    side.wait()
+    for step in range(ring.last):
+        for view in range(3):
+            for way in range(2):
+                leg(view, way, step).wait_send()
+
+
+def sum_grads(up, gate, down, x, y, collective_id):
+    blocks, chips, _, rows, half = up.shape
+    _, _, sub, width = down.shape
+    _, n_dp, tokens, _ = x.shape
+    steps = chips // 2
+    side = (2, rows, half)
+    vmem = pltpu.VMEM
+    return pl.pallas_call(
+        grads_kernel,
+        out_shape=[
+            jax.ShapeDtypeStruct((2 * blocks, rows, 2 * half), bf),
+            jax.ShapeDtypeStruct((blocks, sub, width), bf),
+            jax.ShapeDtypeStruct((tokens, width), f32),
+            jax.ShapeDtypeStruct((tokens, width), f32),
+        ],
+        in_specs=[ANY] * 3 + [VMEM] * 2,
+        out_specs=[VMEM] * 4,
+        scratch_shapes=[vmem((2, blocks // 2) + s, bf) for s in ((sub, width), side, side)]
+        + [vmem((max(steps - 1, 1), 2, blocks) + s, bf) for s in ((sub, width), side, side)] * 2
+        + [vmem((blocks,) + s, bf) for s in ((sub, width), side, side)]
+        + [
+            vmem((2 * blocks, rows, half), bf),
+            vmem((n_dp, tokens, width), bf),
+            vmem((n_dp, tokens, width), bf),
+            vmem((2, n_dp, tokens, width), bf),
+            vmem((2, n_dp + 1, tokens, width), bf),
+            DMA((3, 2, steps)),
+            DMA((3, 2, steps)),
+            DMA((2, 1, 2, n_dp)),
+            DMA((2, 1, 2, n_dp)),
+            DMA((n_dp,)),
+            DMA((n_dp,)),
+            DMA((n_dp,)),
+            DMA((n_dp,)),
+            DMA,
+            DMA,
+            DMA((3, 2, steps)),
+        ],
+        compiler_params=comm_params(collective_id, 58),
+        cost_estimate=takes(120),
+        name="sum_grads",
+    )(up, gate, down, x, y)
 
 
 def local(block_input, cotangent, doc_lengths, owners, master, first_moment, second_moment):
@@ -777,12 +1306,7 @@
     slot_unit = slot_unit.reshape(n_dp, per_owner)
     own_units = lax.dynamic_index_in_dim(slot_unit, dp_index, 0, keepdims=False)
     is_col = (own_units >= 4) & (own_units < 4 + 2 * ff_blocks)
-    chip_groups = [[2 * k + c for k in range(chips)] for c in range(2)]
-
-    sibling = [(i, i ^ 1) for i in range(n_seq)]
-
-    def exchange(packed):
-        return lax.all_to_all(packed, "dp", 0, 0)
+
 
     tokens = block_input.astype(f32).reshape(shard_len, width)
     normed_one, inv_one = norm_parts(tokens)
@@ -790,14 +1314,13 @@
     first_table, normed_one_all = front(packed[0], normed_one.astype(bf), 2)
     first_table = first_table.reshape(n_dp * first_slots, rows, wide)
     normed_one_all = normed_one_all.reshape(seq_len, width)
-    att = jnp.take(first_table, (owners * first_slots + place)[:4], axis=0)
-    att_rows = att[:3].reshape(3, n_dp, sub, n_seq // n_dp, head_cols)
-    att_rows = att_rows.transpose(1, 3, 2, 0, 4).reshape(n_seq, sub, 3 * head_cols)
-    att_out = att[3].reshape(n_dp, sub, wide).transpose(1, 0, 2).reshape(sub, width)
+    att_rows, att_out = pick_attention(
+        first_table, (owners * first_slots + place)[:4], n_seq, sub, width
+    )
     qkv_weight, out_weight = spread_attention(att_rows, att_out, 1)
     if per_owner > first_slots:
         late, qkv_weight = lax.optimization_barrier((packed[1], qkv_weight))
-        late = exchange(late)
+        late = lax.all_to_all(late, "dp", 0, 0)
     qkv_weight = qkv_weight.reshape(width, 3 * head_cols)
     out_weight = out_weight.reshape(rows, width)
 
@@ -826,91 +1349,64 @@
     residual = tokens + attn_out
     normed_two, inv_two = norm_parts(residual)
 
+    upstream = cotangent.reshape(shard_len, width)
+    upstream_column = lax.all_gather(upstream, "dp", axis=0)
     if per_owner > first_slots:
-        second_slots = per_owner - first_slots
         late, normed_two = lax.optimization_barrier((late, normed_two))
-        second = late.reshape(n_dp * second_slots, rows, wide)
-        table = jnp.concatenate([first_table, second], axis=0)
-        index = jnp.where(
-            place < first_slots,
-            owners * first_slots + place,
-            n_dp * first_slots + owners * second_slots + place - first_slots,
-        )
+        late = late.reshape(-1, rows, wide)
     else:
-        table = first_table
-        index = owners * first_slots + place
-    ff = jnp.take(table, index[4:], axis=0)
-    ug = ff[: 2 * ff_blocks]
-    mine = lax.dynamic_slice_in_dim(ug, core * half, half, axis=2)
-    given = lax.dynamic_slice_in_dim(ug, (1 - core) * half, half, axis=2)
-    got = lax.ppermute(given, "seq", sibling)
-    ug = jnp.where(
-        core == 0, jnp.concatenate([mine, got], axis=1), jnp.concatenate([got, mine], axis=1)
-    )
-    up_weight = lax.all_gather(
-        ug[:ff_blocks], "seq", axis=1, tiled=True, axis_index_groups=chip_groups
-    )
-    gate_weight = lax.all_gather(
-        ug[ff_blocks:], "seq", axis=1, tiled=True, axis_index_groups=chip_groups
-    )
-    down = ff[2 * ff_blocks :].reshape(ff_blocks, n_dp, sub, wide).transpose(0, 2, 1, 3)
-    down_weight = lax.all_gather(
-        down.reshape(ff_blocks, sub, width), "seq", axis=1, tiled=True, axis_index_groups=chip_groups
-    )
-
-    def gather_tokens(part):
-        return gather_dp(part, 4).reshape(-1, width)
-
-    def scatter_tokens(part):
-        return sum_dp(part.astype(bf).reshape(2, n_dp, shard_len, width), 5)
-
-    upstream = cotangent.reshape(shard_len, width)
-    every = lax.all_gather(upstream, "dp", axis=0, tiled=True)
-    other = lax.ppermute(every, "seq", sibling)
-    upstream_all = jnp.where(
-        core == 0,
-        jnp.concatenate([every, other], axis=0),
-        jnp.concatenate([other, every], axis=0),
-    )
-    normed_two_all = gather_tokens(normed_two.astype(bf))
+        late = None
+    mine, given, down = pick_ff(
+        first_table, late, owners, place, core, ff_blocks, sub, first_slots
+    )
+    ug_weight, down_weight, normed_two_all, upstream_all = gather_weights(
+        mine, given, down, normed_two.astype(bf), upstream_column, 4
+    )
+    up_weight = ug_weight[:ff_blocks].reshape(ff_blocks, width, half)
+    gate_weight = ug_weight[ff_blocks:].reshape(ff_blocks, width, half)
+    down_weight = down_weight.reshape(ff_blocks, half, width)
+    normed_two_all = normed_two_all.reshape(-1, width)
+    upstream_all = upstream_all.reshape(-1, width)
     up_proj = jnp.einsum("tr,jrc->tjc", normed_two_all, up_weight, preferred_element_type=f32)
     gate_proj = jnp.einsum("tr,jrc->tjc", normed_two_all, gate_weight, preferred_element_type=f32)
     gate_sig = jax.nn.sigmoid(gate_proj)
     silu_value = gate_proj * gate_sig
     hidden_low = (silu_value * up_proj).astype(bf)
-    ff_out = scatter_tokens(
-        jnp.einsum("tjh,jhc->tc", hidden_low, down_weight, preferred_element_type=f32)
-    )
-    block_output = (residual + ff_out).astype(bf).reshape(block_input.shape)
+    ff_part = jnp.einsum("tjh,jhc->tc", hidden_low, down_weight, preferred_element_type=f32)
     hidden_grad = jnp.einsum("tc,jhc->tjh", upstream_all, down_weight, preferred_element_type=f32)
     up_grad_low = (hidden_grad * silu_value).astype(bf)
     gate_grad_low = (
         hidden_grad * up_proj * (gate_sig + gate_proj * gate_sig * (1.0 - gate_sig))
     ).astype(bf)
 
-    def chip_sum(part):
-        return lax.psum_scatter(
-            part.astype(bf),
-            "seq",
-            scatter_dimension=1,
-            tiled=True,
-            axis_index_groups=chip_groups,
-        )
-
-    down_grad = chip_sum(
-        jnp.einsum("tjh,tc->jhc", hidden_low, upstream_all, preferred_element_type=f32)
-    )
-    up_grad = chip_sum(
-        jnp.einsum("tr,tjc->jrc", normed_two_all, up_grad_low, preferred_element_type=f32)
-    )
-    gate_grad = chip_sum(
-        jnp.einsum("tr,tjc->jrc", normed_two_all, gate_grad_low, preferred_element_type=f32)
-    )
+    down_grad = jnp.einsum(
+        "tjh,tc->jhc", hidden_low, upstream_all, preferred_element_type=f32
+    ).astype(bf)
+    up_grad = jnp.einsum(
+        "tr,tjc->jrc", normed_two_all, up_grad_low, preferred_element_type=f32
+    ).astype(bf)
+    gate_grad = jnp.einsum(
+        "tr,tjc->jrc", normed_two_all, gate_grad_low, preferred_element_type=f32
+    ).astype(bf)
     norm_two_grad = jnp.einsum("tjc,jrc->tr", up_grad_low, up_weight, preferred_element_type=f32)
     norm_two_grad = norm_two_grad + jnp.einsum(
         "tjc,jrc->tr", gate_grad_low, gate_weight, preferred_element_type=f32
     )
-    norm_two_grad = scatter_tokens(norm_two_grad)
+    side = (ff_blocks, chips, 2, rows, half)
+    column = (2, n_dp, shard_len, width)
+    ug_piece, down_piece, norm_two_grad, ff_out = sum_grads(
+        up_grad.reshape(side),
+        gate_grad.reshape(side),
+        down_grad.reshape(ff_blocks, chips, sub, width),
+        norm_two_grad.astype(bf).reshape(column),
+        ff_part.astype(bf).reshape(column),
+        5,
+    )
+    block_output = (residual + ff_out).astype(bf).reshape(block_input.shape)
+    grads = []
+    if per_owner > first_slots:
+        late = arrange(slot_unit[:, first_slots:], ug_piece, down_piece, ())
+        grads.append(lax.all_to_all(late, "dp", 0, 0))
     residual_grad = upstream.astype(f32) + norm_back(normed_two, inv_two, norm_two_grad)
     residual_grad_all = gather_seq(residual_grad.astype(bf), 7).reshape(seq_len, width)
 
@@ -948,33 +1444,8 @@
     qkv_piece, out_piece = collect_attention(
         qkv_wgrad.reshape(n_seq, n_dp, sub, 3 * head_cols), out_wgrad.reshape(n_dp, sub, width), 6
     )
-    qkv_piece = qkv_piece.reshape(n_dp, n_seq // n_dp, sub, 3, head_cols).transpose(3, 0, 2, 1, 4)
-    qkv_piece = qkv_piece.reshape(3, rows, wide)
-    out_piece = out_piece.reshape(sub, n_dp, wide).transpose(1, 0, 2).reshape(1, rows, wide)
-
-    up_grad, gate_grad, down_grad, _ = lax.optimization_barrier(
-        (up_grad, gate_grad, down_grad, residual_grad_all)
-    )
-    ug_grad = jnp.concatenate([up_grad, gate_grad], axis=0)
-    kept = lax.dynamic_slice_in_dim(ug_grad, core * rows, rows, axis=1)
-    sent = lax.dynamic_slice_in_dim(ug_grad, (1 - core) * rows, rows, axis=1)
-    got = lax.ppermute(sent, "seq", sibling)
-    ug_piece = jnp.where(
-        core == 0, jnp.concatenate([kept, got], axis=2), jnp.concatenate([got, kept], axis=2)
-    )
-    down_piece = down_grad.reshape(ff_blocks, sub, n_dp, wide).transpose(0, 2, 1, 3)
-    down_piece = down_piece.reshape(ff_blocks, rows, wide)
-    ff_pieces = jnp.concatenate([ug_piece, down_piece], axis=0)
-
-    def give_back(pieces, low_slot, high_slot, skipped):
-        units = jnp.maximum(slot_unit[:, low_slot:high_slot] - skipped, 0)
-        return lax.all_to_all(jnp.take(pieces, units, axis=0), "dp", 0, 0)
-
-    grads = []
-    if per_owner > first_slots:
-        grads.append(give_back(ff_pieces, first_slots, per_owner, 4))
-    every_piece = jnp.concatenate([qkv_piece, out_piece, ff_pieces], axis=0)
-    grads.insert(0, give_back(every_piece, 0, first_slots, 0))
+    early = arrange(slot_unit[:, :first_slots], ug_piece, down_piece, (qkv_piece, out_piece))
+    grads.insert(0, lax.all_to_all(early, "dp", 0, 0))
     kinds = jnp.where(own_units < 0, 2, is_col.astype(jnp.int32)).astype(jnp.int32)
     owned_grads, new_first, new_second, new_master = adam(
         kinds, grads, master, first_moment, second_moment, n_dp, n_seq, first_slots

time: 1160 us -> 998 us (0.86)
  waiting for transfers between devices: 195 us -> 91.6 us
  other arithmetic: 48.7 us -> 16.5 us
  Pallas kernels: 648 us -> 679 us
  local copies, waits for them, and re-layouts: 74.2 us -> 43.2 us
  matrix products: 158 us -> 133 us
    all_gather x4 -> x1, waiting for transfers between devices: 95.4 us -> 0.01 us  [local(): upstream_column = lax.all_gather(upstream, 'dp', axis=0)]
    reduce_scatter x3 -> x0, waiting for transfers between devices: 60.9 us -> none  [chip_sum(): lax.psum_scatter(part.astype(bf), 'seq', scatter_dimension=1, tiled=True,...]
    all_to_all x3, waiting for transfers between devices: 34.9 us -> 90.9 us  [the longest x1 57.1 us: local(): grads.insert(0, lax.all_to_all(early, 'dp', 0, 0))]
    pallas_call x3 -> x6, Pallas kernels: 199 us -> 237 us  [the longest x1 122 us: sum_grads(): pl.pallas_call(grads_kernel, out_shape=[jax.ShapeDtypeStruct((2 * blocks,...]
    gather x6 -> x0, local copies, waits for them, and re-layouts: 31.3 us -> none  [the longest x4 22.6 us: give_back(): return lax.all_to_all(jnp.take(pieces, units, axis=0), 'dp', 0, 0)]
    select_n x7 -> x0, other arithmetic: 17.3 us -> none  [the longest x2 9.39 us: give_back(): return lax.all_to_all(jnp.take(pieces, units, axis=0), 'dp', 0, 0)]
    reshape x11 -> x2, local copies, waits for them, and re-layouts: 14.7 us -> 0.16 us  [arrange(): units.reshape(-1)]
    concatenate x3 -> x0, other arithmetic: 12.7 us -> none  [the longest x1 7.58 us: local(): table = jnp.concatenate([first_table, second], axis=0)]
  transfers between devices with their start and end apart: 13 -> 4, of which waited for: 7 -> 2; matrix products, arithmetic and copies ran while one was open for 19% -> 9% of each run, Pallas kernels for 52% -> 40%
where the time goes in v4:
time: 998 us; the launch traced here: 994 us
  Pallas kernels  679 us (68%)
  matrix products  133 us (13%)
  waiting for transfers between devices  91.6 us (9%)
  local copies, waits for them, and re-layouts  43.2 us (4%)
  other arithmetic  16.5 us (2%)
  starting transfers between devices  15.9 us (2%)
  between operations  15 us (2%)
    pallas_call x1, Pallas kernels, sum_grads(): pl.pallas_call(grads_kernel, out_shape=[jax.ShapeDtypeStruct((2 * blocks,...  122 us
    pallas_call x1, Pallas kernels, spread_attention(): pl.pallas_call(spread_kernel, out_shape=[jax.ShapeDtypeStruct((n_seq, n_d...  107 us
    pallas_call x1, Pallas kernels, gather_weights(): pl.pallas_call(weights_kernel, out_shape=[jax.ShapeDtypeStruct((units, ch...  105 us
    pallas_call x1, Pallas kernels, front(): pl.pallas_call(front_kernel, out_shape=[jax.ShapeDtypeStruct(packed.shape...  92.4 us
    pallas_call x1, Pallas kernels, collect_attention(): pl.pallas_call(collect_kernel, out_shape=[jax.ShapeDtypeStruct((n_seq,) +...  83.2 us
    pallas_call x2, Pallas kernels, sum_seq(): pl.pallas_call(sum_seq_kernel, out_shape=jax.ShapeDtypeStruct((rows, colu...  58.4 us
    all_to_all x1, waiting for transfers between devices, local(): grads.insert(0, lax.all_to_all(early, 'dp', 0, 0))  57.1 us
    pallas_call x1, Pallas kernels, adam(): pl.pallas_call(functools.partial(adam_kernel, n_dp, n_seq // 2, first_slo...  55.1 us
  transfers between devices with their start and end apart: 4, of which 2 were waited for; matrix products, arithmetic and copies ran while one was open for 9% of the time, Pallas kernels for 40%

profile of v4, /device:TPU:0, one launch (start us, length us, event | category | flops | bytes accessed | tf_op | source)
XLA Modules:
  0.0 994.5 jit_solution(4875643539530888355)
XLA Ops:
  13.6 17.2 %pack.1 = (bf16[4,4,256,512]{3,2,1,0:T(8,128)(2,1)}, bf16[4,4,256,512]{3,2,1,0:T(8,128)(2,1)}) custom-call(s32[8]{0:T(128)S(1)} %fusion.67.flags, f32[256,8,2048]{2,1,0:T(8,128)} %refs_4_.1), custom_call_target="tpu_custom_call" | custom-call | tf_op jit(solution)/shard_map/pack/pallas_call | solution.py:113
  33.1 92.4 %front.1 = (bf16[4,4,256,512]{3,2,1,0:T(8,128)(2,1)S(1)}, bf16[8,128,2048]{2,1,0:T(8,128)(2,1)S(1)}) custom-call(bf16[4,4,256,512]{3,2,1,0:T(8,128)(2,1)S(1)} %copy-done.10, bf16[128,2048]{1,0:T(8,128)(2,1)S(1)} %fusion.40.x_ref), custom_call_target="tpu_custom_call" | custom-call | bytes 270000000 | tf_op jit(solution)/shard_map/front/pallas_call | solution.py:430
  128.8 106.5 %spread_attention.1 = (bf16[8,4,64,768]{3,2,1,0:T(8,128)(2,1)S(1)}, bf16[4,64,2048]{2,1,0:T(8,128)(2,1)S(1)}) custom-call(bf16[8,64,768]{2,1,0:T(8,128)(2,1)S(1)} %get-tuple-element.39.qkv_ref, bf16[64,2048]{1,0:T(8,128)(2,1)S(1)} %get-tuple-element.40.out_ref), custom_call_target="tpu_custom_call" | custom-call | bytes 225000000 | tf_op jit(solution)/shard_map/spread_attention/pallas_call | solution.py:663
  246.1 6.6 fusion.85
  256.3 8.3 fusion.82
  270.3 29.0 %sum_seq.2 = f32[128,2048]{1,0:T(8,128)S(1)} custom-call(bf16[8,128,2048]{2,1,0:T(8,128)(2,1)S(1)} %bitcast.176), custom_call_target="tpu_custom_call" | custom-call | bytes 84000000 | tf_op jit(solution)/shard_map/sum_seq/pallas_call | solution.py:552
  300.4 33.8 %all-to-all-done = bf16[4,4,256,512]{3,2,1,0:T(8,128)(2,1)} async-done(((bf16[4,4,256,512]{3,2,1,0:T(8,128)(2,1)}), bf16[4,4,256,512]{3,2,1,0:T(8,128)(2,1)}, u32[]{:S(2)}, u32[]{:S(2)}) %all-to-all-start) | async-done | bytes 4194336 | tf_op jit(solution)/shard_map/all_to_all | solution.py:1323
  336.5 6.4 pick_ff.1
  346.7 105.2 %gather_weights.1 = (bf16[8,4,2,256,256]{4,3,2,1,0:T(8,128)(2,1)S(1)}, bf16[4,4,64,2048]{3,2,1,0:T(8,128)(2,1)S(1)}, bf16[2,4,128,2048]{3,2,1,0:T(8,128)(2,1)S(1)}, bf16[2,4,128,2048]{3,2,1,0:T(8,128)(2,1)S(1)}) custom-call(bf16[8,256,256]{2,1,0:T(8,128)(2,1)S(1)} %get-tuple-element.46.mine_ref, bf16[8,256,256]{2,1,0:T(8,128)(2,1)S(1)} %get-tuple-element.47.given_ref, ...), custom_call_target="tpu_custom_call" | custom-call | bytes 300000000 | tf_op jit(solution)/shard_map/gather_weights/pallas_call | solution.py:1082
  466.4 8.7 multiply_convert_fusion.1
  487.4 6.2 convert_bitcast_fusion.1
  493.6 6.7 fusion.88
  500.4 6.2 convert_bitcast_fusion
  506.6 6.2 copy.46
  512.8 6.2 copy.48
  519.0 9.6 fusion.2
  528.6 122.0 %sum_grads.1 = (bf16[8,256,512]{2,1,0:T(8,128)(2,1)}, bf16[4,64,2048]{2,1,0:T(8,128)(2,1)}, f32[128,2048]{1,0:T(8,128)}, f32[128,2048]{1,0:T(8,128)}) custom-call(bf16[4,4,2,256,256]{4,3,2,1,0:T(8,128)(2,1)} %bitcast.201, bf16[4,4,2,256,256]{4,3,2,1,0:T(8,128)(2,1)} %bitcast.202, bf16[4,4,64,2048]{3,2,1,0:T(8,128)(2,1)} %bitcast.204, ...), custom_call_target="tpu_custom_call" | custom-call | bytes 360000000 | tf_op jit(solution)/shard_map/sum_grads/pallas_call | solution.py:1241
  663.6 29.5 %gather_seq.1 = bf16[8,128,2048]{2,1,0:T(8,128)(2,1)S(1)} custom-call(bf16[128,2048]{1,0:T(8,128)(2,1)S(1)} %get-tuple-element.70.x_ref), custom_call_target="tpu_custom_call" | custom-call | bytes 84000000 | tf_op jit(solution)/shard_map/gather_seq/pallas_call | solution.py:461
  703.3 13.5 %fusion.25 = f32[1024,2,128]{0,2,1:T(8,128)} fusion(bf16[1024,2,128]{0,2,1:T(8,128)(2,1)S(1)} %copy-done.44, f32[2,1024,1024]{1,2,0:T(8,128)} %fusion.62, f32[2,1024,1024]{1,2,0:T(8,128)} %get-tuple-element.104, f32[2,1024]{1,0:T(2,128)S(1)} %get-tuple-element.103), kind=kOutput, calls=%fused_computation.37 | convolution fusion | flops 551554048 | bytes 18358272 | tf_op jit(solution)/shard_map/hqk,qhd->khd/dot_general | solution.py:1422
  716.7 14.9 %broadcast_multiply_fusion.1 = (f32[1024,2,128]{0,2,1:T(8,128)S(1)}, f32[1024,2,128]{0,2,1:T(8,128)S(1)}, f32[1024,2,128]{0,2,1:T(8,128)}) fusion(f32[1024,128]{0,1:T(8,128)S(1)} %copy-done.35, f32[1024,2,128]{0,2,1:T(8,128)} %fusion.25, bf16[1024,2,128]{0,2,1:T(8,128)(2,1)S(1)} %copy-done.43, f32[2,1024,1024]{1,2,0:T(8,128)} %fusion.62, ...), kind=kOutput, calls=%fused_computation.87 | convolution fusion | flops 552078336 | bytes 22028288 | tf_op jit(solution)/shard_map/hqk,khd->qhd/dot_general | solution.py:1421
  745.9 83.2 %collect_attention.1 = (bf16[8,64,768]{2,1,0:T(8,128)(2,1)S(1)}, bf16[64,2048]{1,0:T(8,128)(2,1)S(1)}) custom-call(bf16[8,4,64,768]{3,2,1,0:T(8,128)(2,1)S(1)} %bitcast.186, bf16[4,64,2048]{2,1,0:T(8,128)(2,1)S(1)} %bitcast.187), custom_call_target="tpu_custom_call" | custom-call | bytes 225000000 | tf_op jit(solution)/shard_map/collect_attention/pallas_call | solution.py:723
  843.7 29.4 %sum_seq.3 = f32[128,2048]{1,0:T(8,128)S(1)} custom-call(bf16[8,128,2048]{2,1,0:T(8,128)(2,1)S(1)} %bitcast.181), custom_call_target="tpu_custom_call" | custom-call | bytes 84000000 | tf_op jit(solution)/shard_map/sum_seq/pallas_call | solution.py:552
  875.1 57.1 %all-to-all-done.1.refs_0_ = bf16[4,4,256,512]{3,2,1,0:T(8,128)(2,1)} async-done(((bf16[4,4,256,512]{3,2,1,0:T(8,128)(2,1)}), bf16[4,4,256,512]{3,2,1,0:T(8,128)(2,1)}, u32[]{:S(2)}, u32[]{:S(2)}) %all-to-all-start.1) | async-done | bytes 4194336 | tf_op jit(solution)/shard_map/all_to_all | solution.py:1448
  932.3 55.1 %adam.1 = (f32[256,8,2048]{2,1,0:T(8,128)}, f32[256,8,2048]{2,1,0:T(8,128)}, f32[256,8,2048]{2,1,0:T(8,128)}, f32[256,8,2048]{2,1,0:T(8,128)}) custom-call(s32[8]{0:T(128)S(1)} %get-tuple-element.69.kinds, bf16[4,4,256,512]{3,2,1,0:T(8,128)(2,1)} %all-to-all-done.1.refs_0_, bf16[4,4,256,512]{3,2,1,0:T(8,128)(2,1)} %all-to-all-done.2.refs_1_, ...), custom_call_target="tpu_custom_call" | custom-call | tf_op jit(solution)/shard_map/adam/pallas_call | solution.py:190
  (181 shorter events, 119.5 us)
Async XLA Ops:
  7.2 336.7 %all-gather.2.cloned.1.call-start = ((), (), s32[]{:S(2)}) async-start(), calls=%async_computation.3 | async-start | bytes 2621440 | tf_op jit(solution)/shard_map/all_gather | solution.py:1353
  10.0 20.8 %copy-start.48 = (f32[128]{0:T(128)}, f32[128]{0:T(128)S(1)}, u32[]{:S(2)}) copy-start(f32[128]{0:T(128)S(1)} %broadcast_multiply_fusion.7) | copy-start | bytes 1540
  11.4 19.5 %copy-start.50 = (f32[128]{0:T(128)}, f32[128]{0:T(128)S(1)}, u32[]{:S(2)}) copy-start(f32[128]{0:T(128)S(1)} %add_rsqrt_fusion.1) | copy-start | bytes 1540
  12.2 229.3 %copy-start.47 = (s32[4,8]{1,0:T(4,128)}, s32[4,8]{1,0:T(4,128)S(1)}, u32[]{:S(2)}) copy-start(s32[4,8]{1,0:T(4,128)S(1)} %sub.68) | copy-start | bytes 388
  125.5 109.9 %copy-start.21 = (bf16[8,128,2048]{2,1,0:T(8,128)(2,1)}, bf16[8,128,2048]{2,1,0:T(8,128)(2,1)S(1)}, u32[]{:S(2)}) copy-start(bf16[8,128,2048]{2,1,0:T(8,128)(2,1)S(1)} %get-tuple-element.36) | copy-start | bytes 12582916
  236.3 97.9 %all-to-all-start = ((bf16[4,4,256,512]{3,2,1,0:T(8,128)(2,1)}), bf16[4,4,256,512]{3,2,1,0:T(8,128)(2,1)}, u32[]{:S(2)}, u32[]{:S(2)}) async-start(bf16[4,4,256,512]{3,2,1,0:T(8,128)(2,1)} %get-tuple-element.44), calls=%async_computation | async-start | bytes 8388608 | tf_op jit(solution)/shard_map/all_to_all | solution.py:1323
  246.0 7.0 copy-start.28
  252.6 12.0 %copy-start.27 = (f32[1024,3,2,128]{0,3,2,1:T(8,128)}, f32[1024,3,2,128]{0,3,2,1:T(8,128)S(1)}, u32[]{:S(2)}) copy-start(f32[1024,3,2,128]{0,3,2,1:T(8,128)S(1)} %fusion.85) | copy-start | bytes 9437188
  270.2 29.0 %copy-start.23 = (bf16[1,128,2048]{2,1,0:T(8,128)(2,1)S(1)}, bf16[1,128,2048]{2,1,0:T(8,128)(2,1)}, u32[]{:S(2)}) copy-start(bf16[1,128,2048]{2,1,0:T(8,128)(2,1)} %param.7) | copy-start | bytes 1572868
  270.2 29.6 %copy-start.52 = (s32[16]{0:T(128)S(1)}, s32[16]{0:T(128)}, u32[]{:S(2)}) copy-start(s32[16]{0:T(128)} %param.10) | copy-start | bytes 196
  300.4 33.9 %copy-start.25 = (f32[128,2048]{1,0:T(8,128)}, f32[128,2048]{1,0:T(8,128)S(1)}, u32[]{:S(2)}) copy-start(f32[128,2048]{1,0:T(8,128)S(1)} %subtract_multiply_fusion) | copy-start | bytes 3145732
  656.4 176.2 %all-to-all-start.2 = ((bf16[4,4,256,512]{3,2,1,0:T(8,128)(2,1)}), bf16[4,4,256,512]{3,2,1,0:T(8,128)(2,1)}, u32[]{:S(2)}, u32[]{:S(2)}) async-start(bf16[4,4,256,512]{3,2,1,0:T(8,128)(2,1)} %bitcast.179), calls=%async_computation.2 | async-start | bytes 8388608 | tf_op jit(solution)/shard_map/all_to_all | solution.py:1409
  662.3 32.9 %copy-start.20 = (bf16[4,64,2048]{2,1,0:T(8,128)(2,1)S(1)}, bf16[4,64,2048]{2,1,0:T(8,128)(2,1)}, u32[]{:S(2)}) copy-start(bf16[4,64,2048]{2,1,0:T(8,128)(2,1)} %copy-done.18) | copy-start | bytes 3145732
  703.3 13.5 %copy-start.35 = (f32[1024,128]{0,1:T(8,128)S(1)}, f32[1024,128]{0,1:T(8,128)}, u32[]{:S(2)}) copy-start(f32[1024,128]{0,1:T(8,128)} %copy-done.34) | copy-start | bytes 1572868
  703.3 13.5 %copy-start.43 = (bf16[1024,2,128]{0,2,1:T(8,128)(2,1)S(1)}, bf16[1024,2,128]{0,2,1:T(8,128)(2,1)}, u32[]{:S(2)}) copy-start(bf16[1024,2,128]{0,2,1:T(8,128)(2,1)} %get-tuple-element.77) | copy-start | bytes 1572868
  745.9 83.2 %copy-start.7 = (bf16[8,256,512]{2,1,0:T(8,128)(2,1)S(1)}, bf16[8,256,512]{2,1,0:T(8,128)(2,1)}, u32[]{:S(2)}) copy-start(bf16[8,256,512]{2,1,0:T(8,128)(2,1)} %get-tuple-element.56.ug_ref) | copy-start | bytes 6291460
  745.9 83.2 %copy-start.12 = (bf16[4,64,2048]{2,1,0:T(8,128)(2,1)S(1)}, bf16[4,64,2048]{2,1,0:T(8,128)(2,1)}, u32[]{:S(2)}) copy-start(bf16[4,64,2048]{2,1,0:T(8,128)(2,1)} %get-tuple-element.57.down_ref) | copy-start | bytes 3145732
  832.6 99.6 %all-to-all-start.1 = ((bf16[4,4,256,512]{3,2,1,0:T(8,128)(2,1)}), bf16[4,4,256,512]{3,2,1,0:T(8,128)(2,1)}, u32[]{:S(2)}, u32[]{:S(2)}) async-start(bf16[4,4,256,512]{3,2,1,0:T(8,128)(2,1)} %bitcast.180), calls=%async_computation.1 | async-start | bytes 8388608 | tf_op jit(solution)/shard_map/all_to_all | solution.py:1448
  843.6 29.5 %copy-start.24 = (bf16[1,128,2048]{2,1,0:T(8,128)(2,1)S(1)}, bf16[1,128,2048]{2,1,0:T(8,128)(2,1)}, u32[]{:S(2)}) copy-start(bf16[1,128,2048]{2,1,0:T(8,128)(2,1)} %param.7) | copy-start | bytes 1572868
  843.6 29.5 %copy-start.49 = (f32[128]{0:T(128)S(1)}, f32[128]{0:T(128)}, u32[]{:S(2)}) copy-start(f32[128]{0:T(128)} %copy-done.48) | copy-start | bytes 1540
  843.6 29.5 %copy-start.51 = (f32[128]{0:T(128)S(1)}, f32[128]{0:T(128)}, u32[]{:S(2)}) copy-start(f32[128]{0:T(128)} %copy-done.50) | copy-start | bytes 1540
  843.6 29.8 %copy-start.1 = (f32[128,2048]{1,0:T(8,128)S(1)}, f32[128,2048]{1,0:T(8,128)}, u32[]{:S(2)}) copy-start(f32[128,2048]{1,0:T(8,128)} %copy-done) | copy-start | bytes 3145732
  843.6 29.8 %copy-start.31 = (f32[128,2048]{1,0:T(8,128)S(1)}, f32[128,2048]{1,0:T(8,128)}, u32[]{:S(2)}) copy-start(f32[128,2048]{1,0:T(8,128)} %get-tuple-element.71) | copy-start | bytes 3145732
  843.7 29.8 %copy-start.40 = (f32[128,2048]{1,0:T(8,128)S(1)}, f32[128,2048]{1,0:T(8,128)}, u32[]{:S(2)}) copy-start(f32[128,2048]{1,0:T(8,128)} %get-tuple-element.54) | copy-start | bytes 3145732
  (34 other events, 113.5 us)
Sparse Core Ops, SparseCore 0:
  9.6 103.0 all-gather.1

commit v5 on v4

--- a/solution.py
+++ b/solution.py
@@ -252,7 +252,7 @@
     )
 
 
-def relay_gather(views, place, count, device_of, send_sem, recv_sem, arrived):
+def relay_gather(views, place, count, device_of, send_sem, recv_sem, arrived, between=None):
     def leg(view, way, step, block, target):
         ref = views[view](block)
         return send(ref, ref, send_sem.at[view, way, step], recv_sem.at[view, way, step], device_of(target))
@@ -280,6 +280,9 @@
                 for view in range(len(views)):
                     leg(view, way, step, block, lax.rem(place + 1, count)).wait_recv()
                 arrived(block)
+
+        if between:
+            between(step)
 
     for step in range(1, count):
         for way in range(2):
@@ -433,10 +436,10 @@
             jax.ShapeDtypeStruct(packed.shape, packed.dtype),
             jax.ShapeDtypeStruct((2 * chips,) + x.shape, x.dtype),
         ],
-        in_specs=[ANY, ANY],
+        in_specs=[VMEM, VMEM],
         out_specs=[ANY, ANY],
         scratch_shapes=[DMA((2,)), DMA((n_dp,)), DMA((n_dp,))] + [DMA((chips,))] * 4,
-        compiler_params=comm_params(collective_id, 16),
+        compiler_params=comm_params(collective_id, 24),
         cost_estimate=takes(90),
         name="front",
     )(packed, x)
@@ -461,55 +464,12 @@
     return pl.pallas_call(
         gather_seq_kernel,
         out_shape=jax.ShapeDtypeStruct((2 * chips,) + x.shape, x.dtype),
-        in_specs=[ANY],
+        in_specs=[VMEM],
         out_specs=ANY,
         scratch_shapes=[DMA] + [DMA((chips,))] * 4,
         compiler_params=comm_params(collective_id, 16),
         cost_estimate=takes(28),
         name="gather_seq",
-    )(x)
-
-
-def gather_dp_kernel(x_ref, out_ref, own_sem, send_sem, recv_sem, pass_sem, take_sem):
-    n_seq, n_dp, seq_index, dp_index = places()
-    core = lax.rem(seq_index, 2)
-    sibling = (dp_index, seq_index + 1 - 2 * core)
-    greet([(lax.rem(dp_index + k, n_dp), seq_index) for k in range(1, n_dp)] + [sibling])
-    own = pltpu.make_async_copy(x_ref, out_ref.at[core, dp_index], own_sem)
-    own.start()
-    own.wait()
-
-    def onward(block):
-        ref = out_ref.at[core, block]
-        return send(ref, ref, pass_sem.at[block], take_sem.at[block], sibling)
-
-    onward(dp_index).start()
-    relay_gather(
-        [lambda block: out_ref.at[core, block]],
-        dp_index,
-        n_dp,
-        lambda place: (place, seq_index),
-        send_sem,
-        recv_sem,
-        lambda block: onward(block).start(),
-    )
-    for block in range(n_dp):
-        onward(block).wait_send()
-        ref = out_ref.at[1 - core, block]
-        send(ref, ref, pass_sem.at[block], take_sem.at[block], sibling).wait_recv()
-
-
-def gather_dp(x, collective_id):
-    n_dp = lax.axis_size("dp")
-    return pl.pallas_call(
-        gather_dp_kernel,
-        out_shape=jax.ShapeDtypeStruct((2, n_dp) + x.shape, x.dtype),
-        in_specs=[ANY],
-        out_specs=ANY,
-        scratch_shapes=[DMA, DMA((1, 2, n_dp)), DMA((1, 2, n_dp)), DMA((n_dp,)), DMA((n_dp,))],
-        compiler_params=comm_params(collective_id, 16),
-        cost_estimate=takes(40),
-        name="gather_dp",
     )(x)
 
 
@@ -561,120 +521,6 @@
     )(x)
 
 
-def sum_dp_kernel(x_ref, out_ref, taken, sent, came, pass_sem, take_sem, send_sem, recv_sem):
-    n_seq, n_dp, seq_index, dp_index = places()
-    core = lax.rem(seq_index, 2)
-    sibling = (dp_index, seq_index + 1 - 2 * core)
-    greet([(lax.rem(dp_index + k, n_dp), seq_index) for k in range(1, n_dp)] + [sibling])
-
-    def onward(block):
-        return send(
-            x_ref.at[1 - core, block], taken.at[block], pass_sem.at[block], take_sem.at[block], sibling
-        )
-
-    half = n_dp // 2
-    for block in [b for k in range(half) for b in (n_dp - 1 - k, k)]:
-        onward(block).start()
-    waited = []
-
-    def ready(block):
-        onward(block).wait_recv()
-
-    total = relay_sum(
-        [lambda block: x_ref[core, block].astype(f32) + taken[block].astype(f32)],
-        [sent],
-        [came],
-        dp_index,
-        n_dp,
-        lambda place: (place, seq_index),
-        send_sem,
-        recv_sem,
-        ready,
-    )[0]
-    out_ref[...] = total
-    for block in range(n_dp):
-        onward(block).wait_send()
-
-
-def sum_dp(x, collective_id):
-    _, n_dp, rows, columns = x.shape
-    return pl.pallas_call(
-        sum_dp_kernel,
-        out_shape=jax.ShapeDtypeStruct((rows, columns), f32),
-        in_specs=[VMEM],
-        out_specs=VMEM,
-        scratch_shapes=[
-            pltpu.VMEM((n_dp, rows, columns), x.dtype),
-            pltpu.VMEM((n_dp, rows, columns), x.dtype),
-            pltpu.VMEM((n_dp + 1, rows, columns), x.dtype),
-            DMA((n_dp,)),
-            DMA((n_dp,)),
-            DMA((1, 2, n_dp)),
-            DMA((1, 2, n_dp)),
-        ],
-        compiler_params=comm_params(collective_id, 40),
-        cost_estimate=takes(40),
-        name="sum_dp",
-    )(x)
-
-
-def spread_kernel(
-    qkv_ref, out_ref, qkv_all, out_all, own_sem, a_send, a_recv, send_sem, recv_sem
-):
-    n_seq, n_dp, seq_index, dp_index = places()
-    seq_peers = [lax.rem(seq_index + k, n_seq) for k in range(n_seq)]
-    greet(
-        [(dp_index, p) for p in seq_peers[1:]]
-        + [(lax.rem(dp_index + k, n_dp), seq_index) for k in range(1, n_dp)]
-    )
-    own = [
-        pltpu.make_async_copy(qkv_ref.at[seq_index], qkv_all.at[seq_index, dp_index], own_sem.at[0]),
-        pltpu.make_async_copy(out_ref, out_all.at[dp_index], own_sem.at[1]),
-    ]
-    for copy in own:
-        copy.start()
-    landing = qkv_all.at[seq_index, dp_index]
-    across = []
-    for k in range(1, n_seq):
-        device = (dp_index, seq_peers[k])
-        copy = send(qkv_ref.at[seq_peers[k]], landing, a_send.at[k], a_recv.at[k], device)
-        copy.start()
-        across.append(copy)
-    for copy in own:
-        copy.wait()
-    for copy in across:
-        copy.wait_recv()
-    relay_gather(
-        [lambda block: qkv_all.at[:, block], lambda block: out_all.at[block]],
-        dp_index,
-        n_dp,
-        lambda place: (place, seq_index),
-        send_sem,
-        recv_sem,
-        lambda block: None,
-    )
-    for copy in across:
-        copy.wait_send()
-
-
-def spread_attention(qkv, out, collective_id):
-    n_seq = lax.axis_size("seq")
-    n_dp = lax.axis_size("dp")
-    return pl.pallas_call(
-        spread_kernel,
-        out_shape=[
-            jax.ShapeDtypeStruct((n_seq, n_dp) + qkv.shape[1:], qkv.dtype),
-            jax.ShapeDtypeStruct((n_dp,) + out.shape, out.dtype),
-        ],
-        in_specs=[ANY, ANY],
-        out_specs=[ANY, ANY],
-        scratch_shapes=[DMA((2,)), DMA((n_seq,)), DMA((n_seq,)), DMA((2, 2, n_dp)), DMA((2, 2, n_dp))],
-        compiler_params=comm_params(collective_id, 16),
-        cost_estimate=takes(75),
-        name="spread_attention",
-    )(qkv, out)
-
-
 def collect_kernel(
     qkv_ref, out_ref, qkv_sum, out_sum, qkv_sent, qkv_came, out_sent, out_came, total, own_sem,
     send_sem, recv_sem, a_send, a_recv
@@ -775,146 +621,6 @@
         return send(
             src, dst, self.send_sem.at[view, way, step], self.recv_sem.at[view, way, step], self.device(way)
         )
-
-
-def ring_gather_leg(ring, views, view, way, step, arriving):
-    distance = step if arriving else step - 1
-    block = ring.at(-distance if way == 0 else distance)
-    ref = views[view](block, way if step == ring.last else None)
-    return ring.leg(view, way, step - 1, ref, ref)
-
-
-def pick_kernel(first_slots, ff_blocks, info, first_ref, *refs):
-    late_ref = refs[0] if len(refs) == 5 else None
-    mine_ref, given_ref, down_ref, piece_ref = refs[-4:]
-    unit = pl.program_id(0)
-    rows, wide = piece_ref.shape
-    half = wide // 2
-    sub, width = down_ref.shape[1:]
-    groups = width // wide
-
-    @pl.when(info[2, unit] == 0)
-    def _():
-        piece_ref[...] = first_ref[0]
-
-    if late_ref is not None:
-
-        @pl.when(info[2, unit] != 0)
-        def _():
-            piece_ref[...] = late_ref[0]
-
-    @pl.when(unit < 2 * ff_blocks)
-    def _():
-        @pl.when(info[3, 0] == 0)
-        def _():
-            mine_ref[0] = piece_ref[:, :half]
-            given_ref[0] = piece_ref[:, half:]
-
-        @pl.when(info[3, 0] != 0)
-        def _():
-            mine_ref[0] = piece_ref[:, half:]
-            given_ref[0] = piece_ref[:, :half]
-
-    @pl.when(unit >= 2 * ff_blocks)
-    def _():
-        for g in range(groups):
-            down_ref[0, :, g * wide : (g + 1) * wide] = piece_ref[g * sub : (g + 1) * sub, :]
-
-
-def pick_ff(first_table, late_table, owners, place, core, ff_blocks, sub, first_slots):
-    rows, wide = first_table.shape[1:]
-    width = rows // sub * wide
-    units = 3 * ff_blocks
-    owners, place = owners[4:], place[4:]
-    in_late = place >= first_slots
-    late_slots = 1 if late_table is None else late_table.shape[0] // lax.axis_size("dp")
-    info = jnp.stack(
-        [
-            owners * first_slots + jnp.minimum(place, first_slots - 1),
-            owners * late_slots + jnp.maximum(place - first_slots, 0),
-            in_late.astype(jnp.int32),
-            jnp.full((units,), core, jnp.int32),
-        ]
-    ).astype(jnp.int32)
-    tables = [first_table] if late_table is None else [first_table, late_table]
-    specs = [
-        pl.BlockSpec((1, rows, wide), lambda u, info: (info[0, u], 0, 0)),
-        pl.BlockSpec((1, rows, wide), lambda u, info: (info[1, u], 0, 0)),
-    ]
-    side = pl.BlockSpec(
-        (1, rows, wide // 2), lambda u, info: (jnp.minimum(u, 2 * ff_blocks - 1), 0, 0)
-    )
-    return pl.pallas_call(
-        functools.partial(pick_kernel, first_slots, ff_blocks),
-        out_shape=[
-            jax.ShapeDtypeStruct((2 * ff_blocks, rows, wide // 2), bf),
-            jax.ShapeDtypeStruct((2 * ff_blocks, rows, wide // 2), bf),
-            jax.ShapeDtypeStruct((ff_blocks, sub, width), bf),
-        ],
-        grid_spec=pltpu.PrefetchScalarGridSpec(
-            num_scalar_prefetch=1,
-            grid=(units,),
-            in_specs=specs[: len(tables)],
-            out_specs=[
-                side,
-                side,
-                pl.BlockSpec(
-                    (1, sub, width), lambda u, info: (jnp.maximum(u - 2 * ff_blocks, 0), 0, 0)
-                ),
-            ],
-            scratch_shapes=[pltpu.VMEM((rows, wide), bf)],
-        ),
-        compiler_params=pltpu.CompilerParams(vmem_limit_bytes=16 << 20),
-        cost_estimate=takes(6),
-        name="pick_ff",
-    )(info, *tables)
-
-
-def pick_attention_kernel(info, piece_ref, rows_ref, out_ref):
-    unit = pl.program_id(0)
-    blocks, sub, columns = rows_ref.shape
-    step = columns // 3
-    groups = out_ref.shape[1] // piece_ref.shape[2]
-    wide = piece_ref.shape[2]
-    share = wide // step
-    for u in range(3):
-
-        @pl.when(unit == u)
-        def _():
-            for block in range(blocks):
-                g, h = block // share, block % share
-                rows_ref[block, :, u * step : (u + 1) * step] = piece_ref[
-                    0, g * sub : (g + 1) * sub, h * step : (h + 1) * step
-                ]
-
-    @pl.when(unit == 3)
-    def _():
-        for g in range(groups):
-            out_ref[:, g * wide : (g + 1) * wide] = piece_ref[0, g * sub : (g + 1) * sub, :]
-
-
-def pick_attention(first_table, index, n_seq, sub, width):
-    rows, wide = first_table.shape[1:]
-    columns = 3 * (width // n_seq)
-    return pl.pallas_call(
-        pick_attention_kernel,
-        out_shape=[
-            jax.ShapeDtypeStruct((n_seq, sub, columns), bf),
-            jax.ShapeDtypeStruct((sub, width), bf),
-        ],
-        grid_spec=pltpu.PrefetchScalarGridSpec(
-            num_scalar_prefetch=1,
-            grid=(4,),
-            in_specs=[pl.BlockSpec((1, rows, wide), lambda u, info: (info[u], 0, 0))],
-            out_specs=[
-                pl.BlockSpec((n_seq, sub, columns), lambda u, info: (0, 0, 0)),
-                pl.BlockSpec((sub, width), lambda u, info: (0, 0)),
-            ],
-        ),
-        compiler_params=pltpu.CompilerParams(vmem_limit_bytes=16 << 20),
-        cost_estimate=takes(3),
-        name="pick_attention",
-    )(index.astype(jnp.int32), first_table)
 
 
 def arrange_kernel(ff_blocks, units, ug_ref, down_ref, *refs):
@@ -984,126 +690,6 @@
         cost_estimate=takes(7),
         name="arrange",
     )(units.reshape(-1), ug, down, *attention).reshape(n_dp, slots, rows, wide)
-
-
-def weights_kernel(
-    mine_ref, given_ref, down_ref, x_ref, cot_ref, ug_all, down_all, x_all, cot_all,
-    own_sem, side_send, side_recv, ring_send, ring_recv, send_sem, recv_sem, pass_sem, take_sem
-):
-    n_seq, n_dp, seq_index, dp_index = places()
-    chips, chip, core = n_seq // 2, seq_index // 2, lax.rem(seq_index, 2)
-    sibling = (dp_index, chip * 2 + 1 - core)
-    ring = Ring(chips, chip, core, dp_index, ring_send, ring_recv)
-    blocks = down_ref.shape[0]
-    greet(
-        [(lax.rem(dp_index + k, n_dp), seq_index) for k in range(1, n_dp)]
-        + [sibling, ring.device(0), ring.device(1)]
-    )
-    sides = [
-        send(
-            given_ref.at[pl.ds(k * blocks, blocks)],
-            ug_all.at[pl.ds(k * blocks, blocks), chip, core],
-            side_send.at[k],
-            side_recv.at[k],
-            sibling,
-        )
-        for k in range(2)
-    ]
-    sides.append(send(cot_ref, cot_all.at[core], side_send.at[2], side_recv.at[2], sibling))
-    own = [
-        pltpu.make_async_copy(x_ref, x_all.at[core, dp_index], own_sem.at[0]),
-        pltpu.make_async_copy(down_ref, down_all.at[:, chip], own_sem.at[1]),
-        pltpu.make_async_copy(mine_ref, ug_all.at[:, chip, core], own_sem.at[2]),
-        pltpu.make_async_copy(cot_ref, cot_all.at[core], own_sem.at[3]),
-    ]
-    for copy in sides + own:
-        copy.start()
-
-    def part_of(base, part):
-        if part is None:
-            return pl.ds(base, blocks)
-        return pl.ds(base + part * (blocks // 2), blocks // 2)
-
-    views = [
-        lambda block, part: down_all.at[part_of(0, part), block],
-        lambda block, part: ug_all.at[part_of(0, part), block],
-        lambda block, part: ug_all.at[part_of(blocks, part), block],
-    ]
-    for copy in own:
-        copy.wait()
-    for view in range(3):
-        if view:
-            sides[view - 1].wait_recv()
-        for way in range(2):
-            ring_gather_leg(ring, views, view, way, 1, False).start()
-
-    def onward(block):
-        ref = x_all.at[core, block]
-        return send(ref, ref, pass_sem.at[block], take_sem.at[block], sibling)
-
-    onward(dp_index).start()
-    relay_gather(
-        [lambda block: x_all.at[core, block]],
-        dp_index,
-        n_dp,
-        lambda place: (place, seq_index),
-        send_sem,
-        recv_sem,
-        lambda block: onward(block).start(),
-    )
-    for step in range(2, ring.last + 1):
-        for view in range(3):
-            for way in range(2):
-                ring_gather_leg(ring, views, view, way, step - 1, True).wait_recv()
-                ring_gather_leg(ring, views, view, way, step, False).start()
-    for view in range(3):
-        for way in range(2):
-            ring_gather_leg(ring, views, view, way, ring.last, True).wait_recv()
-    for step in range(1, ring.last + 1):
-        for view in range(3):
-            for way in range(2):
-                ring_gather_leg(ring, views, view, way, step, False).wait_send()
-    for block in range(n_dp):
-        onward(block).wait_send()
-        ref = x_all.at[1 - core, block]
-        send(ref, ref, pass_sem.at[block], take_sem.at[block], sibling).wait_recv()
-    for copy in sides:
-        copy.wait_send()
-    ref = cot_all.at[1 - core]
-    send(ref, ref, side_send.at[2], side_recv.at[2], sibling).wait_recv()
-
-
-def gather_weights(mine, given, down, x, cot, collective_id):
-    n_dp = lax.axis_size("dp")
-    chips = lax.axis_size("seq") // 2
-    units, rows, half = mine.shape
-    blocks, sub, width = down.shape
-    steps = chips // 2
-    return pl.pallas_call(
-        weights_kernel,
-        out_shape=[
-            jax.ShapeDtypeStruct((units, chips, 2, rows, half), bf),
-            jax.ShapeDtypeStruct((blocks, chips, sub, width), bf),
-            jax.ShapeDtypeStruct((2, n_dp) + x.shape, bf),
-            jax.ShapeDtypeStruct((2,) + cot.shape, bf),
-        ],
-        in_specs=[ANY] * 5,
-        out_specs=[ANY] * 4,
-        scratch_shapes=[
-            DMA((4,)),
-            DMA((3,)),
-            DMA((3,)),
-            DMA((3, 2, steps)),
-            DMA((3, 2, steps)),
-            DMA((1, 2, n_dp)),
-            DMA((1, 2, n_dp)),
-            DMA((n_dp,)),
-            DMA((n_dp,)),
-        ],
-        compiler_params=comm_params(collective_id, 16),
-        cost_estimate=takes(100),
-        name="gather_weights",
-    )(mine, given, down, x, cot)
 
 
 def grads_kernel(
@@ -1275,6 +861,417 @@
     )(up, gate, down, x, y)
 
 
+def turn_half(values):
+    half = values.shape[-1] // 2
+    return jnp.concatenate([-values[:, half:], values[:, :half]], axis=-1)
+
+
+def forward_kernel(has_late, first_slots, ff_blocks, *refs):
+    info, first_ref = refs[:2]
+    refs = refs[2:]
+    if has_late:
+        late_ref, refs = refs[0], refs[1:]
+    x1_ref, cos_ref, sin_ref, doc_row, doc_col, tokens_ref, cot_ref = refs[:7]
+    qkv_all, out_all, query_out, key_out, value_out, mixed_out, stat_out, residual_out = refs[7:15]
+    ug_all, down_all, x_all, cot_all = refs[15:19]
+    att_stage, out_stage, part, taken, sent, arrived, x_stage = refs[19:26]
+    mine_stage, given_stage, down_stage = refs[26:29]
+    (own_sem, a_send, a_recv, w_send, w_recv, s_pass, s_take, s_send, s_recv, cot_send, cot_recv,
+     late_send, late_recv, late_own, stage_own, side_send, side_recv, ring_send, ring_recv,
+     send_sem, recv_sem, pass_sem, take_sem) = refs[29:52]
+    late_tables = refs[52:]
+    n_seq, n_dp, seq_index, dp_index = places()
+    chips, chip, core = n_seq // 2, seq_index // 2, lax.rem(seq_index, 2)
+    sibling = (dp_index, chip * 2 + 1 - core)
+    seq_peers = [lax.rem(seq_index + k, n_seq) for k in range(n_seq)]
+    dp_peers = [lax.rem(dp_index + k, n_dp) for k in range(n_dp)]
+    rows, wide = first_ref.shape[1:]
+    sub = rows // n_dp
+    half = wide // 2
+    step_cols = att_stage.shape[2] // 3
+    share = wide // step_cols
+    tokens, width = tokens_ref.shape
+    greet([(dp_index, p) for p in seq_peers[1:]] + [(p, seq_index) for p in dp_peers[1:]])
+
+    for u in range(3):
+        for block in range(n_seq):
+            g, h = block // share, block % share
+            att_stage[block, :, u * step_cols : (u + 1) * step_cols] = first_ref[
+                info[u], g * sub : (g + 1) * sub, h * step_cols : (h + 1) * step_cols
+            ]
+    for g in range(n_dp):
+        out_stage[:, g * wide : (g + 1) * wide] = first_ref[info[3], g * sub : (g + 1) * sub, :]
+    own = [
+        pltpu.make_async_copy(att_stage.at[seq_index], qkv_all.at[seq_index, dp_index], own_sem.at[0]),
+        pltpu.make_async_copy(out_stage, out_all.at[dp_index], own_sem.at[1]),
+    ]
+    cot_own = pltpu.make_async_copy(cot_ref, cot_all.at[core], own_sem.at[2])
+    cot_copy = send(cot_ref, cot_all.at[core], cot_send, cot_recv, sibling)
+    across = []
+    for k in range(1, n_seq):
+        copy = send(
+            att_stage.at[seq_peers[k]],
+            qkv_all.at[seq_index, dp_index],
+            a_send.at[k],
+            a_recv.at[k],
+            (dp_index, seq_peers[k]),
+        )
+        copy.start()
+        across.append(copy)
+    for copy in own:
+        copy.start()
+    cot_copy.start()
+    cot_own.start()
+    for copy in own:
+        copy.wait()
+    for copy in across:
+        copy.wait_recv()
+    relay_gather(
+        [lambda block: qkv_all.at[:, block], lambda block: out_all.at[block]],
+        dp_index,
+        n_dp,
+        lambda place: (place, seq_index),
+        w_send,
+        w_recv,
+        lambda block: None,
+    )
+
+    def band(c):
+        return pl.ds(c * sub, sub)
+
+    def late_copies(c):
+        copies = []
+        for k in range(1, n_dp):
+            copies.append(
+                send(
+                    late_ref.at[dp_peers[k], :, band(c)],
+                    late_tables[c].at[dp_index],
+                    late_send.at[c, k],
+                    late_recv.at[c, k],
+                    (dp_peers[k], seq_index),
+                )
+            )
+        return copies
+
+    def late_own_copy(c):
+        return pltpu.make_async_copy(
+            late_ref.at[dp_index, :, band(c)], late_tables[c].at[dp_index], late_own.at[c]
+        )
+
+    def late_start(c):
+        if not has_late or c >= n_dp:
+            return
+        if c:
+            for copy in late_copies(c - 1):
+                copy.wait_send()
+        for copy in late_copies(c):
+            copy.start()
+        late_own_copy(c).start()
+
+    late_start(0)
+
+    seq_len = x1_ref.shape[0]
+    heads = query_out.shape[1] // HD
+    block_rows = min(256, seq_len)
+    head_cols = heads * HD
+    qkv_weight = qkv_all[...].reshape(width, 3 * head_cols)
+
+    def project(b, carry):
+        at = pl.ds(pl.multiple_of(b * block_rows, block_rows), block_rows)
+        result = jnp.dot(x1_ref[at, :], qkv_weight, preferred_element_type=f32)
+        cosine, sine = cos_ref[at, :], sin_ref[at, :]
+        for h in range(heads):
+            place = slice(h * HD, (h + 1) * HD)
+            for part_id, out in ((0, query_out), (1, key_out)):
+                begin = part_id * head_cols + h * HD
+                values = result[:, begin : begin + HD]
+                out[at, place] = (values * cosine + turn_half(values) * sine).astype(bf)
+        value_out[at, :] = result[:, 2 * head_cols :].astype(bf)
+        return carry
+
+    lax.fori_loop(0, seq_len // block_rows, project, 0)
+
+    def attend(b, carry):
+        begin = pl.multiple_of(b * block_rows, block_rows)
+        at = pl.ds(begin, block_rows)
+        query_pos = begin + lax.broadcasted_iota(jnp.int32, (block_rows, seq_len), 0)
+        key_pos = lax.broadcasted_iota(jnp.int32, (block_rows, seq_len), 1)
+        allowed = (doc_col[at, :] == doc_row[...]) & (key_pos <= query_pos)
+        for h in range(heads):
+            place = slice(h * HD, (h + 1) * HD)
+            scores = lax.dot_general(
+                query_out[at, place],
+                key_out[:, place],
+                (((1,), (1,)), ((), ())),
+                preferred_element_type=f32,
+            )
+            scores = jnp.where(allowed, scores * (float(HD) ** (-0.5)), masked_score)
+            peak = jnp.max(scores, axis=-1, keepdims=True)
+            raised = jnp.exp(scores - peak)
+            total = jnp.sum(raised, axis=-1, keepdims=True)
+            prob = (raised * (1.0 / total)).astype(bf)
+            mixed = jnp.dot(prob, value_out[:, place], preferred_element_type=f32)
+            mixed_out[at, place] = mixed.astype(bf)
+            stat_out[at, place] = jnp.broadcast_to(peak + jnp.log(total), (block_rows, HD))
+        return carry
+
+    lax.fori_loop(0, seq_len // block_rows, attend, 0)
+    out_weight = out_all[...].reshape(rows, width)
+
+    def combine(b, carry):
+        at = pl.ds(pl.multiple_of(b * tokens, tokens), tokens)
+        part[b] = jnp.dot(mixed_out[at, :], out_weight, preferred_element_type=f32).astype(bf)
+        return carry
+
+    lax.fori_loop(0, n_seq, combine, 0)
+
+    chip_peers = [lax.rem(chip + k, chips) for k in range(chips)]
+    order = list(range(chips - 1, 0, -1)) + [0]
+    passed = {}
+    for k in order:
+        block = part.at[chip_peers[k] * 2 + 1 - core]
+        passed[k] = send(block, taken.at[k], s_pass.at[k], s_take.at[k], sibling)
+        passed[k].start()
+    copies = {}
+    for k in order[:-1]:
+        passed[k].wait_recv()
+        value = part[chip_peers[k] * 2 + core].astype(f32)
+        sent[k] = (value + taken[k].astype(f32)).astype(bf)
+        device = (dp_index, chip_peers[k] * 2 + core)
+        copies[k] = send(sent.at[k], arrived.at[k], s_send.at[k], s_recv.at[k], device)
+        copies[k].start()
+
+    ring = Ring(chips, chip, core, dp_index, None, None)
+    pair = ff_blocks // 2
+
+    def ring_leg(c, view, way, step, arriving):
+        distance = step if arriving else step - 1
+        block = ring.at(-distance if way == 0 else distance)
+        begin = ff_blocks if view == 2 else 0
+        units = pl.ds(begin, ff_blocks)
+        if step == ring.last:
+            units = pl.ds(begin + way * pair, pair)
+        if view == 0:
+            ref = down_all.at[units, block, :, pl.ds(c * wide, wide)]
+        else:
+            ref = ug_all.at[units, block, :, band(c)]
+        return send(
+            ref, ref, ring_send.at[c, view, way, step - 1], ring_recv.at[c, view, way, step - 1],
+            ring.device(way),
+        )
+
+    def side_copy(c):
+        return send(
+            given_stage.at[c],
+            ug_all.at[:, chip, core, band(c)],
+            side_send.at[c],
+            side_recv.at[c],
+            sibling,
+        )
+
+    def begin_band(c):
+        if has_late:
+            for copy in late_copies(c):
+                copy.wait_recv()
+            late_own_copy(c).wait()
+            late_start(c + 1)
+            table = late_tables[c]
+            late_slots = table.shape[1]
+        for u in range(3 * ff_blocks):
+            value = first_ref[info[4 + u], band(c), :]
+            if has_late:
+                code = info[4 + 3 * ff_blocks + u]
+                other = table[code // late_slots, lax.rem(code, late_slots)]
+                use_late = jnp.full(value.shape, info[4 + 6 * ff_blocks + u], jnp.int32) != 0
+                value = jnp.where(use_late, other, value)
+            if u < 2 * ff_blocks:
+                left, right = value[:, :half], value[:, half:]
+
+                @pl.when(core == 0)
+                def _():
+                    mine_stage[c, u] = left
+                    given_stage[c, u] = right
+
+                @pl.when(core != 0)
+                def _():
+                    mine_stage[c, u] = right
+                    given_stage[c, u] = left
+            else:
+                down_stage[c, u - 2 * ff_blocks] = value
+        side_copy(c).start()
+        local = [
+            pltpu.make_async_copy(mine_stage.at[c], ug_all.at[:, chip, core, band(c)], stage_own.at[c, 0]),
+            pltpu.make_async_copy(
+                down_stage.at[c], down_all.at[:, chip, :, pl.ds(c * wide, wide)], stage_own.at[c, 1]
+            ),
+        ]
+        for copy in local:
+            copy.start()
+        for copy in local:
+            copy.wait()
+        side_copy(c).wait_recv()
+        for view in range(3):
+            for way in range(2):
+                ring_leg(c, view, way, 1, False).start()
+
+    def carry_band(c, step):
+        for view in range(3):
+            for way in range(2):
+                ring_leg(c, view, way, step - 1, True).wait_recv()
+                ring_leg(c, view, way, step, False).start()
+
+    begin_band(0)
+    passed[0].wait_recv()
+    total = part[seq_index].astype(f32) + taken[0].astype(f32)
+    for k in range(1, chips):
+        copies[k].wait_recv()
+        total = total + arrived[k].astype(f32)
+    residual = tokens_ref[...] + total
+    residual_out[...] = residual
+    center = residual - jnp.mean(residual, axis=-1, keepdims=True)
+    spread = jnp.mean(center * center, axis=-1, keepdims=True)
+    x_stage[...] = (center * lax.rsqrt(spread + norm_eps)).astype(bf)
+    for c in range(1, n_dp):
+        begin_band(c)
+        for step in range(2, ring.last + 1):
+            carry_band(c - 1, step)
+
+    own_x = pltpu.make_async_copy(x_stage, x_all.at[core, dp_index], own_sem.at[3])
+    own_x.start()
+    own_x.wait()
+
+    def onward(block):
+        ref = x_all.at[core, block]
+        return send(ref, ref, pass_sem.at[block], take_sem.at[block], sibling)
+
+    onward(dp_index).start()
+    relay_gather(
+        [lambda block: x_all.at[core, block]],
+        dp_index,
+        n_dp,
+        lambda place: (place, seq_index),
+        send_sem,
+        recv_sem,
+        lambda block: onward(block).start(),
+        lambda step: carry_band(n_dp - 1, 2) if step == 1 and ring.last > 1 else None,
+    )
+    for step in range(3, ring.last + 1):
+        carry_band(n_dp - 1, step)
+    for c in range(n_dp):
+        for view in range(3):
+            for way in range(2):
+                ring_leg(c, view, way, ring.last, True).wait_recv()
+                for step in range(1, ring.last + 1):
+                    ring_leg(c, view, way, step, False).wait_send()
+        side_copy(c).wait_send()
+        if has_late:
+            if c == n_dp - 1:
+                for copy in late_copies(c):
+                    copy.wait_send()
+    for block in range(n_dp):
+        onward(block).wait_send()
+        ref = x_all.at[1 - core, block]
+        send(ref, ref, pass_sem.at[block], take_sem.at[block], sibling).wait_recv()
+    for k in order:
+        passed[k].wait_send()
+    for k in order[:-1]:
+        copies[k].wait_send()
+    for copy in across:
+        copy.wait_send()
+    cot_copy.wait_send()
+    cot_own.wait()
+    ref = cot_all.at[1 - core]
+    send(ref, ref, cot_send, cot_recv, sibling).wait_recv()
+
+
+def forward(info, first_table, late, x1, cosine, sine, doc, tokens, cot, ff_blocks, first_slots, collective_id):
+    n_seq = lax.axis_size("seq")
+    n_dp = lax.axis_size("dp")
+    chips = n_seq // 2
+    rows, wide = first_table.shape[1:]
+    sub = rows // n_dp
+    half = wide // 2
+    seq_len, width = x1.shape
+    head_cols = width // n_seq
+    shard = tokens.shape[0]
+    steps = chips // 2
+    vmem = pltpu.VMEM
+    low = lambda *shape: jax.ShapeDtypeStruct(shape, bf)
+    has_late = late is not None
+    blocks = vmem((chips, shard, width), bf)
+    return pl.pallas_call(
+        functools.partial(forward_kernel, has_late, first_slots, ff_blocks),
+        out_shape=[
+            low(n_seq, n_dp, sub, 3 * head_cols),
+            low(n_dp, sub, width),
+            low(seq_len, head_cols),
+            low(seq_len, head_cols),
+            low(seq_len, head_cols),
+            low(seq_len, head_cols),
+            jax.ShapeDtypeStruct((seq_len, head_cols), f32),
+            jax.ShapeDtypeStruct((shard, width), f32),
+            low(2 * ff_blocks, chips, 2, rows, half),
+            low(ff_blocks, chips, sub, width),
+            low(2, n_dp, shard, width),
+            low(2, n_dp, shard, width),
+        ],
+        in_specs=[pl.BlockSpec(memory_space=pltpu.SMEM), VMEM]
+        + [ANY] * has_late
+        + [VMEM] * 7,
+        out_specs=[VMEM] * 8 + [ANY] * 4,
+        scratch_shapes=[
+            vmem((n_seq, sub, 3 * head_cols), bf),
+            vmem((sub, width), bf),
+            vmem((n_seq, shard, width), bf),
+            blocks,
+            blocks,
+            blocks,
+            vmem((shard, width), bf),
+            vmem((n_dp, 2 * ff_blocks, sub, half), bf),
+            vmem((n_dp, 2 * ff_blocks, sub, half), bf),
+            vmem((n_dp, ff_blocks, sub, wide), bf),
+            DMA((4,)),
+            DMA((n_seq,)),
+            DMA((n_seq,)),
+            DMA((2, 2, n_dp)),
+            DMA((2, 2, n_dp)),
+            DMA((chips,)),
+            DMA((chips,)),
+            DMA((chips,)),
+            DMA((chips,)),
+            DMA,
+            DMA,
+            DMA((n_dp, n_dp)),
+            DMA((n_dp, n_dp)),
+            DMA((n_dp,)),
+            DMA((n_dp, 2)),
+            DMA((n_dp,)),
+            DMA((n_dp,)),
+            DMA((n_dp, 3, 2, steps)),
+            DMA((n_dp, 3, 2, steps)),
+            DMA((1, 2, n_dp)),
+            DMA((1, 2, n_dp)),
+            DMA((n_dp,)),
+            DMA((n_dp,)),
+        ]
+        + [vmem((n_dp, late.shape[1], sub, wide), bf) for _ in range(n_dp if has_late else 0)],
+        compiler_params=comm_params(collective_id, 58),
+        cost_estimate=takes(230),
+        name="forward",
+    )(
+        info,
+        first_table,
+        *([late] if has_late else []),
+        x1,
+        cosine,
+        sine,
+        doc[None, :],
+        doc[:, None],
+        tokens,
+        cot,
+    )
+
+
 def local(block_input, cotangent, doc_lengths, owners, master, first_moment, second_moment):
     n_seq = lax.axis_size("seq")
     n_dp = lax.axis_size("dp")
@@ -1314,54 +1311,54 @@
     first_table, normed_one_all = front(packed[0], normed_one.astype(bf), 2)
     first_table = first_table.reshape(n_dp * first_slots, rows, wide)
     normed_one_all = normed_one_all.reshape(seq_len, width)
-    att_rows, att_out = pick_attention(
-        first_table, (owners * first_slots + place)[:4], n_seq, sub, width
-    )
-    qkv_weight, out_weight = spread_attention(att_rows, att_out, 1)
-    if per_owner > first_slots:
-        late, qkv_weight = lax.optimization_barrier((packed[1], qkv_weight))
-        late = lax.all_to_all(late, "dp", 0, 0)
+    upstream = cotangent.reshape(shard_len, width)
+    upstream_column = lax.all_gather(upstream, "dp", axis=0)
+    positions = jnp.arange(seq_len, dtype=jnp.int32)
+    cosine, sine = rope_tables(positions.astype(f32), HD)
+    doc_ends = jnp.cumsum(doc_lengths[0])
+    doc = jnp.sum((positions[:, None] >= doc_ends[None, :]).astype(jnp.int32), axis=1)
+    late_slots = per_owner - first_slots
+    info = jnp.concatenate(
+        [
+            owners * first_slots + jnp.minimum(place, first_slots - 1),
+            (owners * late_slots + jnp.maximum(place - first_slots, 0))[4:],
+            (place >= first_slots)[4:],
+        ]
+    ).astype(jnp.int32)
+    (
+        qkv_weight,
+        out_weight,
+        queries,
+        keys,
+        values,
+        attended_low,
+        log_total,
+        residual,
+        ug_weight,
+        down_weight,
+        normed_two_all,
+        upstream_all,
+    ) = forward(
+        info,
+        first_table,
+        packed[1] if late_slots else None,
+        normed_one_all,
+        cosine,
+        sine,
+        doc,
+        tokens,
+        upstream_column,
+        ff_blocks,
+        first_slots,
+        1,
+    )
     qkv_weight = qkv_weight.reshape(width, 3 * head_cols)
     out_weight = out_weight.reshape(rows, width)
-
-    qkv_proj = jnp.dot(normed_one_all, qkv_weight, preferred_element_type=f32)
-    qkv_proj = qkv_proj.reshape(seq_len, 3, heads, HD)
-    positions = jnp.arange(seq_len, dtype=jnp.int32)
-    cosine, sine = rope_tables(positions.astype(f32), HD)
+    queries, keys, values = (a.reshape(seq_len, heads, HD) for a in (queries, keys, values))
+    log_total = log_total.reshape(seq_len, heads, HD)[:, :, :1].transpose(1, 0, 2)
     cosine = cosine[:, None, :]
     sine = sine[:, None, :]
-    queries = rotate(qkv_proj[:, 0], cosine, sine).astype(bf)
-    keys = rotate(qkv_proj[:, 1], cosine, sine).astype(bf)
-    values = qkv_proj[:, 2].astype(bf)
-    doc_ends = jnp.cumsum(doc_lengths[0])
-    doc = jnp.sum((positions[:, None] >= doc_ends[None, :]).astype(jnp.int32), axis=1)
-    allowed = (doc[:, None] == doc[None, :]) & (positions[None, :] <= positions[:, None])
-    scores = jnp.einsum("qhd,khd->hqk", queries, keys, preferred_element_type=f32) * score_scale
-    scores = jnp.where(allowed[None], scores, masked_score)
-    peak = jnp.max(scores, axis=-1, keepdims=True)
-    raised = jnp.exp(scores - peak)
-    prob = raised / jnp.sum(raised, axis=-1, keepdims=True)
-    prob_low = prob.astype(bf)
-    attended = jnp.einsum("hqk,khd->qhd", prob_low, values, preferred_element_type=f32)
-    attended_low = attended.reshape(seq_len, head_cols).astype(bf)
-    attn_part = jnp.dot(attended_low, out_weight, preferred_element_type=f32).astype(bf)
-    attn_out = sum_seq(attn_part.reshape(n_seq, shard_len, width), 3)
-    residual = tokens + attn_out
     normed_two, inv_two = norm_parts(residual)
-
-    upstream = cotangent.reshape(shard_len, width)
-    upstream_column = lax.all_gather(upstream, "dp", axis=0)
-    if per_owner > first_slots:
-        late, normed_two = lax.optimization_barrier((late, normed_two))
-        late = late.reshape(-1, rows, wide)
-    else:
-        late = None
-    mine, given, down = pick_ff(
-        first_table, late, owners, place, core, ff_blocks, sub, first_slots
-    )
-    ug_weight, down_weight, normed_two_all, upstream_all = gather_weights(
-        mine, given, down, normed_two.astype(bf), upstream_column, 4
-    )
     up_weight = ug_weight[:ff_blocks].reshape(ff_blocks, width, half)
     gate_weight = ug_weight[ff_blocks:].reshape(ff_blocks, width, half)
     down_weight = down_weight.reshape(ff_blocks, half, width)
@@ -1414,6 +1411,11 @@
         "tc,rc->tr", residual_grad_all, out_weight, preferred_element_type=f32
     )
     attended_grad = attended_grad.astype(bf).reshape(seq_len, heads, HD)
+    allowed = (doc[:, None] == doc[None, :]) & (positions[None, :] <= positions[:, None])
+    scores = jnp.einsum("qhd,khd->hqk", queries, keys, preferred_element_type=f32) * score_scale
+    scores = jnp.where(allowed[None], scores, masked_score)
+    prob = jnp.exp(scores - log_total)
+    prob_low = prob.astype(bf)
     value_grad = jnp.einsum("hqk,qhd->khd", prob_low, attended_grad, preferred_element_type=f32)
     prob_grad = jnp.einsum("qhd,khd->hqk", attended_grad, values, preferred_element_type=f32)
     inner_sum = jnp.sum(prob * prob_grad, axis=-1, keepdims=True)

time: 998 us -> 978 us (0.980)
  waiting for transfers between devices: 91.6 us -> 57.4 us
  Pallas kernels: 679 us -> 700 us
    pallas_call x4 -> x1, Pallas kernels: 219 us -> 274 us  [forward(): pl.pallas_call(functools.partial(forward_kernel, has_late, first_slots, f...]
    all_to_all x1 -> x0, waiting for transfers between devices: 33.8 us -> none  [local(): late = lax.all_to_all(late, 'dp', 0, 0)]
    pallas_call x2 -> x1, Pallas kernels: 58.4 us -> 29.4 us  [sum_seq(): pl.pallas_call(sum_seq_kernel, out_shape=jax.ShapeDtypeStruct((rows, colu...]
    unnamed x108 -> x89, local copies, waits for them, and re-layouts: 24.8 us -> 20.4 us
  transfers between devices with their start and end apart: 4 -> 3, of which waited for: 2 -> 1; matrix products, arithmetic and copies ran while one was open for 9% -> 8% of each run, Pallas kernels for 40% -> 26%
where the time goes in v5:
time: 978 us; the launch traced here: 969 us
  Pallas kernels  700 us (72%)
  matrix products  124 us (13%)
  waiting for transfers between devices  57.4 us (6%)
  local copies, waits for them, and re-layouts  43.3 us (4%)
  other arithmetic  18.6 us (2%)
  between operations  15.2 us (2%)
  starting transfers between devices  10.5 us (1%)
    pallas_call x1, Pallas kernels, forward(): pl.pallas_call(functools.partial(forward_kernel, has_late, first_slots, f...  274 us
    pallas_call x1, Pallas kernels, sum_grads(): pl.pallas_call(grads_kernel, out_shape=[jax.ShapeDtypeStruct((2 * blocks,...  122 us
    pallas_call x1, Pallas kernels, front(): pl.pallas_call(front_kernel, out_shape=[jax.ShapeDtypeStruct(packed.shape...  89.8 us
    pallas_call x1, Pallas kernels, collect_attention(): pl.pallas_call(collect_kernel, out_shape=[jax.ShapeDtypeStruct((n_seq,) +...  83.3 us
    all_to_all x1, waiting for transfers between devices, local(): grads.insert(0, lax.all_to_all(early, 'dp', 0, 0))  56.8 us
    pallas_call x1, Pallas kernels, adam(): pl.pallas_call(functools.partial(adam_kernel, n_dp, n_seq // 2, first_slo...  53 us
    pallas_call x1, Pallas kernels, gather_seq(): pl.pallas_call(gather_seq_kernel, out_shape=jax.ShapeDtypeStruct((2 * chi...  29.6 us
    pallas_call x1, Pallas kernels, sum_seq(): pl.pallas_call(sum_seq_kernel, out_shape=jax.ShapeDtypeStruct((rows, colu...  29.4 us
  transfers between devices with their start and end apart: 3, of which 1 were waited for; matrix products, arithmetic and copies ran while one was open for 8% of the time, Pallas kernels for 26%

profile of v5, /device:TPU:0, one launch (start us, length us, event | category | flops | bytes accessed | tf_op | source)
XLA Modules:
  0.0 969.4 jit_solution(10110669780805924796)
XLA Ops:
  16.4 16.3 %pack.1 = (bf16[4,4,256,512]{3,2,1,0:T(8,128)(2,1)}, bf16[4,4,256,512]{3,2,1,0:T(8,128)(2,1)}) custom-call(s32[8]{0:T(128)S(1)} %fusion.55.flags, f32[256,8,2048]{2,1,0:T(8,128)} %refs_4_.1), custom_call_target="tpu_custom_call" | custom-call | tf_op jit(solution)/shard_map/pack/pallas_call | solution.py:113
  35.8 89.8 %front.1 = (bf16[4,4,256,512]{3,2,1,0:T(8,128)(2,1)S(1)}, bf16[8,128,2048]{2,1,0:T(8,128)(2,1)S(1)}) custom-call(bf16[4,4,256,512]{3,2,1,0:T(8,128)(2,1)S(1)} %copy-done.6, bf16[128,2048]{1,0:T(8,128)(2,1)S(1)} %fusion.47.x_ref), custom_call_target="tpu_custom_call" | custom-call | bytes 270000000 | tf_op jit(solution)/shard_map/front/pallas_call | solution.py:433
  133.1 273.9 %forward.1 = (bf16[8,4,64,768]{3,2,1,0:T(8,128)(2,1)}, bf16[4,64,2048]{2,1,0:T(8,128)(2,1)}, bf16[1024,256]{1,0:T(8,128)(2,1)}, bf16[1024,256]{1,0:T(8,128)(2,1)...) custom-call(s32[40]{0:T(128)} %pad_add_fusion.refs_0_, ...), custom_call_target="tpu_custom_call" | custom-call | bytes 690000000 | tf_op jit(solution)/shard_map/forward/pallas_call | solution.py:1202
  414.5 6.1 fusion.77
  420.5 6.0 fusion.78
  426.5 9.7 %multiply_convert_fusion.1 = (bf16[1024,4,256]{2,0,1:T(8,128)(2,1)S(1)}, bf16[1024,4,256]{2,0,1:T(8,128)(2,1)}, bf16[1024,4,256]{2,0,1:T(8,128)(2,1)S(1)}) fusion(f32[1024,4,256]{2,0,1:T(8,128)} %fusion.78, f32[1024,4,256]{2,0,1:T(8,128)} %fusion.77, bf16[1024,2048,1]{1,0,2:T(8,128)(2,1)S(1)} %bitcast.163, bf16[4,2048,256]{2,1,0:T(8,128)(2,1)S(1)} %bitcast.145), kind=kOutput, calls=%fused_computation.18 | convolution fusion | flops 4309647360 | bytes 23068672 | tf_op jit(solution)/shard_map/tr,jrc->tjc/dot_general | solution.py:1367
  436.3 6.1 bitcast_convert_fusion
  442.3 6.2 convolution_convert_fusion.1
  448.6 6.5 convert_bitcast_fusion.1
  455.1 6.8 fusion.79
  465.4 9.3 convert_bitcast_fusion
  474.7 6.2 copy.68
  480.9 6.3 copy.70
  487.2 9.6 fusion.1
  496.9 122.4 %sum_grads.1 = (bf16[8,256,512]{2,1,0:T(8,128)(2,1)}, bf16[4,64,2048]{2,1,0:T(8,128)(2,1)}, f32[128,2048]{1,0:T(8,128)}, f32[128,2048]{1,0:T(8,128)}) custom-call(bf16[4,4,2,256,256]{4,3,2,1,0:T(8,128)(2,1)} %bitcast.137, bf16[4,4,2,256,256]{4,3,2,1,0:T(8,128)(2,1)} %bitcast.138, bf16[4,4,64,2048]{3,2,1,0:T(8,128)(2,1)} %bitcast.140, ...), custom_call_target="tpu_custom_call" | custom-call | bytes 360000000 | tf_op jit(solution)/shard_map/sum_grads/pallas_call | solution.py:827
  633.6 29.6 %gather_seq.1 = bf16[8,128,2048]{2,1,0:T(8,128)(2,1)S(1)} custom-call(bf16[128,2048]{1,0:T(8,128)(2,1)S(1)} %get-tuple-element.64.x_ref), custom_call_target="tpu_custom_call" | custom-call | bytes 84000000 | tf_op jit(solution)/shard_map/gather_seq/pallas_call | solution.py:464
  675.8 14.1 %fusion.36 = f32[1024,2,128]{0,2,1:T(8,128)} fusion(bf16[1024,2,128]{0,2,1:T(8,128)(2,1)S(1)} %bitcast.150, f32[2,1024,1024]{1,2,0:T(8,128)} %fusion.51, f32[2,1024,1024]{1,2,0:T(8,128)} %fusion.80, f32[2,1024]{1,0:T(2,128)S(1)} %bitcast.157, pred[1024,1024]{0,1:T(8,128)(4,1)S(1)} %copy-done.23), kind=kOutput, calls=%fused_computation.36 | convolution fusion | flops 559942656 | bytes 19406848 | tf_op jit(solution)/shard_map/hqk,qhd->khd/dot_general | solution.py:1424
  689.9 16.2 %broadcast_multiply_fusion.1 = (f32[1024,2,128]{0,2,1:T(8,128)}, f32[1024,2,128]{0,2,1:T(8,128)}, f32[1024,2,128]{0,2,1:T(8,128)}) fusion(f32[1024,128]{0,1:T(8,128)} %copy.80, f32[1024,2,128]{0,2,1:T(8,128)} %fusion.36, bf16[1024,2,128]{0,2,1:T(8,128)(2,1)S(1)} %bitcast.148, f32[2,1024,1024]{1,2,0:T(8,128)} %fusion.51, f32[2,1024,1024]{1,2,0:T(8,128)} %fusion.80, ...), kind=kOutput, calls=%fused_computation.68 | convolution fusion | flops 560466944 | bytes 23076864 | tf_op jit(solution)/shard_map/hqk,khd->qhd/dot_general | solution.py:1423
  709.6 6.1 fusion.42
  722.5 83.3 %collect_attention.1 = (bf16[8,64,768]{2,1,0:T(8,128)(2,1)S(1)}, bf16[64,2048]{1,0:T(8,128)(2,1)S(1)}) custom-call(bf16[8,4,64,768]{3,2,1,0:T(8,128)(2,1)S(1)} %bitcast.135, bf16[4,64,2048]{2,1,0:T(8,128)(2,1)S(1)} %bitcast.136), custom_call_target="tpu_custom_call" | custom-call | bytes 225000000 | tf_op jit(solution)/shard_map/collect_attention/pallas_call | solution.py:569
  815.2 5.8 convolution_convert_fusion
  821.0 29.4 %sum_seq.1 = f32[128,2048]{1,0:T(8,128)S(1)} custom-call(bf16[8,128,2048]{2,1,0:T(8,128)(2,1)S(1)} %bitcast.129), custom_call_target="tpu_custom_call" | custom-call | bytes 84000000 | tf_op jit(solution)/shard_map/sum_seq/pallas_call | solution.py:512
  852.2 56.8 %all-to-all-done.refs_0_ = bf16[4,4,256,512]{3,2,1,0:T(8,128)(2,1)} async-done(((bf16[4,4,256,512]{3,2,1,0:T(8,128)(2,1)}), bf16[4,4,256,512]{3,2,1,0:T(8,128)(2,1)}, u32[]{:S(2)}, u32[]{:S(2)}) %all-to-all-start) | async-done | bytes 4194336 | tf_op jit(solution)/shard_map/all_to_all | solution.py:1450
  909.1 53.0 %adam.1 = (f32[256,8,2048]{2,1,0:T(8,128)}, f32[256,8,2048]{2,1,0:T(8,128)}, f32[256,8,2048]{2,1,0:T(8,128)}, f32[256,8,2048]{2,1,0:T(8,128)}) custom-call(s32[8]{0:T(128)S(1)} %get-tuple-element.63.kinds, bf16[4,4,256,512]{3,2,1,0:T(8,128)(2,1)} %all-to-all-done.refs_0_, bf16[4,4,256,512]{3,2,1,0:T(8,128)(2,1)} %all-to-all-done.1.refs_1_, ...), custom_call_target="tpu_custom_call" | custom-call | tf_op jit(solution)/shard_map/adam/pallas_call | solution.py:190
  (153 shorter events, 78.6 us)
Async XLA Ops:
  7.2 125.9 %all-gather.2.cloned.1.call-start = ((), (), s32[]{:S(2)}) async-start(), calls=%async_computation.2 | async-start | bytes 2621440 | tf_op jit(solution)/shard_map/all_gather | solution.py:1315
  9.7 23.1 %copy-start.33 = (s32[4,8]{1,0:T(4,128)}, s32[4,8]{1,0:T(4,128)S(1)}, u32[]{:S(2)}) copy-start(s32[4,8]{1,0:T(4,128)S(1)} %sub.71) | copy-start | bytes 388
  10.7 119.7 %copy-start.32 = (s32[1024]{0:T(1024)}, s32[1024]{0:T(1024)S(1)}, u32[]{:S(2)}) copy-start(s32[1024]{0:T(1024)S(1)} %convert_reduce_fusion.1) | copy-start | bytes 12292
  14.2 18.5 %copy-start.15 = (f32[1024,128]{1,0:T(8,128)}, f32[1024,128]{1,0:T(8,128)S(1)}, u32[]{:S(2)}) copy-start(f32[1024,128]{1,0:T(8,128)S(1)} %get-tuple-element.89.refs_4_) | copy-start | bytes 1572868
  14.2 18.5 %copy-start.16 = (f32[1024,128]{1,0:T(8,128)}, f32[1024,128]{1,0:T(8,128)S(1)}, u32[]{:S(2)}) copy-start(f32[1024,128]{1,0:T(8,128)S(1)} %get-tuple-element.90.refs_5_) | copy-start | bytes 1572868
  16.4 16.3 %copy-start.12 = (bf16[1,128,2048]{2,1,0:T(8,128)(2,1)S(1)}, bf16[1,128,2048]{2,1,0:T(8,128)(2,1)}, u32[]{:S(2)}) copy-start(bf16[1,128,2048]{2,1,0:T(8,128)(2,1)} %param.7) | copy-start | bytes 1572868
  32.9 100.2 %copy-start.34 = (f32[128]{0:T(128)}, f32[128]{0:T(128)S(1)}, u32[]{:S(2)}) copy-start(f32[128]{0:T(128)S(1)} %broadcast_multiply_fusion.7) | copy-start | bytes 1540
  33.2 99.9 %copy-start.36 = (f32[128]{0:T(128)}, f32[128]{0:T(128)S(1)}, u32[]{:S(2)}) copy-start(f32[128]{0:T(128)S(1)} %add_rsqrt_fusion.1) | copy-start | bytes 1540
  407.0 7.4 copy-start.40
  411.1 9.4 copy-start.18
  455.1 6.8 copy-start.14
  455.1 7.2 copy-start.31
  455.1 8.2 copy-start.30
  625.1 184.2 %all-to-all-start.1 = ((bf16[4,4,256,512]{3,2,1,0:T(8,128)(2,1)}), bf16[4,4,256,512]{3,2,1,0:T(8,128)(2,1)}, u32[]{:S(2)}, u32[]{:S(2)}) async-start(bf16[4,4,256,512]{3,2,1,0:T(8,128)(2,1)} %bitcast.127), calls=%async_computation.1 | async-start | bytes 8388608 | tf_op jit(solution)/shard_map/all_to_all | solution.py:1406
  630.7 34.4 %copy-start.41 = (bf16[4,64,2048]{2,1,0:T(8,128)(2,1)S(1)}, bf16[4,64,2048]{2,1,0:T(8,128)(2,1)}, u32[]{:S(2)}) copy-start(bf16[4,64,2048]{2,1,0:T(8,128)(2,1)} %get-tuple-element.46) | copy-start | bytes 3145732
  709.6 6.3 copy-start.5
  709.6 6.3 copy-start.42
  715.9 6.6 copy-start.22
  722.5 83.3 %copy-start.3 = (bf16[8,256,512]{2,1,0:T(8,128)(2,1)S(1)}, bf16[8,256,512]{2,1,0:T(8,128)(2,1)}, u32[]{:S(2)}) copy-start(bf16[8,256,512]{2,1,0:T(8,128)(2,1)} %get-tuple-element.49.ug_ref) | copy-start | bytes 6291460
  722.5 83.3 %copy-start.11 = (bf16[4,64,2048]{2,1,0:T(8,128)(2,1)S(1)}, bf16[4,64,2048]{2,1,0:T(8,128)(2,1)}, u32[]{:S(2)}) copy-start(bf16[4,64,2048]{2,1,0:T(8,128)(2,1)} %get-tuple-element.50.down_ref) | copy-start | bytes 3145732
  809.3 99.7 %all-to-all-start = ((bf16[4,4,256,512]{3,2,1,0:T(8,128)(2,1)}), bf16[4,4,256,512]{3,2,1,0:T(8,128)(2,1)}, u32[]{:S(2)}, u32[]{:S(2)}) async-start(bf16[4,4,256,512]{3,2,1,0:T(8,128)(2,1)} %bitcast.128), calls=%async_computation | async-start | bytes 8388608 | tf_op jit(solution)/shard_map/all_to_all | solution.py:1450
  821.0 29.4 %copy-start.13 = (bf16[1,128,2048]{2,1,0:T(8,128)(2,1)S(1)}, bf16[1,128,2048]{2,1,0:T(8,128)(2,1)}, u32[]{:S(2)}) copy-start(bf16[1,128,2048]{2,1,0:T(8,128)(2,1)} %param.7) | copy-start | bytes 1572868
  821.0 29.4 %copy-start.35 = (f32[128]{0:T(128)S(1)}, f32[128]{0:T(128)}, u32[]{:S(2)}) copy-start(f32[128]{0:T(128)} %copy-done.34) | copy-start | bytes 1540
  821.0 29.4 %copy-start.37 = (f32[128]{0:T(128)S(1)}, f32[128]{0:T(128)}, u32[]{:S(2)}) copy-start(f32[128]{0:T(128)} %copy-done.36) | copy-start | bytes 1540
  (23 other events, 74.0 us)
Sparse Core Ops, SparseCore 0:
  9.6 101.6 all-gather.1

commit v6 on v5

--- a/solution.py
+++ b/solution.py
@@ -126,10 +126,11 @@
     )(flags, master)
 
 
-def adam_kernel(n_dp, chips, first_slots, n_groups, kinds, *refs):
+def adam_kernel(n_dp, chips, first_slots, n_groups, n_kept, kinds, *refs):
     cols = refs[:n_groups]
     rws = refs[n_groups : 2 * n_groups]
-    m_ref, f_ref, s_ref, keep_ref, g_out, f_out, s_out, m_out, held = refs[2 * n_groups :]
+    m_ref, f_ref, s_ref, keep_ref = refs[2 * n_groups : 2 * n_groups + 4]
+    g_out, f_out, s_out, m_out, held = refs[2 * n_groups + 4 + n_kept :]
     rb, slots, width = m_ref.shape
     wide = width // n_dp
     rows = width // (2 * chips)
@@ -172,44 +173,54 @@
     m_out[...] = jnp.where(keep, old - learn_rate * step, 0.0)
 
 
-def adam(kinds, grads, master, first_moment, second_moment, n_dp, n_seq, first_slots):
+def adam(kinds, grads, master, first_moment, second_moment, n_dp, n_seq, first_slots, begin, kept):
     rows, slots, width = master.shape
     wide = width // n_dp
     sub = rows // n_dp
-    rb = min(16, sub)
-    state = pl.BlockSpec((rb, slots, width), lambda i, k: (i, 0, 0))
-    cols = [pl.BlockSpec((n_dp, g.shape[1], rb, wide), lambda i, k: (0, 0, i, 0)) for g in grads]
-    rws = [
-        pl.BlockSpec(
-            (1, g.shape[1], n_dp, rb, wide),
-            lambda i, k: (i * rb // sub, 0, 0, i % (sub // rb), 0),
-        )
+    size = grads[0].shape[2] // n_dp
+    rb = min(16, size)
+    steps = size // rb
+    state = pl.BlockSpec(
+        (rb, slots, width), lambda d, i, k: (d * (sub // rb) + begin // rb + i, 0, 0)
+    )
+    cols = [
+        pl.BlockSpec((n_dp, g.shape[1], rb, wide), lambda d, i, k: (0, 0, d * steps + i, 0))
         for g in grads
     ]
+    rws = [
+        pl.BlockSpec((1, g.shape[1], n_dp, rb, wide), lambda d, i, k: (d, 0, 0, i, 0)) for g in grads
+    ]
     keep = jnp.broadcast_to((kinds != 2).astype(f32)[None, :, None], (1, slots, width))
+    first_kept = 1 + 2 * len(grads) + 4
     return pl.pallas_call(
-        functools.partial(adam_kernel, n_dp, n_seq // 2, first_slots, len(grads)),
+        functools.partial(adam_kernel, n_dp, n_seq // 2, first_slots, len(grads), len(kept)),
         out_shape=[jax.ShapeDtypeStruct(master.shape, f32)] * 4,
         grid_spec=pltpu.PrefetchScalarGridSpec(
             num_scalar_prefetch=1,
-            grid=(rows // rb,),
+            grid=(n_dp, steps),
             in_specs=cols
             + rws
             + [state] * 3
-            + [pl.BlockSpec((1, slots, width), lambda i, k: (0, 0, 0))],
+            + [pl.BlockSpec((1, slots, width), lambda d, i, k: (0, 0, 0))]
+            + [pl.BlockSpec(memory_space=pl.ANY)] * len(kept),
             out_specs=[state] * 4,
             scratch_shapes=[pltpu.VMEM((slots, rb, width), f32)],
         ),
+        input_output_aliases={first_kept + k: k for k in range(len(kept))},
         compiler_params=pltpu.CompilerParams(vmem_limit_bytes=50 << 20),
+        cost_estimate=pl.CostEstimate(
+            flops=0, bytes_accessed=int(150e6 * size / sub), transcendentals=0
+        ),
         name="adam",
     )(
         kinds,
         *grads,
-        *[g.reshape(n_dp, g.shape[1], n_dp, sub, wide) for g in grads],
+        *[g.reshape(n_dp, g.shape[1], n_dp, size, wide) for g in grads],
         master,
         first_moment,
         second_moment,
         keep,
+        *kept,
     )
 
 
@@ -294,7 +305,7 @@
                     leg(view, way, step, block, target).wait_send()
 
 
-def relay_sum(owns, sent, came, place, count, device_of, send_sem, recv_sem, ready):
+def relay_sum(owns, sent, came, place, count, device_of, send_sem, recv_sem, ready, between=None):
     views = range(len(owns))
 
     def spot(way, block, receiver):
@@ -337,6 +348,9 @@
                         sent[view][block] = owns[view](block).astype(sent[view].dtype)
 
                     leg(view, way, block, target, target).start()
+
+        if between:
+            between(step)
 
     ready(place)
     for way in range(2):
@@ -395,9 +409,11 @@
     ]
     for copy in own:
         copy.start()
-    spread_blocks(
+    pass_on, finish = spread_blocks(
         x_ref, out_ref, chips, chip, core, dp_index, sibling, send_sem, recv_sem, pass_sem, take_sem
     )
+    pass_on()
+    finish()
     for copy in along:
         copy.wait()
     for copy in own:
@@ -415,16 +431,22 @@
         copies[k].start()
     passed = [send(x_ref, mine, pass_sem.at[0], take_sem.at[0], sibling)]
     passed[0].start()
-    for k in range(1, chips):
-        copies[k].wait_recv()
-        block = out_ref.at[lax.rem(chip + chips - k, chips) * 2 + core]
-        onward = send(block, block, pass_sem.at[k], take_sem.at[k], sibling)
-        onward.start()
-        passed.append(onward)
-    for copy in copies.values():
-        copy.wait_send()
-    for onward in passed:
-        onward.wait()
+
+    def pass_on():
+        for k in range(1, chips):
+            copies[k].wait_recv()
+            block = out_ref.at[lax.rem(chip + chips - k, chips) * 2 + core]
+            onward = send(block, block, pass_sem.at[k], take_sem.at[k], sibling)
+            onward.start()
+            passed.append(onward)
+
+    def finish():
+        for copy in copies.values():
+            copy.wait_send()
+        for onward in passed:
+            onward.wait()
+
+    return pass_on, finish
 
 
 def front(packed, x, collective_id):
@@ -443,34 +465,6 @@
         cost_estimate=takes(90),
         name="front",
     )(packed, x)
-
-
-def gather_seq_kernel(x_ref, out_ref, own_sem, send_sem, recv_sem, pass_sem, take_sem):
-    n_seq, n_dp, seq_index, dp_index = places()
-    chips, chip, core = n_seq // 2, seq_index // 2, lax.rem(seq_index, 2)
-    chip_peers = [lax.rem(chip + k, chips) for k in range(chips)]
-    sibling = (dp_index, chip * 2 + 1 - core)
-    greet([(dp_index, p * 2 + core) for p in chip_peers[1:]] + [sibling])
-    own = pltpu.make_async_copy(x_ref, out_ref.at[seq_index], own_sem)
-    own.start()
-    spread_blocks(
-        x_ref, out_ref, chips, chip, core, dp_index, sibling, send_sem, recv_sem, pass_sem, take_sem
-    )
-    own.wait()
-
-
-def gather_seq(x, collective_id):
-    chips = lax.axis_size("seq") // 2
-    return pl.pallas_call(
-        gather_seq_kernel,
-        out_shape=jax.ShapeDtypeStruct((2 * chips,) + x.shape, x.dtype),
-        in_specs=[VMEM],
-        out_specs=ANY,
-        scratch_shapes=[DMA] + [DMA((chips,))] * 4,
-        compiler_params=comm_params(collective_id, 16),
-        cost_estimate=takes(28),
-        name="gather_seq",
-    )(x)
 
 
 def sum_seq_kernel(x_ref, out_ref, taken, sent, arrived, pass_sem, take_sem, send_sem, recv_sem):
@@ -692,173 +686,249 @@
     )(units.reshape(-1), ug, down, *attention).reshape(n_dp, slots, rows, wide)
 
 
-def grads_kernel(
-    up_ref, gate_ref, down_ref, x_ref, y_ref, ug_out, down_out, x_out, y_out, *refs
-):
-    half_came, full_sent, full_came, mine = refs[0:3], refs[3:6], refs[6:9], refs[9:12]
-    side_out, x_taken, y_taken, z_sent, z_came = refs[12:17]
-    ring_send, ring_recv, z_send, z_recv, x_pass, x_take, y_pass, y_take = refs[17:25]
-    side_send, side_recv, own_sem = refs[25:]
+def column_sum(ref, taken, sent, came, send_sem, recv_sem, pass_sem, take_sem, between):
+    n_seq, n_dp, seq_index, dp_index = places()
+    core = lax.rem(seq_index, 2)
+    sibling = (dp_index, seq_index + 1 - 2 * core)
+
+    def onward(block):
+        return send(
+            ref.at[1 - core, block], taken.at[block], pass_sem.at[block], take_sem.at[block], sibling
+        )
+
+    for block in [b for k in range(n_dp // 2) for b in (n_dp - 1 - k, k)]:
+        onward(block).start()
+    total = relay_sum(
+        [lambda block: ref[core, block].astype(f32) + taken[block].astype(f32)],
+        [sent],
+        [came],
+        dp_index,
+        n_dp,
+        lambda place: (place, seq_index),
+        send_sem,
+        recv_sem,
+        lambda block: onward(block).wait_recv(),
+        between,
+    )[0]
+    for block in range(n_dp):
+        onward(block).wait_send()
+    return total
+
+
+def grads_kernel(band, has_tokens, *refs):
     n_seq, n_dp, seq_index, dp_index = places()
     chips, chip, core = n_seq // 2, seq_index // 2, lax.rem(seq_index, 2)
     sibling = (dp_index, chip * 2 + 1 - core)
-    ring = Ring(chips, chip, core, dp_index, ring_send, ring_recv)
-    owns = [down_ref, up_ref, gate_ref]
-    blocks = down_ref.shape[0]
-    pair = blocks // 2
-    half = up_ref.shape[-1]
+    refs = list(refs)
+
+    def take(count):
+        taken, refs[:count] = refs[:count], []
+        return taken
+
+    owns = take(3) if band else None
+    (x_ref,) = take(1)
+    tokens_ref = take(1)[0] if has_tokens else None
+    outs = take(2) if band else None
+    (x_out,) = take(1)
+    tokens_out = take(1)[0] if has_tokens else None
+    x_taken, z_sent, z_came, z_send, z_recv, x_pass, x_take = take(7)
+    if has_tokens:
+        token_own, token_send, token_recv, token_pass, token_take = take(5)
     greet(
         [(lax.rem(dp_index + k, n_dp), seq_index) for k in range(1, n_dp)]
-        + [sibling, ring.device(0), ring.device(1)]
-    )
-
-    def leg(view, way, step):
-        if step == 0:
-            src = owns[view].at[pl.ds(way * pair, pair), ring.at(ring.last)]
-            return ring.leg(view, way, step, src, half_came[view].at[way])
-        src, dst = full_sent[view].at[step - 1, way], full_came[view].at[step - 1, way]
-        return ring.leg(view, way, step, src, dst)
-
-    def own_copy(view, way, step):
-        distance = ring.last - step
-        if step == ring.last:
+        + [(dp_index, lax.rem(chip + k, chips) * 2 + core) for k in range(1, chips)]
+        + [sibling]
+    )
+    if band:
+        half_came, full_sent, full_came, mine = take(3), take(3), take(3), take(3)
+        side_out, ring_send, ring_recv, side_send, side_recv, own_sem = take(6)
+        ug_out, down_out = outs
+        ring = Ring(chips, chip, core, dp_index, ring_send, ring_recv)
+        begin, size = band
+        blocks = down_out.shape[0]
+        pair = blocks // 2
+        half = ug_out.shape[2] // 2
+        last = ring.last
+
+        def own(view, place, way):
+            if view == 0:
+                units = pl.ds(0, blocks) if way is None else pl.ds(way * pair, pair)
+                return owns[0].at[units, place, pl.ds(begin, size), :]
+            columns = pl.ds(0, blocks * half) if way is None else pl.ds(way * pair * half, pair * half)
+            return owns[view].at[place, :, :, pl.ds(begin, size), columns]
+
+        def leg(view, way, step):
+            if step == 0:
+                src = own(view, ring.at(last), way)
+                return ring.leg(view, way, step, src, half_came[view].at[way])
+            src, dst = full_sent[view].at[step - 1, way], full_came[view].at[step - 1, way]
+            return ring.leg(view, way, step, src, dst)
+
+        def own_copy(view, way, step):
+            distance = last - step
+            if step == last:
+                return pltpu.make_async_copy(
+                    own(view, chip, None), mine[view], own_sem.at[view, 0, step - 1]
+                )
+            src = own(view, ring.at(distance if way == 0 else -distance), None)
             return pltpu.make_async_copy(
-                owns[view].at[:, chip], mine[view], own_sem.at[view, 0, step - 1]
+                src, full_sent[view].at[step - 1, way], own_sem.at[view, way, step - 1]
             )
-        src = owns[view].at[:, ring.at(distance if way == 0 else -distance)]
-        return pltpu.make_async_copy(
-            src, full_sent[view].at[step - 1, way], own_sem.at[view, way, step - 1]
-        )
-
-    for view in range(3):
-        for way in range(2):
-            leg(view, way, 0).start()
-    for step in range(1, ring.last + 1):
-        for view in range(3):
-            for way in range(2 if step < ring.last else 1):
-                own_copy(view, way, step).start()
-
-    def column_sum(ref, taken, out, pass_sem, take_sem, z):
-        def onward(block):
-            return send(
-                ref.at[1 - core, block], taken.at[block], pass_sem.at[block], take_sem.at[block], sibling
-            )
-
-        for block in [b for k in range(n_dp // 2) for b in (n_dp - 1 - k, k)]:
-            onward(block).start()
-        total = relay_sum(
-            [lambda block: ref[core, block].astype(f32) + taken[block].astype(f32)],
-            [z_sent.at[z]],
-            [z_came.at[z]],
-            dp_index,
-            n_dp,
-            lambda place: (place, seq_index),
-            z_send.at[z],
-            z_recv.at[z],
-            lambda block: onward(block).wait_recv(),
-        )[0]
-        out[...] = total
-        for block in range(n_dp):
-            onward(block).wait_send()
-
-    def ring_step(step):
+
         for view in range(3):
             for way in range(2):
-                own_copy(view, way, step).wait()
-                leg(view, way, step - 1).wait_recv()
-                for k in range(blocks) if step > 1 else range(way * pair, (way + 1) * pair):
-                    value = full_sent[view][step - 1, way, k].astype(f32)
+                leg(view, way, 0).start()
+        for step in range(1, last + 1):
+            for view in range(3):
+                for way in range(2 if step < last else 1):
+                    own_copy(view, way, step).start()
+
+        def ring_step(step):
+            for view in range(3):
+                for way in range(2):
+                    own_copy(view, way, step).wait()
+                    leg(view, way, step - 1).wait_recv()
+                    full = full_sent[view]
                     if step > 1:
-                        value = value + full_came[view][step - 2, way, k].astype(f32)
+                        value = full[step - 1, way].astype(f32)
+                        value = value + full_came[view][step - 2, way].astype(f32)
+                        full[step - 1, way] = value.astype(bf)
+                    elif view == 0:
+                        units = slice(way * pair, (way + 1) * pair)
+                        value = full[0, way, units].astype(f32) + half_came[0][way].astype(f32)
+                        full[0, way, units] = value.astype(bf)
                     else:
-                        value = value + half_came[view][way, k - way * pair].astype(f32)
-                    full_sent[view][step - 1, way, k] = value.astype(bf)
-                leg(view, way, step).start()
-
-    column_sum(x_ref, x_taken, x_out, x_pass, x_take, 0)
-    for step in range(1, ring.last):
-        ring_step(step)
-    column_sum(y_ref, y_taken, y_out, y_pass, y_take, 1)
+                        columns = slice(way * pair * half, (way + 1) * pair * half)
+                        value = full[0, way, :, :, :, columns].astype(f32)
+                        value = value + half_came[view][way].astype(f32)
+                        full[0, way, :, :, :, columns] = value.astype(bf)
+                    leg(view, way, step).start()
+
+    if has_tokens:
+        own_tokens = pltpu.make_async_copy(tokens_ref, tokens_out.at[seq_index], token_own)
+        own_tokens.start()
+        pass_on, finish = spread_blocks(
+            tokens_ref, tokens_out, chips, chip, core, dp_index, sibling,
+            token_send, token_recv, token_pass, token_take,
+        )
+
+    def between(step):
+        if step == 0:
+            if band:
+                for ring_at in range(1, last):
+                    ring_step(ring_at)
+            if has_tokens:
+                pass_on()
+
+    x_out[...] = column_sum(
+        x_ref, x_taken, z_sent, z_came, z_send, z_recv, x_pass, x_take, between
+    )
+    if has_tokens:
+        own_tokens.wait()
+        finish()
+    if not band:
+        return
     for view in range(3):
-        own_copy(view, 0, ring.last).wait()
+        own_copy(view, 0, last).wait()
         for way in range(2):
-            leg(view, way, ring.last - 1).wait_recv()
+            leg(view, way, last - 1).wait_recv()
+        if last > 1:
+            came = [full_came[view][last - 2, way].astype(f32) for way in range(2)]
+            value = mine[view][...].astype(f32) + came[0] + came[1]
+        else:
+            axis = 0 if view == 0 else 3
+            came = [half_came[view][way].astype(f32) for way in range(2)]
+            value = mine[view][...].astype(f32) + jnp.concatenate(came, axis=axis)
+        value = value.astype(bf)
+        if view == 0:
+            down_out[...] = value
+            continue
+        value = value.reshape(2, n_dp * size, blocks * half)
         for k in range(blocks):
-            if ring.last > 1:
-                came = full_came[view]
-                sums = [came[ring.last - 2, way, k].astype(f32) for way in range(2)]
-                value = mine[view][k].astype(f32) + sums[0] + sums[1]
-            else:
-                came = half_came[view][k // pair, k % pair].astype(f32)
-                value = mine[view][k].astype(f32) + came
-            value = value.astype(bf)
-            if view == 0:
-                down_out[k] = value
-            else:
-                unit = (view - 1) * blocks + k
-
-                @pl.when(core == 0)
-                def _():
-                    ug_out[unit, :, :half] = value[0]
-                    side_out[unit] = value[1]
-
-                @pl.when(core != 0)
-                def _():
-                    ug_out[unit, :, half:] = value[1]
-                    side_out[unit] = value[0]
+            unit = (view - 1) * blocks + k
+
+            @pl.when(core == 0)
+            def _():
+                ug_out[unit, :, :half] = value[0, :, k * half : (k + 1) * half]
+                side_out[unit] = value[1, :, k * half : (k + 1) * half]
+
+            @pl.when(core != 0)
+            def _():
+                ug_out[unit, :, half:] = value[1, :, k * half : (k + 1) * half]
+                side_out[unit] = value[0, :, k * half : (k + 1) * half]
 
     place = pl.ds(pl.multiple_of(core * half, half), half)
     side = send(side_out, ug_out.at[:, :, place], side_send, side_recv, sibling)
     side.start()
     side.wait()
-    for step in range(ring.last):
+    for step in range(last):
         for view in range(3):
             for way in range(2):
                 leg(view, way, step).wait_send()
 
 
-def sum_grads(up, gate, down, x, y, collective_id):
-    blocks, chips, _, rows, half = up.shape
-    _, _, sub, width = down.shape
-    _, n_dp, tokens, _ = x.shape
+def sum_grads(band, sums, x, tokens, collective_id):
+    _, n_dp, shard, width = x.shape
+    chips = lax.axis_size("seq") // 2
     steps = chips // 2
-    side = (2, rows, half)
     vmem = pltpu.VMEM
-    return pl.pallas_call(
-        grads_kernel,
-        out_shape=[
-            jax.ShapeDtypeStruct((2 * blocks, rows, 2 * half), bf),
-            jax.ShapeDtypeStruct((blocks, sub, width), bf),
-            jax.ShapeDtypeStruct((tokens, width), f32),
-            jax.ShapeDtypeStruct((tokens, width), f32),
-        ],
-        in_specs=[ANY] * 3 + [VMEM] * 2,
-        out_specs=[VMEM] * 4,
-        scratch_shapes=[vmem((2, blocks // 2) + s, bf) for s in ((sub, width), side, side)]
-        + [vmem((max(steps - 1, 1), 2, blocks) + s, bf) for s in ((sub, width), side, side)] * 2
-        + [vmem((blocks,) + s, bf) for s in ((sub, width), side, side)]
-        + [
-            vmem((2 * blocks, rows, half), bf),
-            vmem((n_dp, tokens, width), bf),
-            vmem((n_dp, tokens, width), bf),
-            vmem((2, n_dp, tokens, width), bf),
-            vmem((2, n_dp + 1, tokens, width), bf),
+    operands, in_specs, out_shape, out_specs = [], [], [], []
+    scratch = [
+        vmem((n_dp, shard, width), bf),
+        vmem((n_dp, shard, width), bf),
+        vmem((n_dp + 1, shard, width), bf),
+        DMA((1, 2, n_dp)),
+        DMA((1, 2, n_dp)),
+        DMA((n_dp,)),
+        DMA((n_dp,)),
+    ]
+    if tokens is not None:
+        scratch += [DMA] + [DMA((chips,))] * 4
+    if band:
+        size = band[1]
+        blocks = sums[0].shape[0]
+        wide = sums[1].shape[-1]
+        half = wide // blocks
+        operands += sums
+        in_specs += [ANY] * 3
+        out_shape += [
+            jax.ShapeDtypeStruct((2 * blocks, n_dp * size, 2 * half), bf),
+            jax.ShapeDtypeStruct((blocks, size, width), bf),
+        ]
+        out_specs += [VMEM] * 2
+        side = (2, n_dp, size)
+        fulls = [(blocks, size, width), side + (wide,), side + (wide,)]
+        halves = [(blocks // 2, size, width), side + (wide // 2,), side + (wide // 2,)]
+        scratch += [vmem((2,) + s, bf) for s in halves]
+        scratch += [vmem((max(steps - 1, 1), 2) + s, bf) for s in fulls] * 2
+        scratch += [vmem(s, bf) for s in fulls]
+        scratch += [
+            vmem((2 * blocks, n_dp * size, half), bf),
             DMA((3, 2, steps)),
             DMA((3, 2, steps)),
-            DMA((2, 1, 2, n_dp)),
-            DMA((2, 1, 2, n_dp)),
-            DMA((n_dp,)),
-            DMA((n_dp,)),
-            DMA((n_dp,)),
-            DMA((n_dp,)),
             DMA,
             DMA,
             DMA((3, 2, steps)),
-        ],
-        compiler_params=comm_params(collective_id, 58),
-        cost_estimate=takes(120),
+        ]
+    operands.append(x)
+    in_specs.append(VMEM)
+    out_shape.append(jax.ShapeDtypeStruct((shard, width), f32))
+    out_specs.append(VMEM)
+    if tokens is not None:
+        operands.append(tokens)
+        in_specs.append(VMEM)
+        out_shape.append(jax.ShapeDtypeStruct((2 * chips,) + tokens.shape, bf))
+        out_specs.append(ANY)
+    return pl.pallas_call(
+        functools.partial(grads_kernel, band, tokens is not None),
+        out_shape=out_shape,
+        in_specs=in_specs,
+        out_specs=out_specs,
+        scratch_shapes=scratch,
+        compiler_params=comm_params(collective_id, 56),
+        cost_estimate=takes(75),
         name="sum_grads",
-    )(up, gate, down, x, y)
+    )(*operands)
 
 
 def turn_half(values):
@@ -873,7 +943,9 @@
         late_ref, refs = refs[0], refs[1:]
     x1_ref, cos_ref, sin_ref, doc_row, doc_col, tokens_ref, cot_ref = refs[:7]
     qkv_all, out_all, query_out, key_out, value_out, mixed_out, stat_out, residual_out = refs[7:15]
-    ug_all, down_all, x_all, cot_all = refs[15:19]
+    up_all, gate_all, down_all, x_all, cot_all = refs[15:20]
+    ug_all = (up_all, gate_all)
+    refs = refs[1:]
     att_stage, out_stage, part, taken, sent, arrived, x_stage = refs[19:26]
     mine_stage, given_stage, down_stage = refs[26:29]
     (own_sem, a_send, a_recv, w_send, w_recv, s_pass, s_take, s_send, s_recv, cot_send, cot_recv,
@@ -1047,27 +1119,30 @@
     def ring_leg(c, view, way, step, arriving):
         distance = step if arriving else step - 1
         block = ring.at(-distance if way == 0 else distance)
-        begin = ff_blocks if view == 2 else 0
-        units = pl.ds(begin, ff_blocks)
-        if step == ring.last:
-            units = pl.ds(begin + way * pair, pair)
+        units = pl.ds(way * pair, pair) if step == ring.last else pl.ds(0, ff_blocks)
         if view == 0:
             ref = down_all.at[units, block, :, pl.ds(c * wide, wide)]
         else:
-            ref = ug_all.at[units, block, :, band(c)]
+            columns = pl.ds(0, ff_blocks * half)
+            if step == ring.last:
+                columns = pl.ds(way * pair * half, pair * half)
+            ref = ug_all[view - 1].at[block, :, band(c), columns]
         return send(
             ref, ref, ring_send.at[c, view, way, step - 1], ring_recv.at[c, view, way, step - 1],
             ring.device(way),
         )
 
-    def side_copy(c):
-        return send(
-            given_stage.at[c],
-            ug_all.at[:, chip, core, band(c)],
-            side_send.at[c],
-            side_recv.at[c],
-            sibling,
-        )
+    def side_copies(c):
+        return [
+            send(
+                given_stage.at[c, k],
+                ug_all[k].at[chip, core, band(c)],
+                side_send.at[c, k],
+                side_recv.at[c, k],
+                sibling,
+            )
+            for k in range(2)
+        ]
 
     def begin_band(c):
         if has_late:
@@ -1086,30 +1161,39 @@
                 value = jnp.where(use_late, other, value)
             if u < 2 * ff_blocks:
                 left, right = value[:, :half], value[:, half:]
+                k, j = u // ff_blocks, u % ff_blocks
+                columns = slice(j * half, (j + 1) * half)
 
                 @pl.when(core == 0)
                 def _():
-                    mine_stage[c, u] = left
-                    given_stage[c, u] = right
+                    mine_stage[c, k, :, columns] = left
+                    given_stage[c, k, :, columns] = right
 
                 @pl.when(core != 0)
                 def _():
-                    mine_stage[c, u] = right
-                    given_stage[c, u] = left
+                    mine_stage[c, k, :, columns] = right
+                    given_stage[c, k, :, columns] = left
             else:
                 down_stage[c, u - 2 * ff_blocks] = value
-        side_copy(c).start()
+        for copy in side_copies(c):
+            copy.start()
         local = [
-            pltpu.make_async_copy(mine_stage.at[c], ug_all.at[:, chip, core, band(c)], stage_own.at[c, 0]),
             pltpu.make_async_copy(
-                down_stage.at[c], down_all.at[:, chip, :, pl.ds(c * wide, wide)], stage_own.at[c, 1]
-            ),
+                mine_stage.at[c, k], ug_all[k].at[chip, core, band(c)], stage_own.at[c, k]
+            )
+            for k in range(2)
         ]
+        local.append(
+            pltpu.make_async_copy(
+                down_stage.at[c], down_all.at[:, chip, :, pl.ds(c * wide, wide)], stage_own.at[c, 2]
+            )
+        )
         for copy in local:
             copy.start()
         for copy in local:
             copy.wait()
-        side_copy(c).wait_recv()
+        for copy in side_copies(c):
+            copy.wait_recv()
         for view in range(3):
             for way in range(2):
                 ring_leg(c, view, way, 1, False).start()
@@ -1163,7 +1247,8 @@
                 ring_leg(c, view, way, ring.last, True).wait_recv()
                 for step in range(1, ring.last + 1):
                     ring_leg(c, view, way, step, False).wait_send()
-        side_copy(c).wait_send()
+        for copy in side_copies(c):
+            copy.wait_send()
         if has_late:
             if c == n_dp - 1:
                 for copy in late_copies(c):
@@ -1210,7 +1295,8 @@
             low(seq_len, head_cols),
             jax.ShapeDtypeStruct((seq_len, head_cols), f32),
             jax.ShapeDtypeStruct((shard, width), f32),
-            low(2 * ff_blocks, chips, 2, rows, half),
+            low(chips, 2, rows, ff_blocks * half),
+            low(chips, 2, rows, ff_blocks * half),
             low(ff_blocks, chips, sub, width),
             low(2, n_dp, shard, width),
             low(2, n_dp, shard, width),
@@ -1218,7 +1304,7 @@
         in_specs=[pl.BlockSpec(memory_space=pltpu.SMEM), VMEM]
         + [ANY] * has_late
         + [VMEM] * 7,
-        out_specs=[VMEM] * 8 + [ANY] * 4,
+        out_specs=[VMEM] * 8 + [ANY] * 5,
         scratch_shapes=[
             vmem((n_seq, sub, 3 * head_cols), bf),
             vmem((sub, width), bf),
@@ -1227,8 +1313,8 @@
             blocks,
             blocks,
             vmem((shard, width), bf),
-            vmem((n_dp, 2 * ff_blocks, sub, half), bf),
-            vmem((n_dp, 2 * ff_blocks, sub, half), bf),
+            vmem((n_dp, 2, sub, ff_blocks * half), bf),
+            vmem((n_dp, 2, sub, ff_blocks * half), bf),
             vmem((n_dp, ff_blocks, sub, wide), bf),
             DMA((4,)),
             DMA((n_seq,)),
@@ -1244,9 +1330,9 @@
             DMA((n_dp, n_dp)),
             DMA((n_dp, n_dp)),
             DMA((n_dp,)),
+            DMA((n_dp, 3)),
             DMA((n_dp, 2)),
-            DMA((n_dp,)),
-            DMA((n_dp,)),
+            DMA((n_dp, 2)),
             DMA((n_dp, 3, 2, steps)),
             DMA((n_dp, 3, 2, steps)),
             DMA((1, 2, n_dp)),
@@ -1334,7 +1420,8 @@
         attended_low,
         log_total,
         residual,
-        ug_weight,
+        up_weight,
+        gate_weight,
         down_weight,
         normed_two_all,
         upstream_all,
@@ -1359,54 +1446,65 @@
     cosine = cosine[:, None, :]
     sine = sine[:, None, :]
     normed_two, inv_two = norm_parts(residual)
-    up_weight = ug_weight[:ff_blocks].reshape(ff_blocks, width, half)
-    gate_weight = ug_weight[ff_blocks:].reshape(ff_blocks, width, half)
-    down_weight = down_weight.reshape(ff_blocks, half, width)
+    columns = ff_blocks * half
+    up_weight = up_weight.reshape(width, columns)
+    gate_weight = gate_weight.reshape(width, columns)
+    down_weight = down_weight.reshape(columns, width)
     normed_two_all = normed_two_all.reshape(-1, width)
     upstream_all = upstream_all.reshape(-1, width)
-    up_proj = jnp.einsum("tr,jrc->tjc", normed_two_all, up_weight, preferred_element_type=f32)
-    gate_proj = jnp.einsum("tr,jrc->tjc", normed_two_all, gate_weight, preferred_element_type=f32)
+
+    def times(left, right, left_axis, right_axis):
+        return lax.dot_general(
+            left, right, (((left_axis,), (right_axis,)), ((), ())), preferred_element_type=f32
+        )
+
+    up_proj = times(normed_two_all, up_weight, 1, 0)
+    gate_proj = times(normed_two_all, gate_weight, 1, 0)
     gate_sig = jax.nn.sigmoid(gate_proj)
     silu_value = gate_proj * gate_sig
     hidden_low = (silu_value * up_proj).astype(bf)
-    ff_part = jnp.einsum("tjh,jhc->tc", hidden_low, down_weight, preferred_element_type=f32)
-    hidden_grad = jnp.einsum("tc,jhc->tjh", upstream_all, down_weight, preferred_element_type=f32)
+    hidden_grad = times(upstream_all, down_weight, 1, 1)
     up_grad_low = (hidden_grad * silu_value).astype(bf)
     gate_grad_low = (
         hidden_grad * up_proj * (gate_sig + gate_proj * gate_sig * (1.0 - gate_sig))
     ).astype(bf)
-
-    down_grad = jnp.einsum(
-        "tjh,tc->jhc", hidden_low, upstream_all, preferred_element_type=f32
-    ).astype(bf)
-    up_grad = jnp.einsum(
-        "tr,tjc->jrc", normed_two_all, up_grad_low, preferred_element_type=f32
-    ).astype(bf)
-    gate_grad = jnp.einsum(
-        "tr,tjc->jrc", normed_two_all, gate_grad_low, preferred_element_type=f32
-    ).astype(bf)
-    norm_two_grad = jnp.einsum("tjc,jrc->tr", up_grad_low, up_weight, preferred_element_type=f32)
-    norm_two_grad = norm_two_grad + jnp.einsum(
-        "tjc,jrc->tr", gate_grad_low, gate_weight, preferred_element_type=f32
-    )
-    side = (ff_blocks, chips, 2, rows, half)
+    norm_two_grad = times(up_grad_low, up_weight, 1, 1) + times(gate_grad_low, gate_weight, 1, 1)
+    side = (chips, 2, n_dp, sub, columns)
+    sums = [
+        times(hidden_low, upstream_all, 0, 0).astype(bf).reshape(ff_blocks, chips, sub, width),
+        times(normed_two_all, up_grad_low, 0, 0).astype(bf).reshape(side),
+        times(normed_two_all, gate_grad_low, 0, 0).astype(bf).reshape(side),
+    ]
+    ff_part = times(hidden_low, down_weight, 1, 0)
     column = (2, n_dp, shard_len, width)
-    ug_piece, down_piece, norm_two_grad, ff_out = sum_grads(
-        up_grad.reshape(side),
-        gate_grad.reshape(side),
-        down_grad.reshape(ff_blocks, chips, sub, width),
-        norm_two_grad.astype(bf).reshape(column),
+    bands = [(0, sub // 2), (sub // 2, sub // 2)] if sub % 32 == 0 else [(0, sub)]
+    *pieces, norm_two_grad = sum_grads(
+        bands[0], sums, norm_two_grad.astype(bf).reshape(column), None, 5
+    )
+    pieces = [pieces]
+    residual_grad = upstream.astype(f32) + norm_back(normed_two, inv_two, norm_two_grad)
+    late_grads = []
+    if late_slots:
+        send_now = arrange(slot_unit[:, first_slots:], *pieces[0], ())
+        send_now, residual_grad = lax.optimization_barrier((send_now, residual_grad))
+        late_grads.append(lax.all_to_all(send_now, "dp", 0, 0))
+    *second, ff_out, residual_grad_all = sum_grads(
+        bands[1] if len(bands) > 1 else None,
+        sums,
         ff_part.astype(bf).reshape(column),
-        5,
-    )
+        residual_grad.astype(bf),
+        7,
+    )
+    residual_grad_all = residual_grad_all.reshape(seq_len, width)
     block_output = (residual + ff_out).astype(bf).reshape(block_input.shape)
-    grads = []
-    if per_owner > first_slots:
-        late = arrange(slot_unit[:, first_slots:], ug_piece, down_piece, ())
-        grads.append(lax.all_to_all(late, "dp", 0, 0))
-    residual_grad = upstream.astype(f32) + norm_back(normed_two, inv_two, norm_two_grad)
-    residual_grad_all = gather_seq(residual_grad.astype(bf), 7).reshape(seq_len, width)
-
+    if second:
+        pieces.append(second)
+        if late_slots:
+            send_now = arrange(slot_unit[:, first_slots:], *second, ())
+            send_now, residual_grad_all, late_grads[0] = lax.optimization_barrier(
+                (send_now, residual_grad_all, late_grads[0])
+            )
+            late_grads.append(lax.all_to_all(send_now, "dp", 0, 0))
     attended_grad = jnp.einsum(
         "tc,rc->tr", residual_grad_all, out_weight, preferred_element_type=f32
     )
@@ -1433,10 +1531,6 @@
     qkv_grad_low = qkv_grad.astype(bf).reshape(seq_len, 3 * head_cols)
     norm_one_part = jnp.einsum("tf,rf->tr", qkv_grad_low, qkv_weight, preferred_element_type=f32)
     norm_one_grad = sum_seq(norm_one_part.astype(bf).reshape(n_seq, shard_len, width), 3)
-    input_grad = (residual_grad + norm_back(normed_one, inv_one, norm_one_grad)).reshape(
-        block_input.shape
-    )
-
     qkv_wgrad = jnp.einsum(
         "tr,tf->rf", normed_one_all, qkv_grad_low, preferred_element_type=f32
     ).astype(bf)
@@ -1446,11 +1540,35 @@
     qkv_piece, out_piece = collect_attention(
         qkv_wgrad.reshape(n_seq, n_dp, sub, 3 * head_cols), out_wgrad.reshape(n_dp, sub, width), 6
     )
-    early = arrange(slot_unit[:, :first_slots], ug_piece, down_piece, (qkv_piece, out_piece))
-    grads.insert(0, lax.all_to_all(early, "dp", 0, 0))
     kinds = jnp.where(own_units < 0, 2, is_col.astype(jnp.int32)).astype(jnp.int32)
-    owned_grads, new_first, new_second, new_master = adam(
-        kinds, grads, master, first_moment, second_moment, n_dp, n_seq, first_slots
+    kept = ()
+    came = None
+    for k, (begin, size) in enumerate(bands):
+        rows_now = slice(begin, begin + size)
+        attention = (qkv_piece[:, rows_now], out_piece[rows_now])
+        send_now = arrange(slot_unit[:, :first_slots], *pieces[k], attention)
+        if came is not None:
+            send_now, came, norm_one_grad = lax.optimization_barrier(
+                (send_now, came, norm_one_grad)
+            )
+        elif late_grads:
+            send_now, late_grads[-1] = lax.optimization_barrier((send_now, late_grads[-1]))
+        came = lax.all_to_all(send_now, "dp", 0, 0)
+        kept = adam(
+            kinds,
+            [came] + late_grads[k : k + 1],
+            master,
+            first_moment,
+            second_moment,
+            n_dp,
+            n_seq,
+            first_slots,
+            begin,
+            kept,
+        )
+    owned_grads, new_first, new_second, new_master = kept
+    input_grad = (residual_grad + norm_back(normed_one, inv_one, norm_one_grad)).reshape(
+        block_input.shape
     )
     return (block_output, input_grad, owned_grads, new_first, new_second, new_master)
 

time: 978 us -> 965 us (0.987)
  waiting for transfers between devices: 57.4 us -> 26.9 us
  local copies, waits for them, and re-layouts: 43.3 us -> 28.5 us
  Pallas kernels: 700 us -> 711 us
  matrix products: 124 us -> 134 us
    all_to_all x2 -> x4, waiting for transfers between devices: 56.8 us -> 26.2 us  [the longest x2 26.2 us: local(): came = lax.all_to_all(send_now, 'dp', 0, 0)]
    convert_element_type x2 -> x0, local copies, waits for them, and re-layouts: 12.5 us -> none  [the longest x1 6.33 us: local(): gate_grad = jnp.einsum('tr,tjc->jrc', normed_two_all, gate_grad_low, pref...]
    pallas_call x2 -> x4, Pallas kernels: 2.45 us -> 14.4 us  [arrange(): pl.pallas_call(functools.partial(arrange_kernel, ff_blocks), out_shape=ja...]
    unnamed x89 -> x103, local copies, waits for them, and re-layouts: 20.4 us -> 17.1 us
    pallas_call x1 -> x2, Pallas kernels: 53 us -> 52 us  [adam(): pl.pallas_call(functools.partial(adam_kernel, n_dp, n_seq // 2, first_slo...]
  transfers between devices with their start and end apart: 3 -> 5, of which waited for: 1 -> 2; matrix products, arithmetic and copies ran while one was open for 8% -> 11% of each run, Pallas kernels for 26% -> 36%
where the time goes in v6:
time: 965 us; the launch traced here: 956 us
  Pallas kernels  711 us (74%)
  matrix products  134 us (14%)
  local copies, waits for them, and re-layouts  28.5 us (3%)
  waiting for transfers between devices  26.9 us (3%)
  other arithmetic  24 us (2%)
  starting transfers between devices  16.9 us (2%)
  between operations  14.9 us (2%)
    pallas_call x1, Pallas kernels, forward(): pl.pallas_call(functools.partial(forward_kernel, has_late, first_slots, f...  274 us
    pallas_call x2, Pallas kernels, sum_grads(): pl.pallas_call(functools.partial(grads_kernel, band, tokens is not None),...  148 us
    pallas_call x1, Pallas kernels, front(): pl.pallas_call(front_kernel, out_shape=[jax.ShapeDtypeStruct(packed.shape...  95 us
    pallas_call x1, Pallas kernels, collect_attention(): pl.pallas_call(collect_kernel, out_shape=[jax.ShapeDtypeStruct((n_seq,) +...  82.2 us
    dot_general x9, matrix products, times(): lax.dot_general(left, right, (((left_axis,), (right_axis,)), ((), ())), p...  72.8 us
    pallas_call x2, Pallas kernels, adam(): pl.pallas_call(functools.partial(adam_kernel, n_dp, n_seq // 2, first_slo...  52 us
    pallas_call x1, Pallas kernels, sum_seq(): pl.pallas_call(sum_seq_kernel, out_shape=jax.ShapeDtypeStruct((rows, colu...  29.4 us
    all_to_all x2, waiting for transfers between devices, local(): came = lax.all_to_all(send_now, 'dp', 0, 0)  26.2 us
  transfers between devices with their start and end apart: 5, of which 2 were waited for; matrix products, arithmetic and copies ran while one was open for 11% of the time, Pallas kernels for 36%

profile of v6, /device:TPU:0, one launch (start us, length us, event | category | flops | bytes accessed | tf_op | source)
XLA Modules:
  0.0 956.1 jit_solution(14687222907641922515)
XLA Ops:
  11.8 15.9 %pack.1 = (bf16[4,4,256,512]{3,2,1,0:T(8,128)(2,1)}, bf16[4,4,256,512]{3,2,1,0:T(8,128)(2,1)}) custom-call(s32[8]{0:T(128)S(1)} %fusion.54.flags, f32[256,8,2048]{2,1,0:T(8,128)} %refs_4_.3), custom_call_target="tpu_custom_call" | custom-call | tf_op jit(solution)/shard_map/pack/pallas_call | solution.py:113
  30.8 95.0 %front.1 = (bf16[4,4,256,512]{3,2,1,0:T(8,128)(2,1)S(1)}, bf16[8,128,2048]{2,1,0:T(8,128)(2,1)S(1)}) custom-call(bf16[4,4,256,512]{3,2,1,0:T(8,128)(2,1)S(1)} %copy-done.4, bf16[128,2048]{1,0:T(8,128)(2,1)S(1)} %fusion.46.x_ref), custom_call_target="tpu_custom_call" | custom-call | bytes 270000000 | tf_op jit(solution)/shard_map/front/pallas_call | solution.py:455
  134.8 273.7 %forward.1 = (bf16[8,4,64,768]{3,2,1,0:T(8,128)(2,1)}, bf16[4,64,2048]{2,1,0:T(8,128)(2,1)}, bf16[1024,256]{1,0:T(8,128)(2,1)}, bf16[1024,256]{1,0:T(8,128)(2,1)...) custom-call(s32[40]{0:T(128)} %pad_add_fusion.refs_0_, ...), custom_call_target="tpu_custom_call" | custom-call | bytes 690000000 | tf_op jit(solution)/shard_map/forward/pallas_call | solution.py:1287
  408.5 10.1 %fusion.76 = f32[1024,1024]{1,0:T(8,128)} fusion(bf16[1024,2048]{1,0:T(8,128)(2,1)} %bitcast.153, bf16[2048,1024]{1,0:T(8,128)(2,1)} %bitcast.151), kind=kOutput, calls=%fused_computation.113 | convolution fusion | flops 4294967296 | bytes 12582912 | tf_op jit(solution)/shard_map/dot_general | solution.py:1457
  418.7 6.0 fusion.77
  424.7 10.3 %multiply_convert_fusion.1 = (bf16[1024,1024]{1,0:T(8,128)(2,1)}, bf16[1024,1024]{1,0:T(8,128)(2,1)}, bf16[1024,1024]{1,0:T(8,128)(2,1)}) fusion(f32[1024,1024]{1,0:T(8,128)} %fusion.77, f32[1024,1024]{1,0:T(8,128)} %fusion.76, bf16[1024,2048]{1,0:T(8,128)(2,1)S(1)} %bitcast.158, bf16[1024,2048]{1,0:T(8,128)(2,1)S(1)} %bitcast.148), kind=kOutput, calls=%fused_computation.16 | convolution fusion | flops 4309647360 | bytes 23068672 | tf_op jit(solution)/shard_map/dot_general | solution.py:1457
  435.0 7.9 convolution_convert_fusion.3
  443.0 7.2 fusion.78
  450.6 9.6 convolution_convert_fusion.4
  460.2 6.3 convolution_convert_fusion.2
  466.5 6.1 add_convert_fusion
  472.6 60.7 %sum_grads.2 = (bf16[8,128,512]{2,1,0:T(8,128)(2,1)}, bf16[4,32,2048]{2,1,0:T(8,128)(2,1)}, f32[128,2048]{1,0:T(8,128)}) custom-call(bf16[4,4,64,2048]{3,2,1,0:T(8,128)(2,1)} %bitcast.126, bf16[4,2,4,64,1024]{4,3,2,1,0:T(8,128)(2,1)} %bitcast.124, bf16[4,2,4,64,1024]{4,3,2,1,0:T(8,128)(2,1)} %bitcast.128, bf16[2,4,128,2048]{3,2,1,0:T(8,128)(2,1)} %bitcast.132), custom_call_target="tpu_custom_call" | custom-call | bytes 225000000 | tf_op jit(solution)/shard_map/sum_grads/pallas_call | solution.py:922
  537.7 5.9 arrange.4
  561.2 9.3 convolution_convert_fusion.1
  570.6 87.5 %sum_grads.3 = (bf16[8,128,512]{2,1,0:T(8,128)(2,1)}, bf16[4,32,2048]{2,1,0:T(8,128)(2,1)}, f32[128,2048]{1,0:T(8,128)}, bf16[8,128,2048]{2,1,0:T(8,128)(2,1)}) custom-call(bf16[4,4,64,2048]{3,2,1,0:T(8,128)(2,1)} %bitcast.127, bf16[4,2,4,64,1024]{4,3,2,1,0:T(8,128)(2,1)} %bitcast.125, bf16[4,2,4,64,1024]{4,3,2,1,0:T(8,128)(2,1)} %bitcast.129, ...), custom_call_target="tpu_custom_call" | custom-call | bytes 225000000 | tf_op jit(solution)/shard_map/sum_grads/pallas_call | solution.py:922
  684.3 14.6 %fusion.35 = f32[1024,2,128]{0,2,1:T(8,128)} fusion(bf16[1024,2,128]{0,2,1:T(8,128)(2,1)S(1)} %bitcast.136, f32[2,1024,1024]{1,2,0:T(8,128)} %fusion.50, f32[2,1024,1024]{1,2,0:T(8,128)} %fusion.79, f32[2,1024]{1,0:T(2,128)S(1)} %bitcast.143, pred[1024,1024]{0,1:T(8,128)(4,1)} %fusion.25), kind=kOutput, calls=%fused_computation.35 | convolution fusion | flops 559942656 | bytes 19406848 | tf_op jit(solution)/shard_map/hqk,qhd->khd/dot_general | solution.py:1522
  698.9 16.4 %broadcast_multiply_fusion.1 = (f32[1024,2,128]{0,2,1:T(8,128)}, f32[1024,2,128]{0,2,1:T(8,128)}, f32[1024,2,128]{0,2,1:T(8,128)}) fusion(f32[1024,128]{0,1:T(8,128)S(1)} %copy-done.31, f32[1024,2,128]{0,2,1:T(8,128)} %fusion.35, bf16[1024,2,128]{0,2,1:T(8,128)(2,1)S(1)} %bitcast.134, f32[2,1024,1024]{1,2,0:T(8,128)} %fusion.50, ...), kind=kOutput, calls=%fused_computation.67 | convolution fusion | flops 560466944 | bytes 23076864 | tf_op jit(solution)/shard_map/hqk,khd->qhd/dot_general | solution.py:1521
  718.8 6.1 fusion.41
  731.8 82.2 %collect_attention.1 = (bf16[8,64,768]{2,1,0:T(8,128)(2,1)S(1)}, bf16[64,2048]{1,0:T(8,128)(2,1)S(1)}) custom-call(bf16[8,4,64,768]{3,2,1,0:T(8,128)(2,1)S(1)} %bitcast.122, bf16[4,64,2048]{2,1,0:T(8,128)(2,1)S(1)} %bitcast.123), custom_call_target="tpu_custom_call" | custom-call | bytes 225000000 | tf_op jit(solution)/shard_map/collect_attention/pallas_call | solution.py:563
  827.0 29.4 %sum_seq.1 = f32[128,2048]{1,0:T(8,128)S(1)} custom-call(bf16[8,128,2048]{2,1,0:T(8,128)(2,1)S(1)} %bitcast.118), custom_call_target="tpu_custom_call" | custom-call | bytes 84000000 | tf_op jit(solution)/shard_map/sum_seq/pallas_call | solution.py:506
  859.2 10.7 %all-to-all-done.2.refs_0_ = bf16[4,4,128,512]{3,2,1,0:T(8,128)(2,1)S(1)} async-done(((bf16[4,4,128,512]{3,2,1,0:T(8,128)(2,1)}), bf16[4,4,128,512]{3,2,1,0:T(8,128)(2,1)S(1)}, u32[]{:S(2)}, u32[]{:S(2)}) %all-to-all-start.2) | async-done | bytes 2097184 | tf_op jit(solution)/shard_map/all_to_all | solution.py:1556
  879.8 26.0 %adam.2 = (f32[256,8,2048]{2,1,0:T(8,128)}, f32[256,8,2048]{2,1,0:T(8,128)}, f32[256,8,2048]{2,1,0:T(8,128)}, f32[256,8,2048]{2,1,0:T(8,128)}) custom-call(s32[8]{0:T(128)S(1)} %get-tuple-element.97.kinds, bf16[4,4,128,512]{3,2,1,0:T(8,128)(2,1)S(1)} %copy-done.1, bf16[4,4,128,512]{3,2,1,0:T(8,128)(2,1)} %all-to-all-done.refs_1_, ...), custom_call_target="tpu_custom_call" | custom-call | bytes 75000000 | tf_op jit(solution)/shard_map/adam/pallas_call | solution.py:195
  907.6 15.4 %all-to-all-done.3.refs_0_ = bf16[4,4,128,512]{3,2,1,0:T(8,128)(2,1)S(1)} async-done(((bf16[4,4,128,512]{3,2,1,0:T(8,128)(2,1)}), bf16[4,4,128,512]{3,2,1,0:T(8,128)(2,1)S(1)}, u32[]{:S(2)}, u32[]{:S(2)}) %all-to-all-start.3) | async-done | bytes 2097184 | tf_op jit(solution)/shard_map/all_to_all | solution.py:1556
  923.0 26.0 %adam.3 = (f32[256,8,2048]{2,1,0:T(8,128)}, f32[256,8,2048]{2,1,0:T(8,128)}, f32[256,8,2048]{2,1,0:T(8,128)}, f32[256,8,2048]{2,1,0:T(8,128)}) custom-call(s32[8]{0:T(128)S(1)} %get-tuple-element.97.kinds, bf16[4,4,128,512]{3,2,1,0:T(8,128)(2,1)S(1)} %all-to-all-done.3.refs_0_, ...), custom_call_target="tpu_custom_call", output_to_operand_aliasing={{0}: (9, {}), {1}: (10, {}), {2}: (11, {}), {3}: (12, {})} | custom-call | bytes 75000000 | tf_op jit(solution)/shard_map/adam/pallas_call | solution.py:195
  (176 shorter events, 102.8 us)
Async XLA Ops:
  7.2 127.6 %all-gather.2.cloned.1.call-start = ((), (), s32[]{:S(2)}) async-start(), calls=%async_computation.4 | async-start | bytes 2621440 | tf_op jit(solution)/shard_map/all_gather | solution.py:1401
  9.7 18.1 %copy-start.34 = (s32[4,8]{1,0:T(4,128)}, s32[4,8]{1,0:T(4,128)S(1)}, u32[]{:S(2)}) copy-start(s32[4,8]{1,0:T(4,128)S(1)} %sub.71) | copy-start | bytes 388
  10.8 17.0 %copy-start.32 = (s32[1024]{0:T(1024)}, s32[1024]{0:T(1024)S(1)}, u32[]{:S(2)}) copy-start(s32[1024]{0:T(1024)S(1)} %convert_reduce_fusion.1) | copy-start | bytes 12292
  11.8 15.9 %copy-start.16 = (bf16[1,128,2048]{2,1,0:T(8,128)(2,1)S(1)}, bf16[1,128,2048]{2,1,0:T(8,128)(2,1)}, u32[]{:S(2)}) copy-start(bf16[1,128,2048]{2,1,0:T(8,128)(2,1)} %param.7) | copy-start | bytes 1572868
  27.9 102.6 %copy-start.35 = (f32[128]{0:T(128)}, f32[128]{0:T(128)S(1)}, u32[]{:S(2)}) copy-start(f32[128]{0:T(128)S(1)} %broadcast_multiply_fusion.7) | copy-start | bytes 1540
  28.3 105.4 %copy-start.37 = (f32[128]{0:T(128)}, f32[128]{0:T(128)S(1)}, u32[]{:S(2)}) copy-start(f32[128]{0:T(128)S(1)} %add_rsqrt_fusion.1) | copy-start | bytes 1540
  450.6 15.9 %slice-start = ((s8[8388608]{0:T(1024)(128)(4,1)}), s8[4194304]{0:T(1024)(128)(4,1)S(1)}, s32[]{:S(2)}) async-start(s8[8388608]{0:T(1024)(128)(4,1)} %bitcast.164), calls=%async_computation.5 | async-start | bytes 8388608
  472.6 62.4 %copy-start.21 = (bf16[1,128,2048]{2,1,0:T(8,128)(2,1)S(1)}, bf16[1,128,2048]{2,1,0:T(8,128)(2,1)}, u32[]{:S(2)}) copy-start(bf16[1,128,2048]{2,1,0:T(8,128)(2,1)} %param.8) | copy-start | bytes 1572868
  537.6 12.6 %copy-start.20 = (f32[1024,128]{1,0:T(8,128)S(1)}, f32[1024,128]{1,0:T(8,128)}, u32[]{:S(2)}) copy-start(f32[1024,128]{1,0:T(8,128)} %get-tuple-element.123.refs_5_) | copy-start | bytes 1572868
  537.7 13.6 %copy-start.33 = (s32[1024]{0:T(1024)S(1)}, s32[1024]{0:T(1024)}, u32[]{:S(2)}) copy-start(s32[1024]{0:T(1024)} %copy-done.32) | copy-start | bytes 12292
  543.5 127.4 %all-to-all-start = ((bf16[4,4,128,512]{3,2,1,0:T(8,128)(2,1)}), bf16[4,4,128,512]{3,2,1,0:T(8,128)(2,1)}, u32[]{:S(2)}, u32[]{:S(2)}) async-start(bf16[4,4,128,512]{3,2,1,0:T(8,128)(2,1)} %bitcast.18), calls=%async_computation | async-start | bytes 4194304 | tf_op jit(solution)/shard_map/all_to_all | solution.py:1490
  548.1 12.3 %copy-start.18 = (f32[128,2048]{1,0:T(8,128)S(1)}, f32[128,2048]{1,0:T(8,128)}, u32[]{:S(2)}) copy-start(f32[128,2048]{1,0:T(8,128)} %convert_add_fusion) | copy-start | bytes 3145732
  570.6 95.7 %copy-start.22 = (bf16[1024,256]{0,1:T(8,128)(2,1)S(1)}, bf16[1024,256]{0,1:T(8,128)(2,1)}, u32[]{:S(2)}) copy-start(bf16[1024,256]{0,1:T(8,128)(2,1)} %copy.74) | copy-start | bytes 1572868
  670.9 146.5 %all-to-all-start.1 = ((bf16[4,4,128,512]{3,2,1,0:T(8,128)(2,1)}), bf16[4,4,128,512]{3,2,1,0:T(8,128)(2,1)}, u32[]{:S(2)}, u32[]{:S(2)}) async-start(bf16[4,4,128,512]{3,2,1,0:T(8,128)(2,1)} %bitcast.23), calls=%async_computation.1 | async-start | bytes 4194304 | tf_op jit(solution)/shard_map/all_to_all | solution.py:1507
  684.3 14.6 %copy-start.31 = (f32[1024,128]{0,1:T(8,128)S(1)}, f32[1024,128]{0,1:T(8,128)}, u32[]{:S(2)}) copy-start(f32[1024,128]{0,1:T(8,128)} %copy.64) | copy-start | bytes 1572868
  817.5 52.4 %all-to-all-start.2 = ((bf16[4,4,128,512]{3,2,1,0:T(8,128)(2,1)}), bf16[4,4,128,512]{3,2,1,0:T(8,128)(2,1)S(1)}, u32[]{:S(2)}, u32[]{:S(2)}) async-start(bf16[4,4,128,512]{3,2,1,0:T(8,128)(2,1)} %bitcast.117), calls=%async_computation.2 | async-start | bytes 4194304 | tf_op jit(solution)/shard_map/all_to_all | solution.py:1556
  826.9 29.5 %copy-start.7 = (bf16[8,128,512]{2,1,0:T(8,128)(2,1)S(1)}, bf16[8,128,512]{2,1,0:T(8,128)(2,1)}, u32[]{:S(2)}) copy-start(bf16[8,128,512]{2,1,0:T(8,128)(2,1)} %get-tuple-element.64.ug_ref) | copy-start | bytes 3145732
  826.9 29.5 %copy-start.13 = (bf16[4,32,2048]{2,1,0:T(8,128)(2,1)S(1)}, bf16[4,32,2048]{2,1,0:T(8,128)(2,1)}, u32[]{:S(2)}) copy-start(bf16[4,32,2048]{2,1,0:T(8,128)(2,1)} %get-tuple-element.65.down_ref) | copy-start | bytes 1572868
  827.0 29.5 %copy-start.14 = (bf16[32,2048]{1,0:T(8,128)(2,1)S(1)}, bf16[32,2048]{1,0:T(8,128)(2,1)}, u32[]{:S(2)}) copy-start(bf16[32,2048]{1,0:T(8,128)(2,1)} %get-tuple-element.112.refs_1_) | copy-start | bytes 393220
  871.2 51.8 %all-to-all-start.3 = ((bf16[4,4,128,512]{3,2,1,0:T(8,128)(2,1)}), bf16[4,4,128,512]{3,2,1,0:T(8,128)(2,1)S(1)}, u32[]{:S(2)}, u32[]{:S(2)}) async-start(bf16[4,4,128,512]{3,2,1,0:T(8,128)(2,1)} %bitcast.116), calls=%async_computation.3 | async-start | bytes 4194304 | tf_op jit(solution)/shard_map/all_to_all | solution.py:1556
  879.8 26.0 %copy-start.17 = (bf16[1,128,2048]{2,1,0:T(8,128)(2,1)S(1)}, bf16[1,128,2048]{2,1,0:T(8,128)(2,1)}, u32[]{:S(2)}) copy-start(bf16[1,128,2048]{2,1,0:T(8,128)(2,1)} %param.7) | copy-start | bytes 1572868
  879.8 26.0 %copy-start.36 = (f32[128]{0:T(128)S(1)}, f32[128]{0:T(128)}, u32[]{:S(2)}) copy-start(f32[128]{0:T(128)} %copy-done.35) | copy-start | bytes 1540
  879.8 26.0 %copy-start.38 = (f32[128]{0:T(128)S(1)}, f32[128]{0:T(128)}, u32[]{:S(2)}) copy-start(f32[128]{0:T(128)} %copy-done.37) | copy-start | bytes 1540
  879.8 26.4 %copy-start.19 = (f32[128,2048]{1,0:T(8,128)S(1)}, f32[128,2048]{1,0:T(8,128)}, u32[]{:S(2)}) copy-start(f32[128,2048]{1,0:T(8,128)} %convert_add_fusion) | copy-start | bytes 3145732
  (32 other events, 145.7 us)
Sparse Core Ops, SparseCore 0:
  9.6 103.8 all-gather.1

commit v7 on v6

--- a/solution.py
+++ b/solution.py
@@ -686,36 +686,51 @@
     )(units.reshape(-1), ug, down, *attention).reshape(n_dp, slots, rows, wide)
 
 
-def column_sum(ref, taken, sent, came, send_sem, recv_sem, pass_sem, take_sem, between):
+def column_sums(refs, takens, sents, cames, send_sem, recv_sem, pass_sem, take_sem, between):
     n_seq, n_dp, seq_index, dp_index = places()
     core = lax.rem(seq_index, 2)
     sibling = (dp_index, seq_index + 1 - 2 * core)
-
-    def onward(block):
+    views = range(len(refs))
+
+    def onward(view, block):
         return send(
-            ref.at[1 - core, block], taken.at[block], pass_sem.at[block], take_sem.at[block], sibling
+            refs[view].at[1 - core, block],
+            takens[view].at[block],
+            pass_sem.at[view, block],
+            take_sem.at[view, block],
+            sibling,
         )
 
     for block in [b for k in range(n_dp // 2) for b in (n_dp - 1 - k, k)]:
-        onward(block).start()
-    total = relay_sum(
-        [lambda block: ref[core, block].astype(f32) + taken[block].astype(f32)],
-        [sent],
-        [came],
+        for view in views:
+            onward(view, block).start()
+
+    def ready(block):
+        for view in views:
+            onward(view, block).wait_recv()
+
+    def own(view):
+        return lambda block: refs[view][core, block].astype(f32) + takens[view][block].astype(f32)
+
+    totals = relay_sum(
+        [own(view) for view in views],
+        sents,
+        cames,
         dp_index,
         n_dp,
         lambda place: (place, seq_index),
         send_sem,
         recv_sem,
-        lambda block: onward(block).wait_recv(),
+        ready,
         between,
-    )[0]
+    )
     for block in range(n_dp):
-        onward(block).wait_send()
-    return total
-
-
-def grads_kernel(band, has_tokens, *refs):
+        for view in views:
+            onward(view, block).wait_send()
+    return totals
+
+
+def grads_kernel(band, n_sums, has_tokens, *refs):
     n_seq, n_dp, seq_index, dp_index = places()
     chips, chip, core = n_seq // 2, seq_index // 2, lax.rem(seq_index, 2)
     sibling = (dp_index, chip * 2 + 1 - core)
@@ -726,12 +741,14 @@
         return taken
 
     owns = take(3) if band else None
-    (x_ref,) = take(1)
+    x_refs = take(n_sums)
     tokens_ref = take(1)[0] if has_tokens else None
     outs = take(2) if band else None
-    (x_out,) = take(1)
+    x_outs = take(n_sums)
     tokens_out = take(1)[0] if has_tokens else None
-    x_taken, z_sent, z_came, z_send, z_recv, x_pass, x_take = take(7)
+    if n_sums:
+        takens, sents, cames = take(n_sums), take(n_sums), take(n_sums)
+        z_send, z_recv, x_pass, x_take = take(4)
     if has_tokens:
         token_own, token_send, token_recv, token_pass, token_take = take(5)
     greet(
@@ -820,9 +837,14 @@
             if has_tokens:
                 pass_on()
 
-    x_out[...] = column_sum(
-        x_ref, x_taken, z_sent, z_came, z_send, z_recv, x_pass, x_take, between
-    )
+    if n_sums:
+        totals = column_sums(
+            x_refs, takens, sents, cames, z_send, z_recv, x_pass, x_take, between
+        )
+        for out, total in zip(x_outs, totals):
+            out[...] = total
+    else:
+        between(0)
     if has_tokens:
         own_tokens.wait()
         finish()
@@ -867,21 +889,18 @@
                 leg(view, way, step).wait_send()
 
 
-def sum_grads(band, sums, x, tokens, collective_id):
-    _, n_dp, shard, width = x.shape
+def sum_grads(band, sums, xs, tokens, shape, collective_id):
+    n_dp, shard, width = shape
     chips = lax.axis_size("seq") // 2
     steps = chips // 2
     vmem = pltpu.VMEM
     operands, in_specs, out_shape, out_specs = [], [], [], []
-    scratch = [
-        vmem((n_dp, shard, width), bf),
-        vmem((n_dp, shard, width), bf),
-        vmem((n_dp + 1, shard, width), bf),
-        DMA((1, 2, n_dp)),
-        DMA((1, 2, n_dp)),
-        DMA((n_dp,)),
-        DMA((n_dp,)),
-    ]
+    count = len(xs)
+    scratch = []
+    if count:
+        scratch += [vmem((n_dp, shard, width), bf)] * (2 * count)
+        scratch += [vmem((n_dp + 1, shard, width), bf)] * count
+        scratch += [DMA((count, 2, n_dp))] * 2 + [DMA((count, n_dp))] * 2
     if tokens is not None:
         scratch += [DMA] + [DMA((chips,))] * 4
     if band:
@@ -910,25 +929,120 @@
             DMA,
             DMA((3, 2, steps)),
         ]
-    operands.append(x)
-    in_specs.append(VMEM)
-    out_shape.append(jax.ShapeDtypeStruct((shard, width), f32))
-    out_specs.append(VMEM)
+    operands += xs
+    in_specs += [VMEM] * count
+    out_shape += [jax.ShapeDtypeStruct((shard, width), f32)] * count
+    out_specs += [VMEM] * count
     if tokens is not None:
         operands.append(tokens)
         in_specs.append(VMEM)
         out_shape.append(jax.ShapeDtypeStruct((2 * chips,) + tokens.shape, bf))
         out_specs.append(ANY)
     return pl.pallas_call(
-        functools.partial(grads_kernel, band, tokens is not None),
+        functools.partial(grads_kernel, band, count, tokens is not None),
         out_shape=out_shape,
         in_specs=in_specs,
         out_specs=out_specs,
         scratch_shapes=scratch,
-        compiler_params=comm_params(collective_id, 56),
+        compiler_params=comm_params(collective_id, 58),
         cost_estimate=takes(75),
         name="sum_grads",
     )(*operands)
+
+
+def attention_back_kernel(
+    grad_ref, weight_ref, query_ref, key_ref, value_ref, mixed_ref, stat_ref, cos_ref, sin_ref, doc_row, doc_col, x_ref,
+    qkv_out, qkv_weight_out, out_weight_out, mixed_grad, key_sum, value_sum
+):
+    seq_len, width = grad_ref.shape
+    head_cols = query_ref.shape[1]
+    heads = head_cols // HD
+    block_rows = min(256, seq_len)
+    scale = float(HD) ** (-0.5)
+
+    def rows_of(b):
+        return pl.ds(pl.multiple_of(b * block_rows, block_rows), block_rows)
+
+    def times(left, right, left_axis, right_axis):
+        return lax.dot_general(
+            left, right, (((left_axis,), (right_axis,)), ((), ())), preferred_element_type=f32
+        )
+
+    def mix(b, carry):
+        at = rows_of(b)
+        mixed_grad[at, :] = times(grad_ref[at, :], weight_ref[...], 1, 1).astype(bf)
+        return carry
+
+    lax.fori_loop(0, seq_len // block_rows, mix, 0)
+    key_sum[...] = jnp.zeros_like(key_sum)
+    value_sum[...] = jnp.zeros_like(value_sum)
+
+    def turned(grads, cosine, sine):
+        scaled = grads * sine
+        half = HD // 2
+        other = jnp.concatenate([scaled[:, half:], -scaled[:, :half]], axis=-1)
+        return grads * cosine + other
+
+    def attend(b, carry):
+        at = rows_of(b)
+        begin = b * block_rows
+        query_pos = begin + lax.broadcasted_iota(jnp.int32, (block_rows, seq_len), 0)
+        key_pos = lax.broadcasted_iota(jnp.int32, (block_rows, seq_len), 1)
+        allowed = (doc_col[at, :] == doc_row[...]) & (key_pos <= query_pos)
+        for h in range(heads):
+            place = slice(h * HD, (h + 1) * HD)
+            query, part = query_ref[at, place], mixed_grad[at, place]
+            scores = jnp.where(allowed, times(query, key_ref[:, place], 1, 1) * scale, masked_score)
+            prob = jnp.exp(scores - stat_ref[at, h * HD : h * HD + 1])
+            prob_grad = times(part, value_ref[:, place], 1, 1)
+            inner = jnp.sum(prob * prob_grad, axis=-1, keepdims=True)
+            score_grad = (prob * (prob_grad - inner) * scale).astype(bf)
+            value_sum[:, place] += times(prob.astype(bf), part, 0, 0)
+            key_sum[:, place] += times(score_grad, query, 0, 0)
+            query_grad = times(score_grad, key_ref[:, place], 1, 0)
+            qkv_out[at, place] = turned(query_grad, cos_ref[at, :], sin_ref[at, :]).astype(bf)
+        return carry
+
+    lax.fori_loop(0, seq_len // block_rows, attend, 0)
+
+    def finish(b, carry):
+        at = rows_of(b)
+        for h in range(heads):
+            place = slice(h * HD, (h + 1) * HD)
+            grads = turned(key_sum[at, place], cos_ref[at, :], sin_ref[at, :])
+            qkv_out[at, head_cols + h * HD : head_cols + (h + 1) * HD] = grads.astype(bf)
+        qkv_out[at, 2 * head_cols :] = value_sum[at, :].astype(bf)
+        return carry
+
+    lax.fori_loop(0, seq_len // block_rows, finish, 0)
+    columns = min(512, width)
+    for c in range(width // columns):
+        at = slice(c * columns, (c + 1) * columns)
+        qkv_weight_out[at, :] = times(x_ref[:, at], qkv_out[...], 0, 0).astype(bf)
+        out_weight_out[:, at] = times(mixed_ref[...], grad_ref[:, at], 0, 0).astype(bf)
+
+
+def attention_back(grad, weight, query, key, value, mixed, stat, cosine, sine, doc, x):
+    seq_len, width = grad.shape
+    head_cols = query.shape[1]
+    return pl.pallas_call(
+        attention_back_kernel,
+        out_shape=[
+            jax.ShapeDtypeStruct((seq_len, 3 * head_cols), bf),
+            jax.ShapeDtypeStruct((width, 3 * head_cols), bf),
+            jax.ShapeDtypeStruct((head_cols, width), bf),
+        ],
+        in_specs=[VMEM] * 12,
+        out_specs=[VMEM] * 3,
+        scratch_shapes=[
+            pltpu.VMEM((seq_len, head_cols), bf),
+            pltpu.VMEM((seq_len, head_cols), f32),
+            pltpu.VMEM((seq_len, head_cols), f32),
+        ],
+        compiler_params=pltpu.CompilerParams(vmem_limit_bytes=50 << 20),
+        cost_estimate=takes(35),
+        name="attention_back",
+    )(grad, weight, query, key, value, mixed, stat, cosine, sine, doc[None, :], doc[:, None], x)
 
 
 def turn_half(values):
@@ -964,6 +1078,40 @@
     share = wide // step_cols
     tokens, width = tokens_ref.shape
     greet([(dp_index, p) for p in seq_peers[1:]] + [(p, seq_index) for p in dp_peers[1:]])
+
+    def band(c):
+        return pl.ds(c * sub, sub)
+
+    def late_copies(c):
+        copies = []
+        for k in range(1, n_dp):
+            copies.append(
+                send(
+                    late_ref.at[dp_peers[k], :, band(c)],
+                    late_tables[c].at[dp_index],
+                    late_send.at[c, k],
+                    late_recv.at[c, k],
+                    (dp_peers[k], seq_index),
+                )
+            )
+        return copies
+
+    def late_own_copy(c):
+        return pltpu.make_async_copy(
+            late_ref.at[dp_index, :, band(c)], late_tables[c].at[dp_index], late_own.at[c]
+        )
+
+    def late_start(c):
+        if not has_late or c >= n_dp:
+            return
+        if c:
+            for copy in late_copies(c - 1):
+                copy.wait_send()
+        for copy in late_copies(c):
+            copy.start()
+        late_own_copy(c).start()
+
+    late_start(0)
 
     for u in range(3):
         for block in range(n_seq):
@@ -1007,40 +1155,6 @@
         w_recv,
         lambda block: None,
     )
-
-    def band(c):
-        return pl.ds(c * sub, sub)
-
-    def late_copies(c):
-        copies = []
-        for k in range(1, n_dp):
-            copies.append(
-                send(
-                    late_ref.at[dp_peers[k], :, band(c)],
-                    late_tables[c].at[dp_index],
-                    late_send.at[c, k],
-                    late_recv.at[c, k],
-                    (dp_peers[k], seq_index),
-                )
-            )
-        return copies
-
-    def late_own_copy(c):
-        return pltpu.make_async_copy(
-            late_ref.at[dp_index, :, band(c)], late_tables[c].at[dp_index], late_own.at[c]
-        )
-
-    def late_start(c):
-        if not has_late or c >= n_dp:
-            return
-        if c:
-            for copy in late_copies(c - 1):
-                copy.wait_send()
-        for copy in late_copies(c):
-            copy.start()
-        late_own_copy(c).start()
-
-    late_start(0)
 
     seq_len = x1_ref.shape[0]
     heads = query_out.shape[1] // HD
@@ -1371,13 +1485,11 @@
     sub = rows // n_dp
     wide = width // n_dp
     half = chips * sub
-    heads = H // n_seq
-    head_cols = heads * HD
+    head_cols = H // n_seq * HD
     seq_len = shard_len * n_seq
     ff_blocks = FF // D
     first_slots = min(4, per_owner)
     unit_count = owners.shape[0]
-    score_scale = float(HD) ** (-0.5)
 
     unit_slot = unit_slots(owners, per_owner)
     place = unit_slot - owners * per_owner
@@ -1441,10 +1553,6 @@
     )
     qkv_weight = qkv_weight.reshape(width, 3 * head_cols)
     out_weight = out_weight.reshape(rows, width)
-    queries, keys, values = (a.reshape(seq_len, heads, HD) for a in (queries, keys, values))
-    log_total = log_total.reshape(seq_len, heads, HD)[:, :, :1].transpose(1, 0, 2)
-    cosine = cosine[:, None, :]
-    sine = sine[:, None, :]
     normed_two, inv_two = norm_parts(residual)
     columns = ff_blocks * half
     up_weight = up_weight.reshape(width, columns)
@@ -1479,7 +1587,7 @@
     column = (2, n_dp, shard_len, width)
     bands = [(0, sub // 2), (sub // 2, sub // 2)] if sub % 32 == 0 else [(0, sub)]
     *pieces, norm_two_grad = sum_grads(
-        bands[0], sums, norm_two_grad.astype(bf).reshape(column), None, 5
+        bands[0], sums, [norm_two_grad.astype(bf).reshape(column)], None, column[1:], 5
     )
     pieces = [pieces]
     residual_grad = upstream.astype(f32) + norm_back(normed_two, inv_two, norm_two_grad)
@@ -1491,8 +1599,9 @@
     *second, ff_out, residual_grad_all = sum_grads(
         bands[1] if len(bands) > 1 else None,
         sums,
-        ff_part.astype(bf).reshape(column),
+        [ff_part.astype(bf).reshape(column)],
         residual_grad.astype(bf),
+        column[1:],
         7,
     )
     residual_grad_all = residual_grad_all.reshape(seq_len, width)
@@ -1505,38 +1614,21 @@
                 (send_now, residual_grad_all, late_grads[0])
             )
             late_grads.append(lax.all_to_all(send_now, "dp", 0, 0))
-    attended_grad = jnp.einsum(
-        "tc,rc->tr", residual_grad_all, out_weight, preferred_element_type=f32
-    )
-    attended_grad = attended_grad.astype(bf).reshape(seq_len, heads, HD)
-    allowed = (doc[:, None] == doc[None, :]) & (positions[None, :] <= positions[:, None])
-    scores = jnp.einsum("qhd,khd->hqk", queries, keys, preferred_element_type=f32) * score_scale
-    scores = jnp.where(allowed[None], scores, masked_score)
-    prob = jnp.exp(scores - log_total)
-    prob_low = prob.astype(bf)
-    value_grad = jnp.einsum("hqk,qhd->khd", prob_low, attended_grad, preferred_element_type=f32)
-    prob_grad = jnp.einsum("qhd,khd->hqk", attended_grad, values, preferred_element_type=f32)
-    inner_sum = jnp.sum(prob * prob_grad, axis=-1, keepdims=True)
-    score_grad = (prob * (prob_grad - inner_sum) * score_scale).astype(bf)
-    query_grad = jnp.einsum("hqk,khd->qhd", score_grad, keys, preferred_element_type=f32)
-    key_grad = jnp.einsum("hqk,qhd->khd", score_grad, queries, preferred_element_type=f32)
-    qkv_grad = jnp.stack(
-        [
-            rotate_back(query_grad, cosine, sine),
-            rotate_back(key_grad, cosine, sine),
-            value_grad,
-        ],
-        axis=1,
-    )
-    qkv_grad_low = qkv_grad.astype(bf).reshape(seq_len, 3 * head_cols)
+    qkv_grad_low, qkv_wgrad, out_wgrad = attention_back(
+        residual_grad_all,
+        out_weight,
+        queries,
+        keys,
+        values,
+        attended_low,
+        log_total,
+        cosine,
+        sine,
+        doc,
+        normed_one_all,
+    )
     norm_one_part = jnp.einsum("tf,rf->tr", qkv_grad_low, qkv_weight, preferred_element_type=f32)
     norm_one_grad = sum_seq(norm_one_part.astype(bf).reshape(n_seq, shard_len, width), 3)
-    qkv_wgrad = jnp.einsum(
-        "tr,tf->rf", normed_one_all, qkv_grad_low, preferred_element_type=f32
-    ).astype(bf)
-    out_wgrad = jnp.einsum(
-        "tr,tc->rc", attended_low, residual_grad_all, preferred_element_type=f32
-    ).astype(bf)
     qkv_piece, out_piece = collect_attention(
         qkv_wgrad.reshape(n_seq, n_dp, sub, 3 * head_cols), out_wgrad.reshape(n_dp, sub, width), 6
     )

time: 965 us -> 925 us (0.959)
  matrix products: 134 us -> 75.2 us
  Pallas kernels: 711 us -> 739 us
    dot_general x8 -> x0, matrix products: 55.4 us -> none  [the longest x1 16.4 us: local(): jnp.einsum('hqk,khd->qhd', score_grad, keys, preferred_element_type=f32)]
    pallas_call x2 -> x3, Pallas kernels: 148 us -> 170 us  [the longest x2 147 us: sum_grads(): pl.pallas_call(functools.partial(grads_kernel, band, count, tokens is not...]
    unnamed x103 -> x86, local copies, waits for them, and re-layouts: 17.1 us -> 21.6 us
  transfers between devices with their start and end apart: 5 -> 5, of which waited for: 2 -> 2; matrix products, arithmetic and copies ran while one was open for 11% -> 3% of each run, Pallas kernels for 36% -> 40%
where the time goes in v7:
time: 925 us; the launch traced here: 916 us
  Pallas kernels  739 us (80%)
  matrix products  75.2 us (8%)
  waiting for transfers between devices  28.4 us (3%)
  local copies, waits for them, and re-layouts  23.8 us (3%)
  other arithmetic  18.1 us (2%)
  starting transfers between devices  17.1 us (2%)
  between operations  15 us (2%)
    pallas_call x1, Pallas kernels, forward(): pl.pallas_call(functools.partial(forward_kernel, has_late, first_slots, f...  279 us
    pallas_call x2, Pallas kernels, sum_grads(): pl.pallas_call(functools.partial(grads_kernel, band, count, tokens is not...  147 us
    pallas_call x1, Pallas kernels, front(): pl.pallas_call(front_kernel, out_shape=[jax.ShapeDtypeStruct(packed.shape...  94.9 us
    pallas_call x1, Pallas kernels, collect_attention(): pl.pallas_call(collect_kernel, out_shape=[jax.ShapeDtypeStruct((n_seq,) +...  83.6 us
    dot_general x9, matrix products, times(): lax.dot_general(left, right, (((left_axis,), (right_axis,)), ((), ())), p...  69.3 us
    pallas_call x2, Pallas kernels, adam(): pl.pallas_call(functools.partial(adam_kernel, n_dp, n_seq // 2, first_slo...  52 us
    pallas_call x1, Pallas kernels, sum_seq(): pl.pallas_call(sum_seq_kernel, out_shape=jax.ShapeDtypeStruct((rows, colu...  29.4 us
    all_to_all x2, waiting for transfers between devices, local(): came = lax.all_to_all(send_now, 'dp', 0, 0)  27.7 us
  transfers between devices with their start and end apart: 5, of which 2 were waited for; matrix products, arithmetic and copies ran while one was open for 3% of the time, Pallas kernels for 40%

profile of v7, /device:TPU:0, one launch (start us, length us, event | category | flops | bytes accessed | tf_op | source)
XLA Modules:
  0.0 916.2 jit_solution(10526868506829150089)
XLA Ops:
  11.9 15.9 %pack.1 = (bf16[4,4,256,512]{3,2,1,0:T(8,128)(2,1)}, bf16[4,4,256,512]{3,2,1,0:T(8,128)(2,1)}) custom-call(s32[8]{0:T(128)S(1)} %fusion.4.flags, f32[256,8,2048]{2,1,0:T(8,128)} %refs_4_.3), custom_call_target="tpu_custom_call" | custom-call | tf_op jit(solution)/shard_map/pack/pallas_call | solution.py:113
  30.8 94.9 %front.1 = (bf16[4,4,256,512]{3,2,1,0:T(8,128)(2,1)S(1)}, bf16[8,128,2048]{2,1,0:T(8,128)(2,1)S(1)}) custom-call(bf16[4,4,256,512]{3,2,1,0:T(8,128)(2,1)S(1)} %copy-done.8, bf16[128,2048]{1,0:T(8,128)(2,1)S(1)} %fusion.1.x_ref), custom_call_target="tpu_custom_call" | custom-call | bytes 270000000 | tf_op jit(solution)/shard_map/front/pallas_call | solution.py:455
  134.7 278.7 %forward.1 = (bf16[8,4,64,768]{3,2,1,0:T(8,128)(2,1)}, bf16[4,64,2048]{2,1,0:T(8,128)(2,1)}, bf16[1024,256]{1,0:T(8,128)(2,1)}, bf16[1024,256]{1,0:T(8,128)(2,1)...) custom-call(s32[40]{0:T(128)} %pad_add_fusion.refs_0_, ...), custom_call_target="tpu_custom_call" | custom-call | bytes 690000000 | tf_op jit(solution)/shard_map/forward/pallas_call | solution.py:1401
  413.5 10.1 %fusion.10 = f32[1024,1024]{1,0:T(8,128)} fusion(bf16[1024,2048]{1,0:T(8,128)(2,1)} %bitcast.103, bf16[2048,1024]{1,0:T(8,128)(2,1)} %bitcast.101), kind=kOutput, calls=%fused_computation.62 | convolution fusion | flops 4294967296 | bytes 12582912 | tf_op jit(solution)/shard_map/dot_general | solution.py:1565
  423.6 6.0 fusion.11
  429.6 9.6 %multiply_convert_fusion = (bf16[1024,1024]{1,0:T(8,128)(2,1)}, bf16[1024,1024]{1,0:T(8,128)(2,1)S(1)}, bf16[1024,1024]{1,0:T(8,128)(2,1)S(1)}) fusion(f32[1024,1024]{1,0:T(8,128)} %fusion.11, f32[1024,1024]{1,0:T(8,128)} %fusion.10, bf16[1024,2048]{1,0:T(8,128)(2,1)S(1)} %bitcast.108, bf16[1024,2048]{1,0:T(8,128)(2,1)S(1)} %bitcast.100), kind=kOutput, calls=%fused_computation.1 | convolution fusion | flops 4309647360 | bytes 23068672 | tf_op jit(solution)/shard_map/dot_general | solution.py:1565
  439.1 6.2 convolution_convert_fusion.3
  445.4 6.8 fusion.12
  452.6 8.5 convolution_convert_fusion.4
  461.1 6.7 convolution_convert_fusion.2
  467.9 6.1 add_convert_fusion
  474.0 61.1 %sum_grads.2 = (bf16[8,128,512]{2,1,0:T(8,128)(2,1)}, bf16[4,32,2048]{2,1,0:T(8,128)(2,1)}, f32[128,2048]{1,0:T(8,128)}) custom-call(bf16[4,4,64,2048]{3,2,1,0:T(8,128)(2,1)} %bitcast.90, bf16[4,2,4,64,1024]{4,3,2,1,0:T(8,128)(2,1)} %bitcast.88, bf16[4,2,4,64,1024]{4,3,2,1,0:T(8,128)(2,1)} %bitcast.92, bf16[2,4,128,2048]{3,2,1,0:T(8,128)(2,1)} %bitcast.96), custom_call_target="tpu_custom_call" | custom-call | bytes 225000000 | tf_op jit(solution)/shard_map/sum_grads/pallas_call | solution.py:941
  539.4 5.8 arrange.4
  550.8 9.3 %convolution_convert_fusion.1 = bf16[1024,2048]{1,0:T(8,128)(2,1)} fusion(bf16[1024,1024]{1,0:T(8,128)(2,1)} %copy-done.38, bf16[1024,2048]{1,0:T(8,128)(2,1)} %bitcast.99), kind=kOutput, calls=%fused_computation.6 | convolution fusion | flops 4297064448 | bytes 10485760 | tf_op jit(solution)/shard_map/dot_general | solution.py:1565
  560.2 85.8 %sum_grads.3 = (bf16[8,128,512]{2,1,0:T(8,128)(2,1)}, bf16[4,32,2048]{2,1,0:T(8,128)(2,1)}, f32[128,2048]{1,0:T(8,128)}, bf16[8,128,2048]{2,1,0:T(8,128)(2,1)}) custom-call(bf16[4,4,64,2048]{3,2,1,0:T(8,128)(2,1)} %bitcast.91, bf16[4,2,4,64,1024]{4,3,2,1,0:T(8,128)(2,1)} %bitcast.89, bf16[4,2,4,64,1024]{4,3,2,1,0:T(8,128)(2,1)} %bitcast.93, ...), custom_call_target="tpu_custom_call" | custom-call | bytes 225000000 | tf_op jit(solution)/shard_map/sum_grads/pallas_call | solution.py:941
  648.4 5.9 arrange.5
  663.2 22.8 %attention_back.1 = (bf16[1024,768]{1,0:T(8,128)(2,1)}, bf16[2048,768]{1,0:T(8,128)(2,1)}, bf16[256,2048]{1,0:T(8,128)(2,1)}) custom-call(bf16[1024,2048]{1,0:T(8,128)(2,1)} %bitcast.94, bf16[256,2048]{1,0:T(8,128)(2,1)} %bitcast.97, bf16[1024,256]{1,0:T(8,128)(2,1)S(1)} %copy-done.19, bf16[1024,256]{1,0:T(8,128)(2,1)S(1)} %copy-done.20, ...), custom_call_target="tpu_custom_call" | custom-call | bytes 105000000 | tf_op jit(solution)/shard_map/attention_back/pallas_call | solution.py:1028
  689.2 83.6 %collect_attention.1 = (bf16[8,64,768]{2,1,0:T(8,128)(2,1)S(1)}, bf16[64,2048]{1,0:T(8,128)(2,1)S(1)}) custom-call(bf16[8,4,64,768]{3,2,1,0:T(8,128)(2,1)S(1)} %bitcast.83, bf16[4,64,2048]{2,1,0:T(8,128)(2,1)S(1)} %bitcast.84), custom_call_target="tpu_custom_call" | custom-call | bytes 225000000 | tf_op jit(solution)/shard_map/collect_attention/pallas_call | solution.py:563
  780.3 5.8 convolution_convert_fusion
  786.2 29.4 %sum_seq.1 = f32[128,2048]{1,0:T(8,128)S(1)} custom-call(bf16[8,128,2048]{2,1,0:T(8,128)(2,1)S(1)} %bitcast.81), custom_call_target="tpu_custom_call" | custom-call | bytes 84000000 | tf_op jit(solution)/shard_map/sum_seq/pallas_call | solution.py:506
  818.3 11.2 %all-to-all-done.2.refs_0_ = bf16[4,4,128,512]{3,2,1,0:T(8,128)(2,1)S(1)} async-done(((bf16[4,4,128,512]{3,2,1,0:T(8,128)(2,1)}), bf16[4,4,128,512]{3,2,1,0:T(8,128)(2,1)S(1)}, u32[]{:S(2)}, u32[]{:S(2)}) %all-to-all-start.2) | async-done | bytes 2097184 | tf_op jit(solution)/shard_map/all_to_all | solution.py:1648
  838.6 26.0 %adam.2 = (f32[256,8,2048]{2,1,0:T(8,128)}, f32[256,8,2048]{2,1,0:T(8,128)}, f32[256,8,2048]{2,1,0:T(8,128)}, f32[256,8,2048]{2,1,0:T(8,128)}) custom-call(s32[8]{0:T(128)S(1)} %get-tuple-element.103.kinds, bf16[4,4,128,512]{3,2,1,0:T(8,128)(2,1)S(1)} %copy-done.1, bf16[4,4,128,512]{3,2,1,0:T(8,128)(2,1)} %all-to-all-done.refs_1_, ...), custom_call_target="tpu_custom_call" | custom-call | bytes 75000000 | tf_op jit(solution)/shard_map/adam/pallas_call | solution.py:195
  866.4 16.5 %all-to-all-done.3.refs_0_ = bf16[4,4,128,512]{3,2,1,0:T(8,128)(2,1)S(1)} async-done(((bf16[4,4,128,512]{3,2,1,0:T(8,128)(2,1)}), bf16[4,4,128,512]{3,2,1,0:T(8,128)(2,1)S(1)}, u32[]{:S(2)}, u32[]{:S(2)}) %all-to-all-start.3) | async-done | bytes 2097184 | tf_op jit(solution)/shard_map/all_to_all | solution.py:1648
  882.9 26.0 %adam.3 = (f32[256,8,2048]{2,1,0:T(8,128)}, f32[256,8,2048]{2,1,0:T(8,128)}, f32[256,8,2048]{2,1,0:T(8,128)}, f32[256,8,2048]{2,1,0:T(8,128)}) custom-call(s32[8]{0:T(128)S(1)} %get-tuple-element.103.kinds, bf16[4,4,128,512]{3,2,1,0:T(8,128)(2,1)S(1)} %all-to-all-done.3.refs_0_, ...), custom_call_target="tpu_custom_call", output_to_operand_aliasing={{0}: (9, {}), {1}: (10, {}), {2}: (11, {}), {3}: (12, {})} | custom-call | bytes 75000000 | tf_op jit(solution)/shard_map/adam/pallas_call | solution.py:195
  (142 shorter events, 62.4 us)
Async XLA Ops:
  7.2 127.6 %all-gather.2.cloned.1.call-start = ((), (), s32[]{:S(2)}) async-start(), calls=%async_computation.4 | async-start | bytes 2621440 | tf_op jit(solution)/shard_map/all_gather | solution.py:1513
  10.8 17.0 %copy-start.23 = (s32[1024]{0:T(1024)}, s32[1024]{0:T(1024)S(1)}, u32[]{:S(2)}) copy-start(s32[1024]{0:T(1024)S(1)} %convert_reduce_fusion.1) | copy-start | bytes 12292
  11.8 15.9 %copy-start.26 = (bf16[1,128,2048]{2,1,0:T(8,128)(2,1)S(1)}, bf16[1,128,2048]{2,1,0:T(8,128)(2,1)}, u32[]{:S(2)}) copy-start(bf16[1,128,2048]{2,1,0:T(8,128)(2,1)} %param.7) | copy-start | bytes 1572868
  413.4 10.1 %copy-start.33 = (bf16[2,4,128,2048]{3,2,1,0:T(8,128)(2,1)S(1)}, bf16[2,4,128,2048]{3,2,1,0:T(8,128)(2,1)}, u32[]{:S(2)}) copy-start(bf16[2,4,128,2048]{3,2,1,0:T(8,128)(2,1)} %get-tuple-element.57) | copy-start | bytes 12582916
  413.4 10.1 %copy-start.36 = (bf16[4,2,256,1024]{3,2,1,0:T(8,128)(2,1)S(1)}, bf16[4,2,256,1024]{3,2,1,0:T(8,128)(2,1)}, u32[]{:S(2)}) copy-start(bf16[4,2,256,1024]{3,2,1,0:T(8,128)(2,1)} %get-tuple-element.59) | copy-start | bytes 12582916
  439.1 13.4 %copy-start.38 = (bf16[1024,1024]{1,0:T(8,128)(2,1)}, bf16[1024,1024]{1,0:T(8,128)(2,1)S(1)}, u32[]{:S(2)}) copy-start(bf16[1024,1024]{1,0:T(8,128)(2,1)S(1)} %get-tuple-element.105) | copy-start | bytes 6291460
  452.6 8.5 copy-start.34
  452.6 8.5 copy-start.39
  452.6 15.3 %slice-start = ((s8[8388608]{0:T(1024)(128)(4,1)}), s8[4194304]{0:T(1024)(128)(4,1)S(1)}, s32[]{:S(2)}) async-start(s8[8388608]{0:T(1024)(128)(4,1)} %bitcast.113), calls=%async_computation.5 | async-start | bytes 8388608
  474.0 62.7 %copy-start.30 = (bf16[1,128,2048]{2,1,0:T(8,128)(2,1)S(1)}, bf16[1,128,2048]{2,1,0:T(8,128)(2,1)}, u32[]{:S(2)}) copy-start(bf16[1,128,2048]{2,1,0:T(8,128)(2,1)} %param.8) | copy-start | bytes 1572868
  539.4 10.5 %copy-start.28 = (f32[128,2048]{1,0:T(8,128)S(1)}, f32[128,2048]{1,0:T(8,128)}, u32[]{:S(2)}) copy-start(f32[128,2048]{1,0:T(8,128)} %convert_add_fusion) | copy-start | bytes 3145732
  545.3 109.0 %all-to-all-start = ((bf16[4,4,128,512]{3,2,1,0:T(8,128)(2,1)}), bf16[4,4,128,512]{3,2,1,0:T(8,128)(2,1)}, u32[]{:S(2)}, u32[]{:S(2)}) async-start(bf16[4,4,128,512]{3,2,1,0:T(8,128)(2,1)} %bitcast.18), calls=%async_computation | async-start | bytes 4194304 | tf_op jit(solution)/shard_map/all_to_all | solution.py:1598
  560.2 98.9 %copy-start.24 = (s32[1024]{0:T(1024)S(1)}, s32[1024]{0:T(1024)}, u32[]{:S(2)}) copy-start(s32[1024]{0:T(1024)} %copy-done.23) | copy-start | bytes 12292
  646.0 13.0 %copy-start.5 = (s32[1024,1]{1,0:T(8,128)S(1)}, s32[1024,1]{1,0:T(8,128)}, u32[]{:S(2)}) copy-start(s32[1024,1]{1,0:T(8,128)} %copy.21.refs_7_.doc_col) | copy-start | bytes 12292
  646.0 13.0 %copy-start.6 = (f32[1024,128]{1,0:T(8,128)S(1)}, f32[1024,128]{1,0:T(8,128)}, u32[]{:S(2)}) copy-start(f32[1024,128]{1,0:T(8,128)} %get-tuple-element.119.refs_4_.cos_ref) | copy-start | bytes 1572868
  646.0 13.0 %copy-start.7 = (f32[1024,128]{1,0:T(8,128)S(1)}, f32[1024,128]{1,0:T(8,128)}, u32[]{:S(2)}) copy-start(f32[1024,128]{1,0:T(8,128)} %get-tuple-element.120.refs_5_.sin_ref) | copy-start | bytes 1572868
  654.3 121.9 %all-to-all-start.1 = ((bf16[4,4,128,512]{3,2,1,0:T(8,128)(2,1)}), bf16[4,4,128,512]{3,2,1,0:T(8,128)(2,1)}, u32[]{:S(2)}, u32[]{:S(2)}) async-start(bf16[4,4,128,512]{3,2,1,0:T(8,128)(2,1)} %bitcast.21), calls=%async_computation.1 | async-start | bytes 4194304 | tf_op jit(solution)/shard_map/all_to_all | solution.py:1616
  776.2 53.4 %all-to-all-start.2 = ((bf16[4,4,128,512]{3,2,1,0:T(8,128)(2,1)}), bf16[4,4,128,512]{3,2,1,0:T(8,128)(2,1)S(1)}, u32[]{:S(2)}, u32[]{:S(2)}) async-start(bf16[4,4,128,512]{3,2,1,0:T(8,128)(2,1)} %bitcast.80), calls=%async_computation.2 | async-start | bytes 4194304 | tf_op jit(solution)/shard_map/all_to_all | solution.py:1648
  786.1 29.4 %copy-start.11 = (bf16[8,128,512]{2,1,0:T(8,128)(2,1)S(1)}, bf16[8,128,512]{2,1,0:T(8,128)(2,1)}, u32[]{:S(2)}) copy-start(bf16[8,128,512]{2,1,0:T(8,128)(2,1)} %get-tuple-element.67.ug_ref) | copy-start | bytes 3145732
  786.1 29.4 %copy-start.16 = (bf16[4,32,2048]{2,1,0:T(8,128)(2,1)S(1)}, bf16[4,32,2048]{2,1,0:T(8,128)(2,1)}, u32[]{:S(2)}) copy-start(bf16[4,32,2048]{2,1,0:T(8,128)(2,1)} %get-tuple-element.68.down_ref) | copy-start | bytes 1572868
  786.1 29.4 %copy-start.18 = (bf16[32,2048]{1,0:T(8,128)(2,1)S(1)}, bf16[32,2048]{1,0:T(8,128)(2,1)}, u32[]{:S(2)}) copy-start(bf16[32,2048]{1,0:T(8,128)(2,1)} %get-tuple-element.110.refs_1_) | copy-start | bytes 393220
  830.8 52.0 %all-to-all-start.3 = ((bf16[4,4,128,512]{3,2,1,0:T(8,128)(2,1)}), bf16[4,4,128,512]{3,2,1,0:T(8,128)(2,1)S(1)}, u32[]{:S(2)}, u32[]{:S(2)}) async-start(bf16[4,4,128,512]{3,2,1,0:T(8,128)(2,1)} %bitcast.79), calls=%async_computation.3 | async-start | bytes 4194304 | tf_op jit(solution)/shard_map/all_to_all | solution.py:1648
  838.6 26.0 %copy-start.27 = (bf16[1,128,2048]{2,1,0:T(8,128)(2,1)S(1)}, bf16[1,128,2048]{2,1,0:T(8,128)(2,1)}, u32[]{:S(2)}) copy-start(bf16[1,128,2048]{2,1,0:T(8,128)(2,1)} %param.7) | copy-start | bytes 1572868
  838.6 26.3 %copy-start.29 = (f32[128,2048]{1,0:T(8,128)S(1)}, f32[128,2048]{1,0:T(8,128)}, u32[]{:S(2)}) copy-start(f32[128,2048]{1,0:T(8,128)} %convert_add_fusion) | copy-start | bytes 3145732
  (24 other events, 75.6 us)
Sparse Core Ops, SparseCore 0:
  9.6 103.6 all-gather.1

commit v8 on v7

--- a/solution.py
+++ b/solution.py
@@ -169,7 +169,8 @@
     fixed_first = first * (1.0 / (1.0 - beta_one**STEP))
     fixed_second = second * (1.0 / (1.0 - beta_two**STEP))
     old = m_ref[...]
-    step = fixed_first / (jnp.sqrt(fixed_second) + adam_eps) + decay_rate * old
+    root = fixed_second * lax.rsqrt(jnp.maximum(fixed_second, 1e-37))
+    step = fixed_first * pl.reciprocal(root + adam_eps, approx=True) + decay_rate * old
     m_out[...] = jnp.where(keep, old - learn_rate * step, 0.0)
 
 
@@ -730,7 +731,129 @@
     return totals
 
 
-def grads_kernel(band, n_sums, has_tokens, *refs):
+class BandSum:
+    def __init__(self, band, owns, outs, scratch, chips, chip, core, dp_index, n_dp):
+        self.begin, self.size = band
+        self.owns, self.outs = owns, outs
+        self.half_came, self.full_sent, self.full_came = scratch[0:3], scratch[3:6], scratch[6:9]
+        self.mine, self.side_out = scratch[9:12], scratch[12]
+        ring_send, ring_recv, self.side_send, self.side_recv, self.own_sem = scratch[13:]
+        self.ring = Ring(chips, chip, core, dp_index, ring_send, ring_recv)
+        self.chip, self.core, self.n_dp = chip, core, n_dp
+        self.sibling = (dp_index, chip * 2 + 1 - core)
+        self.blocks = outs[1].shape[0]
+        self.pair = self.blocks // 2
+        self.half = outs[0].shape[2] // 2
+
+    def own(self, view, place, way):
+        rows = pl.ds(self.begin, self.size)
+        if view == 0:
+            units = pl.ds(0, self.blocks) if way is None else pl.ds(way * self.pair, self.pair)
+            return self.owns[0].at[units, place, rows, :]
+        columns = pl.ds(0, self.blocks * self.half)
+        if way is not None:
+            columns = pl.ds(way * self.pair * self.half, self.pair * self.half)
+        return self.owns[view].at[place, :, :, rows, columns]
+
+    def leg(self, view, way, step):
+        ring = self.ring
+        if step == 0:
+            src = self.own(view, ring.at(ring.last), way)
+            return ring.leg(view, way, step, src, self.half_came[view].at[way])
+        src = self.full_sent[view].at[step - 1, way]
+        return ring.leg(view, way, step, src, self.full_came[view].at[step - 1, way])
+
+    def own_copy(self, view, way, step):
+        distance = self.ring.last - step
+        if distance == 0:
+            return pltpu.make_async_copy(
+                self.own(view, self.chip, None), self.mine[view], self.own_sem.at[view, 0, step - 1]
+            )
+        src = self.own(view, self.ring.at(distance if way == 0 else -distance), None)
+        return pltpu.make_async_copy(
+            src, self.full_sent[view].at[step - 1, way], self.own_sem.at[view, way, step - 1]
+        )
+
+    def start(self):
+        for view in range(3):
+            for way in range(2):
+                self.leg(view, way, 0).start()
+        for step in range(1, self.ring.last + 1):
+            for view in range(3):
+                for way in range(2 if step < self.ring.last else 1):
+                    self.own_copy(view, way, step).start()
+
+    def steps(self):
+        pair, half = self.pair, self.half
+        for step in range(1, self.ring.last):
+            for view in range(3):
+                for way in range(2):
+                    self.own_copy(view, way, step).wait()
+                    self.leg(view, way, step - 1).wait_recv()
+                    full = self.full_sent[view]
+                    if step > 1:
+                        value = full[step - 1, way].astype(f32)
+                        value = value + self.full_came[view][step - 2, way].astype(f32)
+                        full[step - 1, way] = value.astype(bf)
+                    elif view == 0:
+                        units = slice(way * pair, (way + 1) * pair)
+                        value = full[0, way, units].astype(f32)
+                        value = value + self.half_came[0][way].astype(f32)
+                        full[0, way, units] = value.astype(bf)
+                    else:
+                        columns = slice(way * pair * half, (way + 1) * pair * half)
+                        value = full[0, way, :, :, :, columns].astype(f32)
+                        value = value + self.half_came[view][way].astype(f32)
+                        full[0, way, :, :, :, columns] = value.astype(bf)
+                    self.leg(view, way, step).start()
+
+    def finish(self):
+        ug_out, down_out = self.outs
+        last, blocks, half = self.ring.last, self.blocks, self.half
+        for view in range(3):
+            self.own_copy(view, 0, last).wait()
+            for way in range(2):
+                self.leg(view, way, last - 1).wait_recv()
+            if last > 1:
+                came = [self.full_came[view][last - 2, way].astype(f32) for way in range(2)]
+                value = self.mine[view][...].astype(f32) + came[0] + came[1]
+            else:
+                came = [self.half_came[view][way].astype(f32) for way in range(2)]
+                other = jnp.concatenate(came, axis=0 if view == 0 else 3)
+                value = self.mine[view][...].astype(f32) + other
+            value = value.astype(bf)
+            if view == 0:
+                down_out[...] = value
+                continue
+            value = value.reshape(2, self.n_dp * self.size, blocks * half)
+            for k in range(blocks):
+                unit = (view - 1) * blocks + k
+
+                @pl.when(self.core == 0)
+                def _():
+                    ug_out[unit, :, :half] = value[0, :, k * half : (k + 1) * half]
+                    self.side_out[unit] = value[1, :, k * half : (k + 1) * half]
+
+                @pl.when(self.core != 0)
+                def _():
+                    ug_out[unit, :, half:] = value[1, :, k * half : (k + 1) * half]
+                    self.side_out[unit] = value[0, :, k * half : (k + 1) * half]
+
+        place = pl.ds(pl.multiple_of(self.core * half, half), half)
+        side = send(
+            self.side_out, ug_out.at[:, :, place], self.side_send, self.side_recv, self.sibling
+        )
+        side.start()
+        side.wait()
+
+    def close(self):
+        for step in range(self.ring.last):
+            for view in range(3):
+                for way in range(2):
+                    self.leg(view, way, step).wait_send()
+
+
+def grads_kernel(bands, late_slots, *refs):
     n_seq, n_dp, seq_index, dp_index = places()
     chips, chip, core = n_seq // 2, seq_index // 2, lax.rem(seq_index, 2)
     sibling = (dp_index, chip * 2 + 1 - core)
@@ -740,176 +863,109 @@
         taken, refs[:count] = refs[:count], []
         return taken
 
-    owns = take(3) if band else None
-    x_refs = take(n_sums)
-    tokens_ref = take(1)[0] if has_tokens else None
-    outs = take(2) if band else None
-    x_outs = take(n_sums)
-    tokens_out = take(1)[0] if has_tokens else None
-    if n_sums:
-        takens, sents, cames = take(n_sums), take(n_sums), take(n_sums)
-        z_send, z_recv, x_pass, x_take = take(4)
-    if has_tokens:
-        token_own, token_send, token_recv, token_pass, token_take = take(5)
+    info, residual_ref, cot_ref = take(3)
+    owns, x_refs = take(3), take(2)
+    outs = [take(2) for _ in bands]
+    grad_out, ff_out, tokens_out = take(3)
+    late_out = take(1)[0] if late_slots else None
+    scratch = [take(18) for _ in bands]
+    takens, sents, cames = take(2), take(2), take(2)
+    z_send, z_recv, x_pass, x_take = take(4)
+    stage, token_own, token_send, token_recv, token_pass, token_take = take(6)
     greet(
         [(lax.rem(dp_index + k, n_dp), seq_index) for k in range(1, n_dp)]
         + [(dp_index, lax.rem(chip + k, chips) * 2 + core) for k in range(1, chips)]
         + [sibling]
     )
-    if band:
-        half_came, full_sent, full_came, mine = take(3), take(3), take(3), take(3)
-        side_out, ring_send, ring_recv, side_send, side_recv, own_sem = take(6)
-        ug_out, down_out = outs
-        ring = Ring(chips, chip, core, dp_index, ring_send, ring_recv)
-        begin, size = band
-        blocks = down_out.shape[0]
-        pair = blocks // 2
-        half = ug_out.shape[2] // 2
-        last = ring.last
-
-        def own(view, place, way):
-            if view == 0:
-                units = pl.ds(0, blocks) if way is None else pl.ds(way * pair, pair)
-                return owns[0].at[units, place, pl.ds(begin, size), :]
-            columns = pl.ds(0, blocks * half) if way is None else pl.ds(way * pair * half, pair * half)
-            return owns[view].at[place, :, :, pl.ds(begin, size), columns]
-
-        def leg(view, way, step):
-            if step == 0:
-                src = own(view, ring.at(last), way)
-                return ring.leg(view, way, step, src, half_came[view].at[way])
-            src, dst = full_sent[view].at[step - 1, way], full_came[view].at[step - 1, way]
-            return ring.leg(view, way, step, src, dst)
-
-        def own_copy(view, way, step):
-            distance = last - step
-            if step == last:
-                return pltpu.make_async_copy(
-                    own(view, chip, None), mine[view], own_sem.at[view, 0, step - 1]
-                )
-            src = own(view, ring.at(distance if way == 0 else -distance), None)
-            return pltpu.make_async_copy(
-                src, full_sent[view].at[step - 1, way], own_sem.at[view, way, step - 1]
-            )
-
-        for view in range(3):
-            for way in range(2):
-                leg(view, way, 0).start()
-        for step in range(1, last + 1):
-            for view in range(3):
-                for way in range(2 if step < last else 1):
-                    own_copy(view, way, step).start()
-
-        def ring_step(step):
-            for view in range(3):
-                for way in range(2):
-                    own_copy(view, way, step).wait()
-                    leg(view, way, step - 1).wait_recv()
-                    full = full_sent[view]
-                    if step > 1:
-                        value = full[step - 1, way].astype(f32)
-                        value = value + full_came[view][step - 2, way].astype(f32)
-                        full[step - 1, way] = value.astype(bf)
-                    elif view == 0:
-                        units = slice(way * pair, (way + 1) * pair)
-                        value = full[0, way, units].astype(f32) + half_came[0][way].astype(f32)
-                        full[0, way, units] = value.astype(bf)
-                    else:
-                        columns = slice(way * pair * half, (way + 1) * pair * half)
-                        value = full[0, way, :, :, :, columns].astype(f32)
-                        value = value + half_came[view][way].astype(f32)
-                        full[0, way, :, :, :, columns] = value.astype(bf)
-                    leg(view, way, step).start()
-
-    if has_tokens:
-        own_tokens = pltpu.make_async_copy(tokens_ref, tokens_out.at[seq_index], token_own)
-        own_tokens.start()
-        pass_on, finish = spread_blocks(
-            tokens_ref, tokens_out, chips, chip, core, dp_index, sibling,
-            token_send, token_recv, token_pass, token_take,
-        )
+    sums = [
+        BandSum(band, owns, out, memory, chips, chip, core, dp_index, n_dp)
+        for band, out, memory in zip(bands, outs, scratch)
+    ]
+    sums[0].start()
 
     def between(step):
         if step == 0:
-            if band:
-                for ring_at in range(1, last):
-                    ring_step(ring_at)
-            if has_tokens:
-                pass_on()
-
-    if n_sums:
-        totals = column_sums(
-            x_refs, takens, sents, cames, z_send, z_recv, x_pass, x_take, between
+            sums[0].steps()
+            for later in sums[1:]:
+                later.start()
+
+    norm_two_grad, ff_sum = column_sums(
+        x_refs, takens, sents, cames, z_send, z_recv, x_pass, x_take, between
+    )
+    ff_out[...] = ff_sum
+    residual = residual_ref[...]
+    center = residual - jnp.mean(residual, axis=-1, keepdims=True)
+    variance = jnp.mean(center * center, axis=-1, keepdims=True)
+    scale_inv = lax.rsqrt(variance + norm_eps)
+    grad = norm_back(center * scale_inv, scale_inv, norm_two_grad) + cot_ref[...].astype(f32)
+    grad_out[...] = grad
+    stage[...] = grad.astype(bf)
+    own_tokens = pltpu.make_async_copy(stage, tokens_out.at[seq_index], token_own)
+    own_tokens.start()
+    pass_on, finish_tokens = spread_blocks(
+        stage, tokens_out, chips, chip, core, dp_index, sibling,
+        token_send, token_recv, token_pass, token_take,
+    )
+    for later in sums[1:]:
+        later.steps()
+    sums[0].finish()
+    along = []
+    if late_slots:
+        late_stage, late_send, late_recv, late_own = take(4)
+        ug_ref, down_ref = outs[0]
+        blocks, size, width = down_ref.shape
+        wide = ug_ref.shape[2]
+        for k in range(n_dp * late_slots):
+            unit = info[k]
+            is_down = unit >= 4 + 2 * blocks
+            for g in range(n_dp):
+                rows = slice(g * size, (g + 1) * size)
+                value = ug_ref[jnp.clip(unit - 4, 0, 2 * blocks - 1), rows, :]
+                other = down_ref[
+                    jnp.clip(unit - 4 - 2 * blocks, 0, blocks - 1), :, g * wide : (g + 1) * wide
+                ]
+                use_other = jnp.full(value.shape, is_down.astype(jnp.int32), jnp.int32) != 0
+                late_stage[k // late_slots, k % late_slots, rows, :] = jnp.where(
+                    use_other, other, value
+                )
+        for k in range(1, n_dp):
+            target = lax.rem(dp_index + k, n_dp)
+            along.append(
+                send(
+                    late_stage.at[target],
+                    late_out.at[dp_index],
+                    late_send.at[k],
+                    late_recv.at[k],
+                    (target, seq_index),
+                )
+            )
+        along.append(
+            pltpu.make_async_copy(late_stage.at[dp_index], late_out.at[dp_index], late_own)
         )
-        for out, total in zip(x_outs, totals):
-            out[...] = total
-    else:
-        between(0)
-    if has_tokens:
-        own_tokens.wait()
-        finish()
-    if not band:
-        return
-    for view in range(3):
-        own_copy(view, 0, last).wait()
-        for way in range(2):
-            leg(view, way, last - 1).wait_recv()
-        if last > 1:
-            came = [full_came[view][last - 2, way].astype(f32) for way in range(2)]
-            value = mine[view][...].astype(f32) + came[0] + came[1]
-        else:
-            axis = 0 if view == 0 else 3
-            came = [half_came[view][way].astype(f32) for way in range(2)]
-            value = mine[view][...].astype(f32) + jnp.concatenate(came, axis=axis)
-        value = value.astype(bf)
-        if view == 0:
-            down_out[...] = value
-            continue
-        value = value.reshape(2, n_dp * size, blocks * half)
-        for k in range(blocks):
-            unit = (view - 1) * blocks + k
-
-            @pl.when(core == 0)
-            def _():
-                ug_out[unit, :, :half] = value[0, :, k * half : (k + 1) * half]
-                side_out[unit] = value[1, :, k * half : (k + 1) * half]
-
-            @pl.when(core != 0)
-            def _():
-                ug_out[unit, :, half:] = value[1, :, k * half : (k + 1) * half]
-                side_out[unit] = value[0, :, k * half : (k + 1) * half]
-
-    place = pl.ds(pl.multiple_of(core * half, half), half)
-    side = send(side_out, ug_out.at[:, :, place], side_send, side_recv, sibling)
-    side.start()
-    side.wait()
-    for step in range(last):
-        for view in range(3):
-            for way in range(2):
-                leg(view, way, step).wait_send()
-
-
-def sum_grads(band, sums, xs, tokens, shape, collective_id):
-    n_dp, shard, width = shape
+        for copy in along:
+            copy.start()
+    pass_on()
+    for later in sums[1:]:
+        later.finish()
+    for band in sums:
+        band.close()
+    own_tokens.wait()
+    finish_tokens()
+    for copy in along:
+        copy.wait()
+
+
+def sum_grads(bands, late_units, residual, cot, sums, xs, collective_id):
+    _, n_dp, shard, width = xs[0].shape
     chips = lax.axis_size("seq") // 2
     steps = chips // 2
     vmem = pltpu.VMEM
-    operands, in_specs, out_shape, out_specs = [], [], [], []
-    count = len(xs)
-    scratch = []
-    if count:
-        scratch += [vmem((n_dp, shard, width), bf)] * (2 * count)
-        scratch += [vmem((n_dp + 1, shard, width), bf)] * count
-        scratch += [DMA((count, 2, n_dp))] * 2 + [DMA((count, n_dp))] * 2
-    if tokens is not None:
-        scratch += [DMA] + [DMA((chips,))] * 4
-    if band:
-        size = band[1]
-        blocks = sums[0].shape[0]
-        wide = sums[1].shape[-1]
-        half = wide // blocks
-        operands += sums
-        in_specs += [ANY] * 3
+    blocks = sums[0].shape[0]
+    wide = sums[1].shape[-1]
+    half = wide // blocks
+    late_slots = late_units.shape[1]
+    out_shape, out_specs, scratch = [], [], []
+    for _, size in bands:
         out_shape += [
             jax.ShapeDtypeStruct((2 * blocks, n_dp * size, 2 * half), bf),
             jax.ShapeDtypeStruct((blocks, size, width), bf),
@@ -929,25 +985,28 @@
             DMA,
             DMA((3, 2, steps)),
         ]
-    operands += xs
-    in_specs += [VMEM] * count
-    out_shape += [jax.ShapeDtypeStruct((shard, width), f32)] * count
-    out_specs += [VMEM] * count
-    if tokens is not None:
-        operands.append(tokens)
-        in_specs.append(VMEM)
-        out_shape.append(jax.ShapeDtypeStruct((2 * chips,) + tokens.shape, bf))
+    out_shape += [jax.ShapeDtypeStruct((shard, width), f32)] * 2
+    out_shape.append(jax.ShapeDtypeStruct((2 * chips, shard, width), bf))
+    out_specs += [VMEM, VMEM, ANY]
+    scratch += [vmem((n_dp, shard, width), bf)] * 4
+    scratch += [vmem((n_dp + 1, shard, width), bf)] * 2
+    scratch += [DMA((2, 2, n_dp))] * 2 + [DMA((2, n_dp))] * 2
+    scratch += [vmem((shard, width), bf), DMA] + [DMA((chips,))] * 4
+    if late_slots:
+        piece = (n_dp, late_slots, n_dp * bands[0][1], 2 * half)
+        out_shape.append(jax.ShapeDtypeStruct(piece, bf))
         out_specs.append(ANY)
+        scratch += [vmem(piece, bf), DMA((n_dp,)), DMA((n_dp,)), DMA]
     return pl.pallas_call(
-        functools.partial(grads_kernel, band, count, tokens is not None),
+        functools.partial(grads_kernel, bands, late_slots),
         out_shape=out_shape,
-        in_specs=in_specs,
+        in_specs=[pl.BlockSpec(memory_space=pltpu.SMEM), VMEM, VMEM] + [ANY] * 3 + [VMEM] * 2,
         out_specs=out_specs,
         scratch_shapes=scratch,
-        compiler_params=comm_params(collective_id, 58),
-        cost_estimate=takes(75),
+        compiler_params=comm_params(collective_id, 60),
+        cost_estimate=takes(130),
         name="sum_grads",
-    )(*operands)
+    )(late_units.reshape(-1) if late_slots else jnp.zeros((1,), jnp.int32), residual, cot, *sums, *xs)
 
 
 def attention_back_kernel(
@@ -1586,33 +1645,25 @@
     ff_part = times(hidden_low, down_weight, 1, 0)
     column = (2, n_dp, shard_len, width)
     bands = [(0, sub // 2), (sub // 2, sub // 2)] if sub % 32 == 0 else [(0, sub)]
-    *pieces, norm_two_grad = sum_grads(
-        bands[0], sums, [norm_two_grad.astype(bf).reshape(column)], None, column[1:], 5
-    )
-    pieces = [pieces]
-    residual_grad = upstream.astype(f32) + norm_back(normed_two, inv_two, norm_two_grad)
+    back = sum_grads(
+        bands,
+        slot_unit[:, first_slots:],
+        residual,
+        upstream,
+        sums,
+        [norm_two_grad.astype(bf).reshape(column), ff_part.astype(bf).reshape(column)],
+        5,
+    )
+    pieces = [back[2 * k : 2 * k + 2] for k in range(len(bands))]
+    residual_grad, ff_out, residual_grad_all = back[2 * len(bands) : 2 * len(bands) + 3]
+    residual_grad_all = residual_grad_all.reshape(seq_len, width)
+    block_output = (residual + ff_out).astype(bf).reshape(block_input.shape)
     late_grads = []
     if late_slots:
-        send_now = arrange(slot_unit[:, first_slots:], *pieces[0], ())
-        send_now, residual_grad = lax.optimization_barrier((send_now, residual_grad))
-        late_grads.append(lax.all_to_all(send_now, "dp", 0, 0))
-    *second, ff_out, residual_grad_all = sum_grads(
-        bands[1] if len(bands) > 1 else None,
-        sums,
-        [ff_part.astype(bf).reshape(column)],
-        residual_grad.astype(bf),
-        column[1:],
-        7,
-    )
-    residual_grad_all = residual_grad_all.reshape(seq_len, width)
-    block_output = (residual + ff_out).astype(bf).reshape(block_input.shape)
-    if second:
-        pieces.append(second)
-        if late_slots:
-            send_now = arrange(slot_unit[:, first_slots:], *second, ())
-            send_now, residual_grad_all, late_grads[0] = lax.optimization_barrier(
-                (send_now, residual_grad_all, late_grads[0])
-            )
+        late_grads.append(back[-1])
+        for now in pieces[1:]:
+            send_now = arrange(slot_unit[:, first_slots:], *now, ())
+            send_now, residual_grad_all = lax.optimization_barrier((send_now, residual_grad_all))
             late_grads.append(lax.all_to_all(send_now, "dp", 0, 0))
     qkv_grad_low, qkv_wgrad, out_wgrad = attention_back(
         residual_grad_all,

time: 925 us -> 904 us (0.977)
    pallas_call x2 -> x1, Pallas kernels: 147 us -> 144 us  [sum_grads(): pl.pallas_call(functools.partial(grads_kernel, bands, late_slots), out_sh...]
    unnamed x86 -> x72, local copies, waits for them, and re-layouts: 21.6 us -> 21.5 us
  transfers between devices with their start and end apart: 5 -> 4, of which waited for: 2 -> 2; matrix products, arithmetic and copies ran while one was open for 3% -> 2% of each run, Pallas kernels for 40% -> 31%
where the time goes in v8:
time: 904 us; the launch traced here: 895 us
  Pallas kernels  731 us (81%)
  matrix products  72.6 us (8%)
  waiting for transfers between devices  28 us (3%)
  local copies, waits for them, and re-layouts  24.3 us (3%)
  between operations  14.6 us (2%)
  other arithmetic  12.5 us (1%)
  starting transfers between devices  12.2 us (1%)
    pallas_call x1, Pallas kernels, forward(): pl.pallas_call(functools.partial(forward_kernel, has_late, first_slots, f...  279 us
    pallas_call x1, Pallas kernels, sum_grads(): pl.pallas_call(functools.partial(grads_kernel, bands, late_slots), out_sh...  144 us
    pallas_call x1, Pallas kernels, front(): pl.pallas_call(front_kernel, out_shape=[jax.ShapeDtypeStruct(packed.shape...  94.4 us
    pallas_call x1, Pallas kernels, collect_attention(): pl.pallas_call(collect_kernel, out_shape=[jax.ShapeDtypeStruct((n_seq,) +...  84.3 us
    dot_general x9, matrix products, times(): lax.dot_general(left, right, (((left_axis,), (right_axis,)), ((), ())), p...  66.8 us
    pallas_call x2, Pallas kernels, adam(): pl.pallas_call(functools.partial(adam_kernel, n_dp, n_seq // 2, first_slo...  50.3 us
    pallas_call x1, Pallas kernels, sum_seq(): pl.pallas_call(sum_seq_kernel, out_shape=jax.ShapeDtypeStruct((rows, colu...  30.7 us
    all_to_all x2, waiting for transfers between devices, local(): came = lax.all_to_all(send_now, 'dp', 0, 0)  27.3 us
  transfers between devices with their start and end apart: 4, of which 2 were waited for; matrix products, arithmetic and copies ran while one was open for 2% of the time, Pallas kernels for 31%

profile of v8, /device:TPU:0, one launch (start us, length us, event | category | flops | bytes accessed | tf_op | source)
XLA Modules:
  0.0 894.8 jit_solution(17294769311379817328)
XLA Ops:
  12.4 15.6 %pack.1 = (bf16[4,4,256,512]{3,2,1,0:T(8,128)(2,1)}, bf16[4,4,256,512]{3,2,1,0:T(8,128)(2,1)}) custom-call(s32[8]{0:T(128)S(1)} %fusion.4.flags, f32[256,8,2048]{2,1,0:T(8,128)} %refs_4_.3), custom_call_target="tpu_custom_call" | custom-call | tf_op jit(solution)/shard_map/pack/pallas_call | solution.py:113
  31.0 94.4 %front.1 = (bf16[4,4,256,512]{3,2,1,0:T(8,128)(2,1)S(1)}, bf16[8,128,2048]{2,1,0:T(8,128)(2,1)S(1)}) custom-call(bf16[4,4,256,512]{3,2,1,0:T(8,128)(2,1)S(1)} %copy-done.8, bf16[128,2048]{1,0:T(8,128)(2,1)S(1)} %fusion.1.x_ref), custom_call_target="tpu_custom_call" | custom-call | bytes 270000000 | tf_op jit(solution)/shard_map/front/pallas_call | solution.py:456
  134.4 279.5 %forward.1 = (bf16[8,4,64,768]{3,2,1,0:T(8,128)(2,1)}, bf16[4,64,2048]{2,1,0:T(8,128)(2,1)}, bf16[1024,256]{1,0:T(8,128)(2,1)}, bf16[1024,256]{1,0:T(8,128)(2,1)...) custom-call(s32[40]{0:T(128)} %pad_add_fusion.refs_0_, ...), custom_call_target="tpu_custom_call" | custom-call | bytes 690000000 | tf_op jit(solution)/shard_map/forward/pallas_call | solution.py:1460
  414.0 10.1 %fusion.9 = f32[1024,1024]{1,0:T(8,128)} fusion(bf16[1024,2048]{1,0:T(8,128)(2,1)} %bitcast.97, bf16[2048,1024]{1,0:T(8,128)(2,1)} %bitcast.95), kind=kOutput, calls=%fused_computation.54 | convolution fusion | flops 4294967296 | bytes 12582912 | tf_op jit(solution)/shard_map/dot_general | solution.py:1624
  424.1 6.0 fusion.10
  430.1 10.5 %multiply_convert_fusion = (bf16[1024,1024]{1,0:T(8,128)(2,1)}, bf16[1024,1024]{1,0:T(8,128)(2,1)S(1)}, bf16[1024,1024]{1,0:T(8,128)(2,1)S(1)}) fusion(f32[1024,1024]{1,0:T(8,128)} %fusion.10, f32[1024,1024]{1,0:T(8,128)} %fusion.9, bf16[1024,2048]{1,0:T(8,128)(2,1)S(1)} %bitcast.103, bf16[1024,2048]{1,0:T(8,128)(2,1)} %bitcast.105), kind=kOutput, calls=%fused_computation.1 | convolution fusion | flops 4309647360 | bytes 23068672 | tf_op jit(solution)/shard_map/dot_general | solution.py:1624
  440.5 8.2 convolution_convert_fusion.1
  448.8 6.2 convolution_convert_fusion.4
  455.0 6.2 convolution_convert_fusion.3
  461.2 7.2 fusion.11
  468.4 6.3 convolution_convert_fusion.2
  474.7 6.1 add_convert_fusion
  480.8 144.2 %sum_grads.1 = (bf16[8,128,512]{2,1,0:T(8,128)(2,1)}, bf16[4,32,2048]{2,1,0:T(8,128)(2,1)}, bf16[8,128,512]{2,1,0:T(8,128)(2,1)}, bf16[4,32,2048]{2,1,0:T(8,128)...) custom-call(s32[16]{0:T(128)} %reshape.208.refs_0_.units, ...), custom_call_target="tpu_custom_call" | custom-call | bytes 390000000 | tf_op jit(solution)/shard_map/sum_grads/pallas_call | solution.py:1000
  627.5 5.9 arrange.3
  633.3 4.5 all-to-all-start
  642.1 22.9 %attention_back.1 = (bf16[1024,768]{1,0:T(8,128)(2,1)}, bf16[2048,768]{1,0:T(8,128)(2,1)}, bf16[256,2048]{1,0:T(8,128)(2,1)}) custom-call(bf16[1024,2048]{1,0:T(8,128)(2,1)} %bitcast.91, bf16[256,2048]{1,0:T(8,128)(2,1)} %bitcast.93, bf16[1024,256]{1,0:T(8,128)(2,1)S(1)} %copy-done.19, bf16[1024,256]{1,0:T(8,128)(2,1)S(1)} %copy-done.20, ...), custom_call_target="tpu_custom_call" | custom-call | bytes 105000000 | tf_op jit(solution)/shard_map/attention_back/pallas_call | solution.py:1087
  668.1 84.3 %collect_attention.1 = (bf16[8,64,768]{2,1,0:T(8,128)(2,1)S(1)}, bf16[64,2048]{1,0:T(8,128)(2,1)S(1)}) custom-call(bf16[8,4,64,768]{3,2,1,0:T(8,128)(2,1)S(1)} %bitcast.80, bf16[4,64,2048]{2,1,0:T(8,128)(2,1)S(1)} %bitcast.81), custom_call_target="tpu_custom_call" | custom-call | bytes 225000000 | tf_op jit(solution)/shard_map/collect_attention/pallas_call | solution.py:564
  755.8 4.1 all-to-all-start.1
  759.9 5.8 convolution_convert_fusion
  765.8 30.7 %sum_seq.1 = f32[128,2048]{1,0:T(8,128)S(1)} custom-call(bf16[8,128,2048]{2,1,0:T(8,128)(2,1)S(1)} %bitcast.78), custom_call_target="tpu_custom_call" | custom-call | bytes 84000000 | tf_op jit(solution)/shard_map/sum_seq/pallas_call | solution.py:507
  799.2 9.9 %all-to-all-done.1.refs_0_ = bf16[4,4,128,512]{3,2,1,0:T(8,128)(2,1)S(1)} async-done(((bf16[4,4,128,512]{3,2,1,0:T(8,128)(2,1)}), bf16[4,4,128,512]{3,2,1,0:T(8,128)(2,1)S(1)}, u32[]{:S(2)}, u32[]{:S(2)}) %all-to-all-start.1) | async-done | bytes 2097184 | tf_op jit(solution)/shard_map/all_to_all | solution.py:1699
  818.2 25.2 %adam.2 = (f32[256,8,2048]{2,1,0:T(8,128)}, f32[256,8,2048]{2,1,0:T(8,128)}, f32[256,8,2048]{2,1,0:T(8,128)}, f32[256,8,2048]{2,1,0:T(8,128)}) custom-call(s32[8]{0:T(128)S(1)} %get-tuple-element.97.kinds, bf16[4,4,128,512]{3,2,1,0:T(8,128)(2,1)S(1)} %copy-done.1, bf16[4,4,128,512]{3,2,1,0:T(8,128)(2,1)} %get-tuple-element.85.refs_1_, ...), custom_call_target="tpu_custom_call" | custom-call | bytes 75000000 | tf_op jit(solution)/shard_map/adam/pallas_call | solution.py:196
  845.2 17.4 %all-to-all-done.2.refs_0_ = bf16[4,4,128,512]{3,2,1,0:T(8,128)(2,1)S(1)} async-done(((bf16[4,4,128,512]{3,2,1,0:T(8,128)(2,1)}), bf16[4,4,128,512]{3,2,1,0:T(8,128)(2,1)S(1)}, u32[]{:S(2)}, u32[]{:S(2)}) %all-to-all-start.2) | async-done | bytes 2097184 | tf_op jit(solution)/shard_map/all_to_all | solution.py:1699
  862.5 25.2 %adam.3 = (f32[256,8,2048]{2,1,0:T(8,128)}, f32[256,8,2048]{2,1,0:T(8,128)}, f32[256,8,2048]{2,1,0:T(8,128)}, f32[256,8,2048]{2,1,0:T(8,128)}) custom-call(s32[8]{0:T(128)S(1)} %get-tuple-element.97.kinds, bf16[4,4,128,512]{3,2,1,0:T(8,128)(2,1)S(1)} %all-to-all-done.2.refs_0_, ...), custom_call_target="tpu_custom_call", output_to_operand_aliasing={{0}: (9, {}), {1}: (10, {}), {2}: (11, {}), {3}: (12, {})} | custom-call | bytes 75000000 | tf_op jit(solution)/shard_map/adam/pallas_call | solution.py:196
  (114 shorter events, 43.8 us)
Async XLA Ops:
  7.2 127.3 %all-gather.2.cloned.1.call-start = ((), (), s32[]{:S(2)}) async-start(), calls=%async_computation.3 | async-start | bytes 2621440 | tf_op jit(solution)/shard_map/all_gather | solution.py:1572
  11.4 16.7 %copy-start.23 = (s32[1024]{0:T(1024)}, s32[1024]{0:T(1024)S(1)}, u32[]{:S(2)}) copy-start(s32[1024]{0:T(1024)S(1)} %convert_reduce_fusion.1) | copy-start | bytes 12292
  12.4 15.6 %copy-start.26 = (bf16[1,128,2048]{2,1,0:T(8,128)(2,1)S(1)}, bf16[1,128,2048]{2,1,0:T(8,128)(2,1)}, u32[]{:S(2)}) copy-start(bf16[1,128,2048]{2,1,0:T(8,128)(2,1)} %param.7) | copy-start | bytes 1572868
  413.9 10.1 %copy-start.30 = (bf16[2,4,128,2048]{3,2,1,0:T(8,128)(2,1)S(1)}, bf16[2,4,128,2048]{3,2,1,0:T(8,128)(2,1)}, u32[]{:S(2)}) copy-start(bf16[2,4,128,2048]{3,2,1,0:T(8,128)(2,1)} %get-tuple-element.55) | copy-start | bytes 12582916
  413.9 10.1 %copy-start.31 = (bf16[4,2,256,1024]{3,2,1,0:T(8,128)(2,1)S(1)}, bf16[4,2,256,1024]{3,2,1,0:T(8,128)(2,1)}, u32[]{:S(2)}) copy-start(bf16[4,2,256,1024]{3,2,1,0:T(8,128)(2,1)} %get-tuple-element.57) | copy-start | bytes 12582916
  461.2 7.2 copy-start.34
  468.4 6.3 copy-start.29
  468.4 6.3 copy-start.33
  468.4 6.3 copy-start.35
  480.8 144.3 %copy-start.25 = (s32[16]{0:T(128)S(1)}, s32[16]{0:T(128)}, u32[]{:S(2)}) copy-start(s32[16]{0:T(128)} %reshape.208.refs_0_.units) | copy-start | bytes 196
  480.8 157.1 %copy-start.24 = (s32[1024]{0:T(1024)S(1)}, s32[1024]{0:T(1024)}, u32[]{:S(2)}) copy-start(s32[1024]{0:T(1024)} %copy-done.23) | copy-start | bytes 12292
  625.0 12.9 %copy-start.5 = (s32[1024,1]{1,0:T(8,128)S(1)}, s32[1024,1]{1,0:T(8,128)}, u32[]{:S(2)}) copy-start(s32[1024,1]{1,0:T(8,128)} %copy.21.refs_7_.doc_col) | copy-start | bytes 12292
  625.0 12.8 %copy-start.6 = (f32[1024,128]{1,0:T(8,128)S(1)}, f32[1024,128]{1,0:T(8,128)}, u32[]{:S(2)}) copy-start(f32[1024,128]{1,0:T(8,128)} %get-tuple-element.113.refs_4_.cos_ref) | copy-start | bytes 1572868
  625.1 12.8 %copy-start.7 = (f32[1024,128]{1,0:T(8,128)S(1)}, f32[1024,128]{1,0:T(8,128)}, u32[]{:S(2)}) copy-start(f32[1024,128]{1,0:T(8,128)} %get-tuple-element.114.refs_5_.sin_ref) | copy-start | bytes 1572868
  633.3 122.5 %all-to-all-start = ((bf16[4,4,128,512]{3,2,1,0:T(8,128)(2,1)}), bf16[4,4,128,512]{3,2,1,0:T(8,128)(2,1)}, u32[]{:S(2)}, u32[]{:S(2)}) async-start(bf16[4,4,128,512]{3,2,1,0:T(8,128)(2,1)} %bitcast.20), calls=%async_computation | async-start | bytes 4194304 | tf_op jit(solution)/shard_map/all_to_all | solution.py:1667
  642.1 111.1 %copy-start.15 = (bf16[8,128,512]{2,1,0:T(8,128)(2,1)S(1)}, bf16[8,128,512]{2,1,0:T(8,128)(2,1)}, u32[]{:S(2)}) copy-start(bf16[8,128,512]{2,1,0:T(8,128)(2,1)} %get-tuple-element.76.ug_ref) | copy-start | bytes 3145732
  642.1 111.1 %copy-start.17 = (bf16[4,32,2048]{2,1,0:T(8,128)(2,1)S(1)}, bf16[4,32,2048]{2,1,0:T(8,128)(2,1)}, u32[]{:S(2)}) copy-start(bf16[4,32,2048]{2,1,0:T(8,128)(2,1)} %get-tuple-element.77.down_ref) | copy-start | bytes 1572868
  755.8 53.3 %all-to-all-start.1 = ((bf16[4,4,128,512]{3,2,1,0:T(8,128)(2,1)}), bf16[4,4,128,512]{3,2,1,0:T(8,128)(2,1)S(1)}, u32[]{:S(2)}, u32[]{:S(2)}) async-start(bf16[4,4,128,512]{3,2,1,0:T(8,128)(2,1)} %bitcast.77), calls=%async_computation.1 | async-start | bytes 4194304 | tf_op jit(solution)/shard_map/all_to_all | solution.py:1699
  765.8 30.8 %copy-start.10 = (bf16[8,128,512]{2,1,0:T(8,128)(2,1)S(1)}, bf16[8,128,512]{2,1,0:T(8,128)(2,1)}, u32[]{:S(2)}) copy-start(bf16[8,128,512]{2,1,0:T(8,128)(2,1)} %get-tuple-element.62.ug_ref) | copy-start | bytes 3145732
  765.8 30.8 %copy-start.14 = (bf16[4,32,2048]{2,1,0:T(8,128)(2,1)S(1)}, bf16[4,32,2048]{2,1,0:T(8,128)(2,1)}, u32[]{:S(2)}) copy-start(bf16[4,32,2048]{2,1,0:T(8,128)(2,1)} %get-tuple-element.63.down_ref) | copy-start | bytes 1572868
  765.8 30.8 %copy-start.18 = (bf16[32,2048]{1,0:T(8,128)(2,1)S(1)}, bf16[32,2048]{1,0:T(8,128)(2,1)}, u32[]{:S(2)}) copy-start(bf16[32,2048]{1,0:T(8,128)(2,1)} %get-tuple-element.104.refs_1_) | copy-start | bytes 393220
  810.5 52.1 %all-to-all-start.2 = ((bf16[4,4,128,512]{3,2,1,0:T(8,128)(2,1)}), bf16[4,4,128,512]{3,2,1,0:T(8,128)(2,1)S(1)}, u32[]{:S(2)}, u32[]{:S(2)}) async-start(bf16[4,4,128,512]{3,2,1,0:T(8,128)(2,1)} %bitcast.76), calls=%async_computation.2 | async-start | bytes 4194304 | tf_op jit(solution)/shard_map/all_to_all | solution.py:1699
  818.2 25.2 %copy-start.27 = (bf16[1,128,2048]{2,1,0:T(8,128)(2,1)S(1)}, bf16[1,128,2048]{2,1,0:T(8,128)(2,1)}, u32[]{:S(2)}) copy-start(bf16[1,128,2048]{2,1,0:T(8,128)(2,1)} %param.7) | copy-start | bytes 1572868
  818.2 25.5 %copy-start.28 = (f32[128,2048]{1,0:T(8,128)S(1)}, f32[128,2048]{1,0:T(8,128)}, u32[]{:S(2)}) copy-start(f32[128,2048]{1,0:T(8,128)} %get-tuple-element.61) | copy-start | bytes 3145732
  (16 other events, 27.5 us)
Sparse Core Ops, SparseCore 0:
  9.6 102.9 all-gather.1

commit v9 on v8

--- a/solution.py
+++ b/solution.py
@@ -264,7 +264,7 @@
     )
 
 
-def relay_gather(views, place, count, device_of, send_sem, recv_sem, arrived, between=None):
+def relay_gather(views, place, count, device_of, send_sem, recv_sem, arrived, between=None, during=None):
     def leg(view, way, step, block, target):
         ref = views[view](block)
         return send(ref, ref, send_sem.at[view, way, step], recv_sem.at[view, way, step], device_of(target))
@@ -283,6 +283,9 @@
             def _():
                 for view in range(len(views)):
                     leg(view, way, step, block, target).start()
+
+        if during:
+            during(step)
 
         for way in range(2):
             block = place - step if way == 0 else place + step
@@ -729,6 +732,205 @@
         for view in views:
             onward(view, block).wait_send()
     return totals
+
+
+def ff_kernel(
+    x_hbm, up_hbm, gate_hbm, down_hbm, cot_ref, ff_out, grad_out, down_grad, up_grad, gate_grad,
+    x_ref, up_ref, gate_ref, down_ref, cot_all, hidden, up_low, gate_low, up_factor, gate_factor, stage, narrow, grad_stage,
+    load_sem, grad_sem, stage_sem, narrow_sem, own_sem, send_sem, recv_sem, pass_sem, take_sem
+):
+    n_seq, n_dp, seq_index, dp_index = places()
+    core = lax.rem(seq_index, 2)
+    sibling = (dp_index, seq_index + 1 - 2 * core)
+    loads = [
+        pltpu.make_async_copy(src, dst, load_sem.at[k])
+        for k, (src, dst) in enumerate(
+            ((x_hbm, x_ref), (up_hbm, up_ref), (gate_hbm, gate_ref), (down_hbm, down_ref))
+        )
+    ]
+    for load in loads:
+        load.start()
+    greet([(lax.rem(dp_index + k, n_dp), seq_index) for k in range(1, n_dp)] + [sibling])
+    own = pltpu.make_async_copy(cot_ref, cot_all.at[core, dp_index], own_sem)
+    own.start()
+    own.wait()
+
+    def onward(block):
+        ref = cot_all.at[core, block]
+        return send(ref, ref, pass_sem.at[block], take_sem.at[block], sibling)
+
+    onward(dp_index).start()
+    count, width = x_ref.shape
+    columns = up_ref.shape[1]
+    shard = cot_ref.shape[0]
+    block_rows = 2 * shard
+    blocks = count // block_rows
+
+    def rows_of(b):
+        return pl.ds(pl.multiple_of(b * block_rows, block_rows), block_rows)
+
+    def times(left, right, left_axis, right_axis):
+        return lax.dot_general(
+            left, right, (((left_axis,), (right_axis,)), ((), ())), preferred_element_type=f32
+        )
+
+    def put(index, buffer, sem, value, dst):
+        slot = lax.rem(index, 2)
+
+        def copy(to):
+            return pltpu.make_async_copy(buffer.at[slot], to, sem.at[slot])
+
+        @pl.when(index >= 2)
+        def _():
+            copy(dst).wait()
+
+        buffer[slot] = value
+        copy(dst).start()
+
+    def drain(buffer, sem, dst):
+        for slot in range(2):
+            pltpu.make_async_copy(buffer.at[slot], dst, sem.at[slot]).wait()
+
+    def ahead(b, carry):
+        at = rows_of(b)
+        up = times(x_ref[at, :], up_ref[...], 1, 0)
+        gate = times(x_ref[at, :], gate_ref[...], 1, 0)
+        sig = jax.nn.sigmoid(gate)
+        silu = gate * sig
+        hidden[at, :] = (silu * up).astype(bf)
+        up_factor[at, :] = silu
+        gate_factor[at, :] = up * (sig + silu * (1.0 - sig))
+        return carry
+
+    def across(b, carry):
+        at = rows_of(b)
+        put(b, stage, stage_sem, times(hidden[at, :], down_ref[...], 1, 0).astype(bf), ff_out.at[at, :])
+        return carry
+
+    def back(place):
+        ref = cot_all.at[1 - core, place]
+        send(ref, ref, pass_sem.at[place], take_sem.at[place], sibling).wait_recv()
+        lines = [
+            pl.ds(pl.multiple_of((c * n_dp + place) * shard, shard), shard) for c in range(2)
+        ]
+
+        def both(source):
+            return jnp.concatenate([source[line, :] for line in lines], axis=0)
+
+        cot = jnp.concatenate([cot_all[c, place] for c in range(2)], axis=0)
+        hidden_grad = times(cot, down_ref[...], 1, 1)
+        up_part = (hidden_grad * both(up_factor)).astype(bf)
+        gate_part = (hidden_grad * both(gate_factor)).astype(bf)
+        value = times(up_part, up_ref[...], 1, 1) + times(gate_part, gate_ref[...], 1, 1)
+        value = value.astype(bf)
+        copies = []
+        for c, line in enumerate(lines):
+            up_low[line, :] = up_part[c * shard : (c + 1) * shard]
+            gate_low[line, :] = gate_part[c * shard : (c + 1) * shard]
+            grad_stage[c] = value[c * shard : (c + 1) * shard]
+            copies.append(
+                pltpu.make_async_copy(grad_stage.at[c], grad_out.at[line, :], grad_sem.at[c])
+            )
+            copies[c].start()
+        for copy in copies:
+            copy.wait()
+
+    def back_at(distance):
+        for place in (dp_index - distance, dp_index + distance):
+
+            @pl.when((place >= 0) & (place < n_dp))
+            def _():
+                back(place)
+
+    def work(step):
+        if step == 1:
+            for load in loads[:3]:
+                load.wait()
+            lax.fori_loop(0, blocks, ahead, 0)
+            loads[3].wait()
+        if step == 2 or n_dp == 2:
+            back(dp_index)
+        if step > 1:
+            back_at(step - 1)
+        if step == n_dp - 1:
+            lax.fori_loop(0, blocks, across, 0)
+
+    relay_gather(
+        [lambda block: cot_all.at[core, block]],
+        dp_index,
+        n_dp,
+        lambda place: (place, seq_index),
+        send_sem,
+        recv_sem,
+        lambda block: onward(block).start(),
+        during=work,
+    )
+    back_at(n_dp - 1)
+    for block in range(n_dp):
+        onward(block).wait_send()
+    down_rows = min(256, columns)
+    down_blocks = columns // down_rows
+    cot_rows = cot_all[...].reshape(count, width)
+    for b in range(down_blocks):
+        at = slice(b * down_rows, (b + 1) * down_rows)
+        value = times(hidden[:, at], cot_rows, 0, 0).astype(bf)
+        put(b + blocks, stage.at[:, pl.ds(0, down_rows)], stage_sem, value, down_grad.at[at, :])
+    side_blocks = width // 256
+    for k, (low, out) in enumerate(((up_low, up_grad), (gate_low, gate_grad))):
+        for b in range(side_blocks):
+            at = slice(b * 256, (b + 1) * 256)
+            value = times(x_ref[:, at], low[...], 0, 0).astype(bf)
+            put(k * side_blocks + b, narrow, narrow_sem, value, out.at[at, :])
+    drain(stage.at[:, pl.ds(0, down_rows)], stage_sem, down_grad.at[pl.ds(0, down_rows), :])
+    drain(narrow, narrow_sem, gate_grad.at[pl.ds(0, 256), :])
+
+
+def feed_forward(x, up, gate, down, cot, collective_id):
+    n_dp = lax.axis_size("dp")
+    count, width = x.shape
+    columns = up.shape[1]
+    shard = cot.shape[0]
+    vmem = pltpu.VMEM
+    low = lambda *shape: jax.ShapeDtypeStruct(shape, bf)
+    return pl.pallas_call(
+        ff_kernel,
+        out_shape=[
+            low(count, width),
+            low(count, width),
+            low(columns, width),
+            low(width, columns),
+            low(width, columns),
+        ],
+        in_specs=[ANY] * 4 + [VMEM],
+        out_specs=[ANY] * 5,
+        scratch_shapes=[
+            vmem((count, width), bf),
+            vmem((width, columns), bf),
+            vmem((width, columns), bf),
+            vmem((columns, width), bf),
+            vmem((2, n_dp, shard, width), bf),
+            vmem((count, columns), bf),
+            vmem((count, columns), bf),
+            vmem((count, columns), bf),
+            vmem((count, columns), f32),
+            vmem((count, columns), f32),
+            vmem((2, 2 * shard, width), bf),
+            vmem((2, 256, columns), bf),
+            vmem((2, shard, width), bf),
+            DMA((4,)),
+            DMA((2,)),
+            DMA((2,)),
+            DMA((2,)),
+            DMA,
+            DMA((1, 2, n_dp)),
+            DMA((1, 2, n_dp)),
+            DMA((n_dp,)),
+            DMA((n_dp,)),
+        ],
+        compiler_params=comm_params(collective_id, 58),
+        cost_estimate=takes(60),
+        name="feed_forward",
+    )(x, up, gate, down, cot)
 
 
 class BandSum:
@@ -1114,17 +1316,17 @@
     refs = refs[2:]
     if has_late:
         late_ref, refs = refs[0], refs[1:]
-    x1_ref, cos_ref, sin_ref, doc_row, doc_col, tokens_ref, cot_ref = refs[:7]
+    x1_ref, cos_ref, sin_ref, doc_row, doc_col, tokens_ref = refs[:6]
+    refs = (None,) + refs
     qkv_all, out_all, query_out, key_out, value_out, mixed_out, stat_out, residual_out = refs[7:15]
-    up_all, gate_all, down_all, x_all, cot_all = refs[15:20]
+    up_all, gate_all, down_all, x_all = refs[15:19]
     ug_all = (up_all, gate_all)
-    refs = refs[1:]
     att_stage, out_stage, part, taken, sent, arrived, x_stage = refs[19:26]
     mine_stage, given_stage, down_stage = refs[26:29]
-    (own_sem, a_send, a_recv, w_send, w_recv, s_pass, s_take, s_send, s_recv, cot_send, cot_recv,
+    (own_sem, a_send, a_recv, w_send, w_recv, s_pass, s_take, s_send, s_recv,
      late_send, late_recv, late_own, stage_own, side_send, side_recv, ring_send, ring_recv,
-     send_sem, recv_sem, pass_sem, take_sem) = refs[29:52]
-    late_tables = refs[52:]
+     send_sem, recv_sem, pass_sem, take_sem) = refs[29:50]
+    late_tables = refs[50:]
     n_seq, n_dp, seq_index, dp_index = places()
     chips, chip, core = n_seq // 2, seq_index // 2, lax.rem(seq_index, 2)
     sibling = (dp_index, chip * 2 + 1 - core)
@@ -1184,8 +1386,6 @@
         pltpu.make_async_copy(att_stage.at[seq_index], qkv_all.at[seq_index, dp_index], own_sem.at[0]),
         pltpu.make_async_copy(out_stage, out_all.at[dp_index], own_sem.at[1]),
     ]
-    cot_own = pltpu.make_async_copy(cot_ref, cot_all.at[core], own_sem.at[2])
-    cot_copy = send(cot_ref, cot_all.at[core], cot_send, cot_recv, sibling)
     across = []
     for k in range(1, n_seq):
         copy = send(
@@ -1199,8 +1399,6 @@
         across.append(copy)
     for copy in own:
         copy.start()
-    cot_copy.start()
-    cot_own.start()
     for copy in own:
         copy.wait()
     for copy in across:
@@ -1436,13 +1634,9 @@
         copies[k].wait_send()
     for copy in across:
         copy.wait_send()
-    cot_copy.wait_send()
-    cot_own.wait()
-    ref = cot_all.at[1 - core]
-    send(ref, ref, cot_send, cot_recv, sibling).wait_recv()
-
-
-def forward(info, first_table, late, x1, cosine, sine, doc, tokens, cot, ff_blocks, first_slots, collective_id):
+
+
+def forward(info, first_table, late, x1, cosine, sine, doc, tokens, ff_blocks, first_slots, collective_id):
     n_seq = lax.axis_size("seq")
     n_dp = lax.axis_size("dp")
     chips = n_seq // 2
@@ -1472,12 +1666,11 @@
             low(chips, 2, rows, ff_blocks * half),
             low(ff_blocks, chips, sub, width),
             low(2, n_dp, shard, width),
-            low(2, n_dp, shard, width),
         ],
         in_specs=[pl.BlockSpec(memory_space=pltpu.SMEM), VMEM]
         + [ANY] * has_late
-        + [VMEM] * 7,
-        out_specs=[VMEM] * 8 + [ANY] * 5,
+        + [VMEM] * 6,
+        out_specs=[VMEM] * 8 + [ANY] * 4,
         scratch_shapes=[
             vmem((n_seq, sub, 3 * head_cols), bf),
             vmem((sub, width), bf),
@@ -1498,8 +1691,6 @@
             DMA((chips,)),
             DMA((chips,)),
             DMA((chips,)),
-            DMA,
-            DMA,
             DMA((n_dp, n_dp)),
             DMA((n_dp, n_dp)),
             DMA((n_dp,)),
@@ -1527,7 +1718,6 @@
         doc[None, :],
         doc[:, None],
         tokens,
-        cot,
     )
 
 
@@ -1569,7 +1759,6 @@
     first_table = first_table.reshape(n_dp * first_slots, rows, wide)
     normed_one_all = normed_one_all.reshape(seq_len, width)
     upstream = cotangent.reshape(shard_len, width)
-    upstream_column = lax.all_gather(upstream, "dp", axis=0)
     positions = jnp.arange(seq_len, dtype=jnp.int32)
     cosine, sine = rope_tables(positions.astype(f32), HD)
     doc_ends = jnp.cumsum(doc_lengths[0])
@@ -1595,7 +1784,6 @@
         gate_weight,
         down_weight,
         normed_two_all,
-        upstream_all,
     ) = forward(
         info,
         first_table,
@@ -1605,7 +1793,6 @@
         sine,
         doc,
         tokens,
-        upstream_column,
         ff_blocks,
         first_slots,
         1,
@@ -1618,31 +1805,15 @@
     gate_weight = gate_weight.reshape(width, columns)
     down_weight = down_weight.reshape(columns, width)
     normed_two_all = normed_two_all.reshape(-1, width)
-    upstream_all = upstream_all.reshape(-1, width)
-
-    def times(left, right, left_axis, right_axis):
-        return lax.dot_general(
-            left, right, (((left_axis,), (right_axis,)), ((), ())), preferred_element_type=f32
-        )
-
-    up_proj = times(normed_two_all, up_weight, 1, 0)
-    gate_proj = times(normed_two_all, gate_weight, 1, 0)
-    gate_sig = jax.nn.sigmoid(gate_proj)
-    silu_value = gate_proj * gate_sig
-    hidden_low = (silu_value * up_proj).astype(bf)
-    hidden_grad = times(upstream_all, down_weight, 1, 1)
-    up_grad_low = (hidden_grad * silu_value).astype(bf)
-    gate_grad_low = (
-        hidden_grad * up_proj * (gate_sig + gate_proj * gate_sig * (1.0 - gate_sig))
-    ).astype(bf)
-    norm_two_grad = times(up_grad_low, up_weight, 1, 1) + times(gate_grad_low, gate_weight, 1, 1)
+    ff_part, norm_two_part, down_grad, up_grad, gate_grad = feed_forward(
+        normed_two_all, up_weight, gate_weight, down_weight, upstream, 7
+    )
     side = (chips, 2, n_dp, sub, columns)
     sums = [
-        times(hidden_low, upstream_all, 0, 0).astype(bf).reshape(ff_blocks, chips, sub, width),
-        times(normed_two_all, up_grad_low, 0, 0).astype(bf).reshape(side),
-        times(normed_two_all, gate_grad_low, 0, 0).astype(bf).reshape(side),
+        down_grad.reshape(ff_blocks, chips, sub, width),
+        up_grad.reshape(side),
+        gate_grad.reshape(side),
     ]
-    ff_part = times(hidden_low, down_weight, 1, 0)
     column = (2, n_dp, shard_len, width)
     bands = [(0, sub // 2), (sub // 2, sub // 2)] if sub % 32 == 0 else [(0, sub)]
     back = sum_grads(
@@ -1651,7 +1822,7 @@
         residual,
         upstream,
         sums,
-        [norm_two_grad.astype(bf).reshape(column), ff_part.astype(bf).reshape(column)],
+        [norm_two_part.reshape(column), ff_part.reshape(column)],
         5,
     )
     pieces = [back[2 * k : 2 * k + 2] for k in range(len(bands))]

time: 904 us -> 869 us (0.961)
  matrix products: 72.6 us -> 5.81 us
  Pallas kernels: 731 us -> 774 us
  between operations: 14.6 us -> 1.17 us
    dot_general x9 -> x0, matrix products: 66.8 us -> none  [times(): lax.dot_general(left, right, (((left_axis,), (right_axis,)), ((), ())), p...]
    pallas_call x0 -> x1, Pallas kernels: none -> 64.9 us  [feed_forward(): pl.pallas_call(ff_kernel, out_shape=[low(count, width), low(count, width)...]
    pallas_call x1, Pallas kernels: 94.4 us -> 75.1 us  [front(): pl.pallas_call(front_kernel, out_shape=[jax.ShapeDtypeStruct(packed.shape...]
    unnamed x72 -> x56, local copies, waits for them, and re-layouts: 21.5 us -> 21.5 us
  transfers between devices with their start and end apart: 4 -> 3, of which waited for: 2 -> 2; matrix products, arithmetic and copies ran while one was open for 2% -> 1% of each run, Pallas kernels for 31% -> 19%
where the time goes in v9:
time: 869 us; the launch traced here: 862 us
  Pallas kernels  774 us (89%)
  waiting for transfers between devices  26.9 us (3%)
  local copies, waits for them, and re-layouts  24.2 us (3%)
  other arithmetic  16.7 us (2%)
  starting transfers between devices  13.4 us (2%)
    pallas_call x1, Pallas kernels, forward(): pl.pallas_call(functools.partial(forward_kernel, has_late, first_slots, f...  276 us
    pallas_call x1, Pallas kernels, sum_grads(): pl.pallas_call(functools.partial(grads_kernel, bands, late_slots), out_sh...  144 us
    pallas_call x1, Pallas kernels, collect_attention(): pl.pallas_call(collect_kernel, out_shape=[jax.ShapeDtypeStruct((n_seq,) +...  83.5 us
    pallas_call x1, Pallas kernels, front(): pl.pallas_call(front_kernel, out_shape=[jax.ShapeDtypeStruct(packed.shape...  75.1 us
    pallas_call x1, Pallas kernels, feed_forward(): pl.pallas_call(ff_kernel, out_shape=[low(count, width), low(count, width)...  64.9 us
    pallas_call x2, Pallas kernels, adam(): pl.pallas_call(functools.partial(adam_kernel, n_dp, n_seq // 2, first_slo...  51 us
    pallas_call x1, Pallas kernels, sum_seq(): pl.pallas_call(sum_seq_kernel, out_shape=jax.ShapeDtypeStruct((rows, colu...  31.4 us
    all_to_all x2, waiting for transfers between devices, local(): came = lax.all_to_all(send_now, 'dp', 0, 0)  26.9 us
  transfers between devices with their start and end apart: 3, of which 2 were waited for; matrix products, arithmetic and copies ran while one was open for 1% of the time, Pallas kernels for 19%

profile of v9, /device:TPU:0, one launch (start us, length us, event | category | flops | bytes accessed | tf_op | source)
XLA Modules:
  0.0 862.1 jit_solution(7667122484420812957)
XLA Ops:
  3.4 2.1 convert_bitcast_fusion.refs_8_
  11.2 1.9 multiply_sine_fusion
  14.4 16.0 %pack.1 = (bf16[4,4,256,512]{3,2,1,0:T(8,128)(2,1)}, bf16[4,4,256,512]{3,2,1,0:T(8,128)(2,1)}) custom-call(s32[8]{0:T(128)S(1)} %fusion.3.flags, f32[256,8,2048]{2,1,0:T(8,128)} %refs_4_.3), custom_call_target="tpu_custom_call" | custom-call | tf_op jit(solution)/shard_map/pack/pallas_call | solution.py:113
  30.4 2.2 copy-done.9
  32.6 75.1 %front.1 = (bf16[4,4,256,512]{3,2,1,0:T(8,128)(2,1)S(1)}, bf16[8,128,2048]{2,1,0:T(8,128)(2,1)S(1)}) custom-call(bf16[4,4,256,512]{3,2,1,0:T(8,128)(2,1)S(1)} %copy-done.9, bf16[128,2048]{1,0:T(8,128)(2,1)S(1)} %fusion.x_ref), custom_call_target="tpu_custom_call" | custom-call | bytes 270000000 | tf_op jit(solution)/shard_map/front/pallas_call | solution.py:459
  107.8 2.0 copy-done.2
  109.8 2.0 copy-done.8
  112.5 276.3 %forward.1 = (bf16[8,4,64,768]{3,2,1,0:T(8,128)(2,1)}, bf16[4,64,2048]{2,1,0:T(8,128)(2,1)}, bf16[1024,256]{1,0:T(8,128)(2,1)}, bf16[1024,256]{1,0:T(8,128)(2,1)...) custom-call(s32[40]{0:T(128)} %pad_add_fusion.refs_0_, ...), custom_call_target="tpu_custom_call" | custom-call | bytes 690000000 | tf_op jit(solution)/shard_map/forward/pallas_call | solution.py:1654
  388.8 64.9 %feed_forward.1 = (bf16[1024,2048]{1,0:T(8,128)(2,1)}, bf16[1024,2048]{1,0:T(8,128)(2,1)}, bf16[1024,2048]{1,0:T(8,128)(2,1)}, bf16[2048,1024]{1,0:T(8,128)(2,1)}, bf16[2048,1024]{1,0:T(8,128)(2,1)}) custom-call(bf16[1024,2048]{1,0:T(8,128)(2,1)} %bitcast.76, bf16[2048,1024]{1,0:T(8,128)(2,1)} %bitcast.73, bf16[2048,1024]{1,0:T(8,128)(2,1)} %bitcast.74, ...), custom_call_target="tpu_custom_call" | custom-call | bytes 180000000 | tf_op jit(solution)/shard_map/feed_forward/pallas_call | solution.py:895
  453.7 144.2 %sum_grads.1 = (bf16[8,128,512]{2,1,0:T(8,128)(2,1)}, bf16[4,32,2048]{2,1,0:T(8,128)(2,1)}, bf16[8,128,512]{2,1,0:T(8,128)(2,1)}, bf16[4,32,2048]{2,1,0:T(8,128)...) custom-call(s32[16]{0:T(128)} %reshape.205.refs_0_.units, ...), custom_call_target="tpu_custom_call" | custom-call | bytes 390000000 | tf_op jit(solution)/shard_map/sum_grads/pallas_call | solution.py:1202
  600.3 5.9 arrange.3
  606.2 5.5 all-to-all-start
  616.0 22.9 %attention_back.1 = (bf16[1024,768]{1,0:T(8,128)(2,1)}, bf16[2048,768]{1,0:T(8,128)(2,1)}, bf16[256,2048]{1,0:T(8,128)(2,1)}) custom-call(bf16[1024,2048]{1,0:T(8,128)(2,1)} %bitcast.72, bf16[256,2048]{1,0:T(8,128)(2,1)} %bitcast.79, bf16[1024,256]{1,0:T(8,128)(2,1)S(1)} %copy-done.19, bf16[1024,256]{1,0:T(8,128)(2,1)S(1)} %copy-done.20, ...), custom_call_target="tpu_custom_call" | custom-call | bytes 105000000 | tf_op jit(solution)/shard_map/attention_back/pallas_call | solution.py:1289
  639.0 1.9 copy-done.12
  642.1 83.5 %collect_attention.1 = (bf16[8,64,768]{2,1,0:T(8,128)(2,1)S(1)}, bf16[64,2048]{1,0:T(8,128)(2,1)S(1)}) custom-call(bf16[8,4,64,768]{3,2,1,0:T(8,128)(2,1)S(1)} %bitcast.61, bf16[4,64,2048]{2,1,0:T(8,128)(2,1)S(1)} %bitcast.62), custom_call_target="tpu_custom_call" | custom-call | bytes 225000000 | tf_op jit(solution)/shard_map/collect_attention/pallas_call | solution.py:567
  729.0 4.3 all-to-all-start.1
  733.3 5.8 convolution_convert_fusion
  739.1 31.4 %sum_seq.1 = f32[128,2048]{1,0:T(8,128)S(1)} custom-call(bf16[8,128,2048]{2,1,0:T(8,128)(2,1)S(1)} %bitcast.60), custom_call_target="tpu_custom_call" | custom-call | bytes 84000000 | tf_op jit(solution)/shard_map/sum_seq/pallas_call | solution.py:510
  773.2 9.5 %all-to-all-done.1.refs_0_ = bf16[4,4,128,512]{3,2,1,0:T(8,128)(2,1)S(1)} async-done(((bf16[4,4,128,512]{3,2,1,0:T(8,128)(2,1)}), bf16[4,4,128,512]{3,2,1,0:T(8,128)(2,1)S(1)}, u32[]{:S(2)}, u32[]{:S(2)}) %all-to-all-start.1) | async-done | bytes 2097184 | tf_op jit(solution)/shard_map/all_to_all | solution.py:1870
  784.0 3.6 all-to-all-start.2
  787.7 2.5 fusion.1
  791.8 25.5 %adam.2 = (f32[256,8,2048]{2,1,0:T(8,128)}, f32[256,8,2048]{2,1,0:T(8,128)}, f32[256,8,2048]{2,1,0:T(8,128)}, f32[256,8,2048]{2,1,0:T(8,128)}) custom-call(s32[8]{0:T(128)S(1)} %get-tuple-element.105.kinds, bf16[4,4,128,512]{3,2,1,0:T(8,128)(2,1)S(1)} %copy-done.1, bf16[4,4,128,512]{3,2,1,0:T(8,128)(2,1)} %get-tuple-element.93.refs_1_, ...), custom_call_target="tpu_custom_call" | custom-call | bytes 75000000 | tf_op jit(solution)/shard_map/adam/pallas_call | solution.py:196
  819.0 17.3 %all-to-all-done.2.refs_0_ = bf16[4,4,128,512]{3,2,1,0:T(8,128)(2,1)S(1)} async-done(((bf16[4,4,128,512]{3,2,1,0:T(8,128)(2,1)}), bf16[4,4,128,512]{3,2,1,0:T(8,128)(2,1)S(1)}, u32[]{:S(2)}, u32[]{:S(2)}) %all-to-all-start.2) | async-done | bytes 2097184 | tf_op jit(solution)/shard_map/all_to_all | solution.py:1870
  836.4 25.5 %adam.3 = (f32[256,8,2048]{2,1,0:T(8,128)}, f32[256,8,2048]{2,1,0:T(8,128)}, f32[256,8,2048]{2,1,0:T(8,128)}, f32[256,8,2048]{2,1,0:T(8,128)}) custom-call(s32[8]{0:T(128)S(1)} %get-tuple-element.105.kinds, bf16[4,4,128,512]{3,2,1,0:T(8,128)(2,1)S(1)} %all-to-all-done.2.refs_0_, ...), custom_call_target="tpu_custom_call", output_to_operand_aliasing={{0}: (9, {}), {1}: (10, {}), {2}: (11, {}), {3}: (12, {})} | custom-call | bytes 75000000 | tf_op jit(solution)/shard_map/adam/pallas_call | solution.py:196
  (87 shorter events, 29.0 us)
Async XLA Ops:
  8.8 21.6 %copy-start.23 = (s32[1024]{0:T(1024)}, s32[1024]{0:T(1024)S(1)}, u32[]{:S(2)}) copy-start(s32[1024]{0:T(1024)S(1)} %convert_reduce_fusion.1) | copy-start | bytes 12292
  30.4 2.2 copy-start.9
  107.8 2.0 copy-start.2
  109.8 2.0 copy-start.8
  453.7 144.2 %copy-start.25 = (s32[16]{0:T(128)S(1)}, s32[16]{0:T(128)}, u32[]{:S(2)}) copy-start(s32[16]{0:T(128)} %reshape.205.refs_0_.units) | copy-start | bytes 196
  453.7 158.1 %copy-start.24 = (s32[1024]{0:T(1024)S(1)}, s32[1024]{0:T(1024)}, u32[]{:S(2)}) copy-start(s32[1024]{0:T(1024)} %copy-done.23) | copy-start | bytes 12292
  597.9 13.9 %copy-start.5 = (s32[1024,1]{1,0:T(8,128)S(1)}, s32[1024,1]{1,0:T(8,128)}, u32[]{:S(2)}) copy-start(s32[1024,1]{1,0:T(8,128)} %copy.19.refs_7_.doc_col) | copy-start | bytes 12292
  597.9 13.9 %copy-start.6 = (f32[1024,128]{1,0:T(8,128)S(1)}, f32[1024,128]{1,0:T(8,128)}, u32[]{:S(2)}) copy-start(f32[1024,128]{1,0:T(8,128)} %get-tuple-element.118.refs_4_.cos_ref) | copy-start | bytes 1572868
  597.9 13.9 %copy-start.7 = (f32[1024,128]{1,0:T(8,128)S(1)}, f32[1024,128]{1,0:T(8,128)}, u32[]{:S(2)}) copy-start(f32[1024,128]{1,0:T(8,128)} %get-tuple-element.119.refs_5_.sin_ref) | copy-start | bytes 1572868
  597.9 1.3 copy-start.10
  606.2 122.8 %all-to-all-start = ((bf16[4,4,128,512]{3,2,1,0:T(8,128)(2,1)}), bf16[4,4,128,512]{3,2,1,0:T(8,128)(2,1)}, u32[]{:S(2)}, u32[]{:S(2)}) async-start(bf16[4,4,128,512]{3,2,1,0:T(8,128)(2,1)} %bitcast.19), calls=%async_computation | async-start | bytes 4194304 | tf_op jit(solution)/shard_map/all_to_all | solution.py:1838
  616.0 110.3 %copy-start.15 = (bf16[8,128,512]{2,1,0:T(8,128)(2,1)S(1)}, bf16[8,128,512]{2,1,0:T(8,128)(2,1)}, u32[]{:S(2)}) copy-start(bf16[8,128,512]{2,1,0:T(8,128)(2,1)} %get-tuple-element.84.ug_ref) | copy-start | bytes 3145732
  616.0 110.3 %copy-start.17 = (bf16[4,32,2048]{2,1,0:T(8,128)(2,1)S(1)}, bf16[4,32,2048]{2,1,0:T(8,128)(2,1)}, u32[]{:S(2)}) copy-start(bf16[4,32,2048]{2,1,0:T(8,128)(2,1)} %get-tuple-element.85.down_ref) | copy-start | bytes 1572868
  638.9 1.9 copy-start.12
  727.7 1.3 copy-start.4
  729.0 53.7 %all-to-all-start.1 = ((bf16[4,4,128,512]{3,2,1,0:T(8,128)(2,1)}), bf16[4,4,128,512]{3,2,1,0:T(8,128)(2,1)S(1)}, u32[]{:S(2)}, u32[]{:S(2)}) async-start(bf16[4,4,128,512]{3,2,1,0:T(8,128)(2,1)} %bitcast.58), calls=%async_computation.1 | async-start | bytes 4194304 | tf_op jit(solution)/shard_map/all_to_all | solution.py:1870
  739.1 31.4 %copy-start.11 = (bf16[8,128,512]{2,1,0:T(8,128)(2,1)S(1)}, bf16[8,128,512]{2,1,0:T(8,128)(2,1)}, u32[]{:S(2)}) copy-start(bf16[8,128,512]{2,1,0:T(8,128)(2,1)} %get-tuple-element.70.ug_ref) | copy-start | bytes 3145732
  739.1 31.4 %copy-start.14 = (bf16[4,32,2048]{2,1,0:T(8,128)(2,1)S(1)}, bf16[4,32,2048]{2,1,0:T(8,128)(2,1)}, u32[]{:S(2)}) copy-start(bf16[4,32,2048]{2,1,0:T(8,128)(2,1)} %get-tuple-element.71.down_ref) | copy-start | bytes 1572868
  739.1 31.4 %copy-start.18 = (bf16[32,2048]{1,0:T(8,128)(2,1)S(1)}, bf16[32,2048]{1,0:T(8,128)(2,1)}, u32[]{:S(2)}) copy-start(bf16[32,2048]{1,0:T(8,128)(2,1)} %get-tuple-element.109.refs_1_) | copy-start | bytes 393220
  771.9 1.3 copy-start.3
  784.0 52.3 %all-to-all-start.2 = ((bf16[4,4,128,512]{3,2,1,0:T(8,128)(2,1)}), bf16[4,4,128,512]{3,2,1,0:T(8,128)(2,1)S(1)}, u32[]{:S(2)}, u32[]{:S(2)}) async-start(bf16[4,4,128,512]{3,2,1,0:T(8,128)(2,1)} %bitcast.57), calls=%async_computation.2 | async-start | bytes 4194304 | tf_op jit(solution)/shard_map/all_to_all | solution.py:1870
  790.2 1.6 copy-start.1
  791.8 25.5 %copy-start.26 = (bf16[1,128,2048]{2,1,0:T(8,128)(2,1)S(1)}, bf16[1,128,2048]{2,1,0:T(8,128)(2,1)}, u32[]{:S(2)}) copy-start(bf16[1,128,2048]{2,1,0:T(8,128)(2,1)} %param.7) | copy-start | bytes 1572868
  791.8 25.8 %copy-start.27 = (f32[128,2048]{1,0:T(8,128)S(1)}, f32[128,2048]{1,0:T(8,128)}, u32[]{:S(2)}) copy-start(f32[128,2048]{1,0:T(8,128)} %get-tuple-element.69) | copy-start | bytes 3145732
  (7 other events, 7.8 us)

commit v10 on v9

--- a/solution.py
+++ b/solution.py
@@ -384,7 +384,7 @@
 
 
 def front_kernel(
-    packed_ref, x_ref, table_ref, out_ref, own_sem, a_send, a_recv, send_sem, recv_sem, pass_sem, take_sem
+    packed_ref, tokens_ref, table_ref, out_ref, x_ref, own_sem, a_send, a_recv, send_sem, recv_sem, pass_sem, take_sem
 ):
     n_seq, n_dp, seq_index, dp_index = places()
     chips, chip, core = n_seq // 2, seq_index // 2, lax.rem(seq_index, 2)
@@ -407,6 +407,7 @@
         )
         copy.start()
         along.append(copy)
+    x_ref[...] = norm_parts(tokens_ref[...].astype(f32))[0].astype(bf)
     own = [
         pltpu.make_async_copy(packed_ref.at[dp_index], table_ref.at[dp_index], own_sem.at[0]),
         pltpu.make_async_copy(x_ref, out_ref.at[seq_index], own_sem.at[1]),
@@ -464,7 +465,8 @@
         ],
         in_specs=[VMEM, VMEM],
         out_specs=[ANY, ANY],
-        scratch_shapes=[DMA((2,)), DMA((n_dp,)), DMA((n_dp,))] + [DMA((chips,))] * 4,
+        scratch_shapes=[pltpu.VMEM(x.shape, bf), DMA((2,)), DMA((n_dp,)), DMA((n_dp,))]
+        + [DMA((chips,))] * 4,
         compiler_params=comm_params(collective_id, 24),
         cost_estimate=takes(90),
         name="front",
@@ -1070,6 +1072,7 @@
     outs = [take(2) for _ in bands]
     grad_out, ff_out, tokens_out = take(3)
     late_out = take(1)[0] if late_slots else None
+    next_out = take(len(bands) - 1) if late_slots else []
     scratch = [take(18) for _ in bands]
     takens, sents, cames = take(2), take(2), take(2)
     z_send, z_recv, x_pass, x_take = take(4)
@@ -1111,10 +1114,8 @@
     for later in sums[1:]:
         later.steps()
     sums[0].finish()
-    along = []
-    if late_slots:
-        late_stage, late_send, late_recv, late_own = take(4)
-        ug_ref, down_ref = outs[0]
+    def fill(pair, target_ref):
+        ug_ref, down_ref = pair
         blocks, size, width = down_ref.shape
         wide = ug_ref.shape[2]
         for k in range(n_dp * late_slots):
@@ -1127,9 +1128,14 @@
                     jnp.clip(unit - 4 - 2 * blocks, 0, blocks - 1), :, g * wide : (g + 1) * wide
                 ]
                 use_other = jnp.full(value.shape, is_down.astype(jnp.int32), jnp.int32) != 0
-                late_stage[k // late_slots, k % late_slots, rows, :] = jnp.where(
+                target_ref[k // late_slots, k % late_slots, rows, :] = jnp.where(
                     use_other, other, value
                 )
+
+    along = []
+    if late_slots:
+        late_stage, late_send, late_recv, late_own = take(4)
+        fill(outs[0], late_stage)
         for k in range(1, n_dp):
             target = lax.rem(dp_index + k, n_dp)
             along.append(
@@ -1147,8 +1153,10 @@
         for copy in along:
             copy.start()
     pass_on()
-    for later in sums[1:]:
+    for k, later in enumerate(sums[1:]):
         later.finish()
+        if late_slots:
+            fill(outs[k + 1], next_out[k])
     for band in sums:
         band.close()
     own_tokens.wait()
@@ -1198,6 +1206,8 @@
         piece = (n_dp, late_slots, n_dp * bands[0][1], 2 * half)
         out_shape.append(jax.ShapeDtypeStruct(piece, bf))
         out_specs.append(ANY)
+        out_shape += [jax.ShapeDtypeStruct(piece, bf)] * (len(bands) - 1)
+        out_specs += [VMEM] * (len(bands) - 1)
         scratch += [vmem(piece, bf), DMA((n_dp,)), DMA((n_dp,)), DMA]
     return pl.pallas_call(
         functools.partial(grads_kernel, bands, late_slots),
@@ -1413,77 +1423,6 @@
         lambda block: None,
     )
 
-    seq_len = x1_ref.shape[0]
-    heads = query_out.shape[1] // HD
-    block_rows = min(256, seq_len)
-    head_cols = heads * HD
-    qkv_weight = qkv_all[...].reshape(width, 3 * head_cols)
-
-    def project(b, carry):
-        at = pl.ds(pl.multiple_of(b * block_rows, block_rows), block_rows)
-        result = jnp.dot(x1_ref[at, :], qkv_weight, preferred_element_type=f32)
-        cosine, sine = cos_ref[at, :], sin_ref[at, :]
-        for h in range(heads):
-            place = slice(h * HD, (h + 1) * HD)
-            for part_id, out in ((0, query_out), (1, key_out)):
-                begin = part_id * head_cols + h * HD
-                values = result[:, begin : begin + HD]
-                out[at, place] = (values * cosine + turn_half(values) * sine).astype(bf)
-        value_out[at, :] = result[:, 2 * head_cols :].astype(bf)
-        return carry
-
-    lax.fori_loop(0, seq_len // block_rows, project, 0)
-
-    def attend(b, carry):
-        begin = pl.multiple_of(b * block_rows, block_rows)
-        at = pl.ds(begin, block_rows)
-        query_pos = begin + lax.broadcasted_iota(jnp.int32, (block_rows, seq_len), 0)
-        key_pos = lax.broadcasted_iota(jnp.int32, (block_rows, seq_len), 1)
-        allowed = (doc_col[at, :] == doc_row[...]) & (key_pos <= query_pos)
-        for h in range(heads):
-            place = slice(h * HD, (h + 1) * HD)
-            scores = lax.dot_general(
-                query_out[at, place],
-                key_out[:, place],
-                (((1,), (1,)), ((), ())),
-                preferred_element_type=f32,
-            )
-            scores = jnp.where(allowed, scores * (float(HD) ** (-0.5)), masked_score)
-            peak = jnp.max(scores, axis=-1, keepdims=True)
-            raised = jnp.exp(scores - peak)
-            total = jnp.sum(raised, axis=-1, keepdims=True)
-            prob = (raised * (1.0 / total)).astype(bf)
-            mixed = jnp.dot(prob, value_out[:, place], preferred_element_type=f32)
-            mixed_out[at, place] = mixed.astype(bf)
-            stat_out[at, place] = jnp.broadcast_to(peak + jnp.log(total), (block_rows, HD))
-        return carry
-
-    lax.fori_loop(0, seq_len // block_rows, attend, 0)
-    out_weight = out_all[...].reshape(rows, width)
-
-    def combine(b, carry):
-        at = pl.ds(pl.multiple_of(b * tokens, tokens), tokens)
-        part[b] = jnp.dot(mixed_out[at, :], out_weight, preferred_element_type=f32).astype(bf)
-        return carry
-
-    lax.fori_loop(0, n_seq, combine, 0)
-
-    chip_peers = [lax.rem(chip + k, chips) for k in range(chips)]
-    order = list(range(chips - 1, 0, -1)) + [0]
-    passed = {}
-    for k in order:
-        block = part.at[chip_peers[k] * 2 + 1 - core]
-        passed[k] = send(block, taken.at[k], s_pass.at[k], s_take.at[k], sibling)
-        passed[k].start()
-    copies = {}
-    for k in order[:-1]:
-        passed[k].wait_recv()
-        value = part[chip_peers[k] * 2 + core].astype(f32)
-        sent[k] = (value + taken[k].astype(f32)).astype(bf)
-        device = (dp_index, chip_peers[k] * 2 + core)
-        copies[k] = send(sent.at[k], arrived.at[k], s_send.at[k], s_recv.at[k], device)
-        copies[k].start()
-
     ring = Ring(chips, chip, core, dp_index, None, None)
     pair = ff_blocks // 2
 
@@ -1520,7 +1459,8 @@
             for copy in late_copies(c):
                 copy.wait_recv()
             late_own_copy(c).wait()
-            late_start(c + 1)
+            if c:
+                late_start(c + 1)
             table = late_tables[c]
             late_slots = table.shape[1]
         for u in range(3 * ff_blocks):
@@ -1575,7 +1515,83 @@
                 ring_leg(c, view, way, step - 1, True).wait_recv()
                 ring_leg(c, view, way, step, False).start()
 
+    late_start(1)
     begin_band(0)
+
+    seq_len = x1_ref.shape[0]
+    heads = query_out.shape[1] // HD
+    block_rows = min(256, seq_len)
+    head_cols = heads * HD
+    qkv_weight = qkv_all[...].reshape(width, 3 * head_cols)
+
+    def project(b, carry):
+        at = pl.ds(pl.multiple_of(b * block_rows, block_rows), block_rows)
+        result = jnp.dot(x1_ref[at, :], qkv_weight, preferred_element_type=f32)
+        cosine, sine = cos_ref[at, :], sin_ref[at, :]
+        for h in range(heads):
+            place = slice(h * HD, (h + 1) * HD)
+            for part_id, out in ((0, query_out), (1, key_out)):
+                begin = part_id * head_cols + h * HD
+                values = result[:, begin : begin + HD]
+                out[at, place] = (values * cosine + turn_half(values) * sine).astype(bf)
+        value_out[at, :] = result[:, 2 * head_cols :].astype(bf)
+        return carry
+
+    lax.fori_loop(0, seq_len // block_rows, project, 0)
+
+    def attend(b, carry):
+        begin = pl.multiple_of(b * block_rows, block_rows)
+        at = pl.ds(begin, block_rows)
+        query_pos = begin + lax.broadcasted_iota(jnp.int32, (block_rows, seq_len), 0)
+        key_pos = lax.broadcasted_iota(jnp.int32, (block_rows, seq_len), 1)
+        allowed = (doc_col[at, :] == doc_row[...]) & (key_pos <= query_pos)
+        for h in range(heads):
+            place = slice(h * HD, (h + 1) * HD)
+            scores = lax.dot_general(
+                query_out[at, place],
+                key_out[:, place],
+                (((1,), (1,)), ((), ())),
+                preferred_element_type=f32,
+            )
+            scores = jnp.where(allowed, scores * (float(HD) ** (-0.5)), masked_score)
+            peak = jnp.max(scores, axis=-1, keepdims=True)
+            raised = jnp.exp(scores - peak)
+            total = jnp.sum(raised, axis=-1, keepdims=True)
+            prob = (raised * (1.0 / total)).astype(bf)
+            mixed = jnp.dot(prob, value_out[:, place], preferred_element_type=f32)
+            mixed_out[at, place] = mixed.astype(bf)
+            stat_out[at, place] = jnp.broadcast_to(peak + jnp.log(total), (block_rows, HD))
+        return carry
+
+    lax.fori_loop(0, seq_len // block_rows, attend, 0)
+    out_weight = out_all[...].reshape(rows, width)
+
+    def combine(b, carry):
+        at = pl.ds(pl.multiple_of(b * tokens, tokens), tokens)
+        part[b] = jnp.dot(mixed_out[at, :], out_weight, preferred_element_type=f32).astype(bf)
+        return carry
+
+    lax.fori_loop(0, n_seq, combine, 0)
+
+    chip_peers = [lax.rem(chip + k, chips) for k in range(chips)]
+    order = list(range(chips - 1, 0, -1)) + [0]
+    passed = {}
+    for k in order:
+        block = part.at[chip_peers[k] * 2 + 1 - core]
+        passed[k] = send(block, taken.at[k], s_pass.at[k], s_take.at[k], sibling)
+        passed[k].start()
+    copies = {}
+    for k in order[:-1]:
+        passed[k].wait_recv()
+        value = part[chip_peers[k] * 2 + core].astype(f32)
+        sent[k] = (value + taken[k].astype(f32)).astype(bf)
+        device = (dp_index, chip_peers[k] * 2 + core)
+        copies[k] = send(sent.at[k], arrived.at[k], s_send.at[k], s_recv.at[k], device)
+        copies[k].start()
+
+    begin_band(1)
+    for step in range(2, ring.last + 1):
+        carry_band(0, step)
     passed[0].wait_recv()
     total = part[seq_index].astype(f32) + taken[0].astype(f32)
     for k in range(1, chips):
@@ -1586,7 +1602,7 @@
     center = residual - jnp.mean(residual, axis=-1, keepdims=True)
     spread = jnp.mean(center * center, axis=-1, keepdims=True)
     x_stage[...] = (center * lax.rsqrt(spread + norm_eps)).astype(bf)
-    for c in range(1, n_dp):
+    for c in range(2, n_dp):
         begin_band(c)
         for step in range(2, ring.last + 1):
             carry_band(c - 1, step)
@@ -1753,9 +1769,8 @@
 
 
     tokens = block_input.astype(f32).reshape(shard_len, width)
-    normed_one, inv_one = norm_parts(tokens)
     packed = pack(master, is_col.astype(jnp.int32), n_dp, n_seq, first_slots)
-    first_table, normed_one_all = front(packed[0], normed_one.astype(bf), 2)
+    first_table, normed_one_all = front(packed[0], block_input.reshape(shard_len, width), 2)
     first_table = first_table.reshape(n_dp * first_slots, rows, wide)
     normed_one_all = normed_one_all.reshape(seq_len, width)
     upstream = cotangent.reshape(shard_len, width)
@@ -1831,9 +1846,8 @@
     block_output = (residual + ff_out).astype(bf).reshape(block_input.shape)
     late_grads = []
     if late_slots:
-        late_grads.append(back[-1])
-        for now in pieces[1:]:
-            send_now = arrange(slot_unit[:, first_slots:], *now, ())
+        late_grads.append(back[2 * len(bands) + 3])
+        for send_now in back[2 * len(bands) + 4 :]:
             send_now, residual_grad_all = lax.optimization_barrier((send_now, residual_grad_all))
             late_grads.append(lax.all_to_all(send_now, "dp", 0, 0))
     qkv_grad_low, qkv_wgrad, out_wgrad = attention_back(
@@ -1881,6 +1895,8 @@
             kept,
         )
     owned_grads, new_first, new_second, new_master = kept
+    tokens_again, norm_one_grad = lax.optimization_barrier((block_input, norm_one_grad))
+    normed_one, inv_one = norm_parts(tokens_again.astype(f32).reshape(shard_len, width))
     input_grad = (residual_grad + norm_back(normed_one, inv_one, norm_one_grad)).reshape(
         block_input.shape
     )

time: 869 us -> 852 us (0.980)
  Pallas kernels: 774 us -> 765 us
    unnamed x56 -> x52, local copies, waits for them, and re-layouts: 21.5 us -> 19 us
  transfers between devices with their start and end apart: 3 -> 3, of which waited for: 2 -> 2; matrix products, arithmetic and copies ran while one was open for 1% -> 1% of each run, Pallas kernels for 19% -> 20%
where the time goes in v10:
time: 852 us; the launch traced here: 843 us
  Pallas kernels  765 us (90%)
  waiting for transfers between devices  24.6 us (3%)
  local copies, waits for them, and re-layouts  21.1 us (2%)
  other arithmetic  13.2 us (2%)
  starting transfers between devices  12.5 us (1%)
    pallas_call x1, Pallas kernels, forward(): pl.pallas_call(functools.partial(forward_kernel, has_late, first_slots, f...  268 us
    pallas_call x1, Pallas kernels, sum_grads(): pl.pallas_call(functools.partial(grads_kernel, bands, late_slots), out_sh...  146 us
    pallas_call x1, Pallas kernels, collect_attention(): pl.pallas_call(collect_kernel, out_shape=[jax.ShapeDtypeStruct((n_seq,) +...  85.1 us
    pallas_call x1, Pallas kernels, front(): pl.pallas_call(front_kernel, out_shape=[jax.ShapeDtypeStruct(packed.shape...  75.9 us
    pallas_call x1, Pallas kernels, feed_forward(): pl.pallas_call(ff_kernel, out_shape=[low(count, width), low(count, width)...  68.2 us
    pallas_call x2, Pallas kernels, adam(): pl.pallas_call(functools.partial(adam_kernel, n_dp, n_seq // 2, first_slo...  51.1 us
    pallas_call x1, Pallas kernels, sum_seq(): pl.pallas_call(sum_seq_kernel, out_shape=jax.ShapeDtypeStruct((rows, colu...  29.4 us
    all_to_all x2, waiting for transfers between devices, local(): came = lax.all_to_all(send_now, 'dp', 0, 0)  24.6 us
  transfers between devices with their start and end apart: 3, of which 2 were waited for; matrix products, arithmetic and copies ran while one was open for 1% of the time, Pallas kernels for 20%

profile of v10, /device:TPU:0, one launch (start us, length us, event | category | flops | bytes accessed | tf_op | source)
XLA Modules:
  0.0 843.5 jit_solution(6707778271720415267)
XLA Ops:
  5.2 2.1 bitcast_convert_fusion.refs_8_
  7.3 1.9 multiply_sine_fusion
  10.5 15.7 %pack.1 = (bf16[4,4,256,512]{3,2,1,0:T(8,128)(2,1)}, bf16[4,4,256,512]{3,2,1,0:T(8,128)(2,1)}) custom-call(s32[8]{0:T(128)S(1)} %fusion.13.flags, f32[256,8,2048]{2,1,0:T(8,128)} %refs_4_.3), custom_call_target="tpu_custom_call" | custom-call | tf_op jit(solution)/shard_map/pack/pallas_call | solution.py:113
  26.3 2.2 copy-done.12
  28.4 75.9 %front.1 = (bf16[4,4,256,512]{3,2,1,0:T(8,128)(2,1)S(1)}, bf16[8,128,2048]{2,1,0:T(8,128)(2,1)S(1)}) custom-call(bf16[4,4,256,512]{3,2,1,0:T(8,128)(2,1)S(1)} %copy-done.12, bf16[128,2048]{1,0:T(8,128)(2,1)S(1)} %bitcast.69), custom_call_target="tpu_custom_call" | custom-call | bytes 270000000 | tf_op jit(solution)/shard_map/front/pallas_call | solution.py:460
  104.4 2.0 copy-done.3
  106.4 2.0 copy-done.11
  109.0 267.8 %forward.1 = (bf16[8,4,64,768]{3,2,1,0:T(8,128)(2,1)}, bf16[4,64,2048]{2,1,0:T(8,128)(2,1)}, bf16[1024,256]{1,0:T(8,128)(2,1)}, bf16[1024,256]{1,0:T(8,128)(2,1)...) custom-call(s32[40]{0:T(128)} %pad_add_fusion.refs_0_, ...), custom_call_target="tpu_custom_call" | custom-call | bytes 690000000 | tf_op jit(solution)/shard_map/forward/pallas_call | solution.py:1670
  376.8 68.2 %feed_forward.1 = (bf16[1024,2048]{1,0:T(8,128)(2,1)}, bf16[1024,2048]{1,0:T(8,128)(2,1)}, bf16[1024,2048]{1,0:T(8,128)(2,1)}, bf16[2048,1024]{1,0:T(8,128)(2,1)}, bf16[2048,1024]{1,0:T(8,128)(2,1)}) custom-call(bf16[1024,2048]{1,0:T(8,128)(2,1)} %bitcast.92, bf16[2048,1024]{1,0:T(8,128)(2,1)} %bitcast.89, bf16[2048,1024]{1,0:T(8,128)(2,1)} %bitcast.90, ...), custom_call_target="tpu_custom_call" | custom-call | bytes 180000000 | tf_op jit(solution)/shard_map/feed_forward/pallas_call | solution.py:897
  445.0 146.1 %sum_grads.1 = (bf16[8,128,512]{2,1,0:T(8,128)(2,1)}, bf16[4,32,2048]{2,1,0:T(8,128)(2,1)}, bf16[8,128,512]{2,1,0:T(8,128)(2,1)}, bf16[4,32,2048]{2,1,0:T(8,128)...) custom-call(s32[16]{0:T(128)} %reshape.208.refs_0_, ...), custom_call_target="tpu_custom_call" | custom-call | bytes 390000000 | tf_op jit(solution)/shard_map/sum_grads/pallas_call | solution.py:1212
  591.2 5.1 all-to-all-start
  599.5 23.1 %attention_back.1 = (bf16[1024,768]{1,0:T(8,128)(2,1)}, bf16[2048,768]{1,0:T(8,128)(2,1)}, bf16[256,2048]{1,0:T(8,128)(2,1)}) custom-call(bf16[1024,2048]{1,0:T(8,128)(2,1)} %bitcast.88, bf16[256,2048]{1,0:T(8,128)(2,1)} %bitcast.95, bf16[1024,256]{1,0:T(8,128)(2,1)S(1)} %copy-done.19, bf16[1024,256]{1,0:T(8,128)(2,1)S(1)} %copy-done.20, ...), custom_call_target="tpu_custom_call" | custom-call | bytes 105000000 | tf_op jit(solution)/shard_map/attention_back/pallas_call | solution.py:1299
  622.6 1.9 copy-done.13
  625.7 85.1 %collect_attention.1 = (bf16[8,64,768]{2,1,0:T(8,128)(2,1)S(1)}, bf16[64,2048]{1,0:T(8,128)(2,1)S(1)}) custom-call(bf16[8,4,64,768]{3,2,1,0:T(8,128)(2,1)S(1)} %bitcast.77, bf16[4,64,2048]{2,1,0:T(8,128)(2,1)S(1)} %bitcast.78), custom_call_target="tpu_custom_call" | custom-call | bytes 225000000 | tf_op jit(solution)/shard_map/collect_attention/pallas_call | solution.py:569
  713.6 3.8 all-to-all-start.1
  717.4 5.8 convolution_convert_fusion
  723.2 29.4 %sum_seq.1 = f32[128,2048]{1,0:T(8,128)S(1)} custom-call(bf16[8,128,2048]{2,1,0:T(8,128)(2,1)S(1)} %bitcast.76), custom_call_target="tpu_custom_call" | custom-call | bytes 84000000 | tf_op jit(solution)/shard_map/sum_seq/pallas_call | solution.py:512
  756.3 8.8 %all-to-all-done.1.refs_0_ = bf16[4,4,128,512]{3,2,1,0:T(8,128)(2,1)S(1)} async-done(((bf16[4,4,128,512]{3,2,1,0:T(8,128)(2,1)}), bf16[4,4,128,512]{3,2,1,0:T(8,128)(2,1)S(1)}, u32[]{:S(2)}, u32[]{:S(2)}) %all-to-all-start.1) | async-done | bytes 2097184 | tf_op jit(solution)/shard_map/all_to_all | solution.py:1884
  766.5 3.6 all-to-all-start.2
  770.1 2.5 fusion.11
  772.6 1.6 copy-done.2
  774.2 25.6 %adam.2 = (f32[256,8,2048]{2,1,0:T(8,128)}, f32[256,8,2048]{2,1,0:T(8,128)}, f32[256,8,2048]{2,1,0:T(8,128)}, f32[256,8,2048]{2,1,0:T(8,128)}) custom-call(s32[8]{0:T(128)S(1)} %get-tuple-element.111.kinds, bf16[4,4,128,512]{3,2,1,0:T(8,128)(2,1)S(1)} %copy-done.2, bf16[4,4,128,512]{3,2,1,0:T(8,128)(2,1)} %get-tuple-element.99.refs_1_, ...), custom_call_target="tpu_custom_call" | custom-call | bytes 75000000 | tf_op jit(solution)/shard_map/adam/pallas_call | solution.py:196
  802.0 15.7 %all-to-all-done.2.refs_0_ = bf16[4,4,128,512]{3,2,1,0:T(8,128)(2,1)S(1)} async-done(((bf16[4,4,128,512]{3,2,1,0:T(8,128)(2,1)}), bf16[4,4,128,512]{3,2,1,0:T(8,128)(2,1)S(1)}, u32[]{:S(2)}, u32[]{:S(2)}) %all-to-all-start.2) | async-done | bytes 2097184 | tf_op jit(solution)/shard_map/all_to_all | solution.py:1884
  817.7 25.6 %adam.3 = (f32[256,8,2048]{2,1,0:T(8,128)}, f32[256,8,2048]{2,1,0:T(8,128)}, f32[256,8,2048]{2,1,0:T(8,128)}, f32[256,8,2048]{2,1,0:T(8,128)}) custom-call(s32[8]{0:T(128)S(1)} %get-tuple-element.111.kinds, bf16[4,4,128,512]{3,2,1,0:T(8,128)(2,1)S(1)} %all-to-all-done.2.refs_0_, ...), custom_call_target="tpu_custom_call", output_to_operand_aliasing={{0}: (9, {}), {1}: (10, {}), {2}: (11, {}), {3}: (12, {})} | custom-call | bytes 75000000 | tf_op jit(solution)/shard_map/adam/pallas_call | solution.py:196
  (81 shorter events, 20.9 us)
Async XLA Ops:
  4.2 22.1 %copy-start.23 = (s32[1024]{0:T(1024)}, s32[1024]{0:T(1024)S(1)}, u32[]{:S(2)}) copy-start(s32[1024]{0:T(1024)S(1)} %convert_reduce_fusion.1) | copy-start | bytes 12292
  10.5 15.7 %copy-start = (bf16[1,128,2048]{2,1,0:T(8,128)(2,1)S(1)}, bf16[1,128,2048]{2,1,0:T(8,128)(2,1)}, u32[]{:S(2)}) copy-start(bf16[1,128,2048]{2,1,0:T(8,128)(2,1)} %param.7) | copy-start | bytes 1572868
  26.3 2.2 copy-start.12
  104.4 2.0 copy-start.3
  106.4 2.0 copy-start.11
  591.1 5.3 copy-start.8
  591.1 5.3 copy-start.9
  591.1 5.2 copy-start.10
  591.1 5.2 copy-start.19
  591.1 5.2 copy-start.24
  591.2 122.5 %all-to-all-start = ((bf16[4,4,128,512]{3,2,1,0:T(8,128)(2,1)}), bf16[4,4,128,512]{3,2,1,0:T(8,128)(2,1)}, u32[]{:S(2)}, u32[]{:S(2)}) async-start(bf16[4,4,128,512]{3,2,1,0:T(8,128)(2,1)} %get-tuple-element.90), calls=%async_computation | async-start | bytes 4194304 | tf_op jit(solution)/shard_map/all_to_all | solution.py:1852
  599.5 111.4 %copy-start.15 = (bf16[8,128,512]{2,1,0:T(8,128)(2,1)S(1)}, bf16[8,128,512]{2,1,0:T(8,128)(2,1)}, u32[]{:S(2)}) copy-start(bf16[8,128,512]{2,1,0:T(8,128)(2,1)} %get-tuple-element.88.ug_ref) | copy-start | bytes 3145732
  599.5 111.4 %copy-start.18 = (bf16[4,32,2048]{2,1,0:T(8,128)(2,1)S(1)}, bf16[4,32,2048]{2,1,0:T(8,128)(2,1)}, u32[]{:S(2)}) copy-start(bf16[4,32,2048]{2,1,0:T(8,128)(2,1)} %get-tuple-element.89.down_ref) | copy-start | bytes 1572868
  622.6 1.9 copy-start.13
  712.3 1.3 copy-start.7
  713.6 51.5 %all-to-all-start.1 = ((bf16[4,4,128,512]{3,2,1,0:T(8,128)(2,1)}), bf16[4,4,128,512]{3,2,1,0:T(8,128)(2,1)S(1)}, u32[]{:S(2)}, u32[]{:S(2)}) async-start(bf16[4,4,128,512]{3,2,1,0:T(8,128)(2,1)} %bitcast.74), calls=%async_computation.1 | async-start | bytes 4194304 | tf_op jit(solution)/shard_map/all_to_all | solution.py:1884
  723.2 30.4 %copy-start.14 = (bf16[8,128,512]{2,1,0:T(8,128)(2,1)S(1)}, bf16[8,128,512]{2,1,0:T(8,128)(2,1)}, u32[]{:S(2)}) copy-start(bf16[8,128,512]{2,1,0:T(8,128)(2,1)} %get-tuple-element.73.ug_ref) | copy-start | bytes 3145732
  723.2 30.4 %copy-start.17 = (bf16[4,32,2048]{2,1,0:T(8,128)(2,1)S(1)}, bf16[4,32,2048]{2,1,0:T(8,128)(2,1)}, u32[]{:S(2)}) copy-start(bf16[4,32,2048]{2,1,0:T(8,128)(2,1)} %get-tuple-element.74.down_ref) | copy-start | bytes 1572868
  755.0 1.3 copy-start.6
  765.1 1.3 copy-start.1
  766.5 51.3 %all-to-all-start.2 = ((bf16[4,4,128,512]{3,2,1,0:T(8,128)(2,1)}), bf16[4,4,128,512]{3,2,1,0:T(8,128)(2,1)S(1)}, u32[]{:S(2)}, u32[]{:S(2)}) async-start(bf16[4,4,128,512]{3,2,1,0:T(8,128)(2,1)} %bitcast.73), calls=%async_computation.2 | async-start | bytes 4194304 | tf_op jit(solution)/shard_map/all_to_all | solution.py:1884
  772.6 1.6 copy-start.2
  774.2 26.0 %copy-start.5 = (f32[128,2048]{1,0:T(8,128)S(1)}, f32[128,2048]{1,0:T(8,128)}, u32[]{:S(2)}) copy-start(f32[128,2048]{1,0:T(8,128)} %copy-done.4) | copy-start | bytes 3145732
  774.2 26.4 %copy-start.25 = (f32[128,2048]{1,0:T(8,128)S(1)}, f32[128,2048]{1,0:T(8,128)}, u32[]{:S(2)}) copy-start(f32[128,2048]{1,0:T(8,128)} %get-tuple-element.72) | copy-start | bytes 3145732
  (5 other events, 5.3 us)

commit v11 on v10

--- a/solution.py
+++ b/solution.py
@@ -2,6 +2,7 @@
 
 import jax
 import jax.numpy as jnp
+import numpy as np
 from jax import lax
 from jax.experimental import pallas as pl
 from jax.experimental.pallas import tpu as pltpu
@@ -49,29 +50,12 @@
     return scale_inv * (upstream - upstream_mean - normed * cross_mean)
 
 
-def rope_tables(positions, head_dim):
+def rope_tables(seq_len, head_dim):
     half_dim = head_dim // 2
-    frequency = jnp.power(rope_base, -(jnp.arange(half_dim, dtype=jnp.float32) * 2.0) / head_dim)
-    angles = positions[:, None] * frequency[None, :]
-    cosine_half = jnp.cos(angles)
-    sine_half = jnp.sin(angles)
-    return (
-        jnp.concatenate([cosine_half, cosine_half], axis=-1),
-        jnp.concatenate([sine_half, sine_half], axis=-1),
-    )
-
-
-def rotate(values, cosine, sine):
-    half_dim = values.shape[-1] // 2
-    turned = jnp.concatenate([-values[..., half_dim:], values[..., :half_dim]], axis=-1)
-    return values * cosine + turned * sine
-
-
-def rotate_back(grads, cosine, sine):
-    half_dim = grads.shape[-1] // 2
-    scaled = grads * sine
-    turned = jnp.concatenate([scaled[..., half_dim:], -scaled[..., :half_dim]], axis=-1)
-    return grads * cosine + turned
+    frequency = rope_base ** (-(np.arange(half_dim) * 2.0) / head_dim)
+    angles = np.arange(seq_len)[:, None] * frequency[None, :]
+    tables = [np.concatenate([half, half], axis=-1) for half in (np.cos(angles), np.sin(angles))]
+    return [jnp.asarray(table.astype(np.float32)) for table in tables]
 
 
 def pack_kernel(n_dp, chips, first_slots, flags, m_ref, *outs):
@@ -1093,6 +1077,9 @@
             sums[0].steps()
             for later in sums[1:]:
                 later.start()
+        if step == n_dp - 2:
+            for later in sums[1:]:
+                later.steps()
 
     norm_two_grad, ff_sum = column_sums(
         x_refs, takens, sents, cames, z_send, z_recv, x_pass, x_take, between
@@ -1111,8 +1098,6 @@
         stage, tokens_out, chips, chip, core, dp_index, sibling,
         token_send, token_recv, token_pass, token_take,
     )
-    for later in sums[1:]:
-        later.steps()
     sums[0].finish()
     def fill(pair, target_ref):
         ug_ref, down_ref = pair
@@ -1336,7 +1321,10 @@
     (own_sem, a_send, a_recv, w_send, w_recv, s_pass, s_take, s_send, s_recv,
      late_send, late_recv, late_own, stage_own, side_send, side_recv, ring_send, ring_recv,
      send_sem, recv_sem, pass_sem, take_sem) = refs[29:50]
-    late_tables = refs[50:]
+    late_tables = refs[50:-2]
+    x1_hbm, x1_ref, x1_sem = x1_ref, refs[-2], refs[-1]
+    x1_copy = pltpu.make_async_copy(x1_hbm, x1_ref, x1_sem)
+    x1_copy.start()
     n_seq, n_dp, seq_index, dp_index = places()
     chips, chip, core = n_seq // 2, seq_index // 2, lax.rem(seq_index, 2)
     sibling = (dp_index, chip * 2 + 1 - core)
@@ -1518,6 +1506,7 @@
     late_start(1)
     begin_band(0)
 
+    x1_copy.wait()
     seq_len = x1_ref.shape[0]
     heads = query_out.shape[1] // HD
     block_rows = min(256, seq_len)
@@ -1597,7 +1586,7 @@
     for k in range(1, chips):
         copies[k].wait_recv()
         total = total + arrived[k].astype(f32)
-    residual = tokens_ref[...] + total
+    residual = tokens_ref[...].astype(f32) + total
     residual_out[...] = residual
     center = residual - jnp.mean(residual, axis=-1, keepdims=True)
     spread = jnp.mean(center * center, axis=-1, keepdims=True)
@@ -1685,7 +1674,8 @@
         ],
         in_specs=[pl.BlockSpec(memory_space=pltpu.SMEM), VMEM]
         + [ANY] * has_late
-        + [VMEM] * 6,
+        + [ANY]
+        + [VMEM] * 5,
         out_specs=[VMEM] * 8 + [ANY] * 4,
         scratch_shapes=[
             vmem((n_seq, sub, 3 * head_cols), bf),
@@ -1720,7 +1710,8 @@
             DMA((n_dp,)),
             DMA((n_dp,)),
         ]
-        + [vmem((n_dp, late.shape[1], sub, wide), bf) for _ in range(n_dp if has_late else 0)],
+        + [vmem((n_dp, late.shape[1], sub, wide), bf) for _ in range(n_dp if has_late else 0)]
+        + [vmem((seq_len, width), bf), DMA],
         compiler_params=comm_params(collective_id, 58),
         cost_estimate=takes(230),
         name="forward",
@@ -1768,14 +1759,14 @@
     is_col = (own_units >= 4) & (own_units < 4 + 2 * ff_blocks)
 
 
-    tokens = block_input.astype(f32).reshape(shard_len, width)
+    tokens = block_input.reshape(shard_len, width)
     packed = pack(master, is_col.astype(jnp.int32), n_dp, n_seq, first_slots)
-    first_table, normed_one_all = front(packed[0], block_input.reshape(shard_len, width), 2)
+    first_table, normed_one_all = front(packed[0], tokens, 2)
     first_table = first_table.reshape(n_dp * first_slots, rows, wide)
     normed_one_all = normed_one_all.reshape(seq_len, width)
     upstream = cotangent.reshape(shard_len, width)
     positions = jnp.arange(seq_len, dtype=jnp.int32)
-    cosine, sine = rope_tables(positions.astype(f32), HD)
+    cosine, sine = rope_tables(seq_len, HD)
     doc_ends = jnp.cumsum(doc_lengths[0])
     doc = jnp.sum((positions[:, None] >= doc_ends[None, :]).astype(jnp.int32), axis=1)
     late_slots = per_owner - first_slots

time: 852 us -> 839 us (0.985)
  Pallas kernels: 765 us -> 756 us
where the time goes in v11:
time: 839 us; the launch traced here: 833 us
  Pallas kernels  756 us (90%)
  waiting for transfers between devices  27.4 us (3%)
  local copies, waits for them, and re-layouts  21.9 us (3%)
  starting transfers between devices  12.8 us (2%)
    pallas_call x1, Pallas kernels, forward(): pl.pallas_call(functools.partial(forward_kernel, has_late, first_slots, f...  266 us
    pallas_call x1, Pallas kernels, sum_grads(): pl.pallas_call(functools.partial(grads_kernel, bands, late_slots), out_sh...  141 us
    pallas_call x1, Pallas kernels, collect_attention(): pl.pallas_call(collect_kernel, out_shape=[jax.ShapeDtypeStruct((n_seq,) +...  83.1 us
    pallas_call x1, Pallas kernels, front(): pl.pallas_call(front_kernel, out_shape=[jax.ShapeDtypeStruct(packed.shape...  76 us
    pallas_call x1, Pallas kernels, feed_forward(): pl.pallas_call(ff_kernel, out_shape=[low(count, width), low(count, width)...  68.1 us
    pallas_call x2, Pallas kernels, adam(): pl.pallas_call(functools.partial(adam_kernel, n_dp, n_seq // 2, first_slo...  49.7 us
    pallas_call x1, Pallas kernels, sum_seq(): pl.pallas_call(sum_seq_kernel, out_shape=jax.ShapeDtypeStruct((rows, colu...  30.8 us
    all_to_all x2, waiting for transfers between devices, local(): came = lax.all_to_all(send_now, 'dp', 0, 0)  27.4 us
  transfers between devices with their start and end apart: 3, of which 2 were waited for; matrix products, arithmetic and copies ran while one was open for 1% of the time, Pallas kernels for 20%

profile of v11, /device:TPU:0, one launch (start us, length us, event | category | flops | bytes accessed | tf_op | source)
XLA Modules:
  0.0 832.8 jit_solution(14531289203134039968)
XLA Ops:
  5.3 15.5 %pack.1 = (bf16[4,4,256,512]{3,2,1,0:T(8,128)(2,1)}, bf16[4,4,256,512]{3,2,1,0:T(8,128)(2,1)}) custom-call(s32[8]{0:T(128)S(1)} %fusion.13.flags, f32[256,8,2048]{2,1,0:T(8,128)} %refs_4_.4), custom_call_target="tpu_custom_call" | custom-call | tf_op jit(solution)/shard_map/pack/pallas_call | solution.py:97
  20.7 2.2 copy-done.9
  22.9 76.0 %front.1 = (bf16[4,4,256,512]{3,2,1,0:T(8,128)(2,1)S(1)}, bf16[8,128,2048]{2,1,0:T(8,128)(2,1)S(1)}) custom-call(bf16[4,4,256,512]{3,2,1,0:T(8,128)(2,1)S(1)} %copy-done.9, bf16[128,2048]{1,0:T(8,128)(2,1)S(1)} %bitcast.69), custom_call_target="tpu_custom_call" | custom-call | bytes 270000000 | tf_op jit(solution)/shard_map/front/pallas_call | solution.py:444
  98.9 2.0 copy-done.4
  100.9 2.0 copy-done.8
  103.5 265.8 %forward.1 = (bf16[8,4,64,768]{3,2,1,0:T(8,128)(2,1)}, bf16[4,64,2048]{2,1,0:T(8,128)(2,1)}, bf16[1024,256]{1,0:T(8,128)(2,1)}, bf16[1024,256]{1,0:T(8,128)(2,1)...) custom-call(s32[40]{0:T(128)} %pad_add_fusion.refs_0_, ...), custom_call_target="tpu_custom_call" | custom-call | bytes 690000000 | tf_op jit(solution)/shard_map/forward/pallas_call | solution.py:1659
  369.3 68.1 %feed_forward.1 = (bf16[1024,2048]{1,0:T(8,128)(2,1)}, bf16[1024,2048]{1,0:T(8,128)(2,1)}, bf16[1024,2048]{1,0:T(8,128)(2,1)}, bf16[2048,1024]{1,0:T(8,128)(2,1)}, bf16[2048,1024]{1,0:T(8,128)(2,1)}) custom-call(bf16[1024,2048]{1,0:T(8,128)(2,1)} %bitcast.92, bf16[2048,1024]{1,0:T(8,128)(2,1)} %bitcast.89, bf16[2048,1024]{1,0:T(8,128)(2,1)} %bitcast.90, ...), custom_call_target="tpu_custom_call" | custom-call | bytes 180000000 | tf_op jit(solution)/shard_map/feed_forward/pallas_call | solution.py:881
  437.5 141.0 %sum_grads.1 = (bf16[8,128,512]{2,1,0:T(8,128)(2,1)}, bf16[4,32,2048]{2,1,0:T(8,128)(2,1)}, bf16[8,128,512]{2,1,0:T(8,128)(2,1)}, bf16[4,32,2048]{2,1,0:T(8,128)...) custom-call(s32[16]{0:T(128)} %reshape.193.refs_0_, ...), custom_call_target="tpu_custom_call" | custom-call | bytes 390000000 | tf_op jit(solution)/shard_map/sum_grads/pallas_call | solution.py:1197
  578.5 5.0 all-to-all-start
  587.9 23.1 %attention_back.1 = (bf16[1024,768]{1,0:T(8,128)(2,1)}, bf16[2048,768]{1,0:T(8,128)(2,1)}, bf16[256,2048]{1,0:T(8,128)(2,1)}) custom-call(bf16[1024,2048]{1,0:T(8,128)(2,1)} %bitcast.88, bf16[256,2048]{1,0:T(8,128)(2,1)} %bitcast.95, bf16[1024,256]{1,0:T(8,128)(2,1)S(1)} %copy-done.19, bf16[1024,256]{1,0:T(8,128)(2,1)S(1)} %copy-done.20, ...), custom_call_target="tpu_custom_call" | custom-call | bytes 105000000 | tf_op jit(solution)/shard_map/attention_back/pallas_call | solution.py:1284
  611.0 1.9 copy-done.10
  614.1 83.1 %collect_attention.1 = (bf16[8,64,768]{2,1,0:T(8,128)(2,1)S(1)}, bf16[64,2048]{1,0:T(8,128)(2,1)S(1)}) custom-call(bf16[8,4,64,768]{3,2,1,0:T(8,128)(2,1)S(1)} %bitcast.77, bf16[4,64,2048]{2,1,0:T(8,128)(2,1)S(1)} %bitcast.78), custom_call_target="tpu_custom_call" | custom-call | bytes 225000000 | tf_op jit(solution)/shard_map/collect_attention/pallas_call | solution.py:553
  700.6 4.2 all-to-all-start.1
  704.8 5.8 convolution_convert_fusion
  710.6 30.8 %sum_seq.1 = f32[128,2048]{1,0:T(8,128)S(1)} custom-call(bf16[8,128,2048]{2,1,0:T(8,128)(2,1)S(1)} %bitcast.76), custom_call_target="tpu_custom_call" | custom-call | bytes 84000000 | tf_op jit(solution)/shard_map/sum_seq/pallas_call | solution.py:496
  741.5 1.3 arrange.2
  744.1 9.9 %all-to-all-done.1.refs_0_ = bf16[4,4,128,512]{3,2,1,0:T(8,128)(2,1)S(1)} async-done(((bf16[4,4,128,512]{3,2,1,0:T(8,128)(2,1)}), bf16[4,4,128,512]{3,2,1,0:T(8,128)(2,1)S(1)}, u32[]{:S(2)}, u32[]{:S(2)}) %all-to-all-start.1) | async-done | bytes 2097184 | tf_op jit(solution)/shard_map/all_to_all | solution.py:1875
  755.3 3.6 all-to-all-start.2
  759.0 2.5 fusion.11
  761.5 1.6 copy-done.3
  763.1 24.8 %adam.2 = (f32[256,8,2048]{2,1,0:T(8,128)}, f32[256,8,2048]{2,1,0:T(8,128)}, f32[256,8,2048]{2,1,0:T(8,128)}, f32[256,8,2048]{2,1,0:T(8,128)}) custom-call(s32[8]{0:T(128)S(1)} %get-tuple-element.111.kinds, bf16[4,4,128,512]{3,2,1,0:T(8,128)(2,1)S(1)} %copy-done.3, bf16[4,4,128,512]{3,2,1,0:T(8,128)(2,1)} %get-tuple-element.99.refs_1_, ...), custom_call_target="tpu_custom_call" | custom-call | bytes 75000000 | tf_op jit(solution)/shard_map/adam/pallas_call | solution.py:180
  788.8 1.4 fusion.9
  790.2 17.6 %all-to-all-done.2.refs_0_ = bf16[4,4,128,512]{3,2,1,0:T(8,128)(2,1)S(1)} async-done(((bf16[4,4,128,512]{3,2,1,0:T(8,128)(2,1)}), bf16[4,4,128,512]{3,2,1,0:T(8,128)(2,1)S(1)}, u32[]{:S(2)}, u32[]{:S(2)}) %all-to-all-start.2) | async-done | bytes 2097184 | tf_op jit(solution)/shard_map/all_to_all | solution.py:1875
  807.7 24.8 %adam.3 = (f32[256,8,2048]{2,1,0:T(8,128)}, f32[256,8,2048]{2,1,0:T(8,128)}, f32[256,8,2048]{2,1,0:T(8,128)}, f32[256,8,2048]{2,1,0:T(8,128)}) custom-call(s32[8]{0:T(128)S(1)} %get-tuple-element.111.kinds, bf16[4,4,128,512]{3,2,1,0:T(8,128)(2,1)S(1)} %all-to-all-done.2.refs_0_, ...), custom_call_target="tpu_custom_call", output_to_operand_aliasing={{0}: (9, {}), {1}: (10, {}), {2}: (11, {}), {3}: (12, {})} | custom-call | bytes 75000000 | tf_op jit(solution)/shard_map/adam/pallas_call | solution.py:180
  (76 shorter events, 17.6 us)
Async XLA Ops:
  4.2 16.5 %copy-start.23 = (s32[1024]{0:T(1024)}, s32[1024]{0:T(1024)S(1)}, u32[]{:S(2)}) copy-start(s32[1024]{0:T(1024)S(1)} %convert_reduce_fusion.1) | copy-start | bytes 12292
  5.2 15.5 %copy-start = (bf16[1,128,2048]{2,1,0:T(8,128)(2,1)S(1)}, bf16[1,128,2048]{2,1,0:T(8,128)(2,1)}, u32[]{:S(2)}) copy-start(bf16[1,128,2048]{2,1,0:T(8,128)(2,1)} %param.9) | copy-start | bytes 1572868
  20.7 2.2 copy-start.9
  98.9 2.0 copy-start.4
  100.9 2.0 copy-start.8
  578.5 5.2 copy-start.7
  578.5 5.2 copy-start.11
  578.5 5.2 copy-start.12
  578.5 5.2 copy-start.24
  578.5 122.0 %all-to-all-start = ((bf16[4,4,128,512]{3,2,1,0:T(8,128)(2,1)}), bf16[4,4,128,512]{3,2,1,0:T(8,128)(2,1)}, u32[]{:S(2)}, u32[]{:S(2)}) async-start(bf16[4,4,128,512]{3,2,1,0:T(8,128)(2,1)} %get-tuple-element.90), calls=%async_computation | async-start | bytes 4194304 | tf_op jit(solution)/shard_map/all_to_all | solution.py:1843
  587.9 110.0 %copy-start.14 = (bf16[8,128,512]{2,1,0:T(8,128)(2,1)S(1)}, bf16[8,128,512]{2,1,0:T(8,128)(2,1)}, u32[]{:S(2)}) copy-start(bf16[8,128,512]{2,1,0:T(8,128)(2,1)} %get-tuple-element.88.ug_ref) | copy-start | bytes 3145732
  587.9 110.0 %copy-start.17 = (bf16[4,32,2048]{2,1,0:T(8,128)(2,1)S(1)}, bf16[4,32,2048]{2,1,0:T(8,128)(2,1)}, u32[]{:S(2)}) copy-start(bf16[4,32,2048]{2,1,0:T(8,128)(2,1)} %get-tuple-element.89.down_ref) | copy-start | bytes 1572868
  611.0 1.9 copy-start.10
  699.3 1.3 copy-start.6
  700.6 53.4 %all-to-all-start.1 = ((bf16[4,4,128,512]{3,2,1,0:T(8,128)(2,1)}), bf16[4,4,128,512]{3,2,1,0:T(8,128)(2,1)S(1)}, u32[]{:S(2)}, u32[]{:S(2)}) async-start(bf16[4,4,128,512]{3,2,1,0:T(8,128)(2,1)} %bitcast.74), calls=%async_computation.1 | async-start | bytes 4194304 | tf_op jit(solution)/shard_map/all_to_all | solution.py:1875
  710.6 30.8 %copy-start.13 = (bf16[8,128,512]{2,1,0:T(8,128)(2,1)S(1)}, bf16[8,128,512]{2,1,0:T(8,128)(2,1)}, u32[]{:S(2)}) copy-start(bf16[8,128,512]{2,1,0:T(8,128)(2,1)} %get-tuple-element.73.ug_ref) | copy-start | bytes 3145732
  710.6 30.8 %copy-start.16 = (bf16[4,32,2048]{2,1,0:T(8,128)(2,1)S(1)}, bf16[4,32,2048]{2,1,0:T(8,128)(2,1)}, u32[]{:S(2)}) copy-start(bf16[4,32,2048]{2,1,0:T(8,128)(2,1)} %get-tuple-element.74.down_ref) | copy-start | bytes 1572868
  710.6 30.8 %copy-start.18 = (bf16[32,2048]{1,0:T(8,128)(2,1)S(1)}, bf16[32,2048]{1,0:T(8,128)(2,1)}, u32[]{:S(2)}) copy-start(bf16[32,2048]{1,0:T(8,128)(2,1)} %get-tuple-element.115.refs_1_) | copy-start | bytes 393220
  742.8 1.3 copy-start.5
  754.0 1.3 copy-start.2
  755.3 52.4 %all-to-all-start.2 = ((bf16[4,4,128,512]{3,2,1,0:T(8,128)(2,1)}), bf16[4,4,128,512]{3,2,1,0:T(8,128)(2,1)S(1)}, u32[]{:S(2)}, u32[]{:S(2)}) async-start(bf16[4,4,128,512]{3,2,1,0:T(8,128)(2,1)} %bitcast.73), calls=%async_computation.2 | async-start | bytes 4194304 | tf_op jit(solution)/shard_map/all_to_all | solution.py:1875
  761.5 1.6 copy-start.3
  763.1 24.8 %copy-start.1 = (bf16[1,128,2048]{2,1,0:T(8,128)(2,1)S(1)}, bf16[1,128,2048]{2,1,0:T(8,128)(2,1)}, u32[]{:S(2)}) copy-start(bf16[1,128,2048]{2,1,0:T(8,128)(2,1)} %param.9) | copy-start | bytes 1572868
  763.1 25.7 %copy-start.25 = (f32[128,2048]{1,0:T(8,128)S(1)}, f32[128,2048]{1,0:T(8,128)}, u32[]{:S(2)}) copy-start(f32[128,2048]{1,0:T(8,128)} %get-tuple-element.72) | copy-start | bytes 3145732
  (5 other events, 5.4 us)

commit v12 on v11

--- a/solution.py
+++ b/solution.py
@@ -1363,7 +1363,7 @@
     def late_start(c):
         if not has_late or c >= n_dp:
             return
-        if c:
+        if c and c < max(2, n_dp - 1):
             for copy in late_copies(c - 1):
                 copy.wait_send()
         for copy in late_copies(c):
@@ -1447,8 +1447,10 @@
             for copy in late_copies(c):
                 copy.wait_recv()
             late_own_copy(c).wait()
-            if c:
+            if c and (c + 1 < n_dp - 1 or n_dp == 3):
                 late_start(c + 1)
+            if c and c + 1 == n_dp - 2:
+                late_start(n_dp - 1)
             table = late_tables[c]
             late_slots = table.shape[1]
         for u in range(3 * ff_blocks):
@@ -1591,10 +1593,15 @@
     center = residual - jnp.mean(residual, axis=-1, keepdims=True)
     spread = jnp.mean(center * center, axis=-1, keepdims=True)
     x_stage[...] = (center * lax.rsqrt(spread + norm_eps)).astype(bf)
-    for c in range(2, n_dp):
+    for c in range(2, n_dp - 1):
         begin_band(c)
         for step in range(2, ring.last + 1):
             carry_band(c - 1, step)
+
+    def last_band():
+        begin_band(n_dp - 1)
+        for step in range(2, ring.last + 1):
+            carry_band(n_dp - 2, step)
 
     own_x = pltpu.make_async_copy(x_stage, x_all.at[core, dp_index], own_sem.at[3])
     own_x.start()
@@ -1613,9 +1620,9 @@
         send_sem,
         recv_sem,
         lambda block: onward(block).start(),
-        lambda step: carry_band(n_dp - 1, 2) if step == 1 and ring.last > 1 else None,
-    )
-    for step in range(3, ring.last + 1):
+        lambda step: last_band() if step == 1 else None,
+    )
+    for step in range(2, ring.last + 1):
         carry_band(n_dp - 1, step)
     for c in range(n_dp):
         for view in range(3):
@@ -1626,7 +1633,7 @@
         for copy in side_copies(c):
             copy.wait_send()
         if has_late:
-            if c == n_dp - 1:
+            if c >= max(1, n_dp - 2):
                 for copy in late_copies(c):
                     copy.wait_send()
     for block in range(n_dp):

time: 839 us -> 829 us (0.988)
  no operation moved by 1% of the time
where the time goes in v12:
time: 829 us; the launch traced here: 825 us
  Pallas kernels  748 us (90%)
  waiting for transfers between devices  26.9 us (3%)
  local copies, waits for them, and re-layouts  21.9 us (3%)
  starting transfers between devices  12.8 us (2%)
    pallas_call x1, Pallas kernels, forward(): pl.pallas_call(functools.partial(forward_kernel, has_late, first_slots, f...  260 us
    pallas_call x1, Pallas kernels, sum_grads(): pl.pallas_call(functools.partial(grads_kernel, bands, late_slots), out_sh...  141 us
    pallas_call x1, Pallas kernels, collect_attention(): pl.pallas_call(collect_kernel, out_shape=[jax.ShapeDtypeStruct((n_seq,) +...  83 us
    pallas_call x1, Pallas kernels, front(): pl.pallas_call(front_kernel, out_shape=[jax.ShapeDtypeStruct(packed.shape...  74.9 us
    pallas_call x1, Pallas kernels, feed_forward(): pl.pallas_call(ff_kernel, out_shape=[low(count, width), low(count, width)...  65.1 us
    pallas_call x2, Pallas kernels, adam(): pl.pallas_call(functools.partial(adam_kernel, n_dp, n_seq // 2, first_slo...  51.7 us
    pallas_call x1, Pallas kernels, sum_seq(): pl.pallas_call(sum_seq_kernel, out_shape=jax.ShapeDtypeStruct((rows, colu...  30.3 us
    all_to_all x2, waiting for transfers between devices, local(): came = lax.all_to_all(send_now, 'dp', 0, 0)  26.9 us
  transfers between devices with their start and end apart: 3, of which 2 were waited for; matrix products, arithmetic and copies ran while one was open for 1% of the time, Pallas kernels for 20%

profile of v12, /device:TPU:0, one launch (start us, length us, event | category | flops | bytes accessed | tf_op | source)
XLA Modules:
  0.0 824.7 jit_solution(17000559117169787055)
XLA Ops:
  5.3 16.3 %pack.1 = (bf16[4,4,256,512]{3,2,1,0:T(8,128)(2,1)}, bf16[4,4,256,512]{3,2,1,0:T(8,128)(2,1)}) custom-call(s32[8]{0:T(128)S(1)} %fusion.13.flags, f32[256,8,2048]{2,1,0:T(8,128)} %refs_4_.4), custom_call_target="tpu_custom_call" | custom-call | tf_op jit(solution)/shard_map/pack/pallas_call | solution.py:97
  21.5 2.2 copy-done.9
  23.7 74.9 %front.1 = (bf16[4,4,256,512]{3,2,1,0:T(8,128)(2,1)S(1)}, bf16[8,128,2048]{2,1,0:T(8,128)(2,1)S(1)}) custom-call(bf16[4,4,256,512]{3,2,1,0:T(8,128)(2,1)S(1)} %copy-done.9, bf16[128,2048]{1,0:T(8,128)(2,1)S(1)} %bitcast.69), custom_call_target="tpu_custom_call" | custom-call | bytes 270000000 | tf_op jit(solution)/shard_map/front/pallas_call | solution.py:444
  98.6 2.0 copy-done.4
  100.6 2.0 copy-done.8
  103.2 259.9 %forward.1 = (bf16[8,4,64,768]{3,2,1,0:T(8,128)(2,1)}, bf16[4,64,2048]{2,1,0:T(8,128)(2,1)}, bf16[1024,256]{1,0:T(8,128)(2,1)}, bf16[1024,256]{1,0:T(8,128)(2,1)...) custom-call(s32[40]{0:T(128)} %pad_add_fusion.refs_0_, ...), custom_call_target="tpu_custom_call" | custom-call | bytes 690000000 | tf_op jit(solution)/shard_map/forward/pallas_call | solution.py:1666
  363.1 65.1 %feed_forward.1 = (bf16[1024,2048]{1,0:T(8,128)(2,1)}, bf16[1024,2048]{1,0:T(8,128)(2,1)}, bf16[1024,2048]{1,0:T(8,128)(2,1)}, bf16[2048,1024]{1,0:T(8,128)(2,1)}, bf16[2048,1024]{1,0:T(8,128)(2,1)}) custom-call(bf16[1024,2048]{1,0:T(8,128)(2,1)} %bitcast.92, bf16[2048,1024]{1,0:T(8,128)(2,1)} %bitcast.89, bf16[2048,1024]{1,0:T(8,128)(2,1)} %bitcast.90, ...), custom_call_target="tpu_custom_call" | custom-call | bytes 180000000 | tf_op jit(solution)/shard_map/feed_forward/pallas_call | solution.py:881
  428.2 141.3 %sum_grads.1 = (bf16[8,128,512]{2,1,0:T(8,128)(2,1)}, bf16[4,32,2048]{2,1,0:T(8,128)(2,1)}, bf16[8,128,512]{2,1,0:T(8,128)(2,1)}, bf16[4,32,2048]{2,1,0:T(8,128)...) custom-call(s32[16]{0:T(128)} %reshape.193.refs_0_, ...), custom_call_target="tpu_custom_call" | custom-call | bytes 390000000 | tf_op jit(solution)/shard_map/sum_grads/pallas_call | solution.py:1197
  569.6 5.0 all-to-all-start
  578.9 23.1 %attention_back.1 = (bf16[1024,768]{1,0:T(8,128)(2,1)}, bf16[2048,768]{1,0:T(8,128)(2,1)}, bf16[256,2048]{1,0:T(8,128)(2,1)}) custom-call(bf16[1024,2048]{1,0:T(8,128)(2,1)} %bitcast.88, bf16[256,2048]{1,0:T(8,128)(2,1)} %bitcast.95, bf16[1024,256]{1,0:T(8,128)(2,1)S(1)} %copy-done.19, bf16[1024,256]{1,0:T(8,128)(2,1)S(1)} %copy-done.20, ...), custom_call_target="tpu_custom_call" | custom-call | bytes 105000000 | tf_op jit(solution)/shard_map/attention_back/pallas_call | solution.py:1284
  602.0 1.9 copy-done.10
  605.1 83.0 %collect_attention.1 = (bf16[8,64,768]{2,1,0:T(8,128)(2,1)S(1)}, bf16[64,2048]{1,0:T(8,128)(2,1)S(1)}) custom-call(bf16[8,4,64,768]{3,2,1,0:T(8,128)(2,1)S(1)} %bitcast.77, bf16[4,64,2048]{2,1,0:T(8,128)(2,1)S(1)} %bitcast.78), custom_call_target="tpu_custom_call" | custom-call | bytes 225000000 | tf_op jit(solution)/shard_map/collect_attention/pallas_call | solution.py:553
  691.5 4.2 all-to-all-start.1
  695.7 5.8 convolution_convert_fusion
  701.6 30.3 %sum_seq.1 = f32[128,2048]{1,0:T(8,128)S(1)} custom-call(bf16[8,128,2048]{2,1,0:T(8,128)(2,1)S(1)} %bitcast.76), custom_call_target="tpu_custom_call" | custom-call | bytes 84000000 | tf_op jit(solution)/shard_map/sum_seq/pallas_call | solution.py:496
  731.8 1.3 arrange.2
  734.5 10.4 %all-to-all-done.1.refs_0_ = bf16[4,4,128,512]{3,2,1,0:T(8,128)(2,1)S(1)} async-done(((bf16[4,4,128,512]{3,2,1,0:T(8,128)(2,1)}), bf16[4,4,128,512]{3,2,1,0:T(8,128)(2,1)S(1)}, u32[]{:S(2)}, u32[]{:S(2)}) %all-to-all-start.1) | async-done | bytes 2097184 | tf_op jit(solution)/shard_map/all_to_all | solution.py:1882
  746.3 3.6 all-to-all-start.2
  749.9 2.5 fusion.11
  752.4 1.6 copy-done.3
  754.0 25.9 %adam.2 = (f32[256,8,2048]{2,1,0:T(8,128)}, f32[256,8,2048]{2,1,0:T(8,128)}, f32[256,8,2048]{2,1,0:T(8,128)}, f32[256,8,2048]{2,1,0:T(8,128)}) custom-call(s32[8]{0:T(128)S(1)} %get-tuple-element.111.kinds, bf16[4,4,128,512]{3,2,1,0:T(8,128)(2,1)S(1)} %copy-done.3, bf16[4,4,128,512]{3,2,1,0:T(8,128)(2,1)} %get-tuple-element.99.refs_1_, ...), custom_call_target="tpu_custom_call" | custom-call | bytes 75000000 | tf_op jit(solution)/shard_map/adam/pallas_call | solution.py:180
  780.7 1.4 fusion.9
  782.1 16.5 %all-to-all-done.2.refs_0_ = bf16[4,4,128,512]{3,2,1,0:T(8,128)(2,1)S(1)} async-done(((bf16[4,4,128,512]{3,2,1,0:T(8,128)(2,1)}), bf16[4,4,128,512]{3,2,1,0:T(8,128)(2,1)S(1)}, u32[]{:S(2)}, u32[]{:S(2)}) %all-to-all-start.2) | async-done | bytes 2097184 | tf_op jit(solution)/shard_map/all_to_all | solution.py:1882
  798.7 25.9 %adam.3 = (f32[256,8,2048]{2,1,0:T(8,128)}, f32[256,8,2048]{2,1,0:T(8,128)}, f32[256,8,2048]{2,1,0:T(8,128)}, f32[256,8,2048]{2,1,0:T(8,128)}) custom-call(s32[8]{0:T(128)S(1)} %get-tuple-element.111.kinds, bf16[4,4,128,512]{3,2,1,0:T(8,128)(2,1)S(1)} %all-to-all-done.2.refs_0_, ...), custom_call_target="tpu_custom_call", output_to_operand_aliasing={{0}: (9, {}), {1}: (10, {}), {2}: (11, {}), {3}: (12, {})} | custom-call | bytes 75000000 | tf_op jit(solution)/shard_map/adam/pallas_call | solution.py:180
  (76 shorter events, 17.6 us)
Async XLA Ops:
  4.2 17.3 %copy-start.23 = (s32[1024]{0:T(1024)}, s32[1024]{0:T(1024)S(1)}, u32[]{:S(2)}) copy-start(s32[1024]{0:T(1024)S(1)} %convert_reduce_fusion.1) | copy-start | bytes 12292
  5.2 16.3 %copy-start = (bf16[1,128,2048]{2,1,0:T(8,128)(2,1)S(1)}, bf16[1,128,2048]{2,1,0:T(8,128)(2,1)}, u32[]{:S(2)}) copy-start(bf16[1,128,2048]{2,1,0:T(8,128)(2,1)} %param.9) | copy-start | bytes 1572868
  21.5 2.2 copy-start.9
  98.6 2.0 copy-start.4
  100.6 2.0 copy-start.8
  569.5 5.2 copy-start.7
  569.5 5.2 copy-start.11
  569.5 5.2 copy-start.12
  569.5 5.2 copy-start.24
  569.6 121.9 %all-to-all-start = ((bf16[4,4,128,512]{3,2,1,0:T(8,128)(2,1)}), bf16[4,4,128,512]{3,2,1,0:T(8,128)(2,1)}, u32[]{:S(2)}, u32[]{:S(2)}) async-start(bf16[4,4,128,512]{3,2,1,0:T(8,128)(2,1)} %get-tuple-element.90), calls=%async_computation | async-start | bytes 4194304 | tf_op jit(solution)/shard_map/all_to_all | solution.py:1850
  578.9 109.9 %copy-start.14 = (bf16[8,128,512]{2,1,0:T(8,128)(2,1)S(1)}, bf16[8,128,512]{2,1,0:T(8,128)(2,1)}, u32[]{:S(2)}) copy-start(bf16[8,128,512]{2,1,0:T(8,128)(2,1)} %get-tuple-element.88.ug_ref) | copy-start | bytes 3145732
  578.9 109.9 %copy-start.17 = (bf16[4,32,2048]{2,1,0:T(8,128)(2,1)S(1)}, bf16[4,32,2048]{2,1,0:T(8,128)(2,1)}, u32[]{:S(2)}) copy-start(bf16[4,32,2048]{2,1,0:T(8,128)(2,1)} %get-tuple-element.89.down_ref) | copy-start | bytes 1572868
  602.0 1.9 copy-start.10
  690.2 1.3 copy-start.6
  691.5 53.4 %all-to-all-start.1 = ((bf16[4,4,128,512]{3,2,1,0:T(8,128)(2,1)}), bf16[4,4,128,512]{3,2,1,0:T(8,128)(2,1)S(1)}, u32[]{:S(2)}, u32[]{:S(2)}) async-start(bf16[4,4,128,512]{3,2,1,0:T(8,128)(2,1)} %bitcast.74), calls=%async_computation.1 | async-start | bytes 4194304 | tf_op jit(solution)/shard_map/all_to_all | solution.py:1882
  701.5 30.3 %copy-start.13 = (bf16[8,128,512]{2,1,0:T(8,128)(2,1)S(1)}, bf16[8,128,512]{2,1,0:T(8,128)(2,1)}, u32[]{:S(2)}) copy-start(bf16[8,128,512]{2,1,0:T(8,128)(2,1)} %get-tuple-element.73.ug_ref) | copy-start | bytes 3145732
  701.5 30.3 %copy-start.16 = (bf16[4,32,2048]{2,1,0:T(8,128)(2,1)S(1)}, bf16[4,32,2048]{2,1,0:T(8,128)(2,1)}, u32[]{:S(2)}) copy-start(bf16[4,32,2048]{2,1,0:T(8,128)(2,1)} %get-tuple-element.74.down_ref) | copy-start | bytes 1572868
  701.5 30.3 %copy-start.18 = (bf16[32,2048]{1,0:T(8,128)(2,1)S(1)}, bf16[32,2048]{1,0:T(8,128)(2,1)}, u32[]{:S(2)}) copy-start(bf16[32,2048]{1,0:T(8,128)(2,1)} %get-tuple-element.115.refs_1_) | copy-start | bytes 393220
  733.2 1.3 copy-start.5
  744.9 1.3 copy-start.2
  746.3 52.4 %all-to-all-start.2 = ((bf16[4,4,128,512]{3,2,1,0:T(8,128)(2,1)}), bf16[4,4,128,512]{3,2,1,0:T(8,128)(2,1)S(1)}, u32[]{:S(2)}, u32[]{:S(2)}) async-start(bf16[4,4,128,512]{3,2,1,0:T(8,128)(2,1)} %bitcast.73), calls=%async_computation.2 | async-start | bytes 4194304 | tf_op jit(solution)/shard_map/all_to_all | solution.py:1882
  752.4 1.6 copy-start.3
  754.0 25.9 %copy-start.1 = (bf16[1,128,2048]{2,1,0:T(8,128)(2,1)S(1)}, bf16[1,128,2048]{2,1,0:T(8,128)(2,1)}, u32[]{:S(2)}) copy-start(bf16[1,128,2048]{2,1,0:T(8,128)(2,1)} %param.9) | copy-start | bytes 1572868
  754.0 26.7 %copy-start.25 = (f32[128,2048]{1,0:T(8,128)S(1)}, f32[128,2048]{1,0:T(8,128)}, u32[]{:S(2)}) copy-start(f32[128,2048]{1,0:T(8,128)} %get-tuple-element.72) | copy-start | bytes 3145732
  (5 other events, 5.4 us)

commit v13 on v12

--- a/solution.py
+++ b/solution.py
@@ -447,7 +447,7 @@
             jax.ShapeDtypeStruct(packed.shape, packed.dtype),
             jax.ShapeDtypeStruct((2 * chips,) + x.shape, x.dtype),
         ],
-        in_specs=[VMEM, VMEM],
+        in_specs=[ANY, VMEM],
         out_specs=[ANY, ANY],
         scratch_shapes=[pltpu.VMEM(x.shape, bf), DMA((2,)), DMA((n_dp,)), DMA((n_dp,))]
         + [DMA((chips,))] * 4,

time: 829 us -> 831 us (level)
  no operation moved by 1% of the time
where the time goes in v13:
time: 831 us; the launch traced here: 824 us
  Pallas kernels  747 us (90%)
  waiting for transfers between devices  27.2 us (3%)
  local copies, waits for them, and re-layouts  21.9 us (3%)
  starting transfers between devices  12.8 us (2%)
    pallas_call x1, Pallas kernels, forward(): pl.pallas_call(functools.partial(forward_kernel, has_late, first_slots, f...  259 us
    pallas_call x1, Pallas kernels, sum_grads(): pl.pallas_call(functools.partial(grads_kernel, bands, late_slots), out_sh...  141 us
    pallas_call x1, Pallas kernels, collect_attention(): pl.pallas_call(collect_kernel, out_shape=[jax.ShapeDtypeStruct((n_seq,) +...  83.1 us
    pallas_call x1, Pallas kernels, front(): pl.pallas_call(front_kernel, out_shape=[jax.ShapeDtypeStruct(packed.shape...  75.7 us
    pallas_call x1, Pallas kernels, feed_forward(): pl.pallas_call(ff_kernel, out_shape=[low(count, width), low(count, width)...  65.2 us
    pallas_call x2, Pallas kernels, adam(): pl.pallas_call(functools.partial(adam_kernel, n_dp, n_seq // 2, first_slo...  51.1 us
    pallas_call x1, Pallas kernels, sum_seq(): pl.pallas_call(sum_seq_kernel, out_shape=jax.ShapeDtypeStruct((rows, colu...  30.3 us
    all_to_all x2, waiting for transfers between devices, local(): came = lax.all_to_all(send_now, 'dp', 0, 0)  27.2 us
  transfers between devices with their start and end apart: 3, of which 2 were waited for; matrix products, arithmetic and copies ran while one was open for 1% of the time, Pallas kernels for 20%

profile of v13, /device:TPU:0, one launch (start us, length us, event | category | flops | bytes accessed | tf_op | source)
XLA Modules:
  0.0 824.2 jit_solution(17000559117169787055)
XLA Ops:
  5.3 15.7 %pack.1 = (bf16[4,4,256,512]{3,2,1,0:T(8,128)(2,1)}, bf16[4,4,256,512]{3,2,1,0:T(8,128)(2,1)}) custom-call(s32[8]{0:T(128)S(1)} %fusion.13.flags, f32[256,8,2048]{2,1,0:T(8,128)} %refs_4_.4), custom_call_target="tpu_custom_call" | custom-call | tf_op jit(solution)/shard_map/pack/pallas_call | solution.py:97
  21.0 2.2 copy-done.9
  23.2 75.7 %front.1 = (bf16[4,4,256,512]{3,2,1,0:T(8,128)(2,1)S(1)}, bf16[8,128,2048]{2,1,0:T(8,128)(2,1)S(1)}) custom-call(bf16[4,4,256,512]{3,2,1,0:T(8,128)(2,1)S(1)} %copy-done.9, bf16[128,2048]{1,0:T(8,128)(2,1)S(1)} %bitcast.69), custom_call_target="tpu_custom_call" | custom-call | bytes 270000000 | tf_op jit(solution)/shard_map/front/pallas_call | solution.py:444
  98.9 2.0 copy-done.4
  100.9 2.0 copy-done.8
  103.5 259.5 %forward.1 = (bf16[8,4,64,768]{3,2,1,0:T(8,128)(2,1)}, bf16[4,64,2048]{2,1,0:T(8,128)(2,1)}, bf16[1024,256]{1,0:T(8,128)(2,1)}, bf16[1024,256]{1,0:T(8,128)(2,1)...) custom-call(s32[40]{0:T(128)} %pad_add_fusion.refs_0_, ...), custom_call_target="tpu_custom_call" | custom-call | bytes 690000000 | tf_op jit(solution)/shard_map/forward/pallas_call | solution.py:1666
  362.9 65.2 %feed_forward.1 = (bf16[1024,2048]{1,0:T(8,128)(2,1)}, bf16[1024,2048]{1,0:T(8,128)(2,1)}, bf16[1024,2048]{1,0:T(8,128)(2,1)}, bf16[2048,1024]{1,0:T(8,128)(2,1)}, bf16[2048,1024]{1,0:T(8,128)(2,1)}) custom-call(bf16[1024,2048]{1,0:T(8,128)(2,1)} %bitcast.92, bf16[2048,1024]{1,0:T(8,128)(2,1)} %bitcast.89, bf16[2048,1024]{1,0:T(8,128)(2,1)} %bitcast.90, ...), custom_call_target="tpu_custom_call" | custom-call | bytes 180000000 | tf_op jit(solution)/shard_map/feed_forward/pallas_call | solution.py:881
  428.1 141.2 %sum_grads.1 = (bf16[8,128,512]{2,1,0:T(8,128)(2,1)}, bf16[4,32,2048]{2,1,0:T(8,128)(2,1)}, bf16[8,128,512]{2,1,0:T(8,128)(2,1)}, bf16[4,32,2048]{2,1,0:T(8,128)...) custom-call(s32[16]{0:T(128)} %reshape.193.refs_0_, ...), custom_call_target="tpu_custom_call" | custom-call | bytes 390000000 | tf_op jit(solution)/shard_map/sum_grads/pallas_call | solution.py:1197
  569.4 5.0 all-to-all-start
  578.7 23.1 %attention_back.1 = (bf16[1024,768]{1,0:T(8,128)(2,1)}, bf16[2048,768]{1,0:T(8,128)(2,1)}, bf16[256,2048]{1,0:T(8,128)(2,1)}) custom-call(bf16[1024,2048]{1,0:T(8,128)(2,1)} %bitcast.88, bf16[256,2048]{1,0:T(8,128)(2,1)} %bitcast.95, bf16[1024,256]{1,0:T(8,128)(2,1)S(1)} %copy-done.19, bf16[1024,256]{1,0:T(8,128)(2,1)S(1)} %copy-done.20, ...), custom_call_target="tpu_custom_call" | custom-call | bytes 105000000 | tf_op jit(solution)/shard_map/attention_back/pallas_call | solution.py:1284
  601.8 1.9 copy-done.10
  604.9 83.1 %collect_attention.1 = (bf16[8,64,768]{2,1,0:T(8,128)(2,1)S(1)}, bf16[64,2048]{1,0:T(8,128)(2,1)S(1)}) custom-call(bf16[8,4,64,768]{3,2,1,0:T(8,128)(2,1)S(1)} %bitcast.77, bf16[4,64,2048]{2,1,0:T(8,128)(2,1)S(1)} %bitcast.78), custom_call_target="tpu_custom_call" | custom-call | bytes 225000000 | tf_op jit(solution)/shard_map/collect_attention/pallas_call | solution.py:553
  691.4 4.2 all-to-all-start.1
  695.5 5.8 convolution_convert_fusion
  701.4 30.3 %sum_seq.1 = f32[128,2048]{1,0:T(8,128)S(1)} custom-call(bf16[8,128,2048]{2,1,0:T(8,128)(2,1)S(1)} %bitcast.76), custom_call_target="tpu_custom_call" | custom-call | bytes 84000000 | tf_op jit(solution)/shard_map/sum_seq/pallas_call | solution.py:496
  731.7 1.3 arrange.2
  734.4 10.4 %all-to-all-done.1.refs_0_ = bf16[4,4,128,512]{3,2,1,0:T(8,128)(2,1)S(1)} async-done(((bf16[4,4,128,512]{3,2,1,0:T(8,128)(2,1)}), bf16[4,4,128,512]{3,2,1,0:T(8,128)(2,1)S(1)}, u32[]{:S(2)}, u32[]{:S(2)}) %all-to-all-start.1) | async-done | bytes 2097184 | tf_op jit(solution)/shard_map/all_to_all | solution.py:1882
  746.1 3.6 all-to-all-start.2
  749.7 2.5 fusion.11
  752.2 1.6 copy-done.3
  753.8 25.5 %adam.2 = (f32[256,8,2048]{2,1,0:T(8,128)}, f32[256,8,2048]{2,1,0:T(8,128)}, f32[256,8,2048]{2,1,0:T(8,128)}, f32[256,8,2048]{2,1,0:T(8,128)}) custom-call(s32[8]{0:T(128)S(1)} %get-tuple-element.111.kinds, bf16[4,4,128,512]{3,2,1,0:T(8,128)(2,1)S(1)} %copy-done.3, bf16[4,4,128,512]{3,2,1,0:T(8,128)(2,1)} %get-tuple-element.99.refs_1_, ...), custom_call_target="tpu_custom_call" | custom-call | bytes 75000000 | tf_op jit(solution)/shard_map/adam/pallas_call | solution.py:180
  780.2 1.4 fusion.9
  781.6 16.9 %all-to-all-done.2.refs_0_ = bf16[4,4,128,512]{3,2,1,0:T(8,128)(2,1)S(1)} async-done(((bf16[4,4,128,512]{3,2,1,0:T(8,128)(2,1)}), bf16[4,4,128,512]{3,2,1,0:T(8,128)(2,1)S(1)}, u32[]{:S(2)}, u32[]{:S(2)}) %all-to-all-start.2) | async-done | bytes 2097184 | tf_op jit(solution)/shard_map/all_to_all | solution.py:1882
  798.5 25.5 %adam.3 = (f32[256,8,2048]{2,1,0:T(8,128)}, f32[256,8,2048]{2,1,0:T(8,128)}, f32[256,8,2048]{2,1,0:T(8,128)}, f32[256,8,2048]{2,1,0:T(8,128)}) custom-call(s32[8]{0:T(128)S(1)} %get-tuple-element.111.kinds, bf16[4,4,128,512]{3,2,1,0:T(8,128)(2,1)S(1)} %all-to-all-done.2.refs_0_, ...), custom_call_target="tpu_custom_call", output_to_operand_aliasing={{0}: (9, {}), {1}: (10, {}), {2}: (11, {}), {3}: (12, {})} | custom-call | bytes 75000000 | tf_op jit(solution)/shard_map/adam/pallas_call | solution.py:180
  (76 shorter events, 17.6 us)
Async XLA Ops:
  4.2 16.8 %copy-start.23 = (s32[1024]{0:T(1024)}, s32[1024]{0:T(1024)S(1)}, u32[]{:S(2)}) copy-start(s32[1024]{0:T(1024)S(1)} %convert_reduce_fusion.1) | copy-start | bytes 12292
  5.2 15.7 %copy-start = (bf16[1,128,2048]{2,1,0:T(8,128)(2,1)S(1)}, bf16[1,128,2048]{2,1,0:T(8,128)(2,1)}, u32[]{:S(2)}) copy-start(bf16[1,128,2048]{2,1,0:T(8,128)(2,1)} %param.9) | copy-start | bytes 1572868
  21.0 2.2 copy-start.9
  98.9 2.0 copy-start.4
  100.9 2.0 copy-start.8
  569.4 5.2 copy-start.7
  569.4 5.2 copy-start.11
  569.4 5.2 copy-start.12
  569.4 5.2 copy-start.24
  569.4 122.0 %all-to-all-start = ((bf16[4,4,128,512]{3,2,1,0:T(8,128)(2,1)}), bf16[4,4,128,512]{3,2,1,0:T(8,128)(2,1)}, u32[]{:S(2)}, u32[]{:S(2)}) async-start(bf16[4,4,128,512]{3,2,1,0:T(8,128)(2,1)} %get-tuple-element.90), calls=%async_computation | async-start | bytes 4194304 | tf_op jit(solution)/shard_map/all_to_all | solution.py:1850
  578.7 110.0 %copy-start.14 = (bf16[8,128,512]{2,1,0:T(8,128)(2,1)S(1)}, bf16[8,128,512]{2,1,0:T(8,128)(2,1)}, u32[]{:S(2)}) copy-start(bf16[8,128,512]{2,1,0:T(8,128)(2,1)} %get-tuple-element.88.ug_ref) | copy-start | bytes 3145732
  578.7 110.0 %copy-start.17 = (bf16[4,32,2048]{2,1,0:T(8,128)(2,1)S(1)}, bf16[4,32,2048]{2,1,0:T(8,128)(2,1)}, u32[]{:S(2)}) copy-start(bf16[4,32,2048]{2,1,0:T(8,128)(2,1)} %get-tuple-element.89.down_ref) | copy-start | bytes 1572868
  601.8 1.9 copy-start.10
  690.0 1.3 copy-start.6
  691.4 53.4 %all-to-all-start.1 = ((bf16[4,4,128,512]{3,2,1,0:T(8,128)(2,1)}), bf16[4,4,128,512]{3,2,1,0:T(8,128)(2,1)S(1)}, u32[]{:S(2)}, u32[]{:S(2)}) async-start(bf16[4,4,128,512]{3,2,1,0:T(8,128)(2,1)} %bitcast.74), calls=%async_computation.1 | async-start | bytes 4194304 | tf_op jit(solution)/shard_map/all_to_all | solution.py:1882
  701.4 30.3 %copy-start.13 = (bf16[8,128,512]{2,1,0:T(8,128)(2,1)S(1)}, bf16[8,128,512]{2,1,0:T(8,128)(2,1)}, u32[]{:S(2)}) copy-start(bf16[8,128,512]{2,1,0:T(8,128)(2,1)} %get-tuple-element.73.ug_ref) | copy-start | bytes 3145732
  701.4 30.3 %copy-start.16 = (bf16[4,32,2048]{2,1,0:T(8,128)(2,1)S(1)}, bf16[4,32,2048]{2,1,0:T(8,128)(2,1)}, u32[]{:S(2)}) copy-start(bf16[4,32,2048]{2,1,0:T(8,128)(2,1)} %get-tuple-element.74.down_ref) | copy-start | bytes 1572868
  701.4 30.3 %copy-start.18 = (bf16[32,2048]{1,0:T(8,128)(2,1)S(1)}, bf16[32,2048]{1,0:T(8,128)(2,1)}, u32[]{:S(2)}) copy-start(bf16[32,2048]{1,0:T(8,128)(2,1)} %get-tuple-element.115.refs_1_) | copy-start | bytes 393220
  733.0 1.3 copy-start.5
  744.8 1.3 copy-start.2
  746.1 52.4 %all-to-all-start.2 = ((bf16[4,4,128,512]{3,2,1,0:T(8,128)(2,1)}), bf16[4,4,128,512]{3,2,1,0:T(8,128)(2,1)S(1)}, u32[]{:S(2)}, u32[]{:S(2)}) async-start(bf16[4,4,128,512]{3,2,1,0:T(8,128)(2,1)} %bitcast.73), calls=%async_computation.2 | async-start | bytes 4194304 | tf_op jit(solution)/shard_map/all_to_all | solution.py:1882
  752.2 1.6 copy-start.3
  753.8 25.6 %copy-start.1 = (bf16[1,128,2048]{2,1,0:T(8,128)(2,1)S(1)}, bf16[1,128,2048]{2,1,0:T(8,128)(2,1)}, u32[]{:S(2)}) copy-start(bf16[1,128,2048]{2,1,0:T(8,128)(2,1)} %param.9) | copy-start | bytes 1572868
  753.8 26.4 %copy-start.25 = (f32[128,2048]{1,0:T(8,128)S(1)}, f32[128,2048]{1,0:T(8,128)}, u32[]{:S(2)}) copy-start(f32[128,2048]{1,0:T(8,128)} %get-tuple-element.72) | copy-start | bytes 3145732
  (5 other events, 5.4 us)
